TPU v7x, 32 devices: a whole 2x2x4 slice. The times are simulated.
32 devices in a mesh: dp: 16 (over z, x, core), tensor: 2 (over y).
Axes of the slice: x: 2, y: 2, z: 4, core: 2. Of those that a mesh axis runs over, the one named last changes fastest.
Arguments:
- tokens: bfloat16 [32768, 1024], P(('dp', 'tensor')), may hold values from -6 to 6
- lengths: int32 [16, 4], P('dp'), may hold values from 64 to 1280, as said below
- attn_gain: float32 [1024], replicated, may hold values from 0.1 to 1.9
- w_query: bfloat16 [1024, 1024], P(None, 'tensor'), may hold values from -0.375 to 0.375
- w_kv: bfloat16 [1024, 256], P(None, 'tensor'), may hold values from -0.1875 to 0.1875
- w_rope: bfloat16 [1024, 32], replicated, may hold values from -0.1875 to 0.1875
- w_out: bfloat16 [1024, 1024], P('tensor'), may hold values from -1 to 1
- mlp_gain: float32 [1024], replicated, may hold values from 0.1 to 1.9
- w_gate: bfloat16 [1024, 2816], P(None, 'tensor'), may hold values from -0.1875 to 0.1875
- w_up: bfloat16 [1024, 2816], P(None, 'tensor'), may hold values from -0.1875 to 0.1875
- w_down: bfloat16 [2816, 1024], P('tensor'), may hold values from -0.21875 to 0.21875
- out_grad: bfloat16 [32768, 1024], P(('dp', 'tensor')), may hold values from -6 to 6
Outputs:
- layer_out: bfloat16 [32768, 1024], P(('dp', 'tensor'))
- tokens_grad: bfloat16 [32768, 1024], P(('dp', 'tensor'))
- attn_gain_grad: float32 [1024], replicated
- w_query_grad: float32 [1024, 1024], P(None, 'tensor')
- w_kv_grad: float32 [1024, 256], P(None, 'tensor')
- w_rope_grad: float32 [1024, 32], replicated
- w_out_grad: float32 [1024, 1024], P('tensor')
- mlp_gain_grad: float32 [1024], replicated
- w_gate_grad: float32 [1024, 2816], P(None, 'tensor')
- w_up_grad: float32 [1024, 2816], P(None, 'tensor')
- w_down_grad: float32 [2816, 1024], P('tensor')
Inputs may be any that keep to these rules, and one draw needn't show every extreme that they name: `lengths`: each group has one sequence of exactly 1280 tokens at a place drawn from the seed and one of exactly 64; the others have 64 to 256; the rest of the group's slots are padding.
All inputs are finite; a program needn't handle non-finite values.
Results may differ from a plain program's by a relative error of at most 0.02.
Values may be sent and summed in bfloat16 or wider, within the bound.
No kernel may reach another device: no remote copies, remote signals or barrier semaphores. Data moves between devices by JAX's collectives and lax.ppermute only.
A program may use at most 256 MiB of HBM per device.

v0:
```python
import jax
import jax.numpy as jnp
from jax import lax
from jax.sharding import PartitionSpec as P

eps_norm = 1e-05
masked_score = -1e30
highest = lax.Precision.HIGHEST


def layout(lengths_row, slots):
    slot = jnp.arange(slots, dtype=jnp.int32)
    ends = jnp.cumsum(lengths_row)
    passed = (slot[:, None] >= ends[None, :]).astype(jnp.int32)
    segment = jnp.sum(passed, axis=1)
    begin = jnp.sum(passed * lengths_row[None, :], axis=1)
    valid = (segment < lengths_row.shape[0]).astype(jnp.float32)
    return (slot, segment, (slot - begin).astype(jnp.float32), valid)


def angles(position, width):
    half = width // 2
    freq = 10000.0 ** (-jnp.arange(half, dtype=jnp.float32) / half)
    angle = position[:, None] * freq[None, :]
    return (jnp.cos(angle), jnp.sin(angle))


def rotate(values, cosine, sine):
    half = values.shape[-1] // 2
    first = values[..., :half]
    second = values[..., half:]
    return jnp.concatenate(
        [first * cosine - second * sine, first * sine + second * cosine], axis=-1
    )


def rms_parts(values):
    factor = lax.rsqrt(jnp.mean(values * values, axis=-1, keepdims=True) + eps_norm)
    return (values * factor, factor)


def norm_back(grad, normed, factor, gain):
    inner = grad * gain
    return factor * (inner - normed * jnp.mean(inner * normed, axis=-1, keepdims=True))


def reduce_mlp(grads):
    parts = (
        lax.psum_scatter(grads[0], "dp", scatter_dimension=0, tiled=True),
        lax.psum_scatter(grads[1], "dp", scatter_dimension=0, tiled=True),
        lax.psum_scatter(grads[2], "dp", scatter_dimension=0, tiled=True),
    )
    return (
        lax.all_gather(parts[0].astype(jnp.bfloat16), "dp", axis=0, tiled=True).astype(jnp.float32),
        lax.all_gather(parts[1].astype(jnp.bfloat16), "dp", axis=0, tiled=True).astype(jnp.float32),
        lax.all_gather(parts[2].astype(jnp.bfloat16), "dp", axis=0, tiled=True).astype(jnp.float32),
    )


def body(
    tokens,
    lengths,
    attn_gain,
    w_query,
    w_kv,
    w_rope,
    w_out,
    mlp_gain,
    w_gate,
    w_up,
    w_down,
    out_grad,
):
    f32 = jnp.float32
    bf16 = jnp.bfloat16
    own_rows = tokens.shape[0]
    slots = own_rows * lax.axis_size("tensor")
    half = w_rope.shape[1]
    head_size = half * 2
    local_groups = w_kv.shape[1] // head_size
    per_group = w_query.shape[1] // w_kv.shape[1]
    slot, segment, position, valid = layout(lengths[0], slots)
    cosine, sine = angles(position, half)
    inputs = tokens.astype(f32)
    normed_one, factor_one = rms_parts(inputs)
    first_in = lax.all_gather((normed_one * attn_gain).astype(bf16), "tensor", axis=0, tiled=True)
    query_raw = jnp.dot(first_in, w_query, preferred_element_type=f32).reshape(
        slots, local_groups, per_group, head_size
    )
    query = jnp.concatenate(
        [
            query_raw[..., :half],
            rotate(query_raw[..., half:], cosine[:, None, None, :], sine[:, None, None, :]),
        ],
        axis=-1,
    ).astype(bf16)
    shared = rotate(jnp.dot(first_in, w_rope, preferred_element_type=f32), cosine, sine).astype(
        bf16
    )
    tied = (
        jnp.dot(first_in, w_kv, preferred_element_type=f32)
        .astype(bf16)
        .reshape(slots, local_groups, head_size)
    )
    key = jnp.concatenate(
        [tied[..., :half], jnp.broadcast_to(shared[:, None, :], (slots, local_groups, half))],
        axis=-1,
    )
    block = min(512, slots)
    blocks = slots // block
    query_blocks = query.reshape(blocks, block, local_groups, per_group, head_size)
    slot_blocks = slot.reshape(blocks, block)
    seg_blocks = segment.reshape(blocks, block)
    factor = head_size ** (-0.5)

    def scores_of(query_block, rows_block, seg_block):
        scores = jnp.einsum("bgjd,kgd->gjbk", query_block, key, preferred_element_type=f32) * factor
        allowed = (seg_block[:, None] == segment[None, :]) & (slot[None, :] <= rows_block[:, None])
        return jnp.where(allowed, scores, masked_score)

    def forward_block(items):
        query_block, rows_block, seg_block = items
        scores = scores_of(query_block, rows_block, seg_block)
        top = jnp.max(scores, axis=-1, keepdims=True)
        weights = jnp.exp(scores - top)
        total = jnp.sum(weights, axis=-1, keepdims=True)
        probs = (weights / total).astype(bf16)
        output = jnp.einsum("gjbk,kgd->bgjd", probs, tied, preferred_element_type=f32)
        return (output, (top + jnp.log(total))[..., 0])

    mixed, log_totals = lax.map(forward_block, (query_blocks, slot_blocks, seg_blocks))
    mixed = (mixed.reshape(slots, -1) * valid[:, None]).astype(bf16)
    middle = inputs + lax.psum_scatter(
        jnp.dot(mixed, w_out, preferred_element_type=f32).astype(jnp.bfloat16),
        "tensor",
        scatter_dimension=0,
        tiled=True,
    ).astype(jnp.float32)
    normed_two, factor_two = rms_parts(middle)
    second_in = lax.all_gather((normed_two * mlp_gain).astype(bf16), "tensor", axis=0, tiled=True)
    gate = jnp.dot(second_in, w_gate, preferred_element_type=f32)
    upward = jnp.dot(second_in, w_up, preferred_element_type=f32)
    hidden = (jax.nn.silu(gate) * upward).astype(bf16)
    layer_out = (
        middle
        + lax.psum_scatter(
            jnp.dot(hidden, w_down, preferred_element_type=f32).astype(jnp.bfloat16),
            "tensor",
            scatter_dimension=0,
            tiled=True,
        ).astype(jnp.float32)
    ).astype(bf16)
    back_out = lax.all_gather(out_grad, "tensor", axis=0, tiled=True)
    hidden_grad = jnp.einsum("sd,fd->sf", back_out, w_down, preferred_element_type=f32)
    sigmoid_gate = jax.nn.sigmoid(gate)
    gate_grad = (hidden_grad * upward * sigmoid_gate * (1.0 + gate * (1.0 - sigmoid_gate))).astype(
        bf16
    )
    up_grad = (hidden_grad * gate * sigmoid_gate).astype(bf16)
    w_down_grad = jnp.einsum("sf,sd->fd", hidden, back_out, preferred_element_type=f32)
    w_gate_grad = jnp.einsum("sd,sf->df", second_in, gate_grad, preferred_element_type=f32)
    w_up_grad = jnp.einsum("sd,sf->df", second_in, up_grad, preferred_element_type=f32)
    pending = (w_gate_grad, w_up_grad, w_down_grad)
    second_grad = lax.psum_scatter(
        (
            jnp.einsum("sf,df->sd", gate_grad, w_gate, preferred_element_type=f32)
            + jnp.einsum("sf,df->sd", up_grad, w_up, preferred_element_type=f32)
        ).astype(jnp.bfloat16),
        "tensor",
        scatter_dimension=0,
        tiled=True,
    ).astype(jnp.float32)
    mlp_gain_part = jnp.sum(second_grad * normed_two, axis=0)
    middle_grad = out_grad.astype(f32) + norm_back(second_grad, normed_two, factor_two, mlp_gain)
    attn_back = lax.all_gather(middle_grad.astype(bf16), "tensor", axis=0, tiled=True)
    w_out_grad = jnp.einsum("sh,sd->hd", mixed, attn_back, preferred_element_type=f32)
    mixed_grad = jnp.einsum("sd,hd->sh", attn_back, w_out, preferred_element_type=f32).astype(
        bf16
    ) * valid[:, None].astype(bf16)
    grad_blocks = mixed_grad.reshape(blocks, block, local_groups, per_group, head_size)

    def backward_block(carry, items):
        key_grad, value_grad = carry
        query_block, rows_block, seg_block, log_block, grad_block = items
        scores = scores_of(query_block, rows_block, seg_block)
        weights = jnp.exp(scores - log_block[..., None])
        weight_grad = jnp.einsum("bgjd,kgd->gjbk", grad_block, tied, preferred_element_type=f32)
        score_grad = (
            weights * (weight_grad - jnp.sum(weights * weight_grad, axis=-1, keepdims=True))
        ).astype(bf16)
        value_grad = value_grad + jnp.einsum(
            "gjbk,bgjd->kgd", weights.astype(bf16), grad_block, preferred_element_type=f32
        )
        key_grad = (
            key_grad
            + jnp.einsum("gjbk,bgjd->kgd", score_grad, query_block, preferred_element_type=f32)
            * factor
        )
        query_grad = (
            jnp.einsum("gjbk,kgd->bgjd", score_grad, key, preferred_element_type=f32) * factor
        )
        return ((key_grad, value_grad), query_grad)

    empty = jnp.zeros((slots, local_groups, head_size), f32)
    (key_grad, value_grad), query_grad = lax.scan(
        backward_block,
        (empty, empty),
        (query_blocks, slot_blocks, seg_blocks, log_totals, grad_blocks),
    )
    query_grad = query_grad.reshape(slots, local_groups, per_group, head_size)
    query_grad = (
        jnp.concatenate(
            [
                query_grad[..., :half],
                rotate(query_grad[..., half:], cosine[:, None, None, :], -sine[:, None, None, :]),
            ],
            axis=-1,
        )
        .astype(bf16)
        .reshape(slots, -1)
    )
    tied_grad = (
        (
            value_grad
            + jnp.concatenate([key_grad[..., :half], jnp.zeros_like(key_grad[..., half:])], axis=-1)
        )
        .astype(bf16)
        .reshape(slots, -1)
    )
    shared_grad = rotate(jnp.sum(key_grad[..., half:], axis=1), cosine, -sine)
    w_query_grad = jnp.einsum("sd,sh->dh", first_in, query_grad, preferred_element_type=f32)
    w_kv_grad = jnp.einsum("sd,sh->dh", first_in, tied_grad, preferred_element_type=f32)
    w_rope_grad = jnp.einsum("sd,sr->dr", first_in.astype(f32), shared_grad, precision=highest)
    rope_weight = w_rope.astype(f32)
    total = jnp.einsum("sh,dh->sd", query_grad, w_query, preferred_element_type=f32)
    total = total + jnp.einsum("sh,dh->sd", tied_grad, w_kv, preferred_element_type=f32)
    first_grad = lax.psum_scatter(
        (total + jnp.einsum("sr,dr->sd", shared_grad, rope_weight, precision=highest)).astype(
            jnp.bfloat16
        ),
        "tensor",
        scatter_dimension=0,
        tiled=True,
    ).astype(jnp.float32)
    attn_gain_part = jnp.sum(first_grad * normed_one, axis=0)
    tokens_grad = (middle_grad + norm_back(first_grad, normed_one, factor_one, attn_gain)).astype(
        bf16
    )
    pending = reduce_mlp(pending)
    shared_sums = lax.psum((attn_gain_part, mlp_gain_part, w_rope_grad), ("dp", "tensor"))
    attention = lax.psum((w_query_grad, w_kv_grad, w_out_grad), "dp")
    return (
        layer_out,
        tokens_grad,
        shared_sums[0],
        attention[0],
        attention[1],
        shared_sums[2],
        attention[2],
        shared_sums[1],
        pending[0],
        pending[1],
        pending[2],
    )


def solution(mesh):
    placed = (
        P(("dp", "tensor"), None),
        P("dp", None),
        P(),
        P(None, "tensor"),
        P(None, "tensor"),
        P(),
        P("tensor", None),
        P(),
        P(None, "tensor"),
        P(None, "tensor"),
        P("tensor", None),
        P(("dp", "tensor"), None),
    )
    return jax.shard_map(
        body,
        mesh=mesh,
        in_specs=placed,
        out_specs=(
            P(("dp", "tensor"), None),
            P(("dp", "tensor"), None),
            P(),
            P(None, "tensor"),
            P(None, "tensor"),
            P(),
            P("tensor", None),
            P(),
            P(None, "tensor"),
            P(None, "tensor"),
            P("tensor", None),
        ),
        check_vma=False,
    )
```

profile of v0, /device:TPU:0, one launch (start us, length us, event | category | flops | bytes accessed | tf_op | source)
XLA Modules:
  0.0 1924.4 jit_solution(15029775902620121485)
XLA Ops:
  15.2 58.0 %all-gather.8.cloned.1.call-done = bf16[2048,1024]{1,0:T(8,128)(2,1)} async-done(((bf16[1024,1024]{1,0:T(8,128)(2,1)}), bf16[2048,1024]{1,0:T(8,128)(2,1)}) %all-gather.8.cloned.1.call-update) | async-done | bytes 4194320 | tf_op jit(solution)/shard_map/all_gather | solution.py:86
  104.7 293.9 %while.28 = (s32[]{:T(128)}, f32[4,512,2,4,64]{1,0,4,3,2:T(4,128)}, f32[4,2,4,512]{3,2,1,0:T(4,128)}, s32[4,512]{1,0:T(4,128)S(1)}, s32[2048]{0:T(1024)S(1)}, /*...) while((s32[]{:T(128)}, f32[4,512,2,4,64]{1,0,4,3,2:T(4,128)}, ...), condition=%wide.region_7.8_spmd.clone, body=%wide.region_4.7_spmd.clone.sunk | while | flops 2251288576 | bytes 116019360 | solution.py:131
  107.1 15.2 bitcast_reduce_fusion.2
  122.3 15.0 fusion.167
  137.3 16.2 fusion.168
  157.4 21.1 %dynamic_update_slice.19 = f32[4,512,2,4,64]{1,0,4,3,2:T(4,128)} dynamic-update-slice(f32[4,512,2,4,64]{1,0,4,3,2:T(4,128)} %get-tuple-element.488, f32[1,512,2,4,64]{1,0,4,3,2:T(1,128)} %copy.58, s32[]{:T(128)S(6)} %copy.66, s32[]{:T(128)} %constant.67.clone.1..sunk, s32[]{:T(128)} %constant.67.clone.1..sunk, s32[]{:T(128)} %constant.67.clone.1..sunk, s32[]{:T(128)} %constant.67.clone.1..sunk) | dynamic-update-slice | bytes 2097156 | tf_op jit(solution)/shard_map/while/body/jit(dynamic_update_index_in_dim)/dynamic_update_slice | solution.py:131
  180.4 15.2 bitcast_reduce_fusion.2
  195.6 15.0 fusion.167
  210.6 16.2 fusion.168
  230.8 21.1 %dynamic_update_slice.19 = f32[4,512,2,4,64]{1,0,4,3,2:T(4,128)} dynamic-update-slice(f32[4,512,2,4,64]{1,0,4,3,2:T(4,128)} %get-tuple-element.488, f32[1,512,2,4,64]{1,0,4,3,2:T(1,128)} %copy.58, s32[]{:T(128)S(6)} %copy.66, s32[]{:T(128)} %constant.67.clone.1..sunk, s32[]{:T(128)} %constant.67.clone.1..sunk, s32[]{:T(128)} %constant.67.clone.1..sunk, s32[]{:T(128)} %constant.67.clone.1..sunk) | dynamic-update-slice | bytes 2097156 | tf_op jit(solution)/shard_map/while/body/jit(dynamic_update_index_in_dim)/dynamic_update_slice | solution.py:131
  253.8 15.2 bitcast_reduce_fusion.2
  269.0 15.0 fusion.167
  284.0 16.2 fusion.168
  304.1 21.1 %dynamic_update_slice.19 = f32[4,512,2,4,64]{1,0,4,3,2:T(4,128)} dynamic-update-slice(f32[4,512,2,4,64]{1,0,4,3,2:T(4,128)} %get-tuple-element.488, f32[1,512,2,4,64]{1,0,4,3,2:T(1,128)} %copy.58, s32[]{:T(128)S(6)} %copy.66, s32[]{:T(128)} %constant.67.clone.1..sunk, s32[]{:T(128)} %constant.67.clone.1..sunk, s32[]{:T(128)} %constant.67.clone.1..sunk, s32[]{:T(128)} %constant.67.clone.1..sunk) | dynamic-update-slice | bytes 2097156 | tf_op jit(solution)/shard_map/while/body/jit(dynamic_update_index_in_dim)/dynamic_update_slice | solution.py:131
  327.1 15.2 bitcast_reduce_fusion.2
  342.3 15.0 fusion.167
  357.3 16.2 fusion.168
  377.4 21.1 %dynamic_update_slice.19 = f32[4,512,2,4,64]{1,0,4,3,2:T(4,128)} dynamic-update-slice(f32[4,512,2,4,64]{1,0,4,3,2:T(4,128)} %get-tuple-element.488, f32[1,512,2,4,64]{1,0,4,3,2:T(1,128)} %copy.58, s32[]{:T(128)S(6)} %copy.66, s32[]{:T(128)} %constant.67.clone.1..sunk, s32[]{:T(128)} %constant.67.clone.1..sunk, s32[]{:T(128)} %constant.67.clone.1..sunk, s32[]{:T(128)} %constant.67.clone.1..sunk) | dynamic-update-slice | bytes 2097156 | tf_op jit(solution)/shard_map/while/body/jit(dynamic_update_index_in_dim)/dynamic_update_slice | solution.py:131
  409.4 54.4 %reduce-scatter.8.cloned.1.call-done = bf16[1024,1024]{1,0:T(8,128)(2,1)} async-done(((bf16[2048,1024]{1,0:T(8,128)(2,1)}), bf16[1024,1024]{1,0:T(8,128)(2,1)}) %reduce-scatter.8.cloned.1.call-update) | async-done | bytes 2097168 | tf_op jit(solution)/shard_map/reduce_scatter | solution.py:133
  470.0 56.3 %all-gather.10.cloned.1.call-done = bf16[2048,1024]{1,0:T(8,128)(2,1)} async-done(((bf16[1024,1024]{1,0:T(8,128)(2,1)}), bf16[2048,1024]{1,0:T(8,128)(2,1)}) %all-gather.10.cloned.1.call-update) | async-done | bytes 4194320 | tf_op jit(solution)/shard_map/all_gather | solution.py:140
  526.3 12.1 fusion.97
  538.5 9.3 fusion.96
  547.8 36.8 %all-gather.12.cloned.1.call-done = bf16[2048,1024]{1,0:T(8,128)(2,1)} async-done(((bf16[1024,1024]{1,0:T(8,128)(2,1)}), bf16[2048,1024]{1,0:T(8,128)(2,1)}) %all-gather.12.cloned.1.call-update) | async-done | bytes 4194320 | tf_op jit(solution)/shard_map/all_gather | solution.py:153
  584.6 20.5 %multiply_convert_fusion = (bf16[2048,1408]{1,0:T(8,128)(2,1)}, bf16[2048,1408]{1,0:T(8,128)(2,1)}, bf16[2048,1408]{1,0:T(8,128)(2,1)}) fusion(f32[2048,1408]{1,0:T(8,128)} %fusion.96, f32[2048,1408]{1,0:T(8,128)} %fusion.97, bf16[2048,1024]{1,0:T(8,128)(2,1)} %all-gather.12.cloned.1.call-done, bf16[1408,1024]{1,0:T(8,128)(2,1)S(1)} %copy-done), kind=kOutput, calls=%fused_computation.65 | convolution fusion | flops 5951717376 | bytes 47448064 | tf_op jit(solution)/shard_map/sd,fd->sf/dot_general | solution.py:154
  605.1 9.7 fusion.98
  623.5 11.3 fusion.105
  634.9 11.8 fusion.103
  646.8 11.8 fusion.104
  659.2 18.8 reduce-scatter.12.cloned.1.call-done
  688.0 75.3 %reduce-scatter.20.cloned.1.call-done = f32[88,1024]{1,0:T(8,128)} async-done(((f32[1408,1024]{1,0:T(8,128)}), f32[88,1024]{1,0:T(8,128)}) %reduce-scatter.20.cloned.1.call-update) | async-done | bytes 360464 | tf_op jit(solution)/shard_map/reduce_scatter | solution.py:51
  765.0 82.9 %reduce-scatter.16.cloned.1.call-done = f32[64,1408]{1,0:T(8,128)} async-done(((f32[1024,1408]{1,0:T(8,128)}), f32[64,1408]{1,0:T(8,128)}) %reduce-scatter.16.cloned.1.call-update) | async-done | bytes 360464 | tf_op jit(solution)/shard_map/reduce_scatter | solution.py:49
  849.7 83.5 %reduce-scatter.18.cloned.1.call-done = f32[64,1408]{1,0:T(8,128)} async-done(((f32[1024,1408]{1,0:T(8,128)}), f32[64,1408]{1,0:T(8,128)}) %reduce-scatter.18.cloned.1.call-update) | async-done | bytes 360464 | tf_op jit(solution)/shard_map/reduce_scatter | solution.py:50
  934.9 56.3 %all-gather.14.cloned.1.call-done = bf16[2048,1024]{1,0:T(8,128)(2,1)} async-done(((bf16[1024,1024]{1,0:T(8,128)(2,1)}), bf16[2048,1024]{1,0:T(8,128)(2,1)}) %all-gather.14.cloned.1.call-update) | async-done | bytes 4194320 | tf_op jit(solution)/shard_map/all_gather | solution.py:175
  1014.6 513.9 %while.29 = (s32[]{:T(128)}, f32[2048,2,64]{0,2,1:T(8,128)}, f32[2048,2,64]{0,2,1:T(8,128)}, f32[4,512,2,4,64]{1,0,4,3,2:T(4,128)}, bf16[4,512,2,4,64]{1,4,3,2,0...) while((s32[]{:T(128)}, f32[2048,2,64]{0,2,1:T(8,128)}, ...), condition=%wide.region_15.16_spmd.clone, body=%wide.region_13.15_spmd.clone.sunk | while | flops 5499252736 | bytes 357175616 | solution.py:205
  1017.5 17.5 fusion.177
  1034.9 15.1 fusion.182
  1050.1 24.4 %fusion.179 = (f32[2,4,512]{2,1,0:T(4,128)S(1)}, f32[2,512,4,2048]{3,1,2,0:T(8,128)}) fusion(f32[2,512,4,2048]{3,1,2,0:T(8,128)} %fusion.177, f32[2,4,512]{2,1,0:T(4,128)S(1)} %dynamic-slice_bitcast_fusion.2, pred[512,2048]{1,0:T(8,128)(4,1)S(1)} %fusion.178, bf16[2048,2,64]{0,2,1:T(8,128)(2,1)} %get-tuple-element.548, ...), kind=kOutput, calls=%fused_computation.25.clone.1 | convolution fusion | flops 1115680768 | bytes 69238784 | tf_op jit(solution)/shard_map/while/body/eval_jaxpr/bgjd,kgd->gjbk/dot_general | solution.py:187
  1074.5 28.7 %fusion.180 = bf16[2,4,512,2048]{3,2,1,0:T(8,128)(2,1)} fusion(f32[2,512,4,2048]{3,1,2,0:T(8,128)} %get-tuple-element.474, f32[2,512,4,2048]{3,1,2,0:T(8,128)} %fusion.177, f32[2,4,512]{2,1,0:T(4,128)S(1)} %get-tuple-element.475, f32[2,4,512]{2,1,0:T(4,128)S(1)} %dynamic-slice_bitcast_fusion.2, pred[512,2048]{1,0:T(8,128)(4,1)} %copy-done.2), kind=kLoop, calls=%fused_computation.27.clone.1 | loop fusion | flops 50331648 | bytes 84967424 | tf_op jit(solution)/shard_map/while/body/eval_jaxpr/convert_element_type | solution.py:190
  1103.2 10.2 fusion.181
  1122.9 21.1 %dynamic_update_slice.20 = f32[4,512,2,4,64]{1,0,4,3,2:T(4,128)} dynamic-update-slice(f32[4,512,2,4,64]{1,0,4,3,2:T(4,128)} %get-tuple-element.526, f32[1,512,2,4,64]{1,0,4,3,2:T(1,128)} %copy.59, s32[]{:T(128)S(6)} %copy.76, s32[]{:T(128)} %constant.67.clone.1..sunk.1, s32[]{:T(128)} %constant.67.clone.1..sunk.1, s32[]{:T(128)} %constant.67.clone.1..sunk.1, s32[]{:T(128)} %constant.67.clone.1..sunk.1) | dynamic-update-slice | bytes 2097156 | tf_op jit(solution)/shard_map/while/body/jit(dynamic_update_index_in_dim)/dynamic_update_slice | solution.py:131
  1146.7 17.2 fusion.177
  1163.9 15.0 fusion.182
  1178.9 24.3 %fusion.179 = (f32[2,4,512]{2,1,0:T(4,128)S(1)}, f32[2,512,4,2048]{3,1,2,0:T(8,128)}) fusion(f32[2,512,4,2048]{3,1,2,0:T(8,128)} %fusion.177, f32[2,4,512]{2,1,0:T(4,128)S(1)} %dynamic-slice_bitcast_fusion.2, pred[512,2048]{1,0:T(8,128)(4,1)S(1)} %fusion.178, bf16[2048,2,64]{0,2,1:T(8,128)(2,1)} %get-tuple-element.548, ...), kind=kOutput, calls=%fused_computation.25.clone.1 | convolution fusion | flops 1115680768 | bytes 69238784 | tf_op jit(solution)/shard_map/while/body/eval_jaxpr/bgjd,kgd->gjbk/dot_general | solution.py:187
  1203.2 28.1 %fusion.180 = bf16[2,4,512,2048]{3,2,1,0:T(8,128)(2,1)} fusion(f32[2,512,4,2048]{3,1,2,0:T(8,128)} %get-tuple-element.474, f32[2,512,4,2048]{3,1,2,0:T(8,128)} %fusion.177, f32[2,4,512]{2,1,0:T(4,128)S(1)} %get-tuple-element.475, f32[2,4,512]{2,1,0:T(4,128)S(1)} %dynamic-slice_bitcast_fusion.2, pred[512,2048]{1,0:T(8,128)(4,1)} %copy-done.2), kind=kLoop, calls=%fused_computation.27.clone.1 | loop fusion | flops 50331648 | bytes 84967424 | tf_op jit(solution)/shard_map/while/body/eval_jaxpr/convert_element_type | solution.py:190
  1231.3 10.3 fusion.181
  1251.0 21.1 %dynamic_update_slice.20 = f32[4,512,2,4,64]{1,0,4,3,2:T(4,128)} dynamic-update-slice(f32[4,512,2,4,64]{1,0,4,3,2:T(4,128)} %get-tuple-element.526, f32[1,512,2,4,64]{1,0,4,3,2:T(1,128)} %copy.59, s32[]{:T(128)S(6)} %copy.76, s32[]{:T(128)} %constant.67.clone.1..sunk.1, s32[]{:T(128)} %constant.67.clone.1..sunk.1, s32[]{:T(128)} %constant.67.clone.1..sunk.1, s32[]{:T(128)} %constant.67.clone.1..sunk.1) | dynamic-update-slice | bytes 2097156 | tf_op jit(solution)/shard_map/while/body/jit(dynamic_update_index_in_dim)/dynamic_update_slice | solution.py:131
  1274.7 17.2 fusion.177
  1291.9 15.0 fusion.182
  1307.0 24.3 %fusion.179 = (f32[2,4,512]{2,1,0:T(4,128)S(1)}, f32[2,512,4,2048]{3,1,2,0:T(8,128)}) fusion(f32[2,512,4,2048]{3,1,2,0:T(8,128)} %fusion.177, f32[2,4,512]{2,1,0:T(4,128)S(1)} %dynamic-slice_bitcast_fusion.2, pred[512,2048]{1,0:T(8,128)(4,1)S(1)} %fusion.178, bf16[2048,2,64]{0,2,1:T(8,128)(2,1)} %get-tuple-element.548, ...), kind=kOutput, calls=%fused_computation.25.clone.1 | convolution fusion | flops 1115680768 | bytes 69238784 | tf_op jit(solution)/shard_map/while/body/eval_jaxpr/bgjd,kgd->gjbk/dot_general | solution.py:187
  1331.2 28.1 %fusion.180 = bf16[2,4,512,2048]{3,2,1,0:T(8,128)(2,1)} fusion(f32[2,512,4,2048]{3,1,2,0:T(8,128)} %get-tuple-element.474, f32[2,512,4,2048]{3,1,2,0:T(8,128)} %fusion.177, f32[2,4,512]{2,1,0:T(4,128)S(1)} %get-tuple-element.475, f32[2,4,512]{2,1,0:T(4,128)S(1)} %dynamic-slice_bitcast_fusion.2, pred[512,2048]{1,0:T(8,128)(4,1)} %copy-done.2), kind=kLoop, calls=%fused_computation.27.clone.1 | loop fusion | flops 50331648 | bytes 84967424 | tf_op jit(solution)/shard_map/while/body/eval_jaxpr/convert_element_type | solution.py:190
  1359.3 10.3 fusion.181
  1379.0 21.1 %dynamic_update_slice.20 = f32[4,512,2,4,64]{1,0,4,3,2:T(4,128)} dynamic-update-slice(f32[4,512,2,4,64]{1,0,4,3,2:T(4,128)} %get-tuple-element.526, f32[1,512,2,4,64]{1,0,4,3,2:T(1,128)} %copy.59, s32[]{:T(128)S(6)} %copy.76, s32[]{:T(128)} %constant.67.clone.1..sunk.1, s32[]{:T(128)} %constant.67.clone.1..sunk.1, s32[]{:T(128)} %constant.67.clone.1..sunk.1, s32[]{:T(128)} %constant.67.clone.1..sunk.1) | dynamic-update-slice | bytes 2097156 | tf_op jit(solution)/shard_map/while/body/jit(dynamic_update_index_in_dim)/dynamic_update_slice | solution.py:131
  1402.8 17.2 fusion.177
  1420.0 15.0 fusion.182
  1435.0 24.3 %fusion.179 = (f32[2,4,512]{2,1,0:T(4,128)S(1)}, f32[2,512,4,2048]{3,1,2,0:T(8,128)}) fusion(f32[2,512,4,2048]{3,1,2,0:T(8,128)} %fusion.177, f32[2,4,512]{2,1,0:T(4,128)S(1)} %dynamic-slice_bitcast_fusion.2, pred[512,2048]{1,0:T(8,128)(4,1)S(1)} %fusion.178, bf16[2048,2,64]{0,2,1:T(8,128)(2,1)} %get-tuple-element.548, ...), kind=kOutput, calls=%fused_computation.25.clone.1 | convolution fusion | flops 1115680768 | bytes 69238784 | tf_op jit(solution)/shard_map/while/body/eval_jaxpr/bgjd,kgd->gjbk/dot_general | solution.py:187
  1459.3 28.1 %fusion.180 = bf16[2,4,512,2048]{3,2,1,0:T(8,128)(2,1)} fusion(f32[2,512,4,2048]{3,1,2,0:T(8,128)} %get-tuple-element.474, f32[2,512,4,2048]{3,1,2,0:T(8,128)} %fusion.177, f32[2,4,512]{2,1,0:T(4,128)S(1)} %get-tuple-element.475, f32[2,4,512]{2,1,0:T(4,128)S(1)} %dynamic-slice_bitcast_fusion.2, pred[512,2048]{1,0:T(8,128)(4,1)} %copy-done.2), kind=kLoop, calls=%fused_computation.27.clone.1 | loop fusion | flops 50331648 | bytes 84967424 | tf_op jit(solution)/shard_map/while/body/eval_jaxpr/convert_element_type | solution.py:190
  1487.4 10.3 fusion.181
  1507.0 21.1 %dynamic_update_slice.20 = f32[4,512,2,4,64]{1,0,4,3,2:T(4,128)} dynamic-update-slice(f32[4,512,2,4,64]{1,0,4,3,2:T(4,128)} %get-tuple-element.526, f32[1,512,2,4,64]{1,0,4,3,2:T(1,128)} %copy.59, s32[]{:T(128)S(6)} %copy.76, s32[]{:T(128)} %constant.67.clone.1..sunk.1, s32[]{:T(128)} %constant.67.clone.1..sunk.1, s32[]{:T(128)} %constant.67.clone.1..sunk.1, s32[]{:T(128)} %constant.67.clone.1..sunk.1) | dynamic-update-slice | bytes 2097156 | tf_op jit(solution)/shard_map/while/body/jit(dynamic_update_index_in_dim)/dynamic_update_slice | solution.py:131
  1550.2 11.0 convolution_convert_fusion
  1594.2 10.4 reduce-scatter.14.cloned.1.call-done
  1608.3 40.2 %all-reduce = (f32[1024]{0:T(1024)}, f32[1024]{0:T(1024)}) all-reduce(f32[1024]{0:T(1024)S(1)} %get-tuple-element.255, f32[1024]{0:T(1024)S(1)} %copy-done.46), channel_id=1, replica_groups=mesh['dp'=16,'tensor'=2] {'dp','tensor'}, use_global_device_ids=true, to_apply=%region_20.21 | all-reduce | flops 2048 | bytes 16384 | tf_op jit(solution)/shard_map/psum | solution.py:250
  1648.5 14.1 reduce-scatter.10.cloned.1.call-done
  1670.3 120.5 %all-reduce.5.cloned.1.call-done = f32[1024,32]{0,1:T(8,128)} async-done(((f32[1024,32]{0,1:T(8,128)}), f32[1024,32]{0,1:T(8,128)}) %all-reduce.5.cloned.1.call-update) | async-done | bytes 131088 | tf_op jit(solution)/shard_map/psum | solution.py:250
  1790.8 120.8 %all-reduce.7.cloned.1.call-done = (f32[1024,512]{1,0:T(8,128)}, f32[1024,128]{1,0:T(8,128)}, f32[512,1024]{1,0:T(8,128)}) async-done(((f32[1024,512]{1,0:T(8,128)}, f32[1024,128]{1,0:T(8,128)}, f32[512,1024]{1,0:T(8,128)}), (f32[1024,512]{1,0:T(8,128)}, f32[1024,128]{1,0:T(8,128)}, f32[512,1024]{1,0:T(8,128)})) %all-reduce.7.cloned.1.call-update) | async-done | bytes 4718608 | tf_op jit(solution)/shard_map/psum | solution.py:251
  (298 shorter events, 247.2 us)
Async XLA Ops:
  7.2 577.4 %copy-start = (bf16[1408,1024]{1,0:T(8,128)(2,1)S(1)}, bf16[1408,1024]{1,0:T(8,128)(2,1)}, u32[]{:S(2)}) copy-start(bf16[1408,1024]{1,0:T(8,128)(2,1)} %param.26) | copy-start | bytes 8650756
  7.2 66.0 %copy-start.28 = (bf16[1024,128]{1,0:T(8,128)(2,1)S(1)}, bf16[1024,128]{1,0:T(8,128)(2,1)}, u32[]{:S(2)}) copy-start(bf16[1024,128]{1,0:T(8,128)(2,1)} %param.20) | copy-start | bytes 786436
  7.2 66.0 %all-gather.8.cloned.1.call-start = ((), (), s32[]{:S(2)}) async-start(), calls=%async_computation.7 | async-start | bytes 6291456 | tf_op jit(solution)/shard_map/all_gather | solution.py:86
  13.6 450.3 %reduce-scatter.8.cloned.1.call-start = ((), (), s32[]{:S(2)}) async-start(), calls=%async_computation.8 | async-start | bytes 6291456 | tf_op jit(solution)/shard_map/reduce_scatter | solution.py:133
  14.0 77.5 %copy-start.50 = (f32[16]{0:T(128)}, f32[16]{0:T(128)S(1)}, u32[]{:S(2)}) copy-start(f32[16]{0:T(128)S(1)} %multiply_power_fusion) | copy-start | bytes 196
  14.6 76.9 %copy-start.37 = (f32[2048]{0:T(1024)}, f32[2048]{0:T(1024)S(1)}, u32[]{:S(2)}) copy-start(f32[2048]{0:T(1024)S(1)} %subtract_convert_fusion.2) | copy-start | bytes 24580
  107.1 15.2 copy-start.8
  180.4 15.2 copy-start.8
  253.8 15.2 copy-start.8
  327.1 15.2 copy-start.8
  409.4 57.6 %copy-start.39 = (f32[1024]{0:T(1024)S(1)}, f32[1024]{0:T(1024)}, u32[]{:S(2)}) copy-start(f32[1024]{0:T(1024)} %param.23) | copy-start | bytes 12292
  409.4 117.0 %all-gather.10.cloned.1.call-start = ((), (), s32[]{:S(2)}) async-start(), calls=%async_computation.9 | async-start | bytes 6291456 | tf_op jit(solution)/shard_map/all_gather | solution.py:140
  467.3 216.0 %copy-start.34 = (f32[1024]{0:T(1024)}, f32[1024]{0:T(1024)S(1)}, u32[]{:S(2)}) copy-start(f32[1024]{0:T(1024)S(1)} %add_rsqrt_fusion) | copy-start | bytes 12292
  469.4 115.2 %all-gather.12.cloned.1.call-start = ((), (), s32[]{:S(2)}) async-start(), calls=%async_computation.11 | async-start | bytes 6291456 | tf_op jit(solution)/shard_map/all_gather | solution.py:153
  470.0 207.9 %reduce-scatter.12.cloned.1.call-start = ((), (), s32[]{:S(2)}) async-start(), calls=%async_computation.12 | async-start | bytes 6291456 | tf_op jit(solution)/shard_map/reduce_scatter | solution.py:164
  526.3 12.1 copy-start.54
  526.3 12.1 copy-start.55
  605.1 9.8 copy-start.56
  605.1 9.8 copy-start.60
  623.5 139.8 %reduce-scatter.20.cloned.1.call-start = ((), (), s32[]{:S(2)}) async-start(), calls=%async_computation.20 | async-start | bytes 6127616 | tf_op jit(solution)/shard_map/reduce_scatter | solution.py:51
  634.8 213.1 %reduce-scatter.16.cloned.1.call-start = ((), (), s32[]{:S(2)}) async-start(), calls=%async_computation.16 | async-start | bytes 6127616 | tf_op jit(solution)/shard_map/reduce_scatter | solution.py:49
  646.7 286.4 %reduce-scatter.18.cloned.1.call-start = ((), (), s32[]{:S(2)}) async-start(), calls=%async_computation.18 | async-start | bytes 6127616 | tf_op jit(solution)/shard_map/reduce_scatter | solution.py:50
  658.6 332.7 %all-gather.14.cloned.1.call-start = ((), (), s32[]{:S(2)}) async-start(), calls=%async_computation.13 | async-start | bytes 6291456 | tf_op jit(solution)/shard_map/all_gather | solution.py:175
  687.9 303.3 %copy-start.49 = (bf16[2048]{0:T(1024)(128)(2,1)S(1)}, bf16[2048]{0:T(1024)(128)(2,1)}, u32[]{:S(2)}) copy-start(bf16[2048]{0:T(1024)(128)(2,1)} %get-tuple-element.330) | copy-start | bytes 12292
  687.9 891.7 %all-gather.20.cloned.1.call-start = ((), (), s32[]{:S(2)}) async-start(), calls=%async_computation.21 | async-start | bytes 3063808 | tf_op jit(solution)/shard_map/all_gather | solution.py:56
  765.0 819.7 %all-gather.16.cloned.1.call-start = ((), (), s32[]{:S(2)}) async-start(), calls=%async_computation.17 | async-start | bytes 3063808 | tf_op jit(solution)/shard_map/all_gather | solution.py:54
  849.6 739.8 %all-gather.18.cloned.1.call-start = ((), (), s32[]{:S(2)}) async-start(), calls=%async_computation.19 | async-start | bytes 3063808 | tf_op jit(solution)/shard_map/all_gather | solution.py:55
  934.8 669.8 %reduce-scatter.14.cloned.1.call-start = ((), (), s32[]{:S(2)}) async-start(), calls=%async_computation.14 | async-start | bytes 6291456 | tf_op jit(solution)/shard_map/reduce_scatter | solution.py:237
  1004.9 9.7 copy-start.20
  1017.4 32.7 %copy-start.2 = (pred[512,2048]{1,0:T(8,128)(4,1)}, pred[512,2048]{1,0:T(8,128)(4,1)S(1)}, u32[]{:S(2)}) copy-start(pred[512,2048]{1,0:T(8,128)(4,1)S(1)} %fusion.178) | copy-start | bytes 3145732 | tf_op jit(solution)/shard_map/while
  1017.4 17.5 copy-start.12
  1017.4 17.5 copy-start.24
  1050.1 24.4 %copy-start.25 = (f32[2048,2,64]{0,2,1:T(8,128)}, f32[2048,2,64]{0,2,1:T(8,128)S(1)}, u32[]{:S(2)}) copy-start(f32[2048,2,64]{0,2,1:T(8,128)S(1)} %fusion.182) | copy-start | bytes 3145732 | tf_op jit(solution)/shard_map/while
  1103.2 11.5 copy-start.1
  1146.7 32.3 %copy-start.2 = (pred[512,2048]{1,0:T(8,128)(4,1)}, pred[512,2048]{1,0:T(8,128)(4,1)S(1)}, u32[]{:S(2)}) copy-start(pred[512,2048]{1,0:T(8,128)(4,1)S(1)} %fusion.178) | copy-start | bytes 3145732 | tf_op jit(solution)/shard_map/while
  1146.7 17.2 copy-start.12
  1146.7 17.2 copy-start.24
  1178.9 24.3 %copy-start.25 = (f32[2048,2,64]{0,2,1:T(8,128)}, f32[2048,2,64]{0,2,1:T(8,128)S(1)}, u32[]{:S(2)}) copy-start(f32[2048,2,64]{0,2,1:T(8,128)S(1)} %fusion.182) | copy-start | bytes 3145732 | tf_op jit(solution)/shard_map/while
  1231.3 11.4 copy-start.1
  1274.7 32.3 %copy-start.2 = (pred[512,2048]{1,0:T(8,128)(4,1)}, pred[512,2048]{1,0:T(8,128)(4,1)S(1)}, u32[]{:S(2)}) copy-start(pred[512,2048]{1,0:T(8,128)(4,1)S(1)} %fusion.178) | copy-start | bytes 3145732 | tf_op jit(solution)/shard_map/while
  1274.7 17.2 copy-start.12
  1274.7 17.2 copy-start.24
  1307.0 24.3 %copy-start.25 = (f32[2048,2,64]{0,2,1:T(8,128)}, f32[2048,2,64]{0,2,1:T(8,128)S(1)}, u32[]{:S(2)}) copy-start(f32[2048,2,64]{0,2,1:T(8,128)S(1)} %fusion.182) | copy-start | bytes 3145732 | tf_op jit(solution)/shard_map/while
  1359.3 11.4 copy-start.1
  1402.7 32.3 %copy-start.2 = (pred[512,2048]{1,0:T(8,128)(4,1)}, pred[512,2048]{1,0:T(8,128)(4,1)S(1)}, u32[]{:S(2)}) copy-start(pred[512,2048]{1,0:T(8,128)(4,1)S(1)} %fusion.178) | copy-start | bytes 3145732 | tf_op jit(solution)/shard_map/while
  1402.7 17.2 copy-start.12
  1402.7 17.2 copy-start.24
  1435.0 24.3 %copy-start.25 = (f32[2048,2,64]{0,2,1:T(8,128)}, f32[2048,2,64]{0,2,1:T(8,128)S(1)}, u32[]{:S(2)}) copy-start(f32[2048,2,64]{0,2,1:T(8,128)S(1)} %fusion.182) | copy-start | bytes 3145732 | tf_op jit(solution)/shard_map/while
  1487.4 11.4 copy-start.1
  1528.5 9.0 copy-start.38
  1528.5 9.0 copy-start.51
  1528.5 9.6 copy-start.22
  1550.1 112.4 %reduce-scatter.10.cloned.1.call-start = ((), (), s32[]{:S(2)}) async-start(), calls=%async_computation.10 | async-start | bytes 6291456 | tf_op jit(solution)/shard_map/reduce_scatter | solution.py:146
  1561.2 229.5 %all-reduce.5.cloned.1.call-start = ((), (), s32[]{:S(2)}) async-start(), calls=%async_computation.15 | async-start | bytes 262144 | tf_op jit(solution)/shard_map/psum | solution.py:250
  1566.5 345.1 %all-reduce.7.cloned.1.call-start = ((), (), s32[]{:S(2)}) async-start(), calls=%async_computation.22 | async-start | bytes 9437184 | tf_op jit(solution)/shard_map/psum | solution.py:251
  1566.5 7.3 copy-start.7
  1566.5 7.3 copy-start.18
  1589.4 15.2 copy-start.42
  1589.4 15.2 copy-start.45
  1594.2 14.1 copy-start.46
  1594.2 68.4 %copy-start.35 = (f32[1024]{0:T(1024)S(1)}, f32[1024]{0:T(1024)}, u32[]{:S(2)}) copy-start(f32[1024]{0:T(1024)} %copy-done.34) | copy-start | bytes 12292
  1594.2 68.4 %copy-start.40 = (f32[1024]{0:T(1024)S(1)}, f32[1024]{0:T(1024)}, u32[]{:S(2)}) copy-start(f32[1024]{0:T(1024)} %param.23) | copy-start | bytes 12292
  1594.2 68.4 %copy-start.44 = (f32[1024]{0:T(1024)S(1)}, f32[1024]{0:T(1024)}, u32[]{:S(2)}) copy-start(f32[1024]{0:T(1024)} %copy-done.43) | copy-start | bytes 12292
  1790.8 124.8 %copy-start.33 = (f32[1024,32]{0,1:T(8,128)S(1)}, f32[1024,32]{0,1:T(8,128)}, u32[]{:S(2)}) copy-start(f32[1024,32]{0,1:T(8,128)} %all-reduce.5.cloned.1.call-done) | copy-start | bytes 393220
  (31 other events, 120.3 us)
Sparse Core Ops, SparseCore 0:
  13.7 59.4 all-gather.7
  409.5 54.2 reduce-scatter.7
  469.5 56.7 all-gather.9
  527.8 56.7 all-gather.11
  623.6 54.2 reduce-scatter.11
  681.7 81.5 reduce-scatter.19
  767.2 80.7 reduce-scatter.15
  852.4 80.7 reduce-scatter.17
  935.3 55.8 all-gather.13
  993.4 44.3 all-gather.19
  1040.0 42.7 all-gather.15
  1084.9 42.6 all-gather.17
  1550.3 54.3 reduce-scatter.13
  1606.9 55.6 reduce-scatter.9
  1668.6 122.1 all-reduce.4
  1795.1 116.4 all-reduce.6
where the time goes:
time: 1940 us; the launch traced here: 1920 us
  waiting for transfers between devices  789 us (41%)
  matrix products  573 us (30%)
  local copies, waits for them, and re-layouts  258 us (13%)
  other arithmetic  247 us (13%)
  blocking collectives  40.2 us (2%)
    dynamic_update_slice x16, local copies, waits for them, and re-layouts, body(): lax.map(forward_block, (query_blocks, slot_blocks, seg_blocks))  190 us
    dot_general x8, matrix products, scores_of(): jnp.einsum('bgjd,kgd->gjbk', query_block, key, preferred_element_type=f32)  130 us
    psum x1, waiting for transfers between devices, body(): attention = lax.psum((w_query_grad, w_kv_grad, w_out_grad), 'dp')  121 us
    psum x1, waiting for transfers between devices, body(): lax.psum((attn_gain_part, mlp_gain_part, w_rope_grad), ('dp', 'tensor'))  121 us
    convert_element_type x4, other arithmetic, backward_block(): score_grad = (weights * (weight_grad - jnp.sum(weights * weight_grad, axi...  113 us
    dot_general x4, matrix products, backward_block(): jnp.einsum('bgjd,kgd->gjbk', grad_block, tied, preferred_element_type=f32)  97.2 us
    reduce_scatter x1, waiting for transfers between devices, reduce_mlp(): lax.psum_scatter(grads[1], 'dp', scatter_dimension=0, tiled=True)  83.5 us
    reduce_scatter x1, waiting for transfers between devices, reduce_mlp(): lax.psum_scatter(grads[0], 'dp', scatter_dimension=0, tiled=True)  82.9 us
  transfers between devices with their start and end apart: 16, of which 13 were waited for; matrix products, arithmetic and copies ran while one was open for 35% of the time, Pallas kernels for 0%

commit v1 on v0

v1 whole, which is shorter than its diff:
```python
import functools

import jax
import jax.numpy as jnp
from jax import lax
from jax.experimental import pallas as pl
from jax.experimental.pallas import tpu as pltpu
from jax.sharding import PartitionSpec as P

eps_norm = 1e-05
masked_score = -1e30
f32 = jnp.float32
bf16 = jnp.bfloat16


def dot(a,b): return lax.dot_general(a,b,(((1,),(0,)),((),())),preferred_element_type=f32)
def dot_nt(a,b): return lax.dot_general(a,b,(((1,),(1,)),((),())),preferred_element_type=f32)

def block_loops(bounds, i, step):
    k0,k1,k2,k3 = (bounds[i, n] for n in range(4))
    lax.fori_loop(k0,k1,lambda kb,c: step(kb,True),None)
    lax.fori_loop(k1,k2,lambda kb,c: step(kb,False),None)
    lax.fori_loop(k2,k3,lambda kb,c: step(kb,True),None)

def allowed_tile(start, kb, bk, qpos):
    kk = lax.broadcasted_iota(jnp.int32,(bk,start.shape[1]),0)+kb*bk
    return (kk>=start)&(kk<=qpos)

def fwd_kernel(own0, heads, hd, bk, bounds, start_ref, q_ref, tied_ref, shared_ref, o_ref, lse_ref, ks, acc, ms, ls):
    i = pl.program_id(1)
    half = hd//2
    bq = q_ref.shape[2]
    @pl.when(i==0)
    def _():
        kT = jnp.concatenate([tied_ref[0,:half,:], shared_ref[...]],axis=0)
        ks[...] = kT.T
    acc[...] = jnp.zeros_like(acc)
    ms[...] = jnp.full_like(ms, masked_score)
    ls[...] = jnp.zeros_like(ls)
    start = start_ref[...]
    qpos = own0 + i*bq + lax.broadcasted_iota(jnp.int32,(1,bq),1)
    def step(kb, masked):
        rows = pl.ds(pl.multiple_of(kb*bk,bk),bk)
        kblk = ks[rows,:]
        vT = tied_ref[0,:,rows]
        if masked: ok = allowed_tile(start,kb,bk,qpos)
        mold = [ms[j:j+1,:] for j in range(heads)]
        lold = [ls[j:j+1,:] for j in range(heads)]
        aold = [acc[j*hd:(j+1)*hd,:] for j in range(heads)]
        ss = [dot(kblk, q_ref[0,j*hd:(j+1)*hd,:]) for j in range(heads)]
        if masked: ss = [jnp.where(ok,s,masked_score) for s in ss]
        mnew = [jnp.maximum(m,jnp.max(s,axis=0,keepdims=True)) for m,s in zip(mold,ss)]
        ps = [jnp.exp(s-m) for s,m in zip(ss,mnew)]
        als = [jnp.exp(a-b) for a,b in zip(mold,mnew)]
        lnew = [l*al+jnp.sum(p,axis=0,keepdims=True) for l,al,p in zip(lold,als,ps)]
        anew = [a*al+dot(vT,p.astype(bf16)) for a,al,p in zip(aold,als,ps)]
        for j in range(heads):
            ms[j:j+1,:]=mnew[j]; ls[j:j+1,:]=lnew[j]; acc[j*hd:(j+1)*hd,:]=anew[j]
    block_loops(bounds,i,step)
    live = start < (1<<29)
    for j in range(heads):
        l = ls[j:j+1,:]
        safe = jnp.where(l>0,l,1.0)
        o_ref[0,j*hd:(j+1)*hd,:] = jnp.where(live,acc[j*hd:(j+1)*hd,:]/safe,0.0).astype(bf16)
        lse_ref[0,j:j+1,:] = ms[j:j+1,:]+jnp.log(safe)

def attn_fwd(bounds,start,qT,tied,shared,own0,bq,bk):
    G,W,rows = qT.shape
    hd = tied.shape[1]; heads = W//hd; slots = tied.shape[2]
    grid=(G,rows//bq)
    return pl.pallas_call(
        functools.partial(fwd_kernel,own0,heads,hd,bk),
        grid_spec=pltpu.PrefetchScalarGridSpec(
            num_scalar_prefetch=1, grid=grid,
            in_specs=[
                pl.BlockSpec((1,bq),lambda g,i,b:(0,i)),
                pl.BlockSpec((1,W,bq),lambda g,i,b:(g,0,i)),
                pl.BlockSpec((1,hd,slots),lambda g,i,b:(g,0,0)),
                pl.BlockSpec((hd//2,slots),lambda g,i,b:(0,0)),
            ],
            out_specs=[
                pl.BlockSpec((1,W,bq),lambda g,i,b:(g,0,i)),
                pl.BlockSpec((1,heads,bq),lambda g,i,b:(g,0,i)),
            ],
            scratch_shapes=[pltpu.VMEM((slots,hd),bf16),pltpu.VMEM((W,bq),f32),pltpu.VMEM((8,bq),f32),pltpu.VMEM((8,bq),f32)],
        ),
        out_shape=[jax.ShapeDtypeStruct((G,W,rows),bf16),jax.ShapeDtypeStruct((G,heads,rows),f32)],
        compiler_params=pltpu.CompilerParams(vmem_limit_bytes=48<<20),
        name="attn_fwd",
    )(bounds,start,qT,tied,shared)

def bwd_kernel(own0, heads, hd, bk, scale, bounds, start_ref, q_ref, tied_ref, shared_ref, o_ref, lse_ref, do_ref, cos_ref, sin_ref,
               dq_ref, tg_ref, sg_ref, ks, kTs, vs, dk, dv, dqa, dl):
    g = pl.program_id(0); i = pl.program_id(1)
    half = hd//2; quarter=hd//4
    bq = q_ref.shape[2]
    @pl.when(i==0)
    def _():
        kT = jnp.concatenate([tied_ref[0,:half,:], shared_ref[...]],axis=0)
        kTs[...] = kT
        ks[...] = kT.T
        vs[...] = tied_ref[0].T
        dk[...] = jnp.zeros_like(dk)
        dv[...] = jnp.zeros_like(dv)
    @pl.when((i==0)&(g==0))
    def _():
        sg_ref[...] = jnp.zeros_like(sg_ref)
    dqa[...] = jnp.zeros_like(dqa)
    for j in range(heads):
        prod = do_ref[0,j*hd:(j+1)*hd,:].astype(f32)*o_ref[0,j*hd:(j+1)*hd,:].astype(f32)
        dl[j:j+1,:] = jnp.sum(prod,axis=0,keepdims=True)
    start = start_ref[...]
    qpos = own0 + i*bq + lax.broadcasted_iota(jnp.int32,(1,bq),1)
    def step(kb, masked):
        rows = pl.ds(pl.multiple_of(kb*bk,bk),bk)
        kblk = ks[rows,:]
        vblk = vs[rows,:]
        kT = kTs[:,rows]
        if masked: ok = allowed_tile(start,kb,bk,qpos)
        dvt = dv[:,rows]; dkt = dk[:,rows]
        sls=[slice(j*hd,(j+1)*hd) for j in range(heads)]
        qs=[q_ref[0,sl,:] for sl in sls]; dos=[do_ref[0,sl,:] for sl in sls]
        lses=[lse_ref[0,j:j+1,:] for j in range(heads)]; dls=[dl[j:j+1,:] for j in range(heads)]
        dqs=[dqa[sl,:] for sl in sls]
        new=[]
        for j in range(heads):
            s = dot(kblk, qs[j])
            if masked: s = jnp.where(ok,s,masked_score)
            p = jnp.exp(s-lses[j])
            dp = dot(vblk, dos[j])
            ds = (p*(dp-dls[j])).astype(bf16)
            dvt = dvt + dot_nt(dos[j], p.astype(bf16))
            dkt = dkt + dot_nt(qs[j], ds)
            new.append(dqs[j]+dot(kT,ds))
        for sl,n in zip(sls,new): dqa[sl,:]=n
        dv[:,rows] = dvt
        dk[:,rows] = dkt
    block_loops(bounds,i,step)
    cosv=cos_ref[...]; sinv=sin_ref[...]
    for j in range(heads):
        b0=j*hd
        x = dqa[b0:b0+hd,:]*scale
        a = x[half:half+quarter]; b=x[half+quarter:]
        dq_ref[0,b0:b0+hd,:] = jnp.concatenate([x[:half],a*cosv+b*sinv,b*cosv-a*sinv],axis=0).astype(bf16)
    @pl.when(i==pl.num_programs(1)-1)
    def _():
        tg_ref[0,:half,:] = dv[:half,:]+dk[:half,:]
        tg_ref[0,half:,:] = dv[half:,:]
        sg_ref[...] += dk[half:,:]

def attn_bwd(bounds,start,qT,tied,shared,oT,lse,doT,cosT,sinT,own0,bq,bk):
    G,W,rows = qT.shape
    hd = tied.shape[1]; heads = W//hd; slots = tied.shape[2]
    grid=(G,rows//bq)
    tile=pl.BlockSpec((1,W,bq),lambda g,i,b:(g,0,i))
    ang=pl.BlockSpec((hd//4,bq),lambda g,i,b:(0,i))
    return pl.pallas_call(
        functools.partial(bwd_kernel,own0,heads,hd,bk,hd**-0.5),
        grid_spec=pltpu.PrefetchScalarGridSpec(
            num_scalar_prefetch=1, grid=grid,
            in_specs=[
                pl.BlockSpec((1,bq),lambda g,i,b:(0,i)),
                tile,
                pl.BlockSpec((1,hd,slots),lambda g,i,b:(g,0,0)),
                pl.BlockSpec((hd//2,slots),lambda g,i,b:(0,0)),
                tile,
                pl.BlockSpec((1,heads,bq),lambda g,i,b:(g,0,i)),
                tile, ang, ang,
            ],
            out_specs=[
                tile,
                pl.BlockSpec((1,hd,slots),lambda g,i,b:(g,0,0)),
                pl.BlockSpec((hd//2,slots),lambda g,i,b:(0,0)),
            ],
            scratch_shapes=[pltpu.VMEM((slots,hd),bf16),pltpu.VMEM((hd,slots),bf16),pltpu.VMEM((slots,hd),bf16),
                pltpu.VMEM((hd,slots),f32),pltpu.VMEM((hd,slots),f32),pltpu.VMEM((W,bq),f32),pltpu.VMEM((8,bq),f32)],
        ),
        out_shape=[jax.ShapeDtypeStruct((G,W,rows),bf16),jax.ShapeDtypeStruct((G,hd,slots),f32),jax.ShapeDtypeStruct((hd//2,slots),f32)],
        compiler_params=pltpu.CompilerParams(vmem_limit_bytes=48<<20),
        name="attn_bwd",
    )(bounds,start,qT,tied,shared,oT,lse,doT,cosT,sinT)

def local_layout(lengths_row, t, rows, bq, bk, own0):
    slot = t*rows + jnp.arange(rows,dtype=jnp.int32)
    ends = jnp.cumsum(lengths_row)
    passed = (slot[:,None]>=ends[None,:]).astype(jnp.int32)
    begin = jnp.sum(passed*lengths_row[None,:],axis=1)
    total = ends[-1]
    valid = slot < total
    shift = own0 - t*rows
    start = jnp.where(valid, begin+shift, 1<<30)
    nqb = rows//bq
    first = begin.reshape(nqb,bq)[:,0]+shift
    lastvalid = jnp.max(jnp.where(valid,begin+shift,0).reshape(nqb,bq),axis=1)
    anyvalid = valid.reshape(nqb,bq)[:,0]
    allvalid = valid.reshape(nqb,bq)[:,-1]
    q0 = own0+jnp.arange(nqb,dtype=jnp.int32)*bq
    k0 = first//bk
    k3 = (q0+bq-1)//bk+1
    k1 = jnp.minimum((lastvalid+bk-1)//bk, k3)
    k2 = jnp.maximum((q0+1)//bk, k1)
    k1 = jnp.where(allvalid,k1,k3); k2=jnp.where(allvalid,k2,k3)
    k0 = jnp.where(anyvalid,k0,0); k1=jnp.where(anyvalid,k1,0); k2=jnp.where(anyvalid,k2,0); k3=jnp.where(anyvalid,k3,0)
    bounds = jnp.stack([k0,k1,k2,k3],axis=1).astype(jnp.int32)
    return slot, (slot-begin).astype(f32), valid, start[None,:], bounds


def rms_parts(values):
    factor = lax.rsqrt(jnp.mean(values * values, axis=-1, keepdims=True) + eps_norm)
    return values * factor, factor


def norm_back(grad, normed, factor, gain):
    inner = grad * gain
    return factor * (inner - normed * jnp.mean(inner * normed, axis=-1, keepdims=True))


def mm(a, b, ca, cb):
    return lax.dot_general(a, b, (((ca,), (cb,)), ((), ())), preferred_element_type=f32)


def rot_T(x, cosT, sinT):
    n = x.shape[-2] // 2
    a, b = x[..., :n, :], x[..., n:, :]
    return jnp.concatenate([a * cosT - b * sinT, a * sinT + b * cosT], axis=-2)


def swap(x, axis, bit):
    n = lax.axis_size(axis)
    return lax.ppermute(x, axis, [(i, i ^ bit) for i in range(n)])


def halves(x, bit):
    n = x.shape[0] // 2
    keep = lax.dynamic_slice_in_dim(x, bit * n, n, 0)
    send = lax.dynamic_slice_in_dim(x, (1 - bit) * n, n, 0)
    return keep, send


def joined(mine, other, bit):
    first = bit == 0
    return jnp.concatenate([jnp.where(first, mine, other), jnp.where(first, other, mine)], axis=0)


def fetch_other(w, core):
    n = w.shape[0] // 2
    piece = lax.dynamic_slice_in_dim(w, core * n, n, 0)
    got = swap(piece, "tensor", 1)
    return joined(got, swap(got, "dp", 1), core)


def add(a, b):
    return (a.astype(f32) + b.astype(f32)).astype(bf16)


def reduce_half(own, other, index):
    size = lax.axis_size("dp")
    bit = index & 1
    keep, send = halves(other, bit)
    theirs = add(keep, swap(send, "dp", 1))
    keep, send = halves(own, bit)
    mine = keep.astype(f32) + swap(send, "dp", 1).astype(f32)
    mine = (mine + swap(theirs, "tensor", 1).astype(f32)).astype(bf16)
    split = [1]
    step = 2
    while step < size:
        b = (index // step) & 1
        if mine.shape[0] % 32 == 0 or mine.shape[0] > 64:
            keep, send = halves(mine, b)
            mine = add(keep, swap(send, "dp", step))
            split.append(step)
        else:
            mine = add(mine, swap(mine, "dp", step))
        step *= 2
    for step in reversed(split):
        mine = joined(mine, swap(mine, "dp", step), (index // step) & 1)
    return mine.astype(f32)


def body(tokens, lengths, attn_gain, w_query, w_kv, w_rope, w_out, mlp_gain, w_gate, w_up, w_down, out_grad):
    rows, width = tokens.shape
    shards = lax.axis_size("tensor")
    t = lax.axis_index("tensor")
    index = lax.axis_index("dp")
    core = index & 1
    half = w_rope.shape[1]
    hd = 2 * half
    quarter = half // 2
    kv_own = w_kv.shape[1]
    q_own = w_query.shape[1]
    groups = 2 * kv_own // hd
    per = q_own // kv_own
    own0 = rows
    bq_f, bk_f, bq_b, bk_b = 256, 512, 512, 256

    slot, position, valid, start, bounds_f = local_layout(lengths[0], t, rows, bq_f, bk_f, own0)
    bounds_b = local_layout(lengths[0], t, rows, bq_b, bk_b, own0)[4]
    freq = 10000.0 ** (-jnp.arange(quarter, dtype=f32) / quarter)
    angle = freq[:, None] * position[None, :]
    cosT, sinT = jnp.cos(angle), jnp.sin(angle)

    w_kv_o = fetch_other(w_kv, core)
    w_query_o = fetch_other(w_query, core)
    w_out_o = fetch_other(w_out, core)
    w_gate_o = fetch_other(w_gate, core)
    w_up_o = fetch_other(w_up, core)
    w_down_o = fetch_other(w_down, core)

    inputs = tokens.astype(f32)
    normed_one, factor_one = rms_parts(inputs)
    first_in = (normed_one * attn_gain).astype(bf16)

    shared = rot_T(mm(w_rope, first_in, 0, 1), cosT, sinT).astype(bf16)
    tied = jnp.concatenate([mm(w_kv, first_in, 0, 1), mm(w_kv_o, first_in, 0, 1)], axis=0).astype(bf16)
    sent = jnp.concatenate([tied, shared], axis=0)
    got = lax.ppermute(sent, "tensor", [(i, i + 1) for i in range(shards - 1)])
    tied_all = jnp.concatenate(
        [jnp.concatenate([got[kv_own : 2 * kv_own], got[:kv_own]], axis=0), tied], axis=1
    ).reshape(groups, hd, 2 * rows)
    shared_all = jnp.concatenate([got[2 * kv_own :], shared], axis=1)

    def queries(w):
        raw = mm(w, first_in, 0, 1).reshape(-1, hd, rows)
        turned = jnp.concatenate([raw[:, :half], rot_T(raw[:, half:], cosT, sinT)], axis=1)
        return (turned.astype(bf16) * bf16(hd**-0.5)).reshape(-1, per * hd, rows)

    q = jnp.concatenate([queries(w_query), queries(w_query_o)], axis=0)
    mixed, lse = attn_fwd(bounds_f, start, q, tied_all, shared_all, own0, bq_f, bk_f)
    mixed_t = mixed.reshape(-1, rows)
    w_out_all = jnp.concatenate([w_out, w_out_o], axis=0)
    middle = inputs + mm(mixed_t, w_out_all, 0, 0)
    normed_two, factor_two = rms_parts(middle)
    second_in = (normed_two * mlp_gain).astype(bf16)

    def mlp(wg, wu, wd):
        gate = mm(second_in, wg, 1, 0)
        up = mm(second_in, wu, 1, 0)
        sig = jax.nn.sigmoid(gate)
        hidden = (gate * sig * up).astype(bf16)
        out = mm(hidden, wd, 1, 0)
        hidden_grad = mm(out_grad, wd, 1, 1)
        gate_grad = (hidden_grad * up * sig * (1.0 + gate * (1.0 - sig))).astype(bf16)
        up_grad = (hidden_grad * gate * sig).astype(bf16)
        wd_grad = mm(hidden, out_grad, 0, 0).astype(bf16)
        wg_grad = mm(second_in, gate_grad, 0, 0).astype(bf16)
        wu_grad = mm(second_in, up_grad, 0, 0).astype(bf16)
        second_grad = mm(gate_grad, wg, 1, 1) + mm(up_grad, wu, 1, 1)
        return out, second_grad, (wg_grad, wu_grad, wd_grad)

    out_b, second_b, grads_b = mlp(w_gate_o, w_up_o, w_down_o)
    out_a, second_a, grads_a = mlp(w_gate, w_up, w_down)
    layer_out = (middle + out_a + out_b).astype(bf16)
    second_grad = second_a + second_b
    mlp_gain_part = jnp.sum(second_grad * normed_two, axis=0)
    middle_grad = out_grad.astype(f32) + norm_back(second_grad, normed_two, factor_two, mlp_gain)
    attn_back = middle_grad.astype(bf16)
    w_out_grad = mm(mixed_t, attn_back, 1, 0).astype(bf16)
    mixed_grad = (mm(w_out_all, attn_back, 1, 1).astype(bf16) * valid[None, :].astype(bf16)).reshape(mixed.shape)

    dq, tied_grad, shared_grad = attn_bwd(
        bounds_b, start, q, tied_all, shared_all, mixed, lse, mixed_grad, cosT, sinT, own0, bq_b, bk_b
    )
    tied_grad = tied_grad.reshape(2 * kv_own, 2 * rows)
    back = jnp.concatenate([tied_grad[:, :rows], shared_grad[:, :rows]], axis=0).astype(bf16)
    back = lax.ppermute(back, "tensor", [(i + 1, i) for i in range(shards - 1)]).astype(f32)
    tied_own = tied_grad[:, rows:] + jnp.concatenate([back[kv_own : 2 * kv_own], back[:kv_own]], axis=0)
    shared_own = rot_T(shared_grad[:, rows:] + back[2 * kv_own :], cosT, -sinT)
    grads_in = jnp.concatenate([dq.reshape(-1, rows), tied_own.astype(bf16), shared_own.astype(bf16)], axis=0)
    weights_in = jnp.concatenate([w_query, w_query_o, w_kv, w_kv_o, w_rope], axis=1)
    first_grad = mm(grads_in, weights_in, 0, 1)
    in_grads = mm(first_in, grads_in, 0, 1).astype(bf16)
    attn_gain_part = jnp.sum(first_grad * normed_one, axis=0)
    tokens_grad = (middle_grad + norm_back(first_grad, normed_one, factor_one, attn_gain)).astype(bf16)

    gate_sum = reduce_half(grads_a[0], grads_b[0], index)
    up_sum = reduce_half(grads_a[1], grads_b[1], index)
    down_sum = reduce_half(grads_a[2], grads_b[2], index)
    out_sum = reduce_half(w_out_grad[:q_own], w_out_grad[q_own:], index)
    small = jnp.concatenate(
        [in_grads[:, 2 * (q_own + kv_own) :], attn_gain_part[:, None].astype(bf16), mlp_gain_part[:, None].astype(bf16)],
        axis=1,
    )
    q2 = 2 * q_own
    tail = reduce_half(
        jnp.concatenate([in_grads[:, :q_own], in_grads[:, q2 : q2 + kv_own], small], axis=1),
        jnp.concatenate([in_grads[:, q_own:q2], in_grads[:, q2 + kv_own : q2 + 2 * kv_own], small], axis=1),
        index,
    )
    k0 = q_own + kv_own
    return (
        layer_out,
        tokens_grad,
        tail[:, k0 + half],
        tail[:, :q_own],
        tail[:, q_own:k0],
        tail[:, k0 : k0 + half],
        out_sum,
        tail[:, k0 + half + 1],
        gate_sum,
        up_sum,
        down_sum,
    )


def solution(mesh):
    rows = P(("dp", "tensor"), None)
    columns = P(None, "tensor")
    down = P("tensor", None)
    return jax.shard_map(
        body,
        mesh=mesh,
        in_specs=(rows, P("dp", None), P(), columns, columns, P(), down, P(), columns, columns, down, rows),
        out_specs=(rows, rows, P(), columns, columns, P(), down, P(), columns, columns, down),
        check_vma=False,
    )
```

time: 1940 us -> 719 us (0.37)
  waiting for transfers between devices: 789 us -> 303 us
  matrix products: 573 us -> 135 us
  local copies, waits for them, and re-layouts: 258 us -> 71.1 us
  other arithmetic: 247 us -> 62.4 us
  Pallas kernels: 0 us -> 72.1 us
  starting transfers between devices: 1.36 us -> 64.5 us
  blocking collectives: 40.2 us -> 0 us
    dot_general x49 -> x28, matrix products: 573 us -> 135 us  [mm(): lax.dot_general(a, b, (((ca,), (cb,)), ((), ())), preferred_element_type=...]
    reduce_scatter x7 -> x0, waiting for transfers between devices: 339 us -> none  [the longest x1 83.5 us: reduce_mlp(): lax.psum_scatter(grads[1], 'dp', scatter_dimension=0, tiled=True)]
    ppermute x0 -> x64, waiting for transfers between devices: none -> 303 us  [the longest x62 220 us: swap(): return lax.ppermute(x, axis, [(i, i ^ bit) for i in range(n)])]
    psum x2 -> x0, waiting for transfers between devices: 241 us -> none  [the longest x1 121 us: body(): attention = lax.psum((w_query_grad, w_kv_grad, w_out_grad), 'dp')]
    all_gather x7 -> x0, waiting for transfers between devices: 207 us -> none  [the longest x1 58 us: body(): lax.all_gather((normed_one * attn_gain).astype(bf16), 'tensor', axis=0, t...]
    dynamic_update_slice x16 -> x0, local copies, waits for them, and re-layouts: 190 us -> none  [body(): lax.map(forward_block, (query_blocks, slot_blocks, seg_blocks))]
    convert_element_type x16 -> x37, other arithmetic: 143 us -> 29.9 us  [the longest x5 11 us: reduce_half(): return mine.astype(f32)]
    pallas_call x0 -> x2, Pallas kernels: none -> 72.1 us  [the longest x1 44 us: attn_bwd(): pl.pallas_call(functools.partial(bwd_kernel, own0, heads, hd, bk, hd ** (...]
  transfers between devices with their start and end apart: 16 -> 64, of which waited for: 13 -> 27; matrix products, arithmetic and copies ran while one was open for 35% -> 36% of each run, Pallas kernels for 0% -> 10%
where the time goes in v1:
time: 719 us; the launch traced here: 712 us
  waiting for transfers between devices  303 us (42%)
  matrix products  135 us (19%)
  Pallas kernels  72.1 us (10%)
  local copies, waits for them, and re-layouts  71.1 us (10%)
  starting transfers between devices  64.5 us (9%)
  other arithmetic  62.4 us (9%)
    ppermute x62, waiting for transfers between devices, swap(): return lax.ppermute(x, axis, [(i, i ^ bit) for i in range(n)])  220 us
    dot_general x28, matrix products, mm(): lax.dot_general(a, b, (((ca,), (cb,)), ((), ())), preferred_element_type=...  135 us
    ppermute x62, starting transfers between devices, swap(): return lax.ppermute(x, axis, [(i, i ^ bit) for i in range(n)])  59.1 us
    ppermute x1, waiting for transfers between devices, body(): got = lax.ppermute(sent, 'tensor', [(i, i + 1) for i in range(shards - 1)])  51.8 us
    pallas_call x1, Pallas kernels, attn_bwd(): pl.pallas_call(functools.partial(bwd_kernel, own0, heads, hd, bk, hd ** (...  44 us
    unnamed x209, local copies, waits for them, and re-layouts  33.8 us
    ppermute x1, waiting for transfers between devices, body(): lax.ppermute(back, 'tensor', [(i + 1, i) for i in range(shards - 1)])  31.3 us
    pallas_call x1, Pallas kernels, attn_fwd(): pl.pallas_call(functools.partial(fwd_kernel, own0, heads, hd, bk), grid_s...  28.1 us
  transfers between devices with their start and end apart: 64, of which 27 were waited for; matrix products, arithmetic and copies ran while one was open for 36% of the time, Pallas kernels for 10%

profile of v1, /device:TPU:0, one launch (start us, length us, event | category | flops | bytes accessed | tf_op | source)
XLA Modules:
  0.0 711.6 jit_solution(11727151128609702808)
XLA Ops:
  2.7 3.0 collective-permute-start
  15.1 3.9 copy.47
  21.8 2.6 fusion.86
  39.8 3.8 collective-permute-start.4
  47.5 4.1 copy.54
  55.0 51.8 %collective-permute-done.4 = bf16[288,1024]{1,0:T(8,128)(2,1)} collective-permute-done((bf16[288,1024]{1,0:T(8,128)(2,1)}, bf16[288,1024]{1,0:T(8,128)(2,1)}, u32[]{:S(2)}, u32[]{:S(2)}) %collective-permute-start.4) | collective-permute-done | bytes 589856 | tf_op jit(solution)/shard_map/ppermute | solution.py:316
  113.8 28.1 %attn_fwd.1 = (bf16[4,256,1024]{2,1,0:T(8,128)(2,1)S(1)}, f32[4,4,1024]{2,1,0:T(4,128)S(1)}) custom-call(s32[4,4]{1,0:T(4,128)S(1)} %pad_add_fusion.bounds, s32[1,1024]{1,0:T(1,128)S(1)} %compare_select_fusion.start_ref, bf16[4,256,1024]{2,1,0:T(8,128)(2,1)S(1)} %pad_maximum_fusion.4.q_ref, bf16[4,64,2048]{2,1,0:T(8,128)(2,1)S(1)} %pad_maximum_fusion.17.tied_ref, ...), custom_call_target="tpu_custom_call" | custom-call | tf_op jit(solution)/shard_map/attn_fwd/pallas_call | solution.py:71
  143.6 2.8 multiply_reduce_fusion.2
  148.3 5.3 fusion.87
  153.6 5.3 fusion.88
  158.9 10.2 %multiply_convert_fusion = (bf16[1024,1408]{1,0:T(8,128)(2,1)}, bf16[1024,1408]{1,0:T(8,128)(2,1)S(1)}, bf16[1024,1408]{1,0:T(8,128)(2,1)}) fusion(f32[1024,1408]{1,0:T(8,128)} %fusion.87, f32[1024,1408]{1,0:T(8,128)} %fusion.88, bf16[1024,1024]{1,0:T(8,128)(2,1)S(1)} %copy-done.47, bf16[1408,1024]{1,0:T(8,128)(2,1)S(1)} %copy-done), kind=kOutput, calls=%fused_computation.14 | convolution fusion | flops 2975858688 | bytes 25165824 | tf_op jit(solution)/shard_map/dot_general | solution.py:219
  169.2 7.9 %fusion.89 = f32[1024,1024]{0,1:T(8,128)} fusion(bf16[1024,1408]{1,0:T(8,128)(2,1)} %get-tuple-element.54, bf16[1408,1024]{1,0:T(8,128)(2,1)S(1)} %copy-done), kind=kOutput, calls=%fused_computation.345 | convolution fusion | flops 2952790016 | bytes 9961472 | tf_op jit(solution)/shard_map/dot_general | solution.py:219
  178.9 3.6 convolution_convert_fusion.5
  185.9 3.4 convolution_convert_fusion.1
  189.4 3.4 fusion.90
  193.4 3.6 convolution_convert_fusion.3
  197.1 5.0 fusion.91
  208.4 5.4 fusion.17
  215.5 5.3 fusion.20
  220.9 2.7 broadcast_select_fusion.9
  223.6 10.7 %fusion.6 = (bf16[1024,1408]{1,0:T(8,128)(2,1)S(1)}, bf16[1024,1408]{1,0:T(8,128)(2,1)}, bf16[1024,1408]{1,0:T(8,128)(2,1)}) fusion(f32[1408,1024]{0,1:T(8,128)} %fusion.17, f32[1024,1408]{1,0:T(8,128)} %fusion.20, bf16[1024,1024]{0,1:T(8,128)(2,1)S(1)} %copy-done.50, bf16[512,1408]{1,0:T(8,128)(2,1)} %get-tuple-element.66, ...), kind=kOutput, calls=%fused_computation.11 | convolution fusion | flops 2981625856 | bytes 25165824 | tf_op jit(solution)/shard_map/dot_general | solution.py:219
  234.3 8.8 %fusion.18 = f32[1024,1024]{0,1:T(8,128)} fusion(bf16[1024,1408]{1,0:T(8,128)(2,1)} %get-tuple-element.50, bf16[512,1408]{1,0:T(8,128)(2,1)} %get-tuple-element.66, bf16[512,1408]{1,0:T(8,128)(2,1)S(1)} %get-tuple-element.65), kind=kOutput, calls=%fused_computation.60 | convolution fusion | flops 2958557184 | bytes 9961472 | tf_op jit(solution)/shard_map/dot_general | solution.py:219
  243.1 4.7 convolution_convert_fusion.2
  247.8 4.6 convolution_convert_fusion
  252.5 7.6 %add_convert_fusion = bf16[1024,1024]{0,1:T(8,128)(2,1)} fusion(f32[1024,1024]{0,1:T(8,128)S(1)} %get-tuple-element.141, f32[1024,1024]{0,1:T(8,128)} %fusion.89, bf16[1024,1408]{1,0:T(8,128)(2,1)} %get-tuple-element.51, bf16[704,1024]{1,0:T(8,128)(2,1)S(1)} %copy-done.56, bf16[704,1024]{1,0:T(8,128)(2,1)S(1)} %get-tuple-element.61), kind=kOutput, calls=%fused_computation.32 | convolution fusion | flops 2961702912 | bytes 16252928 | tf_op jit(solution)/shard_map/dot_general | solution.py:219
  260.1 4.7 convolution_convert_fusion.4
  264.8 9.1 %multiply_reduce_fusion = (bf16[1024]{0:T(1024)(128)(2,1)S(1)}, f32[1024]{0:T(1024)S(1)}, f32[1024,1024]{0,1:T(8,128)S(1)}) fusion(f32[1024,1024]{0,1:T(8,128)S(1)} %get-tuple-element.141, f32[1024]{0:T(1024)S(1)} %add_rsqrt_fusion, f32[1024]{0:T(1024)S(1)} %copy-done.80, f32[1024,1024]{0,1:T(8,128)} %fusion.18, bf16[1024,1408]{1,0:T(8,128)(2,1)} %copy-done.25, ...), kind=kOutput, calls=%fused_computation.28 | convolution fusion | flops 2967992320 | bytes 26753024 | tf_op jit(solution)/shard_map/dot_general | solution.py:219
  277.6 3.7 convert_multiply_fusion.2
  281.3 44.0 %attn_bwd.1 = (bf16[4,256,1024]{2,1,0:T(8,128)(2,1)S(1)}, f32[4,64,2048]{2,1,0:T(8,128)S(1)}, f32[32,2048]{1,0:T(8,128)S(1)}) custom-call(s32[2,4]{1,0:T(2,128)S(1)} %pad_add_fusion.1.bounds, s32[1,1024]{1,0:T(1,128)S(1)} %copy-done.9, bf16[4,256,1024]{2,1,0:T(8,128)(2,1)} %copy-done.2, bf16[4,64,2048]{2,1,0:T(8,128)(2,1)S(1)} %copy-done.4, ...), custom_call_target="tpu_custom_call" | custom-call | tf_op jit(solution)/shard_map/attn_bwd/pallas_call | solution.py:157
  333.5 3.9 copy.67
  338.0 2.7 constant_dynamic-slice_fusion.8
  341.0 31.3 %collective-permute-done.13 = bf16[288,1024]{1,0:T(8,128)(2,1)S(1)} collective-permute-done((bf16[288,1024]{1,0:T(8,128)(2,1)}, bf16[288,1024]{1,0:T(8,128)(2,1)S(1)}, u32[]{:S(2)}, u32[]{:S(2)}) %collective-permute-start.13) | collective-permute-done | bytes 589856 | tf_op jit(solution)/shard_map/ppermute | solution.py:365
  374.7 6.2 convolution_convert_fusion.6
  381.0 3.8 fusion.15
  388.5 27.4 %collective-permute-start.27 = (bf16[128,1024]{1,0:T(8,128)(2,1)S(1)}, bf16[128,1024]{1,0:T(8,128)(2,1)}, u32[]{:S(2)}, u32[]{:S(2)}) collective-permute-start(bf16[128,1024]{1,0:T(8,128)(2,1)S(1)} %constant_dynamic-slice_fusion.17), channel_id=1, source_target_pairs={{0,4},{2,6},{4,0},{6,2},{8,12},{10,14},{12,8},{14,10},{16,20},{18,... | collective-permute-start | bytes 786440 | tf_op jit(solution)/shard_map/ppermute | solution.py:230
  418.3 4.0 copy.68
  422.3 4.2 concatenate.158
  429.4 4.6 collective-permute-done.28
  442.8 4.7 collective-permute-done.30
  449.4 10.1 %collective-permute-done.16 = bf16[512,674]{0,1:T(8,128)(2,1)S(1)} collective-permute-done((bf16[512,674]{0,1:T(8,128)(2,1)S(1)}, bf16[512,674]{0,1:T(8,128)(2,1)S(1)}, u32[]{:S(2)}, u32[]{:S(2)}) %collective-permute-start.16) | collective-permute-done | bytes 690208 | tf_op jit(solution)/shard_map/ppermute | solution.py:230
  460.4 4.0 collective-permute-done.31
  465.1 8.7 %collective-permute-done.17 = bf16[256,674]{0,1:T(8,128)(2,1)S(1)} collective-permute-done((bf16[256,674]{0,1:T(8,128)(2,1)S(1)}, bf16[256,674]{0,1:T(8,128)(2,1)S(1)}, u32[]{:S(2)}, u32[]{:S(2)}) %collective-permute-start.17) | collective-permute-done | bytes 345120 | tf_op jit(solution)/shard_map/ppermute | solution.py:230
  474.2 5.9 collective-permute-done.32
  480.2 6.5 collective-permute-done.18
  488.5 5.9 collective-permute-done.19
  495.7 10.4 %collective-permute-done.20 = bf16[64,674]{0,1:T(8,128)(2,1)S(1)} collective-permute-done((bf16[64,674]{0,1:T(8,128)(2,1)S(1)}, bf16[64,674]{0,1:T(8,128)(2,1)S(1)}, u32[]{:S(2)}, u32[]{:S(2)}) %collective-permute-start.20) | collective-permute-done | bytes 86304 | tf_op jit(solution)/shard_map/ppermute | solution.py:230
  508.3 4.3 collective-permute-done.21
  518.8 21.8 %collective-permute-done.46 = bf16[512,1408]{1,0:T(8,128)(2,1)S(1)} collective-permute-done((bf16[512,1408]{1,0:T(8,128)(2,1)S(1)}, bf16[512,1408]{1,0:T(8,128)(2,1)S(1)}, u32[]{:S(2)}, u32[]{:S(2)}) %collective-permute-start.46) | collective-permute-done | bytes 1441824 | tf_op jit(solution)/shard_map/ppermute | solution.py:230
  543.0 27.3 %collective-permute-done.56 = bf16[704,1024]{1,0:T(8,128)(2,1)S(1)} collective-permute-done((bf16[704,1024]{1,0:T(8,128)(2,1)S(1)}, bf16[704,1024]{1,0:T(8,128)(2,1)S(1)}, u32[]{:S(2)}, u32[]{:S(2)}) %collective-permute-start.56) | collective-permute-done | bytes 1441824 | tf_op jit(solution)/shard_map/ppermute | solution.py:230
  576.2 12.3 %collective-permute-done.57 = bf16[352,1024]{1,0:T(8,128)(2,1)S(1)} collective-permute-done((bf16[352,1024]{1,0:T(8,128)(2,1)S(1)}, bf16[352,1024]{1,0:T(8,128)(2,1)S(1)}, u32[]{:S(2)}, u32[]{:S(2)}) %collective-permute-start.57) | collective-permute-done | bytes 720928 | tf_op jit(solution)/shard_map/ppermute | solution.py:230
  591.7 3.1 copy.69
  606.1 10.7 %collective-permute-done.39 = bf16[64,1408]{1,0:T(8,128)(2,1)S(1)} collective-permute-done((bf16[64,1408]{1,0:T(8,128)(2,1)S(1)}, bf16[64,1408]{1,0:T(8,128)(2,1)S(1)}, u32[]{:S(2)}, u32[]{:S(2)}) %collective-permute-start.39) | collective-permute-done | bytes 180256 | tf_op jit(solution)/shard_map/ppermute | solution.py:230
  616.9 9.5 %collective-permute-done.49 = bf16[64,1408]{1,0:T(8,128)(2,1)S(1)} collective-permute-done((bf16[64,1408]{1,0:T(8,128)(2,1)S(1)}, bf16[64,1408]{1,0:T(8,128)(2,1)S(1)}, u32[]{:S(2)}, u32[]{:S(2)}) %collective-permute-start.49) | collective-permute-done | bytes 180256 | tf_op jit(solution)/shard_map/ppermute | solution.py:230
  626.6 7.6 %collective-permute-done.59 = bf16[88,1024]{1,0:T(8,128)(2,1)S(1)} collective-permute-done((bf16[88,1024]{1,0:T(8,128)(2,1)S(1)}, bf16[88,1024]{1,0:T(8,128)(2,1)S(1)}, u32[]{:S(2)}, u32[]{:S(2)}) %collective-permute-start.59) | collective-permute-done | bytes 180256 | tf_op jit(solution)/shard_map/ppermute | solution.py:230
  634.3 4.4 collective-permute-done.40
  638.9 5.1 collective-permute-done.50
  646.6 7.6 %collective-permute-done.41 = bf16[128,1408]{1,0:T(8,128)(2,1)S(1)} collective-permute-done((bf16[128,1408]{1,0:T(8,128)(2,1)S(1)}, bf16[128,1408]{1,0:T(8,128)(2,1)S(1)}, u32[]{:S(2)}, u32[]{:S(2)}) %collective-permute-start.41) | collective-permute-done | bytes 360480 | tf_op jit(solution)/shard_map/ppermute | solution.py:230
  654.5 7.4 %collective-permute-done.51 = bf16[128,1408]{1,0:T(8,128)(2,1)S(1)} collective-permute-done((bf16[128,1408]{1,0:T(8,128)(2,1)S(1)}, bf16[128,1408]{1,0:T(8,128)(2,1)S(1)}, u32[]{:S(2)}, u32[]{:S(2)}) %collective-permute-start.51) | collective-permute-done | bytes 360480 | tf_op jit(solution)/shard_map/ppermute | solution.py:230
  662.3 11.3 %collective-permute-done.42 = bf16[256,1408]{1,0:T(8,128)(2,1)S(1)} collective-permute-done((bf16[256,1408]{1,0:T(8,128)(2,1)S(1)}, bf16[256,1408]{1,0:T(8,128)(2,1)S(1)}, u32[]{:S(2)}, u32[]{:S(2)}) %collective-permute-start.42) | collective-permute-done | bytes 720928 | tf_op jit(solution)/shard_map/ppermute | solution.py:230
  674.4 14.6 %collective-permute-done.52 = bf16[256,1408]{1,0:T(8,128)(2,1)S(1)} collective-permute-done((bf16[256,1408]{1,0:T(8,128)(2,1)S(1)}, bf16[256,1408]{1,0:T(8,128)(2,1)S(1)}, u32[]{:S(2)}, u32[]{:S(2)}) %collective-permute-start.52) | collective-permute-done | bytes 720928 | tf_op jit(solution)/shard_map/ppermute | solution.py:230
  689.5 10.2 %collective-permute-done.62 = bf16[352,1024]{1,0:T(8,128)(2,1)S(1)} collective-permute-done((bf16[352,1024]{1,0:T(8,128)(2,1)S(1)}, bf16[352,1024]{1,0:T(8,128)(2,1)S(1)}, u32[]{:S(2)}, u32[]{:S(2)}) %collective-permute-start.62) | collective-permute-done | bytes 720928 | tf_op jit(solution)/shard_map/ppermute | solution.py:230
  700.9 2.9 maximum_convert_fusion
  704.4 2.9 maximum_convert_fusion.1
  708.1 3.3 maximum_convert_fusion.2
  (476 shorter events, 138.5 us)
Async XLA Ops:
  2.7 52.2 %collective-permute-start = (bf16[512,512]{1,0:T(8,128)(2,1)}, bf16[512,512]{1,0:T(8,128)(2,1)}, u32[]{:S(2)}, u32[]{:S(2)}) collective-permute-start(bf16[512,512]{1,0:T(8,128)(2,1)} %constant_dynamic-slice_fusion.30), channel_id=1, source_target_pairs={{0,1},{1,0},{2,3},{3,2},{4,5},{5,4},{6,7},{7,6},{8,9},{9,8},{10,11... | collective-permute-start | bytes 1572872 | tf_op jit(solution)/shard_map/ppermute | solution.py:230
  6.6 28.1 %collective-permute-start.2 = (bf16[512,128]{1,0:T(8,128)(2,1)S(1)}, bf16[512,128]{1,0:T(8,128)(2,1)S(1)}, u32[]{:S(2)}, u32[]{:S(2)}) collective-permute-start(bf16[512,128]{1,0:T(8,128)(2,1)S(1)} %constant_dynamic-slice_fusion.29), channel_id=1, source_target_pairs={{0,1},{1,0},{2,3},{3,2},{4,5},{5,4},{6,7},{7,6},{8,9},{9,8},{10,11... | collective-permute-start | bytes 393224 | tf_op jit(solution)/shard_map/ppermute | solution.py:230
  8.5 46.3 %collective-permute-start.5 = (bf16[256,1024]{1,0:T(8,128)(2,1)}, bf16[256,1024]{1,0:T(8,128)(2,1)}, u32[]{:S(2)}, u32[]{:S(2)}) collective-permute-start(bf16[256,1024]{1,0:T(8,128)(2,1)} %constant_dynamic-slice_fusion.28), channel_id=1, source_target_pairs={{0,1},{1,0},{2,3},{3,2},{4,5},{5,4},{6,7},{7,6},{8,9},{9,8},{10,11... | collective-permute-start | bytes 1572872 | tf_op jit(solution)/shard_map/ppermute | solution.py:230
  11.8 181.1 %collective-permute-start.11 = (bf16[704,1024]{1,0:T(8,128)(2,1)}, bf16[704,1024]{1,0:T(8,128)(2,1)}, u32[]{:S(2)}, u32[]{:S(2)}) collective-permute-start(bf16[704,1024]{1,0:T(8,128)(2,1)} %constant_dynamic-slice_fusion.25), channel_id=1, source_target_pairs={{0,1},{1,0},{2,3},{3,2},{4,5},{5,4},{6,7},{7,6},{8,9},{9,8},{10,11... | collective-permute-start | bytes 4325384 | tf_op jit(solution)/shard_map/ppermute | solution.py:230
  14.1 188.0 %collective-permute-start.7 = (bf16[512,1408]{1,0:T(8,128)(2,1)}, bf16[512,1408]{1,0:T(8,128)(2,1)}, u32[]{:S(2)}, u32[]{:S(2)}) collective-permute-start(bf16[512,1408]{1,0:T(8,128)(2,1)} %constant_dynamic-slice_fusion.27), channel_id=1, source_target_pairs={{0,1},{1,0},{2,3},{3,2},{4,5},{5,4},{6,7},{7,6},{8,9},{9,8},{10,11... | collective-permute-start | bytes 4325384 | tf_op jit(solution)/shard_map/ppermute | solution.py:230
  34.7 2.5 collective-permute-start.3
  39.8 67.0 %collective-permute-start.4 = (bf16[288,1024]{1,0:T(8,128)(2,1)}, bf16[288,1024]{1,0:T(8,128)(2,1)}, u32[]{:S(2)}, u32[]{:S(2)}) collective-permute-start(bf16[288,1024]{1,0:T(8,128)(2,1)} %pad_maximum_fusion.25), channel_id=1, source_target_pairs={{0,1},{2,3},{4,5},{6,7},{8,9},{10,11},{12,13},{14,15},{16,17},{18,... | collective-permute-start | bytes 1769480 | tf_op jit(solution)/shard_map/ppermute | solution.py:316
  54.9 151.8 %collective-permute-start.9 = (bf16[512,1408]{1,0:T(8,128)(2,1)}, bf16[512,1408]{1,0:T(8,128)(2,1)}, u32[]{:S(2)}, u32[]{:S(2)}) collective-permute-start(bf16[512,1408]{1,0:T(8,128)(2,1)} %constant_dynamic-slice_fusion.26), channel_id=1, source_target_pairs={{0,1},{1,0},{2,3},{3,2},{4,5},{5,4},{6,7},{7,6},{8,9},{9,8},{10,11... | collective-permute-start | bytes 4325384 | tf_op jit(solution)/shard_map/ppermute | solution.py:230
  54.9 54.2 %collective-permute-start.1 = (bf16[512,512]{1,0:T(8,128)(2,1)}, bf16[512,512]{1,0:T(8,128)(2,1)S(1)}, u32[]{:S(2)}, u32[]{:S(2)}) collective-permute-start(bf16[512,512]{1,0:T(8,128)(2,1)} %collective-permute-done), channel_id=1, source_target_pairs={{0,2},{2,0},{4,6},{6,4},{8,10},{10,8},{12,14},{14,12},{16,18},{18,... | collective-permute-start | bytes 1572872 | tf_op jit(solution)/shard_map/ppermute | solution.py:230
  106.8 35.2 %collective-permute-start.6 = (bf16[256,1024]{1,0:T(8,128)(2,1)}, bf16[256,1024]{1,0:T(8,128)(2,1)S(1)}, u32[]{:S(2)}, u32[]{:S(2)}) collective-permute-start(bf16[256,1024]{1,0:T(8,128)(2,1)} %collective-permute-done.5), channel_id=1, source_target_pairs={{0,2},{2,0},{4,6},{6,4},{8,10},{10,8},{12,14},{14,12},{16,18},{18,... | collective-permute-start | bytes 1572872 | tf_op jit(solution)/shard_map/ppermute | solution.py:230
  184.8 328.1 %collective-permute-start.34 = (bf16[512,1408]{1,0:T(8,128)(2,1)}, bf16[512,1408]{1,0:T(8,128)(2,1)}, u32[]{:S(2)}, u32[]{:S(2)}) collective-permute-start(bf16[512,1408]{1,0:T(8,128)(2,1)} %constant_dynamic-slice_fusion.14), channel_id=1, source_target_pairs={{0,2},{2,0},{4,6},{6,4},{8,10},{10,8},{12,14},{14,12},{16,18},{18,... | collective-permute-start | bytes 4325384 | tf_op jit(solution)/shard_map/ppermute | solution.py:230
  192.9 13.8 %collective-permute-start.12 = (bf16[704,1024]{1,0:T(8,128)(2,1)}, bf16[704,1024]{1,0:T(8,128)(2,1)S(1)}, u32[]{:S(2)}, u32[]{:S(2)}) collective-permute-start(bf16[704,1024]{1,0:T(8,128)(2,1)} %collective-permute-done.11), channel_id=1, source_target_pairs={{0,2},{2,0},{4,6},{6,4},{8,10},{10,8},{12,14},{14,12},{16,18},{18,... | collective-permute-start | bytes 4325384 | tf_op jit(solution)/shard_map/ppermute | solution.py:230
  202.1 11.8 %collective-permute-start.8 = (bf16[512,1408]{1,0:T(8,128)(2,1)}, bf16[512,1408]{1,0:T(8,128)(2,1)S(1)}, u32[]{:S(2)}, u32[]{:S(2)}) collective-permute-start(bf16[512,1408]{1,0:T(8,128)(2,1)} %collective-permute-done.7), channel_id=1, source_target_pairs={{0,2},{2,0},{4,6},{6,4},{8,10},{10,8},{12,14},{14,12},{16,18},{18,... | collective-permute-start | bytes 4325384 | tf_op jit(solution)/shard_map/ppermute | solution.py:230
  203.5 313.5 %collective-permute-start.44 = (bf16[512,1408]{1,0:T(8,128)(2,1)}, bf16[512,1408]{1,0:T(8,128)(2,1)}, u32[]{:S(2)}, u32[]{:S(2)}) collective-permute-start(bf16[512,1408]{1,0:T(8,128)(2,1)} %constant_dynamic-slice_fusion.9), channel_id=1, source_target_pairs={{0,2},{2,0},{4,6},{6,4},{8,10},{10,8},{12,14},{14,12},{16,18},{18,... | collective-permute-start | bytes 4325384 | tf_op jit(solution)/shard_map/ppermute | solution.py:230
  206.6 14.2 %collective-permute-start.10 = (bf16[512,1408]{1,0:T(8,128)(2,1)}, bf16[512,1408]{1,0:T(8,128)(2,1)S(1)}, u32[]{:S(2)}, u32[]{:S(2)}) collective-permute-start(bf16[512,1408]{1,0:T(8,128)(2,1)} %collective-permute-done.9), channel_id=1, source_target_pairs={{0,2},{2,0},{4,6},{6,4},{8,10},{10,8},{12,14},{14,12},{16,18},{18,... | collective-permute-start | bytes 4325384 | tf_op jit(solution)/shard_map/ppermute | solution.py:230
  326.4 45.9 %collective-permute-start.13 = (bf16[288,1024]{1,0:T(8,128)(2,1)}, bf16[288,1024]{1,0:T(8,128)(2,1)S(1)}, u32[]{:S(2)}, u32[]{:S(2)}) collective-permute-start(bf16[288,1024]{1,0:T(8,128)(2,1)} %pad_maximum_fusion.26), channel_id=1, source_target_pairs={{1,0},{3,2},{5,4},{7,6},{9,8},{11,10},{13,12},{15,14},{17,16},{19,... | collective-permute-start | bytes 1769480 | tf_op jit(solution)/shard_map/ppermute | solution.py:365
  329.0 11.7 %collective-permute-start.25 = (bf16[256,1024]{1,0:T(8,128)(2,1)}, bf16[256,1024]{1,0:T(8,128)(2,1)S(1)}, u32[]{:S(2)}, u32[]{:S(2)}) collective-permute-start(bf16[256,1024]{1,0:T(8,128)(2,1)} %constant_dynamic-slice_fusion.18), channel_id=1, source_target_pairs={{0,2},{2,0},{4,6},{6,4},{8,10},{10,8},{12,14},{14,12},{16,18},{18,... | collective-permute-start | bytes 1572872 | tf_op jit(solution)/shard_map/ppermute | solution.py:230
  337.5 50.6 %collective-permute-start.24 = (bf16[256,1024]{1,0:T(8,128)(2,1)}, bf16[256,1024]{1,0:T(8,128)(2,1)S(1)}, u32[]{:S(2)}, u32[]{:S(2)}) collective-permute-start(bf16[256,1024]{1,0:T(8,128)(2,1)} %constant_dynamic-slice_fusion.19), channel_id=1, source_target_pairs={{0,2},{2,0},{4,6},{6,4},{8,10},{10,8},{12,14},{14,12},{16,18},{18,... | collective-permute-start | bytes 1572872 | tf_op jit(solution)/shard_map/ppermute | solution.py:230
  340.7 93.4 %collective-permute-start.35 = (bf16[512,1408]{1,0:T(8,128)(2,1)}, bf16[512,1408]{1,0:T(8,128)(2,1)}, u32[]{:S(2)}, u32[]{:S(2)}) collective-permute-start(bf16[512,1408]{1,0:T(8,128)(2,1)} %constant_dynamic-slice_fusion.13), channel_id=1, source_target_pairs={{0,2},{2,0},{4,6},{6,4},{8,10},{10,8},{12,14},{14,12},{16,18},{18,... | collective-permute-start | bytes 4325384 | tf_op jit(solution)/shard_map/ppermute | solution.py:230
  372.3 15.8 %collective-permute-start.26 = (bf16[256,1024]{1,0:T(8,128)(2,1)S(1)}, bf16[256,1024]{1,0:T(8,128)(2,1)S(1)}, u32[]{:S(2)}, u32[]{:S(2)}) collective-permute-start(bf16[256,1024]{1,0:T(8,128)(2,1)S(1)} %add_convert_fusion.13), channel_id=1, source_target_pairs={{0,1},{1,0},{2,3},{3,2},{4,5},{5,4},{6,7},{7,6},{8,9},{9,8},{10,11... | collective-permute-start | bytes 1572872 | tf_op jit(solution)/shard_map/ppermute | solution.py:230
  388.1 39.9 %collective-permute-start.15 = (bf16[512,674]{0,1:T(8,128)(2,1)}, bf16[512,674]{0,1:T(8,128)(2,1)}, u32[]{:S(2)}, u32[]{:S(2)}) collective-permute-start(bf16[512,674]{0,1:T(8,128)(2,1)} %constant_dynamic-slice_fusion.23), channel_id=1, source_target_pairs={{0,2},{2,0},{4,6},{6,4},{8,10},{10,8},{12,14},{14,12},{16,18},{18,... | collective-permute-start | bytes 2070536 | tf_op jit(solution)/shard_map/ppermute | solution.py:230
  388.5 38.1 %collective-permute-start.27 = (bf16[128,1024]{1,0:T(8,128)(2,1)S(1)}, bf16[128,1024]{1,0:T(8,128)(2,1)}, u32[]{:S(2)}, u32[]{:S(2)}) collective-permute-start(bf16[128,1024]{1,0:T(8,128)(2,1)S(1)} %constant_dynamic-slice_fusion.17), channel_id=1, source_target_pairs={{0,4},{2,6},{4,0},{6,2},{8,12},{10,14},{12,8},{14,10},{16,20},{18,... | collective-permute-start | bytes 786440 | tf_op jit(solution)/shard_map/ppermute | solution.py:230
  426.6 14.5 %collective-permute-start.45 = (bf16[512,1408]{1,0:T(8,128)(2,1)}, bf16[512,1408]{1,0:T(8,128)(2,1)S(1)}, u32[]{:S(2)}, u32[]{:S(2)}) collective-permute-start(bf16[512,1408]{1,0:T(8,128)(2,1)} %constant_dynamic-slice_fusion.8), channel_id=1, source_target_pairs={{0,2},{2,0},{4,6},{6,4},{8,10},{10,8},{12,14},{14,12},{16,18},{18,... | collective-permute-start | bytes 4325384 | tf_op jit(solution)/shard_map/ppermute | solution.py:230
  428.0 6.0 collective-permute-start.28
  434.0 13.5 %collective-permute-start.14 = (bf16[512,674]{0,1:T(8,128)(2,1)S(1)}, bf16[512,674]{0,1:T(8,128)(2,1)S(1)}, u32[]{:S(2)}, u32[]{:S(2)}) collective-permute-start(bf16[512,674]{0,1:T(8,128)(2,1)S(1)} %constant_dynamic-slice_fusion.24), channel_id=1, source_target_pairs={{0,2},{2,0},{4,6},{6,4},{8,10},{10,8},{12,14},{14,12},{16,18},{18,... | collective-permute-start | bytes 2070536 | tf_op jit(solution)/shard_map/ppermute | solution.py:230
  434.1 6.9 collective-permute-start.29
  441.0 18.5 %collective-permute-start.16 = (bf16[512,674]{0,1:T(8,128)(2,1)S(1)}, bf16[512,674]{0,1:T(8,128)(2,1)S(1)}, u32[]{:S(2)}, u32[]{:S(2)}) collective-permute-start(bf16[512,674]{0,1:T(8,128)(2,1)S(1)} %add_convert_fusion.11), channel_id=1, source_target_pairs={{0,1},{1,0},{2,3},{3,2},{4,5},{5,4},{6,7},{7,6},{8,9},{9,8},{10,11... | collective-permute-start | bytes 2070536 | tf_op jit(solution)/shard_map/ppermute | solution.py:230
  441.0 6.5 collective-permute-start.30
  447.5 47.1 %collective-permute-start.55 = (bf16[704,1024]{1,0:T(8,128)(2,1)S(1)}, bf16[704,1024]{1,0:T(8,128)(2,1)S(1)}, u32[]{:S(2)}, u32[]{:S(2)}) collective-permute-start(bf16[704,1024]{1,0:T(8,128)(2,1)S(1)} %copy-done.54), channel_id=1, source_target_pairs={{0,2},{2,0},{4,6},{6,4},{8,10},{10,8},{12,14},{14,12},{16,18},{18,... | collective-permute-start | bytes 4325384 | tf_op jit(solution)/shard_map/ppermute | solution.py:230
  447.6 67.1 %collective-permute-start.36 = (bf16[512,1408]{1,0:T(8,128)(2,1)S(1)}, bf16[512,1408]{1,0:T(8,128)(2,1)S(1)}, u32[]{:S(2)}, u32[]{:S(2)}) collective-permute-start(bf16[512,1408]{1,0:T(8,128)(2,1)S(1)} %add_convert_fusion.6), channel_id=1, source_target_pairs={{0,1},{1,0},{2,3},{3,2},{4,5},{5,4},{6,7},{7,6},{8,9},{9,8},{10,11... | collective-permute-start | bytes 4325384 | tf_op jit(solution)/shard_map/ppermute | solution.py:230
  459.5 5.0 collective-permute-start.31
  464.5 9.3 %collective-permute-start.17 = (bf16[256,674]{0,1:T(8,128)(2,1)S(1)}, bf16[256,674]{0,1:T(8,128)(2,1)S(1)}, u32[]{:S(2)}, u32[]{:S(2)}) collective-permute-start(bf16[256,674]{0,1:T(8,128)(2,1)S(1)} %constant_dynamic-slice_fusion.22), channel_id=1, source_target_pairs={{0,4},{2,6},{4,0},{6,2},{8,12},{10,14},{12,8},{14,10},{16,20},{18,... | collective-permute-start | bytes 1035272 | tf_op jit(solution)/shard_map/ppermute | solution.py:230
  473.7 6.4 collective-permute-start.32
  480.1 6.6 collective-permute-start.18
  486.9 7.6 %collective-permute-start.19 = (bf16[64,674]{0,1:T(8,128)(2,1)S(1)}, bf16[64,674]{0,1:T(8,128)(2,1)S(1)}, u32[]{:S(2)}, u32[]{:S(2)}) collective-permute-start(bf16[64,674]{0,1:T(8,128)(2,1)S(1)} %constant_dynamic-slice_fusion.20), channel_id=1, source_target_pairs={{0,16},{2,18},{4,20},{6,22},{8,24},{10,26},{12,28},{14,30},{16,0},... | collective-permute-start | bytes 258824 | tf_op jit(solution)/shard_map/ppermute | solution.py:230
  494.5 11.9 %collective-permute-start.33 = (bf16[256,1024]{1,0:T(8,128)(2,1)S(1)}, bf16[256,1024]{1,0:T(8,128)(2,1)S(1)}, u32[]{:S(2)}, u32[]{:S(2)}) collective-permute-start(bf16[256,1024]{1,0:T(8,128)(2,1)S(1)} %pad_maximum_fusion.28), channel_id=1, source_target_pairs={{0,2},{2,0},{4,6},{6,4},{8,10},{10,8},{12,14},{14,12},{16,18},{18,... | collective-permute-start | bytes 1572872 | tf_op jit(solution)/shard_map/ppermute | solution.py:230
  494.6 11.5 %collective-permute-start.20 = (bf16[64,674]{0,1:T(8,128)(2,1)S(1)}, bf16[64,674]{0,1:T(8,128)(2,1)S(1)}, u32[]{:S(2)}, u32[]{:S(2)}) collective-permute-start(bf16[64,674]{0,1:T(8,128)(2,1)S(1)} %add_convert_fusion.24), channel_id=1, source_target_pairs={{0,16},{2,18},{4,20},{6,22},{8,24},{10,26},{12,28},{14,30},{16,0},... | collective-permute-start | bytes 258824 | tf_op jit(solution)/shard_map/ppermute | solution.py:230
  506.1 34.5 %collective-permute-start.46 = (bf16[512,1408]{1,0:T(8,128)(2,1)S(1)}, bf16[512,1408]{1,0:T(8,128)(2,1)S(1)}, u32[]{:S(2)}, u32[]{:S(2)}) collective-permute-start(bf16[512,1408]{1,0:T(8,128)(2,1)S(1)} %add_convert_fusion.4), channel_id=1, source_target_pairs={{0,1},{1,0},{2,3},{3,2},{4,5},{5,4},{6,7},{7,6},{8,9},{9,8},{10,11... | collective-permute-start | bytes 4325384 | tf_op jit(solution)/shard_map/ppermute | solution.py:230
  506.4 6.2 collective-permute-start.21
  512.6 30.4 %collective-permute-start.54 = (bf16[704,1024]{1,0:T(8,128)(2,1)S(1)}, bf16[704,1024]{1,0:T(8,128)(2,1)S(1)}, u32[]{:S(2)}, u32[]{:S(2)}) collective-permute-start(bf16[704,1024]{1,0:T(8,128)(2,1)S(1)} %copy-done.53), channel_id=1, source_target_pairs={{0,2},{2,0},{4,6},{6,4},{8,10},{10,8},{12,14},{14,12},{16,18},{18,... | collective-permute-start | bytes 4325384 | tf_op jit(solution)/shard_map/ppermute | solution.py:230
  512.8 57.5 %collective-permute-start.56 = (bf16[704,1024]{1,0:T(8,128)(2,1)S(1)}, bf16[704,1024]{1,0:T(8,128)(2,1)S(1)}, u32[]{:S(2)}, u32[]{:S(2)}) collective-permute-start(bf16[704,1024]{1,0:T(8,128)(2,1)S(1)} %add_convert_fusion.2), channel_id=1, source_target_pairs={{0,1},{1,0},{2,3},{3,2},{4,5},{5,4},{6,7},{7,6},{8,9},{9,8},{10,11... | collective-permute-start | bytes 4325384 | tf_op jit(solution)/shard_map/ppermute | solution.py:230
  514.7 57.1 %collective-permute-start.22 = (bf16[256,674]{0,1:T(8,128)(2,1)S(1)}, bf16[256,674]{0,1:T(8,128)(2,1)S(1)}, u32[]{:S(2)}, u32[]{:S(2)}) collective-permute-start(bf16[256,674]{0,1:T(8,128)(2,1)S(1)} %pad_maximum_fusion.34), channel_id=1, source_target_pairs={{0,4},{2,6},{4,0},{6,2},{8,12},{10,14},{12,8},{14,10},{16,20},{18,... | collective-permute-start | bytes 1035272 | tf_op jit(solution)/shard_map/ppermute | solution.py:230
  517.0 55.1 %collective-permute-start.37 = (bf16[256,1408]{1,0:T(8,128)(2,1)S(1)}, bf16[256,1408]{1,0:T(8,128)(2,1)S(1)}, u32[]{:S(2)}, u32[]{:S(2)}) collective-permute-start(bf16[256,1408]{1,0:T(8,128)(2,1)S(1)} %constant_dynamic-slice_fusion.12), channel_id=1, source_target_pairs={{0,4},{2,6},{4,0},{6,2},{8,12},{10,14},{12,8},{14,10},{16,20},{18,... | collective-permute-start | bytes 2162696 | tf_op jit(solution)/shard_map/ppermute | solution.py:230
  542.6 30.5 %collective-permute-start.47 = (bf16[256,1408]{1,0:T(8,128)(2,1)S(1)}, bf16[256,1408]{1,0:T(8,128)(2,1)S(1)}, u32[]{:S(2)}, u32[]{:S(2)}) collective-permute-start(bf16[256,1408]{1,0:T(8,128)(2,1)S(1)} %constant_dynamic-slice_fusion.7), channel_id=1, source_target_pairs={{0,4},{2,6},{4,0},{6,2},{8,12},{10,14},{12,8},{14,10},{16,20},{18,... | collective-permute-start | bytes 2162696 | tf_op jit(solution)/shard_map/ppermute | solution.py:230
  571.4 17.1 %collective-permute-start.57 = (bf16[352,1024]{1,0:T(8,128)(2,1)S(1)}, bf16[352,1024]{1,0:T(8,128)(2,1)S(1)}, u32[]{:S(2)}, u32[]{:S(2)}) collective-permute-start(bf16[352,1024]{1,0:T(8,128)(2,1)S(1)} %constant_dynamic-slice_fusion.2), channel_id=1, source_target_pairs={{0,4},{2,6},{4,0},{6,2},{8,12},{10,14},{12,8},{14,10},{16,20},{18,... | collective-permute-start | bytes 2162696 | tf_op jit(solution)/shard_map/ppermute | solution.py:230
  572.0 17.6 %collective-permute-start.23 = (bf16[512,674]{0,1:T(8,128)(2,1)S(1)}, bf16[512,674]{0,1:T(8,128)(2,1)S(1)}, u32[]{:S(2)}, u32[]{:S(2)}) collective-permute-start(bf16[512,674]{0,1:T(8,128)(2,1)S(1)} %pad_maximum_fusion.23), channel_id=1, source_target_pairs={{0,2},{2,0},{4,6},{6,4},{8,10},{10,8},{12,14},{14,12},{16,18},{18,... | collective-permute-start | bytes 2070536 | tf_op jit(solution)/shard_map/ppermute | solution.py:230
  573.2 23.9 %collective-permute-start.38 = (bf16[128,1408]{1,0:T(8,128)(2,1)}, bf16[128,1408]{1,0:T(8,128)(2,1)}, u32[]{:S(2)}, u32[]{:S(2)}) collective-permute-start(bf16[128,1408]{1,0:T(8,128)(2,1)} %constant_dynamic-slice_fusion.11), channel_id=1, source_target_pairs={{0,8},{2,10},{4,12},{6,14},{8,0},{10,2},{12,4},{14,6},{16,24},{18,... | collective-permute-start | bytes 1081352 | tf_op jit(solution)/shard_map/ppermute | solution.py:230
  574.2 26.5 %collective-permute-start.48 = (bf16[128,1408]{1,0:T(8,128)(2,1)}, bf16[128,1408]{1,0:T(8,128)(2,1)}, u32[]{:S(2)}, u32[]{:S(2)}) collective-permute-start(bf16[128,1408]{1,0:T(8,128)(2,1)} %constant_dynamic-slice_fusion.6), channel_id=1, source_target_pairs={{0,8},{2,10},{4,12},{6,14},{8,0},{10,2},{12,4},{14,6},{16,24},{18,... | collective-permute-start | bytes 1081352 | tf_op jit(solution)/shard_map/ppermute | solution.py:230
  589.6 12.9 %collective-permute-start.58 = (bf16[176,1024]{1,0:T(8,128)(2,1)}, bf16[176,1024]{1,0:T(8,128)(2,1)}, u32[]{:S(2)}, u32[]{:S(2)}) collective-permute-start(bf16[176,1024]{1,0:T(8,128)(2,1)} %constant_dynamic-slice_fusion.1), channel_id=1, source_target_pairs={{0,8},{2,10},{4,12},{6,14},{8,0},{10,2},{12,4},{14,6},{16,24},{18,... | collective-permute-start | bytes 1081352 | tf_op jit(solution)/shard_map/ppermute | solution.py:230
  598.3 18.5 %collective-permute-start.39 = (bf16[64,1408]{1,0:T(8,128)(2,1)S(1)}, bf16[64,1408]{1,0:T(8,128)(2,1)S(1)}, u32[]{:S(2)}, u32[]{:S(2)}) collective-permute-start(bf16[64,1408]{1,0:T(8,128)(2,1)S(1)} %constant_dynamic-slice_fusion.10), channel_id=1, source_target_pairs={{0,16},{2,18},{4,20},{6,22},{8,24},{10,26},{12,28},{14,30},{16,0},... | collective-permute-start | bytes 540680 | tf_op jit(solution)/shard_map/ppermute | solution.py:230
  601.9 24.6 %collective-permute-start.49 = (bf16[64,1408]{1,0:T(8,128)(2,1)S(1)}, bf16[64,1408]{1,0:T(8,128)(2,1)S(1)}, u32[]{:S(2)}, u32[]{:S(2)}) collective-permute-start(bf16[64,1408]{1,0:T(8,128)(2,1)S(1)} %constant_dynamic-slice_fusion.5), channel_id=1, source_target_pairs={{0,16},{2,18},{4,20},{6,22},{8,24},{10,26},{12,28},{14,30},{16,0},... | collective-permute-start | bytes 540680 | tf_op jit(solution)/shard_map/ppermute | solution.py:230
  603.6 30.6 %collective-permute-start.59 = (bf16[88,1024]{1,0:T(8,128)(2,1)S(1)}, bf16[88,1024]{1,0:T(8,128)(2,1)S(1)}, u32[]{:S(2)}, u32[]{:S(2)}) collective-permute-start(bf16[88,1024]{1,0:T(8,128)(2,1)S(1)} %constant_dynamic-slice_fusion), channel_id=1, source_target_pairs={{0,16},{2,18},{4,20},{6,22},{8,24},{10,26},{12,28},{14,30},{16,0},... | collective-permute-start | bytes 540680 | tf_op jit(solution)/shard_map/ppermute | solution.py:230
  616.9 21.9 %collective-permute-start.40 = (bf16[64,1408]{1,0:T(8,128)(2,1)S(1)}, bf16[64,1408]{1,0:T(8,128)(2,1)S(1)}, u32[]{:S(2)}, u32[]{:S(2)}) collective-permute-start(bf16[64,1408]{1,0:T(8,128)(2,1)S(1)} %add_convert_fusion.23), channel_id=1, source_target_pairs={{0,16},{2,18},{4,20},{6,22},{8,24},{10,26},{12,28},{14,30},{16,0},... | collective-permute-start | bytes 540680 | tf_op jit(solution)/shard_map/ppermute | solution.py:230
  626.5 17.4 %collective-permute-start.50 = (bf16[64,1408]{1,0:T(8,128)(2,1)S(1)}, bf16[64,1408]{1,0:T(8,128)(2,1)S(1)}, u32[]{:S(2)}, u32[]{:S(2)}) collective-permute-start(bf16[64,1408]{1,0:T(8,128)(2,1)S(1)} %add_convert_fusion.22), channel_id=1, source_target_pairs={{0,16},{2,18},{4,20},{6,22},{8,24},{10,26},{12,28},{14,30},{16,0},... | collective-permute-start | bytes 540680 | tf_op jit(solution)/shard_map/ppermute | solution.py:230
  634.2 12.2 %collective-permute-start.60 = (bf16[88,1024]{1,0:T(8,128)(2,1)S(1)}, bf16[88,1024]{1,0:T(8,128)(2,1)S(1)}, u32[]{:S(2)}, u32[]{:S(2)}) collective-permute-start(bf16[88,1024]{1,0:T(8,128)(2,1)S(1)} %add_convert_fusion.21), channel_id=1, source_target_pairs={{0,16},{2,18},{4,20},{6,22},{8,24},{10,26},{12,28},{14,30},{16,0},... | collective-permute-start | bytes 540680 | tf_op jit(solution)/shard_map/ppermute | solution.py:230
  638.8 15.4 %collective-permute-start.41 = (bf16[128,1408]{1,0:T(8,128)(2,1)S(1)}, bf16[128,1408]{1,0:T(8,128)(2,1)S(1)}, u32[]{:S(2)}, u32[]{:S(2)}) collective-permute-start(bf16[128,1408]{1,0:T(8,128)(2,1)S(1)} %pad_maximum_fusion.31), channel_id=1, source_target_pairs={{0,8},{2,10},{4,12},{6,14},{8,0},{10,2},{12,4},{14,6},{16,24},{18,... | collective-permute-start | bytes 1081352 | tf_op jit(solution)/shard_map/ppermute | solution.py:230
  644.0 18.0 %collective-permute-start.51 = (bf16[128,1408]{1,0:T(8,128)(2,1)S(1)}, bf16[128,1408]{1,0:T(8,128)(2,1)S(1)}, u32[]{:S(2)}, u32[]{:S(2)}) collective-permute-start(bf16[128,1408]{1,0:T(8,128)(2,1)S(1)} %pad_maximum_fusion.32), channel_id=1, source_target_pairs={{0,8},{2,10},{4,12},{6,14},{8,0},{10,2},{12,4},{14,6},{16,24},{18,... | collective-permute-start | bytes 1081352 | tf_op jit(solution)/shard_map/ppermute | solution.py:230
  646.5 27.5 %collective-permute-start.61 = (bf16[176,1024]{1,0:T(8,128)(2,1)S(1)}, bf16[176,1024]{1,0:T(8,128)(2,1)S(1)}, u32[]{:S(2)}, u32[]{:S(2)}) collective-permute-start(bf16[176,1024]{1,0:T(8,128)(2,1)S(1)} %pad_maximum_fusion.33), channel_id=1, source_target_pairs={{0,8},{2,10},{4,12},{6,14},{8,0},{10,2},{12,4},{14,6},{16,24},{18,... | collective-permute-start | bytes 1081352 | tf_op jit(solution)/shard_map/ppermute | solution.py:230
  654.5 19.1 %collective-permute-start.42 = (bf16[256,1408]{1,0:T(8,128)(2,1)S(1)}, bf16[256,1408]{1,0:T(8,128)(2,1)S(1)}, u32[]{:S(2)}, u32[]{:S(2)}) collective-permute-start(bf16[256,1408]{1,0:T(8,128)(2,1)S(1)} %pad_maximum_fusion.20), channel_id=1, source_target_pairs={{0,4},{2,6},{4,0},{6,2},{8,12},{10,14},{12,8},{14,10},{16,20},{18,... | collective-permute-start | bytes 2162696 | tf_op jit(solution)/shard_map/ppermute | solution.py:230
  662.2 26.9 %collective-permute-start.52 = (bf16[256,1408]{1,0:T(8,128)(2,1)S(1)}, bf16[256,1408]{1,0:T(8,128)(2,1)S(1)}, u32[]{:S(2)}, u32[]{:S(2)}) collective-permute-start(bf16[256,1408]{1,0:T(8,128)(2,1)S(1)} %pad_maximum_fusion.21), channel_id=1, source_target_pairs={{0,4},{2,6},{4,0},{6,2},{8,12},{10,14},{12,8},{14,10},{16,20},{18,... | collective-permute-start | bytes 2162696 | tf_op jit(solution)/shard_map/ppermute | solution.py:230
  674.0 26.3 %collective-permute-start.43 = (bf16[512,1408]{1,0:T(8,128)(2,1)S(1)}, bf16[512,1408]{1,0:T(8,128)(2,1)S(1)}, u32[]{:S(2)}, u32[]{:S(2)}) collective-permute-start(bf16[512,1408]{1,0:T(8,128)(2,1)S(1)} %pad_maximum_fusion.12), channel_id=1, source_target_pairs={{0,2},{2,0},{4,6},{6,4},{8,10},{10,8},{12,14},{14,12},{16,18},{18,... | collective-permute-start | bytes 4325384 | tf_op jit(solution)/shard_map/ppermute | solution.py:230
  674.3 25.4 %collective-permute-start.62 = (bf16[352,1024]{1,0:T(8,128)(2,1)S(1)}, bf16[352,1024]{1,0:T(8,128)(2,1)S(1)}, u32[]{:S(2)}, u32[]{:S(2)}) collective-permute-start(bf16[352,1024]{1,0:T(8,128)(2,1)S(1)} %pad_maximum_fusion.22), channel_id=1, source_target_pairs={{0,4},{2,6},{4,0},{6,2},{8,12},{10,14},{12,8},{14,10},{16,20},{18,... | collective-permute-start | bytes 2162696 | tf_op jit(solution)/shard_map/ppermute | solution.py:230
  689.4 14.4 %collective-permute-start.53 = (bf16[512,1408]{1,0:T(8,128)(2,1)S(1)}, bf16[512,1408]{1,0:T(8,128)(2,1)S(1)}, u32[]{:S(2)}, u32[]{:S(2)}) collective-permute-start(bf16[512,1408]{1,0:T(8,128)(2,1)S(1)} %pad_maximum_fusion.13), channel_id=1, source_target_pairs={{0,2},{2,0},{4,6},{6,4},{8,10},{10,8},{12,14},{14,12},{16,18},{18,... | collective-permute-start | bytes 4325384 | tf_op jit(solution)/shard_map/ppermute | solution.py:230
  700.2 7.0 collective-permute-start.63
  (102 other events, 1166.7 us)

commit v2 on v1

v2 whole, which is shorter than its diff:
```python
import functools

import jax
import jax.numpy as jnp
from jax import lax
from jax.experimental import pallas as pl
from jax.experimental.pallas import tpu as pltpu
from jax.sharding import PartitionSpec as P

eps_norm = 1e-05
masked_score = -1e30
f32 = jnp.float32
bf16 = jnp.bfloat16


def dot(a, b):
    return lax.dot_general(a, b, (((1,), (0,)), ((), ())), preferred_element_type=f32)


def dot_nt(a, b):
    return lax.dot_general(a, b, (((1,), (1,)), ((), ())), preferred_element_type=f32)


ANY = pl.BlockSpec(memory_space=pl.ANY)


def vmem(mib):
    return pltpu.CompilerParams(vmem_limit_bytes=mib << 20)


def block_loops(bounds, i, step):
    k0, k1, k2, k3 = (bounds[i, n] for n in range(4))
    lax.fori_loop(k0, k1, lambda kb, c: step(kb, True), None)
    lax.fori_loop(k1, k2, lambda kb, c: step(kb, False), None)
    lax.fori_loop(k2, k3, lambda kb, c: step(kb, True), None)


def allowed_tile(start, kb, bk, qpos):
    kk = lax.broadcasted_iota(jnp.int32, (bk, start.shape[1]), 0) + kb * bk
    return (kk >= start) & (kk <= qpos)


def load_keys(refs, kT, vT):
    got_ref, sent_ref, got_shared, sent_shared = refs
    rows = sent_ref.shape[1]
    half = sent_shared.shape[0]
    for side, (tied, shared) in enumerate(((got_ref, got_shared), (sent_ref, sent_shared))):
        at = slice(side * rows, (side + 1) * rows)
        vT[:, at] = tied[...]
        kT[:half, at] = tied[:half, :]
        kT[half:, at] = shared[...]


def fwd_kernel(heads, bk, deps, bounds, start_ref, q_ref, *refs):
    kv_refs, refs = refs[:4], refs[4 + deps :]
    o_ref, lse_ref, kT, vT, ks, acc, ms, ls = refs
    i = pl.program_id(1)
    hd = kT.shape[0]
    bq = q_ref.shape[2]
    own0 = kT.shape[1] // 2

    @pl.when(i == 0)
    def _():
        load_keys(kv_refs, kT, vT)
        ks[...] = kT[...].T

    acc[...] = jnp.zeros_like(acc)
    ms[...] = jnp.full_like(ms, masked_score)
    ls[...] = jnp.zeros_like(ls)
    start = start_ref[...]
    qpos = own0 + i * bq + lax.broadcasted_iota(jnp.int32, (1, bq), 1)

    def step(kb, masked):
        rows = pl.ds(pl.multiple_of(kb * bk, bk), bk)
        kblk = ks[rows, :]
        vblk = vT[:, rows]
        mold = [ms[j : j + 1, :] for j in range(heads)]
        lold = [ls[j : j + 1, :] for j in range(heads)]
        aold = [acc[j * hd : (j + 1) * hd, :] for j in range(heads)]
        ss = [dot(kblk, q_ref[0, j * hd : (j + 1) * hd, :]) for j in range(heads)]
        if masked:
            ok = allowed_tile(start, kb, bk, qpos)
            ss = [jnp.where(ok, s, masked_score) for s in ss]
        mnew = [jnp.maximum(m, jnp.max(s, axis=0, keepdims=True)) for m, s in zip(mold, ss)]
        ps = [jnp.exp(s - m) for s, m in zip(ss, mnew)]
        als = [jnp.exp(a - b) for a, b in zip(mold, mnew)]
        lnew = [l * al + jnp.sum(p, axis=0, keepdims=True) for l, al, p in zip(lold, als, ps)]
        anew = [a * al + dot(vblk, p.astype(bf16)) for a, al, p in zip(aold, als, ps)]
        for j in range(heads):
            ms[j : j + 1, :] = mnew[j]
            ls[j : j + 1, :] = lnew[j]
            acc[j * hd : (j + 1) * hd, :] = anew[j]

    block_loops(bounds, i, step)
    live = start < (1 << 29)
    for j in range(heads):
        l = ls[j : j + 1, :]
        safe = jnp.where(l > 0, l, 1.0)
        o_ref[0, j * hd : (j + 1) * hd, :] = jnp.where(live, acc[j * hd : (j + 1) * hd, :] / safe, 0.0).astype(bf16)
        lse_ref[0, j : j + 1, :] = ms[j : j + 1, :] + jnp.log(safe)


def kv_specs(hd, rows, slot_sent, slot_got, n_groups):
    half = hd // 2
    shared_at = 2 * n_groups
    return [
        pl.BlockSpec((hd, rows), lambda g, i, b: (slot_got + g, 0)),
        pl.BlockSpec((hd, rows), lambda g, i, b: (slot_sent + g, 0)),
        pl.BlockSpec((half, rows), lambda g, i, b: (shared_at, 0)),
        pl.BlockSpec((half, rows), lambda g, i, b: (shared_at, 0)),
    ]


def attn_fwd(bounds, start, q, sent, got, hd, slots, bq, bk, deps=()):
    groups, width, rows = q.shape
    heads = width // hd
    n_groups = (sent.shape[0] - hd // 2) // hd
    tile = pl.BlockSpec((1, width, bq), lambda g, i, b: (g, 0, i))
    return pl.pallas_call(
        functools.partial(fwd_kernel, heads, bk, len(deps)),
        grid_spec=pltpu.PrefetchScalarGridSpec(
            num_scalar_prefetch=1,
            grid=(groups, rows // bq),
            in_specs=[pl.BlockSpec((1, bq), lambda g, i, b: (0, i)), tile]
            + kv_specs(hd, rows, *slots, n_groups)
            + [ANY] * len(deps),
            out_specs=[tile, pl.BlockSpec((1, heads, bq), lambda g, i, b: (g, 0, i))],
            scratch_shapes=[
                pltpu.VMEM((hd, 2 * rows), bf16),
                pltpu.VMEM((hd, 2 * rows), bf16),
                pltpu.VMEM((2 * rows, hd), bf16),
                pltpu.VMEM((width, bq), f32),
                pltpu.VMEM((8, bq), f32),
                pltpu.VMEM((8, bq), f32),
            ],
        ),
        out_shape=[jax.ShapeDtypeStruct((groups, width, rows), bf16), jax.ShapeDtypeStruct((groups, heads, rows), f32)],
        compiler_params=vmem(48),
        cost_estimate=pl.CostEstimate(
            flops=48 * groups * width * rows * rows, bytes_accessed=4 * groups * width * rows, transcendentals=0
        ),
        name="attn_fwd",
    )(bounds, start, q, got, sent, got, sent, *deps)


def bwd_kernel(heads, bk, scale, deps, bounds, start_ref, q_ref, o_ref, lse_ref, do_ref, cos_ref, sin_ref, *refs):
    kv_refs, refs = refs[:4], refs[4 + deps :]
    dq_ref, tg_ref, sg_ref, kT, vT, ks, vs, dk, dv, dqa, dl = refs
    g = pl.program_id(0)
    i = pl.program_id(1)
    hd = kT.shape[0]
    half = hd // 2
    quarter = hd // 4
    bq = q_ref.shape[2]
    own0 = kT.shape[1] // 2

    @pl.when(i == 0)
    def _():
        load_keys(kv_refs, kT, vT)
        ks[...] = kT[...].T
        vs[...] = vT[...].T
        dk[...] = jnp.zeros_like(dk)
        dv[...] = jnp.zeros_like(dv)

    @pl.when((i == 0) & (g == 0))
    def _():
        sg_ref[...] = jnp.zeros_like(sg_ref)

    dqa[...] = jnp.zeros_like(dqa)
    sls = [slice(j * hd, (j + 1) * hd) for j in range(heads)]
    for j, sl in enumerate(sls):
        prod = do_ref[0, sl, :].astype(f32) * o_ref[0, sl, :].astype(f32)
        dl[j : j + 1, :] = jnp.sum(prod, axis=0, keepdims=True)
    start = start_ref[...]
    qpos = own0 + i * bq + lax.broadcasted_iota(jnp.int32, (1, bq), 1)

    def step(kb, masked):
        rows = pl.ds(pl.multiple_of(kb * bk, bk), bk)
        kblk = ks[rows, :]
        vblk = vs[rows, :]
        kTb = kT[:, rows]
        if masked:
            ok = allowed_tile(start, kb, bk, qpos)
        dvt = dv[:, rows]
        dkt = dk[:, rows]
        qs = [q_ref[0, sl, :] for sl in sls]
        dos = [do_ref[0, sl, :] for sl in sls]
        lses = [lse_ref[0, j : j + 1, :] for j in range(heads)]
        dls = [dl[j : j + 1, :] for j in range(heads)]
        dqs = [dqa[sl, :] for sl in sls]
        new = []
        for j in range(heads):
            s = dot(kblk, qs[j])
            if masked:
                s = jnp.where(ok, s, masked_score)
            p = jnp.exp(s - lses[j])
            dp = dot(vblk, dos[j])
            ds = (p * (dp - dls[j])).astype(bf16)
            dvt = dvt + dot_nt(dos[j], p.astype(bf16))
            dkt = dkt + dot_nt(qs[j], ds)
            new.append(dqs[j] + dot(kTb, ds))
        for sl, n in zip(sls, new):
            dqa[sl, :] = n
        dv[:, rows] = dvt
        dk[:, rows] = dkt

    block_loops(bounds, i, step)
    cosv = cos_ref[...]
    sinv = sin_ref[...]
    for sl in sls:
        x = dqa[sl, :] * scale
        a, b = x[half : half + quarter], x[half + quarter :]
        turned = jnp.concatenate([x[:half], a * cosv + b * sinv, b * cosv - a * sinv], axis=0)
        dq_ref[0, sl, :] = turned.astype(bf16)

    @pl.when(i == pl.num_programs(1) - 1)
    def _():
        tg_ref[0, :half, :] = dv[:half, :] + dk[:half, :]
        tg_ref[0, half:, :] = dv[half:, :]
        sg_ref[...] += dk[half:, :]


def attn_bwd(bounds, start, q, sent, got, o, lse, do, cosT, sinT, hd, slots, first, groups, bq, bk, deps=()):
    _, width, rows = q.shape
    heads = width // hd
    n_groups = (sent.shape[0] - hd // 2) // hd
    tile = pl.BlockSpec((1, width, bq), lambda g, i, b: (first + g, 0, i))
    angle = pl.BlockSpec((hd // 4, bq), lambda g, i, b: (0, i))
    return pl.pallas_call(
        functools.partial(bwd_kernel, heads, bk, hd**-0.5, len(deps)),
        grid_spec=pltpu.PrefetchScalarGridSpec(
            num_scalar_prefetch=1,
            grid=(groups, rows // bq),
            in_specs=[
                pl.BlockSpec((1, bq), lambda g, i, b: (0, i)),
                tile,
                tile,
                pl.BlockSpec((1, heads, bq), lambda g, i, b: (first + g, 0, i)),
                tile,
                angle,
                angle,
            ]
            + kv_specs(hd, rows, slots[0] + first, slots[1] + first, n_groups)
            + [ANY] * len(deps),
            out_specs=[
                pl.BlockSpec((1, width, bq), lambda g, i, b: (g, 0, i)),
                pl.BlockSpec((1, hd, 2 * rows), lambda g, i, b: (g, 0, 0)),
                pl.BlockSpec((hd // 2, 2 * rows), lambda g, i, b: (0, 0)),
            ],
            scratch_shapes=[
                pltpu.VMEM((hd, 2 * rows), bf16),
                pltpu.VMEM((hd, 2 * rows), bf16),
                pltpu.VMEM((2 * rows, hd), bf16),
                pltpu.VMEM((2 * rows, hd), bf16),
                pltpu.VMEM((hd, 2 * rows), f32),
                pltpu.VMEM((hd, 2 * rows), f32),
                pltpu.VMEM((width, bq), f32),
                pltpu.VMEM((8, bq), f32),
            ],
        ),
        out_shape=[
            jax.ShapeDtypeStruct((groups, width, rows), bf16),
            jax.ShapeDtypeStruct((groups, hd, 2 * rows), f32),
            jax.ShapeDtypeStruct((hd // 2, 2 * rows), f32),
        ],
        compiler_params=vmem(48),
        cost_estimate=pl.CostEstimate(
            flops=90 * groups * width * rows * rows, bytes_accessed=8 * groups * width * rows, transcendentals=0
        ),
        name="attn_bwd",
    )(bounds, start, q, o, lse, do, cosT, sinT, got, sent, got, sent, *deps)


def local_layout(lengths_row, t, rows, bq, bk, own0):
    slot = t * rows + jnp.arange(rows, dtype=jnp.int32)
    ends = jnp.cumsum(lengths_row)
    passed = (slot[:, None] >= ends[None, :]).astype(jnp.int32)
    begin = jnp.sum(passed * lengths_row[None, :], axis=1)
    valid = slot < ends[-1]
    shift = own0 - t * rows
    start = jnp.where(valid, begin + shift, 1 << 30)
    nqb = rows // bq
    first = begin.reshape(nqb, bq)[:, 0] + shift
    last_start = jnp.max(jnp.where(valid, begin + shift, 0).reshape(nqb, bq), axis=1)
    any_valid = valid.reshape(nqb, bq)[:, 0]
    all_valid = valid.reshape(nqb, bq)[:, -1]
    q0 = own0 + jnp.arange(nqb, dtype=jnp.int32) * bq
    k0 = first // bk
    last = jnp.minimum(q0 + bq - 1, ends[-1] + shift - 1)
    k3 = last // bk + 1
    k1 = jnp.minimum((last_start + bk - 1) // bk, k3)
    k2 = jnp.minimum(jnp.maximum((q0 + 1) // bk, k1), k3)
    k1 = jnp.where(all_valid, k1, k3)
    k2 = jnp.where(all_valid, k2, k3)
    bounds = jnp.where(any_valid[:, None], jnp.stack([k0, k1, k2, k3], axis=1), 0).astype(jnp.int32)
    return slot, (slot - begin).astype(f32), valid, start[None, :], bounds


def turned_rows(x, cosv, sinv, n):
    a, b = x[:n], x[n:]
    return jnp.concatenate([a * cosv - b * sinv, a * sinv + b * cosv], axis=0)


def put_queries(raw, cosv, sinv, hd, out):
    half, quarter = hd // 2, hd // 4
    scale = hd**-0.5
    width = out.shape[1]
    for h in range(raw.shape[0] // hd):
        x = raw[h * hd : (h + 1) * hd]
        y = jnp.concatenate([x[:half], turned_rows(x[half:], cosv, sinv, quarter)], axis=0).astype(bf16)
        at = h * hd
        out[at // width, at % width : at % width + hd, :] = (y.astype(f32) * scale).astype(bf16)


def pre_kernel(hd, x_ref, gain_ref, wkv_ref, wr_ref, wq_ref, cos_ref, sin_ref, fin, tied, shared, q, wkvT, wrT, wqT):
    @pl.when(pl.program_id(0) == 0)
    def _():
        wkvT[...] = wkv_ref[...].T
        wrT[...] = wr_ref[...].T
        wqT[...] = wq_ref[...].T

    x = x_ref[...].astype(f32)
    normed = x * lax.rsqrt(jnp.mean(x * x, axis=-1, keepdims=True) + eps_norm)
    f = (normed * gain_ref[...]).astype(bf16)
    fin[...] = f
    cosv, sinv = cos_ref[...], sin_ref[...]
    tied[...] = dot_nt(wkvT[...], f).astype(bf16)
    shared[...] = turned_rows(dot_nt(wrT[...], f), cosv, sinv, hd // 4).astype(bf16)
    put_queries(dot_nt(wqT[...], f), cosv, sinv, hd, q)


def pre_call(x, gain, w_kv, w_rope, w_query, cosT, sinT, hd, per, bt=256):
    rows, width = x.shape
    kv, half, qn = w_kv.shape[1], w_rope.shape[1], w_query.shape[1]
    groups = kv // hd
    full = lambda a: pl.BlockSpec(a.shape, lambda i: (0, 0), pipeline_mode=pl.Buffered(1))
    return pl.pallas_call(
        functools.partial(pre_kernel, hd),
        grid=(rows // bt,),
        in_specs=[
            pl.BlockSpec((bt, width), lambda i: (i, 0)),
            pl.BlockSpec((1, width), lambda i: (0, 0)),
            full(w_kv),
            full(w_rope),
            full(w_query),
            pl.BlockSpec((hd // 4, bt), lambda i: (0, i)),
            pl.BlockSpec((hd // 4, bt), lambda i: (0, i)),
        ],
        out_specs=[
            pl.BlockSpec((bt, width), lambda i: (i, 0)),
            pl.BlockSpec((kv, bt), lambda i: (0, i)),
            pl.BlockSpec((half, bt), lambda i: (0, i)),
            pl.BlockSpec((groups, per * hd, bt), lambda i: (0, 0, i)),
        ],
        out_shape=[
            jax.ShapeDtypeStruct((rows, width), bf16),
            jax.ShapeDtypeStruct((kv, rows), bf16),
            jax.ShapeDtypeStruct((half, rows), bf16),
            jax.ShapeDtypeStruct((groups, per * hd, rows), bf16),
        ],
        scratch_shapes=[pltpu.VMEM((kv, width), bf16), pltpu.VMEM((half, width), bf16), pltpu.VMEM((qn, width), bf16)],
        compiler_params=vmem(32),
        cost_estimate=pl.CostEstimate(flops=4 * rows * width * (qn + kv + half), bytes_accessed=8 * rows * width, transcendentals=0),
        name="first_projections",
    )(x, gain[None, :], w_kv, w_rope, w_query, cosT, sinT)


def kv_kernel(place, f_ref, mine, other, tied_a, shared, sent, w_ref):
    n = mine.shape[0]
    core = place[0]
    w_ref[pl.ds(pl.multiple_of(core * n, n), n), :] = mine[...]
    w_ref[pl.ds(pl.multiple_of((1 - core) * n, n), n), :] = other[...]
    kv = tied_a.shape[0]
    sent[:kv, :] = tied_a[...]
    sent[kv : 2 * kv, :] = dot_nt(w_ref[...].T, f_ref[...]).astype(bf16)
    sent[2 * kv :, :] = shared[...]


def kv_call(place, f, mine, other, tied_a, shared):
    kv, rows = tied_a.shape
    total = 2 * kv + shared.shape[0]
    width = f.shape[1]
    full = lambda a: pl.BlockSpec(a, lambda i, p: (0, 0))
    return pl.pallas_call(
        kv_kernel,
        grid_spec=pltpu.PrefetchScalarGridSpec(
            num_scalar_prefetch=1,
            grid=(1,),
            in_specs=[full(f.shape), full(mine.shape), full(other.shape), full(tied_a.shape), full(shared.shape)],
            out_specs=[full((total, rows)), full((width, kv))],
        ),
        out_shape=[jax.ShapeDtypeStruct((total, rows), bf16), jax.ShapeDtypeStruct((width, kv), bf16)],
        compiler_params=vmem(32),
        cost_estimate=pl.CostEstimate(flops=4 * rows * width * kv, bytes_accessed=2 * rows * width, transcendentals=0),
        name="other_keys",
    )(place, f, mine, other, tied_a, shared)


def query_kernel(hd, place, f_ref, mine, other, cos_ref, sin_ref, q, w_ref, wT):
    @pl.when(pl.program_id(0) == 0)
    def _():
        n = mine.shape[0]
        core = place[0]
        w_ref[pl.ds(pl.multiple_of(core * n, n), n), :] = mine[...]
        w_ref[pl.ds(pl.multiple_of((1 - core) * n, n), n), :] = other[...]
        wT[...] = w_ref[...].T

    put_queries(dot_nt(wT[...], f_ref[...]), cos_ref[...], sin_ref[...], hd, q)


def query_call(place, f, mine, other, cosT, sinT, hd, groups, per, bt=256):
    rows, width = f.shape
    qn = mine.shape[1]
    full = lambda a: pl.BlockSpec(a, lambda i, p: (0, 0))
    return pl.pallas_call(
        functools.partial(query_kernel, hd),
        grid_spec=pltpu.PrefetchScalarGridSpec(
            num_scalar_prefetch=1,
            grid=(rows // bt,),
            in_specs=[
                pl.BlockSpec((bt, width), lambda i, p: (i, 0)),
                full(mine.shape),
                full(other.shape),
                pl.BlockSpec((hd // 4, bt), lambda i, p: (0, i)),
                pl.BlockSpec((hd // 4, bt), lambda i, p: (0, i)),
            ],
            out_specs=[pl.BlockSpec((groups, per * hd, bt), lambda i, p: (0, 0, i)), full((width, qn))],
            scratch_shapes=[pltpu.VMEM((qn, width), bf16)],
        ),
        out_shape=[jax.ShapeDtypeStruct((groups, per * hd, rows), bf16), jax.ShapeDtypeStruct((width, qn), bf16)],
        compiler_params=vmem(32),
        cost_estimate=pl.CostEstimate(flops=4 * rows * width * qn, bytes_accessed=4 * rows * width, transcendentals=0),
        name="other_queries",
    )(place, f, mine, other, cosT, sinT)


def mlp_kernel(first, pieces, edge, deps, place, *refs):
    s_ref, c_ref = refs[:2]
    refs = refs[2:]
    if not first:
        sT, cT = refs[:2]; refs = refs[2:]
    if pieces:
        gs, us, dn, refs = refs[:2], refs[2:4], refs[4:6], refs[6:]
    else:
        wg_ref, wu_ref, wd_ref = refs[:3]; refs = refs[3:]
    refs = refs[deps:]
    hid, gg, ug, keep, send = refs[:5]
    refs = refs[5:]
    if first:
        sT, cT = refs[:2]; refs = refs[2:]
    if pieces:
        wg_ref, wu_ref, wd_ref = refs[:3]
    i = pl.program_id(0)
    core = place[0]
    if first:
        @pl.when(i==0)
        def _():
            sT[...] = s_ref[...].T
            cT[...] = c_ref[...].T
    if pieces:
        n4 = gs[0].shape[0]
        for k in range(2):
            at = pl.multiple_of(place[1+k]*n4, n4)
            wg_ref[pl.ds(at,n4),:] = gs[k][...]
            wu_ref[pl.ds(at,n4),:] = us[k][...]
            wd_ref[:,pl.ds(at,n4)] = dn[k][...]
    rows = s_ref.shape[0]
    width = s_ref.shape[1]
    def tile(n):
        step = rows//4
        for r in range(4):
            rs = slice(r*step,(r+1)*step)
            gate = dot(s_ref[rs,:], wg_ref[:,:n]); up = dot(s_ref[rs,:], wu_ref[:,:n])
            hg = dot_nt(c_ref[rs,:], wd_ref[:n,:])
            sig = 1.0/(1.0+jnp.exp(-gate))
            act = gate*sig
            hid[rs,:n] = (act*up).astype(bf16)
            gg[rs,:n] = (hg*up*(sig+act*(1.0-sig))).astype(bf16)
            ug[rs,:n] = (hg*act).astype(bf16)
        h = hid[:,:n]; g_ = gg[:,:n]; u_ = ug[:,:n]
        hw = width//2
        for ref, side in ((keep,core),(send,1-core)):
            at = pl.ds(pl.multiple_of(side*hw,hw),hw)
            ref[0,:,:n] = dot(sT[at,:],g_).astype(bf16)
            ref[1,:,:n] = dot(sT[at,:],u_).astype(bf16)
            ref[2,:,:n] = dot(cT[at,:],h).astype(bf16)
    bn = wg_ref.shape[1]
    if edge == bn:
        tile(bn)
    else:
        last = pl.num_programs(0)-1
        pl.when(i<last)(lambda: tile(bn))
        pl.when(i==last)(lambda: tile(edge))

def mlp_call(place, s, c, turned, weights, base, cols, bn=256, deps=()):
    rows, width = s.shape
    pieces = len(weights)==6
    first = turned is None
    tiles = -(-cols//bn)
    edge = cols-(tiles-1)*bn
    whole = pl.BlockSpec((rows,width),lambda i,p:(0,0),pipeline_mode=pl.Buffered(1))
    wholeT = pl.BlockSpec((width,rows),lambda i,p:(0,0),pipeline_mode=pl.Buffered(1))
    wholeTo = pl.BlockSpec((width,rows),lambda i,p:(0,0))
    in_specs=[whole,whole]+([] if first else [wholeT,wholeT])
    if pieces:
        n4 = weights[0].shape[0]
        in_specs += [pl.BlockSpec((n4,bn),lambda i,p:(0,base+i))]*4 + [pl.BlockSpec((bn,n4),lambda i,p:(base+i,0))]*2
    else:
        in_specs += [pl.BlockSpec((width,bn),lambda i,p:(0,base+i))]*2 + [pl.BlockSpec((bn,width),lambda i,p:(base+i,0))]
    in_specs += [ANY]*len(deps)
    act = pl.BlockSpec((rows,bn),lambda i,p:(0,i))
    part = pl.BlockSpec((3,width//2,bn),lambda i,p:(0,0,i))
    acts = jax.ShapeDtypeStruct((rows,cols),bf16)
    parts = jax.ShapeDtypeStruct((3,width//2,cols),bf16)
    tsh = jax.ShapeDtypeStruct((width,rows),bf16)
    w_specs = [pl.BlockSpec((width,bn),lambda i,p:(0,i))]*2+[pl.BlockSpec((bn,width),lambda i,p:(i,0))] if pieces else []
    w_shapes = [jax.ShapeDtypeStruct((width,cols),bf16)]*2+[jax.ShapeDtypeStruct((cols,width),bf16)] if pieces else []
    out = pl.pallas_call(
        functools.partial(mlp_kernel,first,pieces,edge,len(deps)),
        grid_spec=pltpu.PrefetchScalarGridSpec(
            num_scalar_prefetch=1, grid=(tiles,), in_specs=in_specs,
            out_specs=[act]*3+[part]*2+([wholeTo]*2 if first else [])+w_specs,
        ),
        out_shape=[acts]*3+[parts]*2+([tsh]*2 if first else [])+w_shapes,
        compiler_params=pltpu.CompilerParams(vmem_limit_bytes=56<<20),
        cost_estimate=pl.CostEstimate(flops=22*rows*width*cols,bytes_accessed=2*(4*rows*width+9*width*cols),transcendentals=rows*cols),
        name="mlp_grads",
    )(place, s, c, *(() if first else turned), *weights, *deps)
    return out


def fold_kernel(counts, sides, deps, bits, *refs):
    n = sum(counts)
    outs = refs[n * sides + deps :]
    for side, out in enumerate(outs):
        at, col = side * n, 0
        for count in counts:
            total = None
            for ref in refs[at : at + count]:
                part = ref[0].astype(f32)
                total = part if total is None else total + part
            width = total.shape[1]
            out[:, col : col + width] = total.astype(out.dtype)
            at, col = at + count, col + width


def fold(groups, bit=None, deps=()):
    groups = [[a if isinstance(a, tuple) else (a[None], 0) for a in g] for g in groups]
    flat = [a for g in groups for a in g]
    rows = flat[0][0].shape[1]
    cols = sum(g[0][0].shape[2] for g in groups)
    sides = 1 if bit is None else 2
    rows_out = rows // sides
    step = rows_out
    while step % 32 == 0 and step * cols > 128 * 1408:
        step //= 2
    blocks = rows_out // step

    def spec(a, k, side):
        shape = (1, step, a.shape[2])
        if sides == 1:
            return pl.BlockSpec(shape, lambda i, b: (k, i, 0))
        if side == 0:
            return pl.BlockSpec(shape, lambda i, b: (k, b[0] * blocks + i, 0))
        return pl.BlockSpec(shape, lambda i, b: (k, (1 - b[0]) * blocks + i, 0))

    out = jax.ShapeDtypeStruct((rows_out, cols), bf16)
    scalars = jnp.reshape(jnp.int32(0) if bit is None else bit, (1,)).astype(jnp.int32)
    result = pl.pallas_call(
        functools.partial(fold_kernel, [len(g) for g in groups], sides, len(deps)),
        grid_spec=pltpu.PrefetchScalarGridSpec(
            num_scalar_prefetch=1,
            grid=(blocks,),
            in_specs=[spec(a, k, side) for side in range(sides) for a, k in flat] + [ANY] * len(deps),
            out_specs=[pl.BlockSpec((step, cols), lambda i, b: (i, 0))] * sides,
        ),
        out_shape=[out] * sides,
        compiler_params=vmem(32),
        cost_estimate=pl.CostEstimate(
            flops=3 * rows * cols, bytes_accessed=8 * rows * cols, transcendentals=0
        ),
        name="fold",
    )(scalars, *[a for _ in range(sides) for a, _ in flat], *deps)
    return result if sides == 2 else result[0]


def take_kernel(deps, place, *refs):
    refs[-1][...] = refs[0][...]


def take(w, at, axis, parts, deps=()):
    shape = list(w.shape)
    shape[axis] //= parts
    block = tuple(shape)
    where = (lambda i, p: (p[0], 0)) if axis == 0 else (lambda i, p: (0, p[0]))
    return pl.pallas_call(
        functools.partial(take_kernel, len(deps)),
        grid_spec=pltpu.PrefetchScalarGridSpec(
            num_scalar_prefetch=1,
            grid=(1,),
            in_specs=[pl.BlockSpec(block, where)] + [pl.BlockSpec(memory_space=pl.ANY)] * len(deps),
            out_specs=pl.BlockSpec(block, lambda i, p: (0, 0)),
        ),
        out_shape=jax.ShapeDtypeStruct(block, w.dtype),
        compiler_params=vmem(32),
        cost_estimate=pl.CostEstimate(flops=0, bytes_accessed=4 * block[0] * block[1], transcendentals=0),
        name="take",
    )(jnp.reshape(at, (1,)).astype(jnp.int32), w, *deps)


def hold(x, dep):
    return pl.pallas_call(
        lambda a, b, c: None,
        in_specs=[ANY, ANY],
        out_specs=ANY,
        out_shape=jax.ShapeDtypeStruct(x.shape, x.dtype),
        input_output_aliases={0: 0},
        name="hold",
    )(x, dep)


def gather_kernel(turn, n, deps, order, *refs):
    pieces, refs = refs[:n], refs[n + deps :]
    out = refs[0]
    rows = pieces[0].shape[0]
    held = refs[1] if turn else out
    for k, piece in enumerate(pieces):
        at = pl.ds(pl.multiple_of(order[k] * rows, rows), rows)
        held[at, :] = piece[...].astype(held.dtype)
    if turn:
        out[...] = held[...].T.astype(f32)


def gathered(pieces, order, turn, deps=(), start=0, cols=None):
    n = len(pieces)
    rows = pieces[0].shape[0]
    cols = cols or pieces[0].shape[1]
    wide = 128 if turn or cols % 256 or start % 256 else 256
    base = start // wide
    total = n * rows
    return pl.pallas_call(
        functools.partial(gather_kernel, turn, n, len(deps)),
        grid_spec=pltpu.PrefetchScalarGridSpec(
            num_scalar_prefetch=1,
            grid=(cols // wide,),
            in_specs=[pl.BlockSpec((rows, wide), lambda i, o: (0, base + i))] * n + [ANY] * len(deps),
            out_specs=pl.BlockSpec((wide, total), lambda i, o: (i, 0))
            if turn
            else pl.BlockSpec((total, wide), lambda i, o: (0, i)),
            scratch_shapes=[pltpu.VMEM((total, wide), bf16)] if turn else [],
        ),
        out_shape=jax.ShapeDtypeStruct((cols, total) if turn else (total, cols), f32),
        compiler_params=vmem(32),
        cost_estimate=pl.CostEstimate(flops=0, bytes_accessed=6 * total * cols, transcendentals=0),
        name="gathered",
    )(order, *pieces, *deps)


def gather_small_kernel(n, kn, half, deps, order, *refs):
    pieces, refs = refs[:n], refs[n + deps :]
    kv, rope, gains, held = refs
    rows = pieces[0].shape[0]
    for k, piece in enumerate(pieces):
        at = pl.ds(pl.multiple_of(order[k] * rows, rows), rows)
        kv[at, :] = piece[:, :kn].astype(f32)
        held[at, :] = piece[:, kn:].astype(f32)
    rope[...] = held[:, :half]
    gains[...] = held[...].T[half : half + 8, :]


def gathered_small(pieces, order, kn, half, deps=()):
    n = len(pieces)
    rows, cols = pieces[0].shape
    total = n * rows
    full = lambda a: pl.BlockSpec(a, lambda i, o: (0, 0))
    shapes = [(total, kn), (total, half), (8, total)]
    return pl.pallas_call(
        functools.partial(gather_small_kernel, n, kn, half, len(deps)),
        grid_spec=pltpu.PrefetchScalarGridSpec(
            num_scalar_prefetch=1,
            grid=(1,),
            in_specs=[full((rows, cols))] * n + [ANY] * len(deps),
            out_specs=[full(a) for a in shapes],
            scratch_shapes=[pltpu.VMEM((total, 128), f32)],
        ),
        out_shape=[jax.ShapeDtypeStruct(a, f32) for a in shapes],
        compiler_params=vmem(32),
        cost_estimate=pl.CostEstimate(flops=0, bytes_accessed=6 * total * cols, transcendentals=0),
        name="gathered_small",
    )(order, *pieces, *deps)


def wgrad_kernel(n, deps, place, l_ref, *refs):
    right, refs = refs[:n], refs[n + deps :]
    keep, send, lT = refs
    lT[...] = l_ref[...].T
    core = place[0]
    hw = keep.shape[0]
    for out, side in ((send, 1 - core), (keep, core)):
        rows = lT[pl.ds(pl.multiple_of(side * hw, hw), hw), :]
        at = 0
        for r in right:
            k = r.shape[-2]
            out[:, at : at + k] = dot_nt(rows, r[...].reshape(r.shape[-2:])).astype(bf16)
            at += k


def wgrad(place, left, right, deps=()):
    rows, width = left.shape
    right = [r if isinstance(r, tuple) else (r[None], 0) for r in right]
    cols = sum(r.shape[1] for r, _ in right)
    full = lambda a: pl.BlockSpec(a, lambda i, p: (0, 0))
    part = jax.ShapeDtypeStruct((width // 2, cols), bf16)

    def spec(r, k):
        return pl.BlockSpec((1, *r.shape[1:]), lambda i, p: (k, 0, 0))

    return pl.pallas_call(
        functools.partial(wgrad_kernel, len(right), len(deps)),
        grid_spec=pltpu.PrefetchScalarGridSpec(
            num_scalar_prefetch=1,
            grid=(1,),
            in_specs=[full(left.shape)] + [spec(r, k) for r, k in right] + [ANY] * len(deps),
            out_specs=[full(part.shape)] * 2,
            scratch_shapes=[pltpu.VMEM((width, rows), bf16)],
        ),
        out_shape=[part] * 2,
        compiler_params=vmem(48),
        cost_estimate=pl.CostEstimate(flops=4 * rows * width * cols, bytes_accessed=4 * rows * width, transcendentals=0),
        name="weight_grads",
    )(place, left, *[r for r, _ in right], *deps)


def back_kernel(n, *refs):
    tgs, sgs, out = refs[:n], refs[n : 2 * n], refs[2 * n]
    hd = tgs[0].shape[1]
    for k, tg in enumerate(tgs):
        out[k * hd : (k + 1) * hd, :] = tg[0].astype(bf16)
    total = sgs[0][...]
    for s in sgs[1:]:
        total = total + s[...]
    out[n * hd :, :] = total.astype(bf16)


def back_call(tgs, sgs):
    n = len(tgs)
    _, hd, two = tgs[0].shape
    rows = two // 2
    return pl.pallas_call(
        functools.partial(back_kernel, n),
        grid=(1,),
        in_specs=[pl.BlockSpec((1, hd, rows), lambda i: (0, 0, 0))] * n
        + [pl.BlockSpec((hd // 2, rows), lambda i: (0, 0))] * n,
        out_specs=pl.BlockSpec((n * hd + hd // 2, rows), lambda i: (0, 0)),
        out_shape=jax.ShapeDtypeStruct((n * hd + hd // 2, rows), bf16),
        compiler_params=vmem(32),
        cost_estimate=pl.CostEstimate(flops=0, bytes_accessed=6 * n * hd * rows, transcendentals=0),
        name="partner_key_grads",
    )(*tgs, *sgs)


def own_kernel(n, deps, *refs):
    tgs, sgs, back, cos_ref, sin_ref = refs[:n], refs[n : 2 * n], refs[2 * n], refs[2 * n + 1], refs[2 * n + 2]
    out = refs[2 * n + 3 + deps]
    hd = tgs[0].shape[1]
    for k, tg in enumerate(tgs):
        other = (k + n // 2) % n
        mine = back[other * hd : (other + 1) * hd, :].astype(f32)
        out[k * hd : (k + 1) * hd, :] = (tg[0] + mine).astype(bf16)
    total = back[n * hd :, :].astype(f32)
    for s in sgs:
        total = total + s[...]
    out[n * hd :, :] = turned_rows(total, cos_ref[...], -sin_ref[...], hd // 4).astype(bf16)


def own_call(tgs, sgs, back, cosT, sinT, deps=()):
    n = len(tgs)
    _, hd, two = tgs[0].shape
    rows = two // 2
    full = lambda a: pl.BlockSpec(a.shape, lambda i: (0, 0))
    return pl.pallas_call(
        functools.partial(own_kernel, n, len(deps)),
        grid=(1,),
        in_specs=[pl.BlockSpec((1, hd, rows), lambda i: (0, 0, 1))] * n
        + [pl.BlockSpec((hd // 2, rows), lambda i: (0, 1))] * n
        + [full(back), full(cosT), full(sinT)]
        + [ANY] * len(deps),
        out_specs=full(back),
        out_shape=jax.ShapeDtypeStruct(back.shape, bf16),
        compiler_params=vmem(32),
        cost_estimate=pl.CostEstimate(flops=0, bytes_accessed=8 * n * hd * rows, transcendentals=0),
        name="own_key_grads",
    )(*tgs, *sgs, back, cosT, sinT, *deps)


def post_kernel(nq, deps, x_ref, mg_ref, gain_ref, kv_ref, wqa, wqb, wka, wkb, wr, *refs):
    dqs, refs = refs[:nq], refs[nq + deps :]
    out, gain_out = refs
    kn = wka.shape[1]
    hn = wqa.shape[1]
    g = [r[0] for r in dqs]
    qa = jnp.concatenate(g[: nq // 2], axis=0).T
    qb = jnp.concatenate(g[nq // 2 :], axis=0).T
    kv = kv_ref[...]
    first = dot_nt(qa, wqa[...]) + dot_nt(qb, wqb[...])
    first = first + dot_nt(kv[:kn].T, wka[...]) + dot_nt(kv[kn : 2 * kn].T, wkb[...])
    first = first + dot_nt(kv[2 * kn :].T, wr[...])
    x = x_ref[...].astype(f32)
    factor = lax.rsqrt(jnp.mean(x * x, axis=-1, keepdims=True) + eps_norm)
    normed = x * factor
    inner = first * gain_ref[...]
    back = factor * (inner - normed * jnp.mean(inner * normed, axis=-1, keepdims=True))
    out[...] = (mg_ref[...] + back).astype(bf16)

    @pl.when(pl.program_id(0) == 0)
    def _():
        gain_out[...] = jnp.zeros_like(gain_out)

    gain_out[...] += jnp.sum(first * normed, axis=0, keepdims=True)


def post_call(x, middle_grad, gain, kv, weights, dqs, deps=(), bt=256):
    rows, width = x.shape
    full = lambda a: pl.BlockSpec(a.shape, lambda i: (0, 0), pipeline_mode=pl.Buffered(1))
    row = pl.BlockSpec((bt, width), lambda i: (i, 0))
    one = pl.BlockSpec((1, width), lambda i: (0, 0))
    return pl.pallas_call(
        functools.partial(post_kernel, len(dqs), len(deps)),
        grid=(rows // bt,),
        in_specs=[row, row, one, pl.BlockSpec((kv.shape[0], bt), lambda i: (0, i))]
        + [full(w) for w in weights]
        + [pl.BlockSpec((1, d.shape[1], bt), lambda i: (0, 0, i)) for d in dqs]
        + [ANY] * len(deps),
        out_specs=[row, one],
        out_shape=[jax.ShapeDtypeStruct((rows, width), bf16), jax.ShapeDtypeStruct((1, width), f32)],
        compiler_params=vmem(40),
        cost_estimate=pl.CostEstimate(flops=5 * rows * width * width, bytes_accessed=16 * rows * width, transcendentals=0),
        name="token_grads",
    )(x, middle_grad, gain[None, :], kv, *weights, *dqs, *deps)


def small_kernel(kn, half, place, f_ref, kv_ref, gain_a, gain_b, keep_a, send_a, keep_b, send_b, lT, rows_s, rows_g):
    lT[...] = f_ref[...].T
    rows_s[...] = jnp.zeros_like(rows_s)
    rows_s[:half, :] = kv_ref[2 * kn :, :]
    rows_g[...] = jnp.zeros_like(rows_g)
    rows_g[half : half + 1, :] = gain_a[...]
    rows_g[half + 1 : half + 2, :] = gain_b[...]
    gains = rows_g[...].T
    rows_g_ref = rows_g
    core = place[0]
    hw = keep_a.shape[0]
    rope = dot_nt(lT[...], rows_s[...]) + gains
    lT_rows = [lT[:hw, :], lT[hw:, :]]
    first = core == 0
    for (a, b), side in (((send_a, send_b), 1), ((keep_a, keep_b), 0)):
        low = jnp.logical_xor(first, side == 1)
        rows = jnp.where(low, lT_rows[0], lT_rows[1])
        small = jnp.where(low, rope[:hw], rope[hw:]).astype(bf16)
        a[:, :kn] = dot_nt(rows, kv_ref[:kn, :]).astype(bf16)
        a[:, kn:] = small
        b[:, :kn] = dot_nt(rows, kv_ref[kn : 2 * kn, :]).astype(bf16)
        b[:, kn:] = small


def small_call(place, f, kv, gain_a, gain_b, kn, half):
    rows, width = f.shape
    full = lambda a: pl.BlockSpec(a, lambda i, p: (0, 0))
    part = jax.ShapeDtypeStruct((width // 2, kn + 128), bf16)
    return pl.pallas_call(
        functools.partial(small_kernel, kn, half),
        grid_spec=pltpu.PrefetchScalarGridSpec(
            num_scalar_prefetch=1,
            grid=(1,),
            in_specs=[full(f.shape), full(kv.shape), full((1, width)), full((1, width))],
            out_specs=[full(part.shape)] * 4,
            scratch_shapes=[pltpu.VMEM((width, rows), bf16), pltpu.VMEM((128, rows), bf16), pltpu.VMEM((128, width), f32)],
        ),
        out_shape=[part] * 4,
        compiler_params=vmem(48),
        cost_estimate=pl.CostEstimate(flops=2 * rows * width * 512, bytes_accessed=3 * rows * width, transcendentals=0),
        name="small_grads",
    )(place, f, kv, gain_a, gain_b)


def rms_parts(values):
    factor = lax.rsqrt(jnp.mean(values * values, axis=-1, keepdims=True) + eps_norm)
    return values * factor, factor


def norm_back(grad, normed, factor, gain):
    inner = grad * gain
    return factor * (inner - normed * jnp.mean(inner * normed, axis=-1, keepdims=True))


def mm(a, b, ca, cb):
    return lax.dot_general(a, b, (((ca,), (cb,)), ((), ())), preferred_element_type=f32)


def swap(x, axis, bit):
    n = lax.axis_size(axis)
    return lax.ppermute(x, axis, [(i, i ^ bit) for i in range(n)])


def joined(mine, other, bit):
    first = bit == 0
    return jnp.concatenate([jnp.where(first, mine, other), jnp.where(first, other, mine)], axis=0)


class Order:
    def __init__(self, first):
        self.last = first

    def after(self, out):
        self.last = out[0] if isinstance(out, (tuple, list)) else out
        return out

    def fold(self, groups, bit=None):
        return self.after(fold(groups, bit, (self.last,)))


def spread(piece, steps):
    pieces = [piece]
    for step in steps:
        pieces = pieces + [swap(p, "dp", step) for p in pieces]
    return pieces


def piece_order(bits):
    order = [jnp.int32(0)]
    for bit in bits:
        order = [2 * o + b for o in order for b in (bit, 1 - bit)]
    return jnp.stack(order).astype(jnp.int32)


class Sum:
    def __init__(self, run, bits):
        self.run, self.bits, self.steps = run, bits, [1]

    def x(self, groups):
        self.keep, send = self.run.fold(groups, self.bits[1])
        self.got = swap(send, "dp", 2)
        self.steps = [2, 1]

    def z(self):
        self.keep, send = self.run.fold([[self.keep, self.got]], self.bits[2])
        self.got = swap(send, "dp", 4)
        self.steps = [4, 2, 1]

    def line(self, step=8):
        self.keep = self.run.fold([[self.keep, self.got]])
        self.got = swap(self.keep, "dp", step)

    def end(self):
        step = 16
        while step < lax.axis_size("dp"):
            self.line(step)
            step *= 2
        self.keep = self.run.fold([[self.keep, self.got]])
        self.pieces = spread(self.keep, self.steps)
        self.order = piece_order(self.bits[: len(self.steps)])


def body(tokens, lengths, attn_gain, w_query, w_kv, w_rope, w_out, mlp_gain, w_gate, w_up, w_down, out_grad):
    rows, width = tokens.shape
    shards = lax.axis_size("tensor")
    t = lax.axis_index("tensor")
    index = lax.axis_index("dp")
    bits = (index & 1, (index >> 1) & 1, (index >> 2) & 1)
    core = bits[0]
    half = w_rope.shape[1]
    hd = 2 * half
    kv_own = w_kv.shape[1]
    q_own = w_query.shape[1]
    groups = kv_own // hd
    per = q_own // kv_own
    ff = w_gate.shape[1]
    own0 = rows
    bq_f, bk_f, bq_b, bk_b = 256, 512, 512, 256
    place = jnp.stack([core, core, 1 - core]).astype(jnp.int32)

    kv_piece = take(w_kv, core, 0, 2)
    kv_got = swap(kv_piece, "tensor", 1)
    q_piece = take(w_query, core, 0, 2, (kv_piece,))
    q_got = swap(q_piece, "tensor", 1)
    gate_piece = take(w_gate, core, 0, 2, (q_piece,))
    gate_got = swap(gate_piece, "tensor", 1)

    slot, position, valid, start, bounds_f = local_layout(lengths[0], t, rows, bq_f, bk_f, own0)
    bounds_b = local_layout(lengths[0], t, rows, bq_b, bk_b, own0)[4]
    quarter = half // 2
    freq = 10000.0 ** (-jnp.arange(quarter, dtype=f32) / quarter)
    angle = freq[:, None] * position[None, :]
    cosT, sinT = jnp.cos(angle), jnp.sin(angle)

    first_in, tied_a, shared, q_a = pre_call(tokens, attn_gain, w_kv, w_rope, w_query, cosT, sinT, hd, per)
    sent, w_kv_o = kv_call(place, first_in, kv_got, swap(kv_got, "dp", 1), tied_a, shared)
    got = lax.ppermute(sent, "tensor", [(i, i + 1) for i in range(shards - 1)])
    up_piece = take(w_up, core, 0, 2, (got,))
    up_got = swap(up_piece, "tensor", 1)
    out_piece = take(w_out, core, 0, 2, (up_piece,))
    out_got = swap(out_piece, "tensor", 1)
    down_piece = take(w_down, core, 1, 2, (out_piece,))
    down_got = swap(down_piece, "tensor", 1)

    def both(p):
        return p, swap(p, "dp", 1)

    at_a, at_b = (0, groups), (groups, 0)
    mixed_a, lse_a = attn_fwd(bounds_f, start, q_a, sent, got, hd, at_a, bq_f, bk_f, (down_piece,))
    q_got = hold(q_got, mixed_a)
    q_b, w_query_o = query_call(place, first_in, q_got, swap(q_got, "dp", 1), cosT, sinT, hd, groups, per)
    mixed_b, lse_b = attn_fwd(bounds_f, start, q_b, sent, got, hd, at_b, bq_f, bk_f)
    out_got = hold(out_got, mixed_b)
    w_out_o = joined(out_got, swap(out_got, "dp", 1), core)
    mix_a, mix_b = mixed_a.reshape(-1, rows), mixed_b.reshape(-1, rows)
    inputs = tokens.astype(f32)
    middle = inputs + mm(mix_a, w_out, 0, 0) + mm(mix_b, w_out_o, 0, 0)
    normed_two, factor_two = rms_parts(middle)
    second_in = (normed_two * mlp_gain).astype(bf16)

    hid_a, gg_a, ug_a, keep_a, send_a, in_T, back_T = mlp_call(
        place, second_in, out_grad, None, (w_gate, w_up, w_down), 0, ff
    )
    core_a = swap(send_a, "dp", 1)
    gates, ups, downs = both(hold(gate_got, mixed_b)), both(hold(up_got, mixed_b)), both(hold(down_got, hid_a))
    second_a = mm(hold(gg_a, downs[0]), w_gate, 1, 1) + mm(hold(ug_a, downs[0]), w_up, 1, 1)
    hid_b, gg_b, ug_b, keep_b, send_b, w_gate_o, w_up_o, w_down_o = mlp_call(
        place, second_in, out_grad, (in_T, back_T), (*gates, *ups, *downs), 0, ff, deps=(second_a,)
    )
    core_b = swap(send_b, "dp", 1)
    hid_a = hold(hid_a, hid_b)
    layer_out = (middle + mm(hid_a, w_down, 1, 0) + mm(hid_b, w_down_o, 1, 0)).astype(bf16)
    run = Order(layer_out)
    ysend = [run.fold([[(keep_b, k), (core_b, k)]]) for k in range(3)]
    ygot = [swap(y, "tensor", 1) for y in ysend]
    gg_b, ug_b = hold(gg_b, run.last), hold(ug_b, run.last)
    second_grad = second_a + mm(gg_b, w_gate_o, 1, 1) + mm(ug_b, w_up_o, 1, 1)
    mlp_gain_part = jnp.sum(second_grad * normed_two, axis=0, keepdims=True)
    middle_grad = out_grad.astype(f32) + norm_back(second_grad, normed_two, factor_two, mlp_gain)
    attn_back = middle_grad.astype(bf16)
    live = valid[None, :].astype(bf16)
    mixed_grad_b = (mm(w_out_o, attn_back, 1, 1).astype(bf16) * live).reshape(mixed_b.shape)
    mixed_grad_a = (mm(w_out, attn_back, 1, 1).astype(bf16) * live).reshape(mixed_a.shape)

    def parts(x):
        return [(x, k) for k in range(groups)]

    def back(q, mixed, lse, grad, at, k):
        return run.after(
            attn_bwd(
                bounds_b, start, q, sent, got, mixed, lse, grad, cosT, sinT, hd, at, k, 1, bq_b, bk_b, (run.last,)
            )
        )

    wo_keep_b, wo_send_b = run.after(wgrad(place, attn_back, parts(mixed_b), (run.last,)))
    wo_core_b = swap(wo_send_b, "dp", 1)
    wo_keep_a, wo_send_a = run.after(wgrad(place, attn_back, parts(mixed_a), (run.last,)))
    wo_core_a = swap(wo_send_a, "dp", 1)

    gate_s, up_s, down_s, rest_s, small_s = (Sum(run, bits) for _ in range(5))
    gate_s.x([[(keep_a, 0), (core_a, 0), ygot[0]]])
    dq_b0, tg_b0, sg_b0 = back(q_b, mixed_b, lse_b, mixed_grad_b, at_b, 0)
    wo_got = swap(run.fold([[wo_keep_b, wo_core_b]]), "tensor", 1)
    gate_s.z()
    dq_b1, tg_b1, sg_b1 = back(q_b, mixed_b, lse_b, mixed_grad_b, at_b, 1)
    wq_keep_b, wq_send_b = run.after(wgrad(place, first_in, [(dq_b0, 0), (dq_b1, 0)], (run.last,)))
    wq_core_b = swap(wq_send_b, "dp", 1)
    up_s.x([[(keep_a, 1), (core_a, 1), ygot[1]]])
    gate_s.line()
    dq_a0, tg_a0, sg_a0 = back(q_a, mixed_a, lse_a, mixed_grad_a, at_a, 0)
    wq_got = swap(run.fold([[wq_keep_b, wq_core_b]]), "tensor", 1)
    up_s.z()
    down_s.x([[(keep_a, 2), (core_a, 2), ygot[2]]])
    gate_s.end()
    dq_a1, tg_a1, sg_a1 = back(q_a, mixed_a, lse_a, mixed_grad_a, at_a, 1)
    tgs, sgs = (tg_a0, tg_a1, tg_b0, tg_b1), (sg_a0, sg_a1, sg_b0, sg_b1)
    key_back = run.after(back_call(tgs, sgs))
    key_got = lax.ppermute(key_back, "tensor", [(i + 1, i) for i in range(shards - 1)])
    wq_keep_a, wq_send_a = run.after(wgrad(place, first_in, [(dq_a0, 0), (dq_a1, 0)], (run.last,)))
    wq_core_a = swap(wq_send_a, "dp", 1)
    down_s.z()
    up_s.line()
    rest_s.x([[wo_keep_a, wo_core_a, wo_got], [wq_keep_a, wq_core_a, wq_got]])
    kv_grad = run.after(own_call(tgs, sgs, key_got, cosT, sinT, (run.last,)))
    tokens_grad, attn_gain_part = post_call(
        tokens, middle_grad, attn_gain, kv_grad, (w_query, w_query_o, w_kv, w_kv_o, w_rope),
        (dq_a0, dq_a1, dq_b0, dq_b1), (run.last,),
    )
    run.last = attn_gain_part
    sm_keep_a, sm_send_a, sm_keep_b, sm_send_b = run.after(
        small_call(place, first_in, kv_grad, attn_gain_part, mlp_gain_part, kv_own, half)
    )
    sm_core_b = swap(sm_send_b, "dp", 1)
    sm_core_a = swap(sm_send_a, "dp", 1)
    down_s.line()
    rest_s.z()
    up_s.end()
    sm_got = swap(run.fold([[sm_keep_b, sm_core_b]]), "tensor", 1)
    gate_sum = run.after(gathered(gate_s.pieces, gate_s.order, False, (run.last,)))
    small_s.x([[sm_keep_a, sm_core_a, sm_got]])
    rest_s.line()
    down_s.end()
    small_s.line(4)
    small_s.line()
    rest_s.end()
    up_sum = run.after(gathered(up_s.pieces, up_s.order, False, (run.last,)))
    small_s.end()
    down_sum = run.after(gathered(down_s.pieces, down_s.order, True, (run.last,)))
    out_sum = run.after(gathered(rest_s.pieces, rest_s.order, True, (run.last,), 0, q_own))
    query_sum = run.after(gathered(rest_s.pieces, rest_s.order, False, (run.last,), q_own, q_own))
    kv_sum, rope_sum, gains = gathered_small(small_s.pieces, small_s.order, kv_own, half, (run.last,))
    return (
        layer_out,
        tokens_grad,
        gains[0],
        query_sum,
        kv_sum,
        rope_sum,
        out_sum,
        gains[1],
        gate_sum,
        up_sum,
        down_sum,
    )


def solution(mesh):
    rows = P(("dp", "tensor"), None)
    columns = P(None, "tensor")
    down = P("tensor", None)
    return jax.shard_map(
        body,
        mesh=mesh,
        in_specs=(rows, P("dp", None), P(), columns, columns, P(), down, P(), columns, columns, down, rows),
        out_specs=(rows, rows, P(), columns, columns, P(), down, P(), columns, columns, down),
        check_vma=False,
    )
```

time: 719 us -> 556 us (0.77)
  waiting for transfers between devices: 303 us -> 93.3 us
  Pallas kernels: 72.1 us -> 223 us
  matrix products: 135 us -> 43.7 us
  other arithmetic: 62.4 us -> 14 us
  starting transfers between devices: 64.5 us -> 102 us
    pallas_call x2 -> x67, Pallas kernels: 72.1 us -> 223 us  [the longest x2 57.7 us: mlp_call(): pl.pallas_call(functools.partial(mlp_kernel, first, pieces, edge, len(dep...]
    ppermute x62 -> x72, waiting for transfers between devices: 220 us -> 83.2 us  [swap(): return lax.ppermute(x, axis, [(i, i ^ bit) for i in range(n)])]
    dot_general x28 -> x10, matrix products: 135 us -> 43.7 us  [mm(): lax.dot_general(a, b, (((ca,), (cb,)), ((), ())), preferred_element_type=...]
    ppermute x1, waiting for transfers between devices: 51.8 us -> 10.1 us  [body(): got = lax.ppermute(sent, 'tensor', [(i, i + 1) for i in range(shards - 1)])]
    ppermute x62 -> x72, starting transfers between devices: 59.1 us -> 95.7 us  [swap(): return lax.ppermute(x, axis, [(i, i ^ bit) for i in range(n)])]
    unnamed x209 -> x282, local copies, waits for them, and re-layouts: 33.8 us -> 67.8 us
    ppermute x1, waiting for transfers between devices: 31.3 us -> 0.01 us  [body(): lax.ppermute(key_back, 'tensor', [(i + 1, i) for i in range(shards - 1)])]
    convert_element_type x36 -> x2, other arithmetic: 31.8 us -> 3.3 us  [the longest x1 2.69 us: body(): attn_back = middle_grad.astype(bf16)]
  transfers between devices with their start and end apart: 64 -> 74, of which waited for: 27 -> 15; matrix products, arithmetic and copies ran while one was open for 36% -> 11% of each run, Pallas kernels for 10% -> 35%
where the time goes in v2:
time: 556 us; the launch traced here: 550 us
  Pallas kernels  223 us (40%)
  starting transfers between devices  102 us (18%)
  waiting for transfers between devices  93.3 us (17%)
  local copies, waits for them, and re-layouts  70.9 us (13%)
  matrix products  43.7 us (8%)
  other arithmetic  14 us (3%)
    ppermute x72, starting transfers between devices, swap(): return lax.ppermute(x, axis, [(i, i ^ bit) for i in range(n)])  95.7 us
    ppermute x72, waiting for transfers between devices, swap(): return lax.ppermute(x, axis, [(i, i ^ bit) for i in range(n)])  83.2 us
    unnamed x282, local copies, waits for them, and re-layouts  67.8 us
    pallas_call x2, Pallas kernels, mlp_call(): pl.pallas_call(functools.partial(mlp_kernel, first, pieces, edge, len(dep...  57.7 us
    pallas_call x4, Pallas kernels, attn_bwd(): pl.pallas_call(functools.partial(bwd_kernel, heads, bk, hd ** (-0.5), len...  45.8 us
    dot_general x10, matrix products, mm(): lax.dot_general(a, b, (((ca,), (cb,)), ((), ())), preferred_element_type=...  43.7 us
    pallas_call x26, Pallas kernels, fold(): pl.pallas_call(functools.partial(fold_kernel, [len(g) for g in groups], s...  30.4 us
    pallas_call x2, Pallas kernels, attn_fwd(): pl.pallas_call(functools.partial(fwd_kernel, heads, bk, len(deps)), grid_...  28.7 us
  transfers between devices with their start and end apart: 74, of which 15 were waited for; matrix products, arithmetic and copies ran while one was open for 11% of the time, Pallas kernels for 35%

profile of v2, /device:TPU:0, one launch (start us, length us, event | category | flops | bytes accessed | tf_op | source)
XLA Modules:
  0.0 550.0 jit_solution(10061564996773396368)
XLA Ops:
  1.6 3.0 collective-permute-start
  14.8 4.4 first_projections.1
  28.3 4.6 collective-permute-start.2
  35.1 10.1 %collective-permute-done.2.refs_1_.refs_0_.refs_2_ = bf16[288,1024]{1,0:T(8,128)(2,1)S(1)} collective-permute-done((bf16[288,1024]{1,0:T(8,128)(2,1)S(1)}, bf16[288,1024]{1,0:T(8,128)(2,1)S(1)}, u32[]{:S(2)}, u32[]{:S(2)}) %collective-permute-start.2) | collective-permute-done | bytes 589856 | tf_op jit(solution)/shard_map/ppermute | solution.py:998
  51.0 14.4 %attn_fwd.2 = (bf16[2,256,1024]{2,1,0:T(8,128)(2,1)S(1)}, f32[2,4,1024]{2,1,0:T(4,128)S(1)}) custom-call(s32[4,4]{1,0:T(4,128)S(1)} %add_select_fusion.4.bounds, s32[1,1024]{1,0:T(1,128)S(1)} %compare_select_fusion.start_ref, bf16[2,256,1024]{2,1,0:T(8,128)(2,1)S(1)} %copy-done.109, bf16[288,1024]{1,0:T(8,128)(2,1)S(1)} %collective-permute-done.2.refs_1_.refs_0_.refs_2_, ...), custom_call_target="tpu_custom_call" | custom-call | flops 25769803776 | bytes 2097152 | tf_op jit(solution)/shard_map/attn_fwd/pallas_call | solution.py:119
  70.0 6.4 %collective-permute-start.7 = (bf16[512,1408]{1,0:T(8,128)(2,1)}, bf16[512,1408]{1,0:T(8,128)(2,1)}, u32[]{:S(2)}, u32[]{:S(2)}) collective-permute-start(bf16[512,1408]{1,0:T(8,128)(2,1)} %take.11), channel_id=1, source_target_pairs={{0,1},{1,0},{2,3},{3,2},{4,5},{5,4},{6,7},{7,6},{8,9},{9,8},{10,11... | collective-permute-start | bytes 4325384 | tf_op jit(solution)/shard_map/ppermute | solution.py:902
  76.5 4.1 other_queries.1
  81.6 14.4 %attn_fwd.3 = (bf16[2,256,1024]{2,1,0:T(8,128)(2,1)S(1)}, f32[2,4,1024]{2,1,0:T(4,128)S(1)}) custom-call(s32[4,4]{1,0:T(4,128)S(1)} %add_select_fusion.4.bounds, s32[1,1024]{1,0:T(1,128)S(1)} %compare_select_fusion.start_ref, bf16[2,256,1024]{2,1,0:T(8,128)(2,1)S(1)} %get-tuple-element.91.q_ref, bf16[288,1024]{1,0:T(8,128)(2,1)S(1)} %copy-done.40, ...), custom_call_target="tpu_custom_call" | custom-call | flops 25769803776 | bytes 2097152 | tf_op jit(solution)/shard_map/attn_fwd/pallas_call | solution.py:119
  97.6 22.5 %collective-permute-done.5.a = bf16[256,1024]{1,0:T(8,128)(2,1)S(1)} collective-permute-done((bf16[256,1024]{1,0:T(8,128)(2,1)}, bf16[256,1024]{1,0:T(8,128)(2,1)S(1)}, u32[]{:S(2)}, u32[]{:S(2)}) %collective-permute-start.5) | collective-permute-done | bytes 524320 | tf_op jit(solution)/shard_map/ppermute | solution.py:902
  123.0 3.3 fusion.24
  128.5 3.9 multiply_reduce_fusion.2
  136.1 28.9 %mlp_grads.2 = (bf16[1024,1408]{1,0:T(8,128)(2,1)}, bf16[1024,1408]{1,0:T(8,128)(2,1)}, bf16[1024,1408]{1,0:T(8,128)(2,1)}, bf16[3,512,1408]{2,1,0:T(8,128)(2,1)...) custom-call(s32[3]{0:T(128)} %copy-done.84, ...), custom_call_target="tpu_custom_call" | custom-call | flops 32480690176 | bytes 34340864 | tf_op jit(solution)/shard_map/mlp_grads/pallas_call | solution.py:518
  165.1 21.1 %collective-permute-done.9.a = bf16[512,1408]{1,0:T(8,128)(2,1)} collective-permute-done((bf16[512,1408]{1,0:T(8,128)(2,1)S(1)}, bf16[512,1408]{1,0:T(8,128)(2,1)}, u32[]{:S(2)}, u32[]{:S(2)}) %collective-permute-start.9) | collective-permute-done | bytes 1441824 | tf_op jit(solution)/shard_map/ppermute | solution.py:902
  188.5 5.4 fusion.25
  193.9 5.0 convolution_add_fusion.refs_10_
  199.0 28.8 %mlp_grads.3 = (bf16[1024,1408]{1,0:T(8,128)(2,1)}, bf16[1024,1408]{1,0:T(8,128)(2,1)}, bf16[1024,1408]{1,0:T(8,128)(2,1)}, bf16[3,512,1408]{2,1,0:T(8,128)(2,1)...) custom-call(s32[3]{0:T(128)} %copy-done.84, ...), custom_call_target="tpu_custom_call" | custom-call | flops 32480690176 | bytes 34340864 | tf_op jit(solution)/shard_map/mlp_grads/pallas_call | solution.py:518
  232.6 5.4 fusion.26
  238.0 3.6 add_convert_fusion.refs_2_
  241.7 2.8 fold.26.refs_2_
  246.4 3.6 fold.27.refs_2_
  250.3 2.7 fold.28.b.refs_2_
  254.8 6.3 %fusion.27 = f32[1024,1024]{1,0:T(8,128)S(1)} fusion(bf16[1024,1408]{1,0:T(8,128)(2,1)} %hold.18, bf16[1024,1408]{1,0:T(8,128)(2,1)} %get-tuple-element.103), kind=kOutput, calls=%fused_computation.108 | convolution fusion | flops 2952790016 | bytes 9961472 | tf_op jit(solution)/shard_map/dot_general | solution.py:897
  261.2 6.2 %multiply_reduce_fusion = (f32[1024]{0:T(1024)S(1)}, f32[1024]{0:T(1024)S(1)}, f32[1024,1024]{1,0:T(8,128)S(1)}) fusion(f32[1024,1024]{1,0:T(8,128)S(1)} %copy-done.119, f32[1024]{0:T(1024)S(1)} %add_rsqrt_fusion, f32[1024]{0:T(1024)S(1)} %copy-done.131, f32[1024,1024]{1,0:T(8,128)S(1)} %copy-done.134, f32[1024,1024]{1,0:T(8,128)S(1)} %fusion.27, ...), kind=kOutput, calls=%fused_computation | convolution fusion | flops 2961176576 | bytes 22560768 | tf_op jit(solution)/shard_map/dot_general | solution.py:897
  267.4 2.7 fusion.21
  270.1 2.7 weight_grads.4
  272.8 2.7 weight_grads.5
  275.5 2.3 fusion.1
  277.8 2.3 fusion
  285.4 12.1 %attn_bwd.4 = (bf16[1,256,1024]{2,1,0:T(8,128)(2,1)S(1)}, f32[1,64,2048]{2,1,0:T(8,128)S(1)}, f32[32,2048]{1,0:T(8,128)S(1)}) custom-call(s32[2,4]{1,0:T(2,128)S(1)} %add_select_fusion.5.bounds, s32[1,1024]{1,0:T(1,128)S(1)} %compare_select_fusion.start_ref, bf16[2,256,1024]{2,1,0:T(8,128)(2,1)S(1)} %copy-done.102, bf16[2,256,1024]{2,1,0:T(8,128)(2,1)S(1)} %copy-done.5, ...), custom_call_target="tpu_custom_call" | custom-call | flops 24159191040 | bytes 2097152 | tf_op jit(solution)/shard_map/attn_bwd/pallas_call | solution.py:229
  301.7 5.6 %collective-permute-start.18 = (bf16[128,1408]{1,0:T(8,128)(2,1)}, bf16[128,1408]{1,0:T(8,128)(2,1)}, u32[]{:S(2)}, u32[]{:S(2)}) collective-permute-start(bf16[128,1408]{1,0:T(8,128)(2,1)} %get-tuple-element.117), channel_id=1, source_target_pairs={{0,8},{2,10},{4,12},{6,14},{8,0},{10,2},{12,4},{14,6},{16,24},{18,... | collective-permute-start | bytes 1081352 | tf_op jit(solution)/shard_map/ppermute | solution.py:902
  313.5 11.2 %attn_bwd.5 = (bf16[1,256,1024]{2,1,0:T(8,128)(2,1)S(1)}, f32[1,64,2048]{2,1,0:T(8,128)S(1)}, f32[32,2048]{1,0:T(8,128)S(1)}) custom-call(s32[2,4]{1,0:T(2,128)S(1)} %add_select_fusion.5.bounds, s32[1,1024]{1,0:T(1,128)S(1)} %compare_select_fusion.start_ref, bf16[2,256,1024]{2,1,0:T(8,128)(2,1)S(1)} %copy-done.103, bf16[2,256,1024]{2,1,0:T(8,128)(2,1)S(1)} %copy-done.5, ...), custom_call_target="tpu_custom_call" | custom-call | flops 24159191040 | bytes 2097152 | tf_op jit(solution)/shard_map/attn_bwd/pallas_call | solution.py:229
  324.7 2.7 weight_grads.6
  327.4 2.8 fold.32
  331.7 2.7 collective-permute-start.20
  341.4 11.4 %attn_bwd.6 = (bf16[1,256,1024]{2,1,0:T(8,128)(2,1)S(1)}, f32[1,64,2048]{2,1,0:T(8,128)S(1)}, f32[32,2048]{1,0:T(8,128)S(1)}) custom-call(s32[2,4]{1,0:T(2,128)S(1)} %add_select_fusion.5.bounds, s32[1,1024]{1,0:T(1,128)S(1)} %compare_select_fusion.start_ref, bf16[2,256,1024]{2,1,0:T(8,128)(2,1)S(1)} %copy-done.110, bf16[2,256,1024]{2,1,0:T(8,128)(2,1)S(1)} %copy-done.13, ...), custom_call_target="tpu_custom_call" | custom-call | flops 24159191040 | bytes 2097152 | tf_op jit(solution)/shard_map/attn_bwd/pallas_call | solution.py:229
  352.8 17.6 %collective-permute-start.26 = (bf16[512,512]{1,0:T(8,128)(2,1)S(1)}, bf16[512,512]{1,0:T(8,128)(2,1)S(1)}, u32[]{:S(2)}, u32[]{:S(2)}) collective-permute-start(bf16[512,512]{1,0:T(8,128)(2,1)S(1)} %fold.30.refs_4_), channel_id=1, source_target_pairs={{0,1},{1,0},{2,3},{3,2},{4,5},{5,4},{6,7},{7,6},{8,9},{9,8},{10,11... | collective-permute-start | bytes 1572872 | tf_op jit(solution)/shard_map/ppermute | solution.py:902
  372.3 5.8 %collective-permute-start.29 = (bf16[128,1408]{1,0:T(8,128)(2,1)}, bf16[128,1408]{1,0:T(8,128)(2,1)}, u32[]{:S(2)}, u32[]{:S(2)}) collective-permute-start(bf16[128,1408]{1,0:T(8,128)(2,1)} %get-tuple-element.138), channel_id=1, source_target_pairs={{0,8},{2,10},{4,12},{6,14},{8,0},{10,2},{12,4},{14,6},{16,24},{18,... | collective-permute-start | bytes 1081352 | tf_op jit(solution)/shard_map/ppermute | solution.py:902
  378.2 2.8 fold.36
  385.3 11.2 %attn_bwd.7 = (bf16[1,256,1024]{2,1,0:T(8,128)(2,1)S(1)}, f32[1,64,2048]{2,1,0:T(8,128)S(1)}, f32[32,2048]{1,0:T(8,128)S(1)}) custom-call(s32[2,4]{1,0:T(2,128)S(1)} %add_select_fusion.5.bounds, s32[1,1024]{1,0:T(1,128)S(1)} %compare_select_fusion.start_ref, bf16[2,256,1024]{2,1,0:T(8,128)(2,1)S(1)} %copy-done.111, bf16[2,256,1024]{2,1,0:T(8,128)(2,1)S(1)} %copy-done.13, ...), custom_call_target="tpu_custom_call" | custom-call | flops 24159191040 | bytes 2097152 | tf_op jit(solution)/shard_map/attn_bwd/pallas_call | solution.py:229
  398.5 2.4 weight_grads.7
  400.9 3.5 collective-permute-start.28
  404.5 4.8 collective-permute-start.37
  411.3 7.1 %collective-permute-done.37.refs_1_ = bf16[128,1408]{1,0:T(8,128)(2,1)} collective-permute-done((bf16[128,1408]{1,0:T(8,128)(2,1)S(1)}, bf16[128,1408]{1,0:T(8,128)(2,1)}, u32[]{:S(2)}, u32[]{:S(2)}) %collective-permute-start.37) | collective-permute-done | bytes 360480 | tf_op jit(solution)/shard_map/ppermute | solution.py:902
  419.8 3.3 collective-permute-start.35
  423.1 2.9 collective-permute-start.33
  426.1 2.2 fold.40
  428.3 3.2 collective-permute-start.34
  431.8 7.3 %token_grads.1 = (bf16[1024,1024]{1,0:T(8,128)(2,1)}, f32[1,1024]{1,0:T(1,128)S(1)}) custom-call(bf16[1024,1024]{1,0:T(8,128)(2,1)S(1)} %copy-done.29, f32[1024,1024]{1,0:T(8,128)S(1)} %copy-done.14, f32[1,1024]{1,0:T(1,128)S(1)} %bitcast.161, bf16[288,1024]{1,0:T(8,128)(2,1)S(1)} %own_key_grads.1.kv_ref.refs_4_, bf16[1024,512]{1,0:T(8,128)(2,1)S(1)} %copy-done.38, ...), custom_call_target="tpu_custom_call" | custom-call | flops 5368709120 | bytes 16777216 | tf_op jit(solution)/shard_map/token_grads/pallas_call | solution.py:827
  439.1 2.4 small_grads.1
  449.5 3.6 collective-permute-start.46
  453.8 2.7 collective-permute-start.50
  463.3 7.2 %gathered.5.refs_6_ = f32[1024,1408]{1,0:T(8,128)} custom-call(s32[8]{0:T(128)S(1)} %stack.111.order, bf16[128,1408]{1,0:T(8,128)(2,1)S(1)} %fold.37.refs_4_.refs_0_, bf16[128,1408]{1,0:T(8,128)(2,1)} %collective-permute-done.37.refs_1_, bf16[128,1408]{1,0:T(8,128)(2,1)S(1)} %collective-permute-done.38.refs_2_, bf16[128,1408]{1,0:T(8,128)(2,1)S(1)} %copy-done.56, ...), custom_call_target="tpu_custom_call" | custom-call | bytes 8650752 | tf_op jit(solution)/shard_map/gathered/pallas_call | solution.py:641
  470.5 2.6 copy-done
  473.2 2.2 collective-permute-start.44
  475.5 2.2 collective-permute-start.56
  482.6 9.1 %collective-permute-done.47 = bf16[256,256]{1,0:T(8,128)(2,1)S(1)} collective-permute-done((bf16[256,256]{1,0:T(8,128)(2,1)S(1)}, bf16[256,256]{1,0:T(8,128)(2,1)S(1)}, u32[]{:S(2)}, u32[]{:S(2)}) %collective-permute-start.47) | collective-permute-done | bytes 131104 | tf_op jit(solution)/shard_map/ppermute | solution.py:902
  493.1 5.2 collective-permute-done.67.refs_1_
  502.7 7.1 %collective-permute-done.60.refs_1_ = bf16[128,1024]{1,0:T(8,128)(2,1)S(1)} collective-permute-done((bf16[128,1024]{1,0:T(8,128)(2,1)S(1)}, bf16[128,1024]{1,0:T(8,128)(2,1)S(1)}, u32[]{:S(2)}, u32[]{:S(2)}) %collective-permute-start.60) | collective-permute-done | bytes 262176 | tf_op jit(solution)/shard_map/ppermute | solution.py:902
  511.8 7.4 %gathered.6.refs_2_ = f32[1024,1408]{1,0:T(8,128)} custom-call(s32[8]{0:T(128)S(1)} %stack.111.order, bf16[128,1408]{1,0:T(8,128)(2,1)S(1)} %fold.43.refs_2_.refs_0_, bf16[128,1408]{1,0:T(8,128)(2,1)} %collective-permute-done.49.refs_1_, bf16[128,1408]{1,0:T(8,128)(2,1)} %collective-permute-done.50.refs_2_, ...), custom_call_target="tpu_custom_call" | custom-call | bytes 8650752 | tf_op jit(solution)/shard_map/gathered/pallas_call | solution.py:641
  519.3 2.6 copy-done.1
  524.5 4.3 collective-permute-done.57.refs_1_
  529.4 6.5 %gathered.7.refs_8_ = f32[1408,1024]{1,0:T(8,128)} custom-call(s32[8]{0:T(128)S(1)} %stack.111.order, bf16[128,1408]{1,0:T(8,128)(2,1)S(1)} %fold.47.refs_2_.refs_0_, bf16[128,1408]{1,0:T(8,128)(2,1)S(1)} %collective-permute-done.67.refs_1_, bf16[128,1408]{1,0:T(8,128)(2,1)S(1)} %collective-permute-done.68.refs_2_, ...), custom_call_target="tpu_custom_call" | custom-call | bytes 8650752 | tf_op jit(solution)/shard_map/gathered/pallas_call | solution.py:641
  535.9 2.6 copy-done.2
  538.5 2.9 gathered.8.refs_8_
  (482 shorter events, 130.2 us)
Async XLA Ops:
  1.6 21.7 %collective-permute-start = (bf16[512,128]{1,0:T(8,128)(2,1)S(1)}, bf16[512,128]{1,0:T(8,128)(2,1)S(1)}, u32[]{:S(2)}, u32[]{:S(2)}) collective-permute-start(bf16[512,128]{1,0:T(8,128)(2,1)S(1)} %take.6.refs_1_), channel_id=1, source_target_pairs={{0,1},{1,0},{2,3},{3,2},{4,5},{5,4},{6,7},{7,6},{8,9},{9,8},{10,11... | collective-permute-start | bytes 393224 | tf_op jit(solution)/shard_map/ppermute | solution.py:902
  5.9 61.1 %collective-permute-start.3 = (bf16[512,512]{1,0:T(8,128)(2,1)S(1)}, bf16[512,512]{1,0:T(8,128)(2,1)}, u32[]{:S(2)}, u32[]{:S(2)}) collective-permute-start(bf16[512,512]{1,0:T(8,128)(2,1)S(1)} %take.10.refs_1_), channel_id=1, source_target_pairs={{0,1},{1,0},{2,3},{3,2},{4,5},{5,4},{6,7},{7,6},{8,9},{9,8},{10,11... | collective-permute-start | bytes 1572872 | tf_op jit(solution)/shard_map/ppermute | solution.py:902
  28.3 16.9 %collective-permute-start.2 = (bf16[288,1024]{1,0:T(8,128)(2,1)S(1)}, bf16[288,1024]{1,0:T(8,128)(2,1)S(1)}, u32[]{:S(2)}, u32[]{:S(2)}) collective-permute-start(bf16[288,1024]{1,0:T(8,128)(2,1)S(1)} %get-tuple-element.89.refs_1_.refs_3_), channel_id=1, source_target_pairs={{0,1},{2,3},{4,5},{6,7},{8,9},{10,11},{12,13},{14,15},{16,17},{18,... | collective-permute-start | bytes 1769480 | tf_op jit(solution)/shard_map/ppermute | solution.py:998
  67.0 9.5 %collective-permute-start.4 = (bf16[512,512]{1,0:T(8,128)(2,1)}, bf16[512,512]{1,0:T(8,128)(2,1)S(1)}, u32[]{:S(2)}, u32[]{:S(2)}) collective-permute-start(bf16[512,512]{1,0:T(8,128)(2,1)} %hold.10.mine), channel_id=1, source_target_pairs={{0,2},{2,0},{4,6},{6,4},{8,10},{10,8},{12,14},{14,12},{16,18},{18,... | collective-permute-start | bytes 1572872 | tf_op jit(solution)/shard_map/ppermute | solution.py:902
  70.0 56.3 %collective-permute-start.7 = (bf16[512,1408]{1,0:T(8,128)(2,1)}, bf16[512,1408]{1,0:T(8,128)(2,1)}, u32[]{:S(2)}, u32[]{:S(2)}) collective-permute-start(bf16[512,1408]{1,0:T(8,128)(2,1)} %take.11), channel_id=1, source_target_pairs={{0,1},{1,0},{2,3},{3,2},{4,5},{5,4},{6,7},{7,6},{8,9},{9,8},{10,11... | collective-permute-start | bytes 4325384 | tf_op jit(solution)/shard_map/ppermute | solution.py:902
  76.4 43.7 %collective-permute-start.5 = (bf16[256,1024]{1,0:T(8,128)(2,1)}, bf16[256,1024]{1,0:T(8,128)(2,1)S(1)}, u32[]{:S(2)}, u32[]{:S(2)}) collective-permute-start(bf16[256,1024]{1,0:T(8,128)(2,1)} %take.8.refs_1_), channel_id=1, source_target_pairs={{0,1},{1,0},{2,3},{3,2},{4,5},{5,4},{6,7},{7,6},{8,9},{9,8},{10,11... | collective-permute-start | bytes 1572872 | tf_op jit(solution)/shard_map/ppermute | solution.py:902
  120.9 65.2 %collective-permute-start.11 = (bf16[1408,512]{1,0:T(8,128)(2,1)}, bf16[1408,512]{1,0:T(8,128)(2,1)}, u32[]{:S(2)}, u32[]{:S(2)}) collective-permute-start(bf16[1408,512]{1,0:T(8,128)(2,1)} %copy-done.31), channel_id=1, source_target_pairs={{0,1},{1,0},{2,3},{3,2},{4,5},{5,4},{6,7},{7,6},{8,9},{9,8},{10,11... | collective-permute-start | bytes 4325384 | tf_op jit(solution)/shard_map/ppermute | solution.py:902
  122.7 63.5 %collective-permute-start.9 = (bf16[512,1408]{1,0:T(8,128)(2,1)S(1)}, bf16[512,1408]{1,0:T(8,128)(2,1)}, u32[]{:S(2)}, u32[]{:S(2)}) collective-permute-start(bf16[512,1408]{1,0:T(8,128)(2,1)S(1)} %take.7.refs_1_), channel_id=1, source_target_pairs={{0,1},{1,0},{2,3},{3,2},{4,5},{5,4},{6,7},{7,6},{8,9},{9,8},{10,11... | collective-permute-start | bytes 4325384 | tf_op jit(solution)/shard_map/ppermute | solution.py:902
  126.3 72.7 %collective-permute-start.8 = (bf16[512,1408]{1,0:T(8,128)(2,1)}, bf16[512,1408]{1,0:T(8,128)(2,1)}, u32[]{:S(2)}, u32[]{:S(2)}) collective-permute-start(bf16[512,1408]{1,0:T(8,128)(2,1)} %hold.12.refs_4_), channel_id=1, source_target_pairs={{0,2},{2,0},{4,6},{6,4},{8,10},{10,8},{12,14},{14,12},{16,18},{18,... | collective-permute-start | bytes 4325384 | tf_op jit(solution)/shard_map/ppermute | solution.py:902
  186.1 12.8 %collective-permute-start.10 = (bf16[512,1408]{1,0:T(8,128)(2,1)}, bf16[512,1408]{1,0:T(8,128)(2,1)}, u32[]{:S(2)}, u32[]{:S(2)}) collective-permute-start(bf16[512,1408]{1,0:T(8,128)(2,1)} %hold.13.refs_6_), channel_id=1, source_target_pairs={{0,2},{2,0},{4,6},{6,4},{8,10},{10,8},{12,14},{14,12},{16,18},{18,... | collective-permute-start | bytes 4325384 | tf_op jit(solution)/shard_map/ppermute | solution.py:902
  186.2 12.8 %collective-permute-start.12 = (bf16[1408,512]{1,0:T(8,128)(2,1)}, bf16[1408,512]{1,0:T(8,128)(2,1)}, u32[]{:S(2)}, u32[]{:S(2)}) collective-permute-start(bf16[1408,512]{1,0:T(8,128)(2,1)} %hold.14.b.refs_8_), channel_id=1, source_target_pairs={{0,2},{2,0},{4,6},{6,4},{8,10},{10,8},{12,14},{14,12},{16,18},{18,... | collective-permute-start | bytes 4325384 | tf_op jit(solution)/shard_map/ppermute | solution.py:902
  227.7 13.9 %collective-permute-start.13 = (bf16[3,512,1408]{2,1,0:T(8,128)(2,1)}, bf16[3,512,1408]{2,1,0:T(8,128)(2,1)}, u32[]{:S(2)}, u32[]{:S(2)}) collective-permute-start(bf16[3,512,1408]{2,1,0:T(8,128)(2,1)} %get-tuple-element.102), channel_id=1, source_target_pairs={{0,2},{2,0},{4,6},{6,4},{8,10},{10,8},{12,14},{14,12},{16,18},{18,... | collective-permute-start | bytes 12976136 | tf_op jit(solution)/shard_map/ppermute | solution.py:902
  230.3 49.7 %collective-permute-start.14 = (bf16[3,512,1408]{2,1,0:T(8,128)(2,1)}, bf16[3,512,1408]{2,1,0:T(8,128)(2,1)}, u32[]{:S(2)}, u32[]{:S(2)}) collective-permute-start(bf16[3,512,1408]{2,1,0:T(8,128)(2,1)} %get-tuple-element.108), channel_id=1, source_target_pairs={{0,2},{2,0},{4,6},{6,4},{8,10},{10,8},{12,14},{14,12},{16,18},{18,... | collective-permute-start | bytes 12976136 | tf_op jit(solution)/shard_map/ppermute | solution.py:902
  244.6 36.0 %collective-permute-start.15 = (bf16[512,1408]{1,0:T(8,128)(2,1)S(1)}, bf16[512,1408]{1,0:T(8,128)(2,1)}, u32[]{:S(2)}, u32[]{:S(2)}) collective-permute-start(bf16[512,1408]{1,0:T(8,128)(2,1)S(1)} %fold.26.refs_2_), channel_id=1, source_target_pairs={{0,1},{1,0},{2,3},{3,2},{4,5},{5,4},{6,7},{7,6},{8,9},{9,8},{10,11... | collective-permute-start | bytes 4325384 | tf_op jit(solution)/shard_map/ppermute | solution.py:902
  250.0 77.4 %collective-permute-start.19 = (bf16[512,1408]{1,0:T(8,128)(2,1)}, bf16[512,1408]{1,0:T(8,128)(2,1)}, u32[]{:S(2)}, u32[]{:S(2)}) collective-permute-start(bf16[512,1408]{1,0:T(8,128)(2,1)} %fold.27.refs_2_), channel_id=1, source_target_pairs={{0,1},{1,0},{2,3},{3,2},{4,5},{5,4},{6,7},{7,6},{8,9},{9,8},{10,11... | collective-permute-start | bytes 4325384 | tf_op jit(solution)/shard_map/ppermute | solution.py:902
  253.0 125.1 %collective-permute-start.21 = (bf16[512,1408]{1,0:T(8,128)(2,1)S(1)}, bf16[512,1408]{1,0:T(8,128)(2,1)}, u32[]{:S(2)}, u32[]{:S(2)}) collective-permute-start(bf16[512,1408]{1,0:T(8,128)(2,1)S(1)} %fold.28.b.refs_2_), channel_id=1, source_target_pairs={{0,1},{1,0},{2,3},{3,2},{4,5},{5,4},{6,7},{7,6},{8,9},{9,8},{10,11... | collective-permute-start | bytes 4325384 | tf_op jit(solution)/shard_map/ppermute | solution.py:902
  275.5 125.5 %collective-permute-start.25 = (bf16[512,512]{1,0:T(8,128)(2,1)}, bf16[512,512]{1,0:T(8,128)(2,1)}, u32[]{:S(2)}, u32[]{:S(2)}) collective-permute-start(bf16[512,512]{1,0:T(8,128)(2,1)} %get-tuple-element.134), channel_id=1, source_target_pairs={{0,2},{2,0},{4,6},{6,4},{8,10},{10,8},{12,14},{14,12},{16,18},{18,... | collective-permute-start | bytes 1572872 | tf_op jit(solution)/shard_map/ppermute | solution.py:902
  280.0 17.5 %collective-permute-start.17 = (bf16[512,512]{1,0:T(8,128)(2,1)}, bf16[512,512]{1,0:T(8,128)(2,1)S(1)}, u32[]{:S(2)}, u32[]{:S(2)}) collective-permute-start(bf16[512,512]{1,0:T(8,128)(2,1)} %get-tuple-element.113), channel_id=1, source_target_pairs={{0,2},{2,0},{4,6},{6,4},{8,10},{10,8},{12,14},{14,12},{16,18},{18,... | collective-permute-start | bytes 1572872 | tf_op jit(solution)/shard_map/ppermute | solution.py:902
  282.7 18.1 %collective-permute-start.16 = (bf16[256,1408]{1,0:T(8,128)(2,1)S(1)}, bf16[256,1408]{1,0:T(8,128)(2,1)S(1)}, u32[]{:S(2)}, u32[]{:S(2)}) collective-permute-start(bf16[256,1408]{1,0:T(8,128)(2,1)S(1)} %get-tuple-element.112), channel_id=1, source_target_pairs={{0,4},{2,6},{4,0},{6,2},{8,12},{10,14},{12,8},{14,10},{16,20},{18,... | collective-permute-start | bytes 2162696 | tf_op jit(solution)/shard_map/ppermute | solution.py:902
  301.7 29.0 %collective-permute-start.18 = (bf16[128,1408]{1,0:T(8,128)(2,1)}, bf16[128,1408]{1,0:T(8,128)(2,1)}, u32[]{:S(2)}, u32[]{:S(2)}) collective-permute-start(bf16[128,1408]{1,0:T(8,128)(2,1)} %get-tuple-element.117), channel_id=1, source_target_pairs={{0,8},{2,10},{4,12},{6,14},{8,0},{10,2},{12,4},{14,6},{16,24},{18,... | collective-permute-start | bytes 1081352 | tf_op jit(solution)/shard_map/ppermute | solution.py:902
  327.4 25.4 %collective-permute-start.23 = (bf16[512,512]{1,0:T(8,128)(2,1)}, bf16[512,512]{1,0:T(8,128)(2,1)}, u32[]{:S(2)}, u32[]{:S(2)}) collective-permute-start(bf16[512,512]{1,0:T(8,128)(2,1)} %get-tuple-element.123), channel_id=1, source_target_pairs={{0,2},{2,0},{4,6},{6,4},{8,10},{10,8},{12,14},{14,12},{16,18},{18,... | collective-permute-start | bytes 1572872 | tf_op jit(solution)/shard_map/ppermute | solution.py:902
  330.2 41.3 %collective-permute-start.22 = (bf16[256,1408]{1,0:T(8,128)(2,1)}, bf16[256,1408]{1,0:T(8,128)(2,1)S(1)}, u32[]{:S(2)}, u32[]{:S(2)}) collective-permute-start(bf16[256,1408]{1,0:T(8,128)(2,1)} %get-tuple-element.122), channel_id=1, source_target_pairs={{0,4},{2,6},{4,0},{6,2},{8,12},{10,14},{12,8},{14,10},{16,20},{18,... | collective-permute-start | bytes 2162696 | tf_op jit(solution)/shard_map/ppermute | solution.py:902
  331.7 51.3 %collective-permute-start.20 = (bf16[128,1408]{1,0:T(8,128)(2,1)S(1)}, bf16[128,1408]{1,0:T(8,128)(2,1)}, u32[]{:S(2)}, u32[]{:S(2)}) collective-permute-start(bf16[128,1408]{1,0:T(8,128)(2,1)S(1)} %fold.33.refs_4_), channel_id=1, source_target_pairs={{0,16},{2,18},{4,20},{6,22},{8,24},{10,26},{12,28},{14,30},{16,0},... | collective-permute-start | bytes 1081352 | tf_op jit(solution)/shard_map/ppermute | solution.py:902
  352.8 58.4 %collective-permute-start.26 = (bf16[512,512]{1,0:T(8,128)(2,1)S(1)}, bf16[512,512]{1,0:T(8,128)(2,1)S(1)}, u32[]{:S(2)}, u32[]{:S(2)}) collective-permute-start(bf16[512,512]{1,0:T(8,128)(2,1)S(1)} %fold.30.refs_4_), channel_id=1, source_target_pairs={{0,1},{1,0},{2,3},{3,2},{4,5},{5,4},{6,7},{7,6},{8,9},{9,8},{10,11... | collective-permute-start | bytes 1572872 | tf_op jit(solution)/shard_map/ppermute | solution.py:902
  372.3 32.1 %collective-permute-start.29 = (bf16[128,1408]{1,0:T(8,128)(2,1)}, bf16[128,1408]{1,0:T(8,128)(2,1)}, u32[]{:S(2)}, u32[]{:S(2)}) collective-permute-start(bf16[128,1408]{1,0:T(8,128)(2,1)} %get-tuple-element.138), channel_id=1, source_target_pairs={{0,8},{2,10},{4,12},{6,14},{8,0},{10,2},{12,4},{14,6},{16,24},{18,... | collective-permute-start | bytes 1081352 | tf_op jit(solution)/shard_map/ppermute | solution.py:902
  381.0 23.5 %collective-permute-start.30 = (bf16[256,1408]{1,0:T(8,128)(2,1)}, bf16[256,1408]{1,0:T(8,128)(2,1)S(1)}, u32[]{:S(2)}, u32[]{:S(2)}) collective-permute-start(bf16[256,1408]{1,0:T(8,128)(2,1)} %get-tuple-element.139), channel_id=1, source_target_pairs={{0,4},{2,6},{4,0},{6,2},{8,12},{10,14},{12,8},{14,10},{16,20},{18,... | collective-permute-start | bytes 2162696 | tf_op jit(solution)/shard_map/ppermute | solution.py:902
  396.7 31.6 %collective-permute-start.24 = (bf16[288,1024]{1,0:T(8,128)(2,1)S(1)}, bf16[288,1024]{1,0:T(8,128)(2,1)S(1)}, u32[]{:S(2)}, u32[]{:S(2)}) collective-permute-start(bf16[288,1024]{1,0:T(8,128)(2,1)S(1)} %partner_key_grads.1.refs_2_), channel_id=1, source_target_pairs={{1,0},{3,2},{5,4},{7,6},{9,8},{11,10},{13,12},{15,14},{17,16},{19,... | collective-permute-start | bytes 1769480 | tf_op jit(solution)/shard_map/ppermute | solution.py:1079
  400.9 18.9 %collective-permute-start.28 = (bf16[512,512]{1,0:T(8,128)(2,1)S(1)}, bf16[512,512]{1,0:T(8,128)(2,1)S(1)}, u32[]{:S(2)}, u32[]{:S(2)}) collective-permute-start(bf16[512,512]{1,0:T(8,128)(2,1)S(1)} %fold.34.refs_4_), channel_id=1, source_target_pairs={{0,1},{1,0},{2,3},{3,2},{4,5},{5,4},{6,7},{7,6},{8,9},{9,8},{10,11... | collective-permute-start | bytes 1572872 | tf_op jit(solution)/shard_map/ppermute | solution.py:902
  404.5 18.6 %collective-permute-start.27 = (bf16[512,512]{1,0:T(8,128)(2,1)S(1)}, bf16[512,512]{1,0:T(8,128)(2,1)S(1)}, u32[]{:S(2)}, u32[]{:S(2)}) collective-permute-start(bf16[512,512]{1,0:T(8,128)(2,1)S(1)} %get-tuple-element.137), channel_id=1, source_target_pairs={{0,2},{2,0},{4,6},{6,4},{8,10},{10,8},{12,14},{14,12},{16,18},{18,... | collective-permute-start | bytes 1572872 | tf_op jit(solution)/shard_map/ppermute | solution.py:902
  404.5 13.9 %collective-permute-start.37 = (bf16[128,1408]{1,0:T(8,128)(2,1)S(1)}, bf16[128,1408]{1,0:T(8,128)(2,1)}, u32[]{:S(2)}, u32[]{:S(2)}) collective-permute-start(bf16[128,1408]{1,0:T(8,128)(2,1)S(1)} %fold.37.refs_4_.refs_0_), channel_id=1, source_target_pairs={{0,8},{2,10},{4,12},{6,14},{8,0},{10,2},{12,4},{14,6},{16,24},{18,... | collective-permute-start | bytes 1081352 | tf_op jit(solution)/shard_map/ppermute | solution.py:902
  411.2 30.3 %collective-permute-start.38 = (bf16[128,1408]{1,0:T(8,128)(2,1)S(1)}, bf16[128,1408]{1,0:T(8,128)(2,1)S(1)}, u32[]{:S(2)}, u32[]{:S(2)}) collective-permute-start(bf16[128,1408]{1,0:T(8,128)(2,1)S(1)} %fold.37.refs_4_.refs_0_), channel_id=1, source_target_pairs={{0,4},{2,6},{4,0},{6,2},{8,12},{10,14},{12,8},{14,10},{16,20},{18,... | collective-permute-start | bytes 1081352 | tf_op jit(solution)/shard_map/ppermute | solution.py:902
  418.4 23.4 %collective-permute-start.39 = (bf16[128,1408]{1,0:T(8,128)(2,1)}, bf16[128,1408]{1,0:T(8,128)(2,1)S(1)}, u32[]{:S(2)}, u32[]{:S(2)}) collective-permute-start(bf16[128,1408]{1,0:T(8,128)(2,1)} %collective-permute-done.37.refs_1_), channel_id=1, source_target_pairs={{0,4},{2,6},{4,0},{6,2},{8,12},{10,14},{12,8},{14,10},{16,20},{18,... | collective-permute-start | bytes 1081352 | tf_op jit(solution)/shard_map/ppermute | solution.py:902
  419.8 23.5 %collective-permute-start.35 = (bf16[128,1408]{1,0:T(8,128)(2,1)}, bf16[128,1408]{1,0:T(8,128)(2,1)}, u32[]{:S(2)}, u32[]{:S(2)}) collective-permute-start(bf16[128,1408]{1,0:T(8,128)(2,1)} %get-tuple-element.151), channel_id=1, source_target_pairs={{0,8},{2,10},{4,12},{6,14},{8,0},{10,2},{12,4},{14,6},{16,24},{18,... | collective-permute-start | bytes 1081352 | tf_op jit(solution)/shard_map/ppermute | solution.py:902
  423.1 20.5 %collective-permute-start.33 = (bf16[128,1408]{1,0:T(8,128)(2,1)S(1)}, bf16[128,1408]{1,0:T(8,128)(2,1)}, u32[]{:S(2)}, u32[]{:S(2)}) collective-permute-start(bf16[128,1408]{1,0:T(8,128)(2,1)S(1)} %fold.39.refs_12_), channel_id=1, source_target_pairs={{0,16},{2,18},{4,20},{6,22},{8,24},{10,26},{12,28},{14,30},{16,0},... | collective-permute-start | bytes 1081352 | tf_op jit(solution)/shard_map/ppermute | solution.py:902
  428.3 15.6 %collective-permute-start.34 = (bf16[256,1024]{1,0:T(8,128)(2,1)}, bf16[256,1024]{1,0:T(8,128)(2,1)S(1)}, u32[]{:S(2)}, u32[]{:S(2)}) collective-permute-start(bf16[256,1024]{1,0:T(8,128)(2,1)} %get-tuple-element.150), channel_id=1, source_target_pairs={{0,4},{2,6},{4,0},{6,2},{8,12},{10,14},{12,8},{14,10},{16,20},{18,... | collective-permute-start | bytes 1572872 | tf_op jit(solution)/shard_map/ppermute | solution.py:902
  443.6 9.5 %collective-permute-start.43 = (bf16[128,1408]{1,0:T(8,128)(2,1)S(1)}, bf16[128,1408]{1,0:T(8,128)(2,1)S(1)}, u32[]{:S(2)}, u32[]{:S(2)}) collective-permute-start(bf16[128,1408]{1,0:T(8,128)(2,1)S(1)} %collective-permute-done.39.refs_3_), channel_id=1, source_target_pairs={{0,2},{2,0},{4,6},{6,4},{8,10},{10,8},{12,14},{14,12},{16,18},{18,... | collective-permute-start | bytes 1081352 | tf_op jit(solution)/shard_map/ppermute | solution.py:902
  443.9 9.2 %collective-permute-start.31 = (bf16[512,256]{1,0:T(8,128)(2,1)S(1)}, bf16[512,256]{1,0:T(8,128)(2,1)S(1)}, u32[]{:S(2)}, u32[]{:S(2)}) collective-permute-start(bf16[512,256]{1,0:T(8,128)(2,1)S(1)} %get-tuple-element.147), channel_id=1, source_target_pairs={{0,2},{2,0},{4,6},{6,4},{8,10},{10,8},{12,14},{14,12},{16,18},{18,... | collective-permute-start | bytes 786440 | tf_op jit(solution)/shard_map/ppermute | solution.py:902
  447.9 8.7 %collective-permute-start.36 = (bf16[512,256]{1,0:T(8,128)(2,1)S(1)}, bf16[512,256]{1,0:T(8,128)(2,1)S(1)}, u32[]{:S(2)}, u32[]{:S(2)}) collective-permute-start(bf16[512,256]{1,0:T(8,128)(2,1)S(1)} %fold.44.refs_8_), channel_id=1, source_target_pairs={{0,1},{1,0},{2,3},{3,2},{4,5},{5,4},{6,7},{7,6},{8,9},{9,8},{10,11... | collective-permute-start | bytes 786440 | tf_op jit(solution)/shard_map/ppermute | solution.py:902
  448.6 26.9 %collective-permute-start.45 = (bf16[128,1408]{1,0:T(8,128)(2,1)S(1)}, bf16[128,1408]{1,0:T(8,128)(2,1)}, u32[]{:S(2)}, u32[]{:S(2)}) collective-permute-start(bf16[128,1408]{1,0:T(8,128)(2,1)S(1)} %fold.41.refs_4_), channel_id=1, source_target_pairs={{0,16},{2,18},{4,20},{6,22},{8,24},{10,26},{12,28},{14,30},{16,0},... | collective-permute-start | bytes 1081352 | tf_op jit(solution)/shard_map/ppermute | solution.py:902
  449.5 23.7 %collective-permute-start.46 = (bf16[128,1024]{1,0:T(8,128)(2,1)}, bf16[128,1024]{1,0:T(8,128)(2,1)S(1)}, u32[]{:S(2)}, u32[]{:S(2)}) collective-permute-start(bf16[128,1024]{1,0:T(8,128)(2,1)} %get-tuple-element.155), channel_id=1, source_target_pairs={{0,8},{2,10},{4,12},{6,14},{8,0},{10,2},{12,4},{14,6},{16,24},{18,... | collective-permute-start | bytes 786440 | tf_op jit(solution)/shard_map/ppermute | solution.py:902
  453.1 25.7 %collective-permute-start.52 = (bf16[128,1408]{1,0:T(8,128)(2,1)S(1)}, bf16[128,1408]{1,0:T(8,128)(2,1)S(1)}, u32[]{:S(2)}, u32[]{:S(2)}) collective-permute-start(bf16[128,1408]{1,0:T(8,128)(2,1)S(1)} %fold.43.refs_2_.refs_0_), channel_id=1, source_target_pairs={{0,2},{2,0},{4,6},{6,4},{8,10},{10,8},{12,14},{14,12},{16,18},{18,... | collective-permute-start | bytes 1081352 | tf_op jit(solution)/shard_map/ppermute | solution.py:902
  453.8 26.6 %collective-permute-start.50 = (bf16[128,1408]{1,0:T(8,128)(2,1)S(1)}, bf16[128,1408]{1,0:T(8,128)(2,1)}, u32[]{:S(2)}, u32[]{:S(2)}) collective-permute-start(bf16[128,1408]{1,0:T(8,128)(2,1)S(1)} %fold.43.refs_2_.refs_0_), channel_id=1, source_target_pairs={{0,4},{2,6},{4,0},{6,2},{8,12},{10,14},{12,8},{14,10},{16,20},{18,... | collective-permute-start | bytes 1081352 | tf_op jit(solution)/shard_map/ppermute | solution.py:902
  456.5 24.0 %collective-permute-start.49 = (bf16[128,1408]{1,0:T(8,128)(2,1)S(1)}, bf16[128,1408]{1,0:T(8,128)(2,1)}, u32[]{:S(2)}, u32[]{:S(2)}) collective-permute-start(bf16[128,1408]{1,0:T(8,128)(2,1)S(1)} %fold.43.refs_2_.refs_0_), channel_id=1, source_target_pairs={{0,8},{2,10},{4,12},{6,14},{8,0},{10,2},{12,4},{14,6},{16,24},{18,... | collective-permute-start | bytes 1081352 | tf_op jit(solution)/shard_map/ppermute | solution.py:902
  475.5 16.8 %collective-permute-start.56 = (bf16[128,1024]{1,0:T(8,128)(2,1)S(1)}, bf16[128,1024]{1,0:T(8,128)(2,1)S(1)}, u32[]{:S(2)}, u32[]{:S(2)}) collective-permute-start(bf16[128,1024]{1,0:T(8,128)(2,1)S(1)} %fold.46.refs_2_), channel_id=1, source_target_pairs={{0,16},{2,18},{4,20},{6,22},{8,24},{10,26},{12,28},{14,30},{16,0},... | collective-permute-start | bytes 786440 | tf_op jit(solution)/shard_map/ppermute | solution.py:902
  478.8 13.6 %collective-permute-start.70 = (bf16[128,1408]{1,0:T(8,128)(2,1)S(1)}, bf16[128,1408]{1,0:T(8,128)(2,1)S(1)}, u32[]{:S(2)}, u32[]{:S(2)}) collective-permute-start(bf16[128,1408]{1,0:T(8,128)(2,1)S(1)} %fold.47.refs_2_.refs_0_), channel_id=1, source_target_pairs={{0,2},{2,0},{4,6},{6,4},{8,10},{10,8},{12,14},{14,12},{16,18},{18,... | collective-permute-start | bytes 1081352 | tf_op jit(solution)/shard_map/ppermute | solution.py:902
  478.9 13.6 %collective-permute-start.68 = (bf16[128,1408]{1,0:T(8,128)(2,1)S(1)}, bf16[128,1408]{1,0:T(8,128)(2,1)S(1)}, u32[]{:S(2)}, u32[]{:S(2)}) collective-permute-start(bf16[128,1408]{1,0:T(8,128)(2,1)S(1)} %fold.47.refs_2_.refs_0_), channel_id=1, source_target_pairs={{0,4},{2,6},{4,0},{6,2},{8,12},{10,14},{12,8},{14,10},{16,20},{18,... | collective-permute-start | bytes 1081352 | tf_op jit(solution)/shard_map/ppermute | solution.py:902
  480.5 11.2 %collective-permute-start.47 = (bf16[256,256]{1,0:T(8,128)(2,1)S(1)}, bf16[256,256]{1,0:T(8,128)(2,1)S(1)}, u32[]{:S(2)}, u32[]{:S(2)}) collective-permute-start(bf16[256,256]{1,0:T(8,128)(2,1)S(1)} %fold.48.refs_2_), channel_id=1, source_target_pairs={{0,8},{2,10},{4,12},{6,14},{8,0},{10,2},{12,4},{14,6},{16,24},{18,... | collective-permute-start | bytes 393224 | tf_op jit(solution)/shard_map/ppermute | solution.py:902
  480.5 17.7 %collective-permute-start.67 = (bf16[128,1408]{1,0:T(8,128)(2,1)S(1)}, bf16[128,1408]{1,0:T(8,128)(2,1)S(1)}, u32[]{:S(2)}, u32[]{:S(2)}) collective-permute-start(bf16[128,1408]{1,0:T(8,128)(2,1)S(1)} %fold.47.refs_2_.refs_0_), channel_id=1, source_target_pairs={{0,8},{2,10},{4,12},{6,14},{8,0},{10,2},{12,4},{14,6},{16,24},{18,... | collective-permute-start | bytes 1081352 | tf_op jit(solution)/shard_map/ppermute | solution.py:902
  491.7 9.4 %collective-permute-start.51 = (bf16[128,1408]{1,0:T(8,128)(2,1)}, bf16[128,1408]{1,0:T(8,128)(2,1)S(1)}, u32[]{:S(2)}, u32[]{:S(2)}) collective-permute-start(bf16[128,1408]{1,0:T(8,128)(2,1)} %collective-permute-done.49.refs_1_), channel_id=1, source_target_pairs={{0,4},{2,6},{4,0},{6,2},{8,12},{10,14},{12,8},{14,10},{16,20},{18,... | collective-permute-start | bytes 1081352 | tf_op jit(solution)/shard_map/ppermute | solution.py:902
  492.3 9.2 %collective-permute-start.54 = (bf16[128,1408]{1,0:T(8,128)(2,1)}, bf16[128,1408]{1,0:T(8,128)(2,1)S(1)}, u32[]{:S(2)}, u32[]{:S(2)}) collective-permute-start(bf16[128,1408]{1,0:T(8,128)(2,1)} %collective-permute-done.50.refs_2_), channel_id=1, source_target_pairs={{0,2},{2,0},{4,6},{6,4},{8,10},{10,8},{12,14},{14,12},{16,18},{18,... | collective-permute-start | bytes 1081352 | tf_op jit(solution)/shard_map/ppermute | solution.py:902
  492.3 8.7 %collective-permute-start.48 = (bf16[256,256]{1,0:T(8,128)(2,1)S(1)}, bf16[256,256]{1,0:T(8,128)(2,1)S(1)}, u32[]{:S(2)}, u32[]{:S(2)}) collective-permute-start(bf16[256,256]{1,0:T(8,128)(2,1)S(1)} %fold.49.refs_2_), channel_id=1, source_target_pairs={{0,16},{2,18},{4,20},{6,22},{8,24},{10,26},{12,28},{14,30},{16,0},... | collective-permute-start | bytes 393224 | tf_op jit(solution)/shard_map/ppermute | solution.py:902
  492.4 9.1 %collective-permute-start.53 = (bf16[128,1408]{1,0:T(8,128)(2,1)}, bf16[128,1408]{1,0:T(8,128)(2,1)S(1)}, u32[]{:S(2)}, u32[]{:S(2)}) collective-permute-start(bf16[128,1408]{1,0:T(8,128)(2,1)} %collective-permute-done.49.refs_1_), channel_id=1, source_target_pairs={{0,2},{2,0},{4,6},{6,4},{8,10},{10,8},{12,14},{14,12},{16,18},{18,... | collective-permute-start | bytes 1081352 | tf_op jit(solution)/shard_map/ppermute | solution.py:902
  498.2 13.1 %collective-permute-start.69 = (bf16[128,1408]{1,0:T(8,128)(2,1)S(1)}, bf16[128,1408]{1,0:T(8,128)(2,1)S(1)}, u32[]{:S(2)}, u32[]{:S(2)}) collective-permute-start(bf16[128,1408]{1,0:T(8,128)(2,1)S(1)} %collective-permute-done.67.refs_1_), channel_id=1, source_target_pairs={{0,4},{2,6},{4,0},{6,2},{8,12},{10,14},{12,8},{14,10},{16,20},{18,... | collective-permute-start | bytes 1081352 | tf_op jit(solution)/shard_map/ppermute | solution.py:902
  501.1 10.8 %collective-permute-start.55 = (bf16[128,1408]{1,0:T(8,128)(2,1)S(1)}, bf16[128,1408]{1,0:T(8,128)(2,1)S(1)}, u32[]{:S(2)}, u32[]{:S(2)}) collective-permute-start(bf16[128,1408]{1,0:T(8,128)(2,1)S(1)} %collective-permute-done.51.refs_3_), channel_id=1, source_target_pairs={{0,2},{2,0},{4,6},{6,4},{8,10},{10,8},{12,14},{14,12},{16,18},{18,... | collective-permute-start | bytes 1081352 | tf_op jit(solution)/shard_map/ppermute | solution.py:902
  501.5 21.0 %collective-permute-start.72 = (bf16[128,1408]{1,0:T(8,128)(2,1)S(1)}, bf16[128,1408]{1,0:T(8,128)(2,1)S(1)}, u32[]{:S(2)}, u32[]{:S(2)}) collective-permute-start(bf16[128,1408]{1,0:T(8,128)(2,1)S(1)} %collective-permute-done.68.refs_2_), channel_id=1, source_target_pairs={{0,2},{2,0},{4,6},{6,4},{8,10},{10,8},{12,14},{14,12},{16,18},{18,... | collective-permute-start | bytes 1081352 | tf_op jit(solution)/shard_map/ppermute | solution.py:902
  502.5 20.5 %collective-permute-start.71 = (bf16[128,1408]{1,0:T(8,128)(2,1)S(1)}, bf16[128,1408]{1,0:T(8,128)(2,1)S(1)}, u32[]{:S(2)}, u32[]{:S(2)}) collective-permute-start(bf16[128,1408]{1,0:T(8,128)(2,1)S(1)} %collective-permute-done.67.refs_1_), channel_id=1, source_target_pairs={{0,2},{2,0},{4,6},{6,4},{8,10},{10,8},{12,14},{14,12},{16,18},{18,... | collective-permute-start | bytes 1081352 | tf_op jit(solution)/shard_map/ppermute | solution.py:902
  509.8 12.1 %collective-permute-start.61 = (bf16[128,1024]{1,0:T(8,128)(2,1)S(1)}, bf16[128,1024]{1,0:T(8,128)(2,1)S(1)}, u32[]{:S(2)}, u32[]{:S(2)}) collective-permute-start(bf16[128,1024]{1,0:T(8,128)(2,1)S(1)} %fold.50.refs_8_.refs_0_), channel_id=1, source_target_pairs={{0,4},{2,6},{4,0},{6,2},{8,12},{10,14},{12,8},{14,10},{16,20},{18,... | collective-permute-start | bytes 786440 | tf_op jit(solution)/shard_map/ppermute | solution.py:902
  511.3 11.6 %collective-permute-start.62 = (bf16[128,1024]{1,0:T(8,128)(2,1)S(1)}, bf16[128,1024]{1,0:T(8,128)(2,1)S(1)}, u32[]{:S(2)}, u32[]{:S(2)}) collective-permute-start(bf16[128,1024]{1,0:T(8,128)(2,1)S(1)} %collective-permute-done.60.refs_1_), channel_id=1, source_target_pairs={{0,4},{2,6},{4,0},{6,2},{8,12},{10,14},{12,8},{14,10},{16,20},{18,... | collective-permute-start | bytes 786440 | tf_op jit(solution)/shard_map/ppermute | solution.py:902
  511.8 17.0 %collective-permute-start.73 = (bf16[128,1408]{1,0:T(8,128)(2,1)S(1)}, bf16[128,1408]{1,0:T(8,128)(2,1)S(1)}, u32[]{:S(2)}, u32[]{:S(2)}) collective-permute-start(bf16[128,1408]{1,0:T(8,128)(2,1)S(1)} %collective-permute-done.69.refs_3_), channel_id=1, source_target_pairs={{0,2},{2,0},{4,6},{6,4},{8,10},{10,8},{12,14},{14,12},{16,18},{18,... | collective-permute-start | bytes 1081352 | tf_op jit(solution)/shard_map/ppermute | solution.py:902
  521.9 14.0 %collective-permute-start.64 = (bf16[128,1024]{1,0:T(8,128)(2,1)S(1)}, bf16[128,1024]{1,0:T(8,128)(2,1)S(1)}, u32[]{:S(2)}, u32[]{:S(2)}) collective-permute-start(bf16[128,1024]{1,0:T(8,128)(2,1)S(1)} %collective-permute-done.60.refs_1_), channel_id=1, source_target_pairs={{0,2},{2,0},{4,6},{6,4},{8,10},{10,8},{12,14},{14,12},{16,18},{18,... | collective-permute-start | bytes 786440 | tf_op jit(solution)/shard_map/ppermute | solution.py:902
  522.5 13.4 %collective-permute-start.65 = (bf16[128,1024]{1,0:T(8,128)(2,1)S(1)}, bf16[128,1024]{1,0:T(8,128)(2,1)S(1)}, u32[]{:S(2)}, u32[]{:S(2)}) collective-permute-start(bf16[128,1024]{1,0:T(8,128)(2,1)S(1)} %collective-permute-done.61.refs_2_), channel_id=1, source_target_pairs={{0,2},{2,0},{4,6},{6,4},{8,10},{10,8},{12,14},{14,12},{16,18},{18,... | collective-permute-start | bytes 786440 | tf_op jit(solution)/shard_map/ppermute | solution.py:902
  522.9 13.0 %collective-permute-start.66 = (bf16[128,1024]{1,0:T(8,128)(2,1)S(1)}, bf16[128,1024]{1,0:T(8,128)(2,1)S(1)}, u32[]{:S(2)}, u32[]{:S(2)}) collective-permute-start(bf16[128,1024]{1,0:T(8,128)(2,1)S(1)} %collective-permute-done.62.refs_3_), channel_id=1, source_target_pairs={{0,2},{2,0},{4,6},{6,4},{8,10},{10,8},{12,14},{14,12},{16,18},{18,... | collective-permute-start | bytes 786440 | tf_op jit(solution)/shard_map/ppermute | solution.py:902
  528.8 16.4 %collective-permute-start.58 = (bf16[256,256]{1,0:T(8,128)(2,1)S(1)}, bf16[256,256]{1,0:T(8,128)(2,1)S(1)}, u32[]{:S(2)}, u32[]{:S(2)}) collective-permute-start(bf16[256,256]{1,0:T(8,128)(2,1)S(1)} %fold.51.refs_8_.refs_0_), channel_id=1, source_target_pairs={{0,2},{2,0},{4,6},{6,4},{8,10},{10,8},{12,14},{14,12},{16,18},{18,... | collective-permute-start | bytes 393224 | tf_op jit(solution)/shard_map/ppermute | solution.py:902
  528.8 16.4 %collective-permute-start.59 = (bf16[256,256]{1,0:T(8,128)(2,1)S(1)}, bf16[256,256]{1,0:T(8,128)(2,1)S(1)}, u32[]{:S(2)}, u32[]{:S(2)}) collective-permute-start(bf16[256,256]{1,0:T(8,128)(2,1)S(1)} %collective-permute-done.57.refs_1_), channel_id=1, source_target_pairs={{0,2},{2,0},{4,6},{6,4},{8,10},{10,8},{12,14},{14,12},{16,18},{18,... | collective-permute-start | bytes 393224 | tf_op jit(solution)/shard_map/ppermute | solution.py:902
  (150 other events, 873.8 us)

commit v3 on v2

--- a/solution.py
+++ b/solution.py
@@ -24,6 +24,17 @@
 ANY = pl.BlockSpec(memory_space=pl.ANY)
 
 
+TOKEN = jax.ShapeDtypeStruct((8, 128), f32)
+
+
+def token_spec():
+    return pl.BlockSpec((8, 128), lambda *a: (0, 0))
+
+
+def mark(token):
+    token[...] = jnp.zeros_like(token)
+
+
 def vmem(mib):
     return pltpu.CompilerParams(vmem_limit_bytes=mib << 20)
 
@@ -40,29 +51,31 @@
     return (kk >= start) & (kk <= qpos)
 
 
-def load_keys(refs, kT, vT):
-    got_ref, sent_ref, got_shared, sent_shared = refs
+def load_keys(own, partner, sent_ref, got_ref, k, kT, vT):
+    hd = kT.shape[1]
+    half = hd // 2
     rows = sent_ref.shape[1]
-    half = sent_shared.shape[0]
-    for side, (tied, shared) in enumerate(((got_ref, got_shared), (sent_ref, sent_shared))):
-        at = slice(side * rows, (side + 1) * rows)
-        vT[:, at] = tied[...]
-        kT[:half, at] = tied[:half, :]
-        kT[half:, at] = shared[...]
-
-
-def fwd_kernel(heads, bk, deps, bounds, start_ref, q_ref, *refs):
-    kv_refs, refs = refs[:4], refs[4 + deps :]
-    o_ref, lse_ref, kT, vT, ks, acc, ms, ls = refs
-    i = pl.program_id(1)
-    hd = kT.shape[0]
-    bq = q_ref.shape[2]
-    own0 = kT.shape[1] // 2
+    shared = sent_ref.shape[0] - half
+    for side, (at, ref) in enumerate(((partner, got_ref), (own, sent_ref))):
+        to = slice(side * rows, (side + 1) * rows)
+        vT[k, :, to] = ref[at * hd : (at + 1) * hd, :]
+        kT[k, :half, to] = ref[at * hd : at * hd + half, :]
+        kT[k, half:, to] = ref[shared:, :]
+
+
+def fwd_kernel(n, heads, bk, deps, bounds, start_ref, qa_ref, qb_ref, sent_ref, got_ref, *refs):
+    oa_ref, ob_ref, lsea_ref, lseb_ref, kT, vT, ks, acc, ms, ls = refs[deps:]
+    i = pl.program_id(0)
+    hd = kT.shape[1]
+    bq = qa_ref.shape[2]
+    own0 = kT.shape[2] // 2
+    width = heads * hd
 
     @pl.when(i == 0)
     def _():
-        load_keys(kv_refs, kT, vT)
-        ks[...] = kT[...].T
+        for k in range(2 * n):
+            load_keys(k, (k + n) % (2 * n), sent_ref, got_ref, k, kT, vT)
+            ks[k] = kT[k].T
 
     acc[...] = jnp.zeros_like(acc)
     ms[...] = jnp.full_like(ms, masked_score)
@@ -72,203 +85,211 @@
 
     def step(kb, masked):
         rows = pl.ds(pl.multiple_of(kb * bk, bk), bk)
-        kblk = ks[rows, :]
-        vblk = vT[:, rows]
-        mold = [ms[j : j + 1, :] for j in range(heads)]
-        lold = [ls[j : j + 1, :] for j in range(heads)]
-        aold = [acc[j * hd : (j + 1) * hd, :] for j in range(heads)]
-        ss = [dot(kblk, q_ref[0, j * hd : (j + 1) * hd, :]) for j in range(heads)]
         if masked:
             ok = allowed_tile(start, kb, bk, qpos)
-            ss = [jnp.where(ok, s, masked_score) for s in ss]
-        mnew = [jnp.maximum(m, jnp.max(s, axis=0, keepdims=True)) for m, s in zip(mold, ss)]
-        ps = [jnp.exp(s - m) for s, m in zip(ss, mnew)]
-        als = [jnp.exp(a - b) for a, b in zip(mold, mnew)]
-        lnew = [l * al + jnp.sum(p, axis=0, keepdims=True) for l, al, p in zip(lold, als, ps)]
-        anew = [a * al + dot(vblk, p.astype(bf16)) for a, al, p in zip(aold, als, ps)]
-        for j in range(heads):
-            ms[j : j + 1, :] = mnew[j]
-            ls[j : j + 1, :] = lnew[j]
-            acc[j * hd : (j + 1) * hd, :] = anew[j]
+        for k in range(2 * n):
+            q_ref = qa_ref if k < n else qb_ref
+            kblk = ks[k, rows, :]
+            vblk = vT[k, :, rows]
+            h0 = k * heads
+            mold = [ms[h : h + 1, :] for h in range(h0, h0 + heads)]
+            lold = [ls[h : h + 1, :] for h in range(h0, h0 + heads)]
+            aold = [acc[h * hd : (h + 1) * hd, :] for h in range(h0, h0 + heads)]
+            ss = [dot(kblk, q_ref[k % n, j * hd : (j + 1) * hd, :]) for j in range(heads)]
+            if masked:
+                ss = [jnp.where(ok, s, masked_score) for s in ss]
+            mnew = [jnp.maximum(m, jnp.max(s, axis=0, keepdims=True)) for m, s in zip(mold, ss)]
+            ps = [jnp.exp(s - m) for s, m in zip(ss, mnew)]
+            als = [jnp.exp(a - b) for a, b in zip(mold, mnew)]
+            lnew = [l * al + jnp.sum(p, axis=0, keepdims=True) for l, al, p in zip(lold, als, ps)]
+            anew = [a * al + dot(vblk, p.astype(bf16)) for a, al, p in zip(aold, als, ps)]
+            for j in range(heads):
+                h = h0 + j
+                ms[h : h + 1, :] = mnew[j]
+                ls[h : h + 1, :] = lnew[j]
+                acc[h * hd : (h + 1) * hd, :] = anew[j]
 
     block_loops(bounds, i, step)
     live = start < (1 << 29)
-    for j in range(heads):
-        l = ls[j : j + 1, :]
+    for h in range(2 * n * heads):
+        l = ls[h : h + 1, :]
         safe = jnp.where(l > 0, l, 1.0)
-        o_ref[0, j * hd : (j + 1) * hd, :] = jnp.where(live, acc[j * hd : (j + 1) * hd, :] / safe, 0.0).astype(bf16)
-        lse_ref[0, j : j + 1, :] = ms[j : j + 1, :] + jnp.log(safe)
-
-
-def kv_specs(hd, rows, slot_sent, slot_got, n_groups):
-    half = hd // 2
-    shared_at = 2 * n_groups
-    return [
-        pl.BlockSpec((hd, rows), lambda g, i, b: (slot_got + g, 0)),
-        pl.BlockSpec((hd, rows), lambda g, i, b: (slot_sent + g, 0)),
-        pl.BlockSpec((half, rows), lambda g, i, b: (shared_at, 0)),
-        pl.BlockSpec((half, rows), lambda g, i, b: (shared_at, 0)),
-    ]
-
-
-def attn_fwd(bounds, start, q, sent, got, hd, slots, bq, bk, deps=()):
-    groups, width, rows = q.shape
+        side, g, j = h // (n * heads), h // heads % n, h % heads
+        o_ref, lse_ref = ((oa_ref, lsea_ref), (ob_ref, lseb_ref))[side]
+        out = jnp.where(live, acc[h * hd : (h + 1) * hd, :] / safe, 0.0)
+        o_ref[g, j * hd : (j + 1) * hd, :] = out.astype(bf16)
+        lse_ref[g, j : j + 1, :] = ms[h : h + 1, :] + jnp.log(safe)
+
+
+def attn_fwd(bounds, start, qa, qb, sent, got, hd, bq, bk, deps=()):
+    n, width, rows = qa.shape
     heads = width // hd
-    n_groups = (sent.shape[0] - hd // 2) // hd
-    tile = pl.BlockSpec((1, width, bq), lambda g, i, b: (g, 0, i))
-    return pl.pallas_call(
-        functools.partial(fwd_kernel, heads, bk, len(deps)),
+    tile = pl.BlockSpec((n, width, bq), lambda i, b: (0, 0, i))
+    logs = pl.BlockSpec((n, heads, bq), lambda i, b: (0, 0, i))
+    kv = pl.BlockSpec(sent.shape, lambda i, b: (0, 0), pipeline_mode=pl.Buffered(1))
+    return pl.pallas_call(
+        functools.partial(fwd_kernel, n, heads, bk, len(deps)),
         grid_spec=pltpu.PrefetchScalarGridSpec(
             num_scalar_prefetch=1,
-            grid=(groups, rows // bq),
-            in_specs=[pl.BlockSpec((1, bq), lambda g, i, b: (0, i)), tile]
-            + kv_specs(hd, rows, *slots, n_groups)
-            + [ANY] * len(deps),
-            out_specs=[tile, pl.BlockSpec((1, heads, bq), lambda g, i, b: (g, 0, i))],
+            grid=(rows // bq,),
+            in_specs=[pl.BlockSpec((1, bq), lambda i, b: (0, i)), tile, tile, kv, kv] + [ANY] * len(deps),
+            out_specs=[tile, tile, logs, logs],
             scratch_shapes=[
-                pltpu.VMEM((hd, 2 * rows), bf16),
-                pltpu.VMEM((hd, 2 * rows), bf16),
-                pltpu.VMEM((2 * rows, hd), bf16),
-                pltpu.VMEM((width, bq), f32),
-                pltpu.VMEM((8, bq), f32),
-                pltpu.VMEM((8, bq), f32),
+                pltpu.VMEM((2 * n, hd, 2 * rows), bf16),
+                pltpu.VMEM((2 * n, hd, 2 * rows), bf16),
+                pltpu.VMEM((2 * n, 2 * rows, hd), bf16),
+                pltpu.VMEM((2 * n * width, bq), f32),
+                pltpu.VMEM((2 * n * heads, bq), f32),
+                pltpu.VMEM((2 * n * heads, bq), f32),
             ],
         ),
-        out_shape=[jax.ShapeDtypeStruct((groups, width, rows), bf16), jax.ShapeDtypeStruct((groups, heads, rows), f32)],
-        compiler_params=vmem(48),
+        out_shape=[jax.ShapeDtypeStruct((n, width, rows), bf16)] * 2
+        + [jax.ShapeDtypeStruct((n, heads, rows), f32)] * 2,
+        compiler_params=vmem(60),
         cost_estimate=pl.CostEstimate(
-            flops=48 * groups * width * rows * rows, bytes_accessed=4 * groups * width * rows, transcendentals=0
+            flops=96 * n * width * rows * rows, bytes_accessed=8 * n * width * rows, transcendentals=0
         ),
         name="attn_fwd",
-    )(bounds, start, q, got, sent, got, sent, *deps)
-
-
-def bwd_kernel(heads, bk, scale, deps, bounds, start_ref, q_ref, o_ref, lse_ref, do_ref, cos_ref, sin_ref, *refs):
-    kv_refs, refs = refs[:4], refs[4 + deps :]
-    dq_ref, tg_ref, sg_ref, kT, vT, ks, vs, dk, dv, dqa, dl = refs
-    g = pl.program_id(0)
-    i = pl.program_id(1)
-    hd = kT.shape[0]
+    )(bounds, start, qa, qb, sent, got, *deps)
+
+
+def bwd_kernel(
+    n, first, partner, heads, bk, scale, deps, bounds, start_ref, q_ref, o_ref, lse_ref, do_ref, cos_ref, sin_ref,
+    sent_ref, got_ref, *refs
+):
+    dq_ref, tg_ref, sg_ref, token, kT, vT, ks, vs, dk, dv, dqa, dl = refs[deps:]
+    mark(token)
+    i = pl.program_id(0)
+    hd = kT.shape[1]
     half = hd // 2
     quarter = hd // 4
     bq = q_ref.shape[2]
-    own0 = kT.shape[1] // 2
+    own0 = kT.shape[2] // 2
 
     @pl.when(i == 0)
     def _():
-        load_keys(kv_refs, kT, vT)
-        ks[...] = kT[...].T
-        vs[...] = vT[...].T
+        for g in range(n):
+            load_keys(first + g, partner + g, sent_ref, got_ref, g, kT, vT)
+            ks[g] = kT[g].T
+            vs[g] = vT[g].T
         dk[...] = jnp.zeros_like(dk)
         dv[...] = jnp.zeros_like(dv)
 
-    @pl.when((i == 0) & (g == 0))
-    def _():
-        sg_ref[...] = jnp.zeros_like(sg_ref)
-
     dqa[...] = jnp.zeros_like(dqa)
     sls = [slice(j * hd, (j + 1) * hd) for j in range(heads)]
-    for j, sl in enumerate(sls):
-        prod = do_ref[0, sl, :].astype(f32) * o_ref[0, sl, :].astype(f32)
-        dl[j : j + 1, :] = jnp.sum(prod, axis=0, keepdims=True)
+    for g in range(n):
+        for j, sl in enumerate(sls):
+            prod = do_ref[g, sl, :].astype(f32) * o_ref[g, sl, :].astype(f32)
+            dl[g * heads + j : g * heads + j + 1, :] = jnp.sum(prod, axis=0, keepdims=True)
     start = start_ref[...]
     qpos = own0 + i * bq + lax.broadcasted_iota(jnp.int32, (1, bq), 1)
 
     def step(kb, masked):
         rows = pl.ds(pl.multiple_of(kb * bk, bk), bk)
-        kblk = ks[rows, :]
-        vblk = vs[rows, :]
-        kTb = kT[:, rows]
         if masked:
             ok = allowed_tile(start, kb, bk, qpos)
-        dvt = dv[:, rows]
-        dkt = dk[:, rows]
-        qs = [q_ref[0, sl, :] for sl in sls]
-        dos = [do_ref[0, sl, :] for sl in sls]
-        lses = [lse_ref[0, j : j + 1, :] for j in range(heads)]
-        dls = [dl[j : j + 1, :] for j in range(heads)]
-        dqs = [dqa[sl, :] for sl in sls]
-        new = []
-        for j in range(heads):
-            s = dot(kblk, qs[j])
-            if masked:
-                s = jnp.where(ok, s, masked_score)
-            p = jnp.exp(s - lses[j])
-            dp = dot(vblk, dos[j])
-            ds = (p * (dp - dls[j])).astype(bf16)
-            dvt = dvt + dot_nt(dos[j], p.astype(bf16))
-            dkt = dkt + dot_nt(qs[j], ds)
-            new.append(dqs[j] + dot(kTb, ds))
-        for sl, n in zip(sls, new):
-            dqa[sl, :] = n
-        dv[:, rows] = dvt
-        dk[:, rows] = dkt
+        for g in range(n):
+            kblk = ks[g, rows, :]
+            vblk = vs[g, rows, :]
+            kTb = kT[g, :, rows]
+            dvt = dv[g, :, rows]
+            dkt = dk[g, :, rows]
+            qs = [q_ref[g, sl, :] for sl in sls]
+            dos = [do_ref[g, sl, :] for sl in sls]
+            lses = [lse_ref[g, j : j + 1, :] for j in range(heads)]
+            dls = [dl[g * heads + j : g * heads + j + 1, :] for j in range(heads)]
+            dqs = [dqa[g, sl, :] for sl in sls]
+            new = []
+            for j in range(heads):
+                s = dot(kblk, qs[j])
+                if masked:
+                    s = jnp.where(ok, s, masked_score)
+                p = jnp.exp(s - lses[j])
+                dp = dot(vblk, dos[j])
+                ds = (p * (dp - dls[j])).astype(bf16)
+                dvt = dvt + dot_nt(dos[j], p.astype(bf16))
+                dkt = dkt + dot_nt(qs[j], ds)
+                new.append(dqs[j] + dot(kTb, ds))
+            for sl, x in zip(sls, new):
+                dqa[g, sl, :] = x
+            dv[g, :, rows] = dvt
+            dk[g, :, rows] = dkt
 
     block_loops(bounds, i, step)
     cosv = cos_ref[...]
     sinv = sin_ref[...]
-    for sl in sls:
-        x = dqa[sl, :] * scale
-        a, b = x[half : half + quarter], x[half + quarter :]
-        turned = jnp.concatenate([x[:half], a * cosv + b * sinv, b * cosv - a * sinv], axis=0)
-        dq_ref[0, sl, :] = turned.astype(bf16)
-
-    @pl.when(i == pl.num_programs(1) - 1)
+    for g in range(n):
+        for sl in sls:
+            x = dqa[g, sl, :] * scale
+            a, b = x[half : half + quarter], x[half + quarter :]
+            turned = jnp.concatenate([x[:half], a * cosv + b * sinv, b * cosv - a * sinv], axis=0)
+            dq_ref[g, sl, :] = turned.astype(bf16)
+
+    @pl.when(i == pl.num_programs(0) - 1)
     def _():
-        tg_ref[0, :half, :] = dv[:half, :] + dk[:half, :]
-        tg_ref[0, half:, :] = dv[half:, :]
-        sg_ref[...] += dk[half:, :]
-
-
-def attn_bwd(bounds, start, q, sent, got, o, lse, do, cosT, sinT, hd, slots, first, groups, bq, bk, deps=()):
-    _, width, rows = q.shape
+        for g in range(n):
+            tg_ref[g, :half, :] = dv[g, :half, :] + dk[g, :half, :]
+            tg_ref[g, half:, :] = dv[g, half:, :]
+        total = dk[0, half:, :]
+        for g in range(1, n):
+            total = total + dk[g, half:, :]
+        sg_ref[...] = total
+
+
+def attn_bwd(bounds, start, q, sent, got, o, lse, do, cosT, sinT, hd, side, g0, n, bq, bk, deps=()):
+    groups, width, rows = q.shape
+    first, partner = side * groups + g0, (1 - side) * groups + g0
     heads = width // hd
-    n_groups = (sent.shape[0] - hd // 2) // hd
-    tile = pl.BlockSpec((1, width, bq), lambda g, i, b: (first + g, 0, i))
-    angle = pl.BlockSpec((hd // 4, bq), lambda g, i, b: (0, i))
-    return pl.pallas_call(
-        functools.partial(bwd_kernel, heads, bk, hd**-0.5, len(deps)),
+    tile = pl.BlockSpec((n, width, bq), lambda i, b: (g0 // n, 0, i))
+    out = pl.BlockSpec((n, width, bq), lambda i, b: (0, 0, i))
+    angle = pl.BlockSpec((hd // 4, bq), lambda i, b: (0, i))
+    kv = pl.BlockSpec(sent.shape, lambda i, b: (0, 0), pipeline_mode=pl.Buffered(1))
+    return pl.pallas_call(
+        functools.partial(bwd_kernel, n, first, partner, heads, bk, hd**-0.5, len(deps)),
         grid_spec=pltpu.PrefetchScalarGridSpec(
             num_scalar_prefetch=1,
-            grid=(groups, rows // bq),
+            grid=(rows // bq,),
             in_specs=[
-                pl.BlockSpec((1, bq), lambda g, i, b: (0, i)),
+                pl.BlockSpec((1, bq), lambda i, b: (0, i)),
                 tile,
                 tile,
-                pl.BlockSpec((1, heads, bq), lambda g, i, b: (first + g, 0, i)),
+                pl.BlockSpec((n, heads, bq), lambda i, b: (g0 // n, 0, i)),
                 tile,
                 angle,
                 angle,
+                kv,
+                kv,
             ]
-            + kv_specs(hd, rows, slots[0] + first, slots[1] + first, n_groups)
             + [ANY] * len(deps),
             out_specs=[
-                pl.BlockSpec((1, width, bq), lambda g, i, b: (g, 0, i)),
-                pl.BlockSpec((1, hd, 2 * rows), lambda g, i, b: (g, 0, 0)),
-                pl.BlockSpec((hd // 2, 2 * rows), lambda g, i, b: (0, 0)),
+                out,
+                pl.BlockSpec((n, hd, 2 * rows), lambda i, b: (0, 0, 0)),
+                pl.BlockSpec((hd // 2, 2 * rows), lambda i, b: (0, 0)),
+                token_spec(),
             ],
             scratch_shapes=[
-                pltpu.VMEM((hd, 2 * rows), bf16),
-                pltpu.VMEM((hd, 2 * rows), bf16),
-                pltpu.VMEM((2 * rows, hd), bf16),
-                pltpu.VMEM((2 * rows, hd), bf16),
-                pltpu.VMEM((hd, 2 * rows), f32),
-                pltpu.VMEM((hd, 2 * rows), f32),
-                pltpu.VMEM((width, bq), f32),
-                pltpu.VMEM((8, bq), f32),
+                pltpu.VMEM((n, hd, 2 * rows), bf16),
+                pltpu.VMEM((n, hd, 2 * rows), bf16),
+                pltpu.VMEM((n, 2 * rows, hd), bf16),
+                pltpu.VMEM((n, 2 * rows, hd), bf16),
+                pltpu.VMEM((n, hd, 2 * rows), f32),
+                pltpu.VMEM((n, hd, 2 * rows), f32),
+                pltpu.VMEM((n, width, bq), f32),
+                pltpu.VMEM((n * heads, bq), f32),
             ],
         ),
         out_shape=[
-            jax.ShapeDtypeStruct((groups, width, rows), bf16),
-            jax.ShapeDtypeStruct((groups, hd, 2 * rows), f32),
+            jax.ShapeDtypeStruct((n, width, rows), bf16),
+            jax.ShapeDtypeStruct((n, hd, 2 * rows), f32),
             jax.ShapeDtypeStruct((hd // 2, 2 * rows), f32),
+            TOKEN,
         ],
-        compiler_params=vmem(48),
+        compiler_params=vmem(60),
         cost_estimate=pl.CostEstimate(
-            flops=90 * groups * width * rows * rows, bytes_accessed=8 * groups * width * rows, transcendentals=0
+            flops=90 * n * width * rows * rows, bytes_accessed=8 * n * width * rows, transcendentals=0
         ),
         name="attn_bwd",
-    )(bounds, start, q, o, lse, do, cosT, sinT, got, sent, got, sent, *deps)
+    )(bounds, start, q, o, lse, do, cosT, sinT, sent, got, *deps)
 
 
 def local_layout(lengths_row, t, rows, bq, bk, own0):
@@ -396,7 +417,9 @@
     )(place, f, mine, other, tied_a, shared)
 
 
-def query_kernel(hd, place, f_ref, mine, other, cos_ref, sin_ref, q, w_ref, wT):
+def query_kernel(hd, place, f_ref, mine, other, cos_ref, sin_ref, q, w_ref, token, wT):
+    mark(token)
+
     @pl.when(pl.program_id(0) == 0)
     def _():
         n = mine.shape[0]
@@ -424,10 +447,10 @@
                 pl.BlockSpec((hd // 4, bt), lambda i, p: (0, i)),
                 pl.BlockSpec((hd // 4, bt), lambda i, p: (0, i)),
             ],
-            out_specs=[pl.BlockSpec((groups, per * hd, bt), lambda i, p: (0, 0, i)), full((width, qn))],
+            out_specs=[pl.BlockSpec((groups, per * hd, bt), lambda i, p: (0, 0, i)), full((width, qn)), token_spec()],
             scratch_shapes=[pltpu.VMEM((qn, width), bf16)],
         ),
-        out_shape=[jax.ShapeDtypeStruct((groups, per * hd, rows), bf16), jax.ShapeDtypeStruct((width, qn), bf16)],
+        out_shape=[jax.ShapeDtypeStruct((groups, per * hd, rows), bf16), jax.ShapeDtypeStruct((width, qn), bf16), TOKEN],
         compiler_params=vmem(32),
         cost_estimate=pl.CostEstimate(flops=4 * rows * width * qn, bytes_accessed=4 * rows * width, transcendentals=0),
         name="other_queries",
@@ -444,13 +467,15 @@
     else:
         wg_ref, wu_ref, wd_ref = refs[:3]; refs = refs[3:]
     refs = refs[deps:]
-    hid, gg, ug, keep, send = refs[:5]
-    refs = refs[5:]
+    hid, gg, ug, keep = refs[:4]
+    sends, refs = refs[4:7], refs[7:]
     if first:
         sT, cT = refs[:2]; refs = refs[2:]
     if pieces:
         wg_ref, wu_ref, wd_ref = refs[:3]
+    token = refs[-1]
     i = pl.program_id(0)
+    mark(token)
     core = place[0]
     if first:
         @pl.when(i==0)
@@ -479,11 +504,11 @@
             ug[rs,:n] = (hg*act).astype(bf16)
         h = hid[:,:n]; g_ = gg[:,:n]; u_ = ug[:,:n]
         hw = width//2
-        for ref, side in ((keep,core),(send,1-core)):
-            at = pl.ds(pl.multiple_of(side*hw,hw),hw)
-            ref[0,:,:n] = dot(sT[at,:],g_).astype(bf16)
-            ref[1,:,:n] = dot(sT[at,:],u_).astype(bf16)
-            ref[2,:,:n] = dot(cT[at,:],h).astype(bf16)
+        lo = pl.ds(pl.multiple_of(core*hw,hw),hw)
+        away = pl.ds(pl.multiple_of((1-core)*hw,hw),hw)
+        for k,(left,right) in enumerate(((sT,g_),(sT,u_),(cT,h))):
+            keep[k,:,:n] = dot(left[lo,:],right).astype(bf16)
+            sends[k][:,:n] = dot(left[away,:],right).astype(bf16)
     bn = wg_ref.shape[1]
     if edge == bn:
         tile(bn)
@@ -510,6 +535,8 @@
     in_specs += [ANY]*len(deps)
     act = pl.BlockSpec((rows,bn),lambda i,p:(0,i))
     part = pl.BlockSpec((3,width//2,bn),lambda i,p:(0,0,i))
+    one = pl.BlockSpec((width//2,bn),lambda i,p:(0,i))
+    ones = jax.ShapeDtypeStruct((width//2,cols),bf16)
     acts = jax.ShapeDtypeStruct((rows,cols),bf16)
     parts = jax.ShapeDtypeStruct((3,width//2,cols),bf16)
     tsh = jax.ShapeDtypeStruct((width,rows),bf16)
@@ -519,9 +546,9 @@
         functools.partial(mlp_kernel,first,pieces,edge,len(deps)),
         grid_spec=pltpu.PrefetchScalarGridSpec(
             num_scalar_prefetch=1, grid=(tiles,), in_specs=in_specs,
-            out_specs=[act]*3+[part]*2+([wholeTo]*2 if first else [])+w_specs,
-        ),
-        out_shape=[acts]*3+[parts]*2+([tsh]*2 if first else [])+w_shapes,
+            out_specs=[act]*3+[part]+[one]*3+([wholeTo]*2 if first else [])+w_specs+[token_spec()],
+        ),
+        out_shape=[acts]*3+[parts]+[ones]*3+([tsh]*2 if first else [])+w_shapes+[TOKEN],
         compiler_params=pltpu.CompilerParams(vmem_limit_bytes=56<<20),
         cost_estimate=pl.CostEstimate(flops=22*rows*width*cols,bytes_accessed=2*(4*rows*width+9*width*cols),transcendentals=rows*cols),
         name="mlp_grads",
@@ -531,7 +558,8 @@
 
 def fold_kernel(counts, sides, deps, bits, *refs):
     n = sum(counts)
-    outs = refs[n * sides + deps :]
+    outs, token = refs[n * sides + deps : -1], refs[-1]
+    mark(token)
     for side, out in enumerate(outs):
         at, col = side * n, 0
         for count in counts:
@@ -572,20 +600,21 @@
             num_scalar_prefetch=1,
             grid=(blocks,),
             in_specs=[spec(a, k, side) for side in range(sides) for a, k in flat] + [ANY] * len(deps),
-            out_specs=[pl.BlockSpec((step, cols), lambda i, b: (i, 0))] * sides,
-        ),
-        out_shape=[out] * sides,
+            out_specs=[pl.BlockSpec((step, cols), lambda i, b: (i, 0))] * sides + [token_spec()],
+        ),
+        out_shape=[out] * sides + [TOKEN],
         compiler_params=vmem(32),
         cost_estimate=pl.CostEstimate(
             flops=3 * rows * cols, bytes_accessed=8 * rows * cols, transcendentals=0
         ),
         name="fold",
     )(scalars, *[a for _ in range(sides) for a, _ in flat], *deps)
-    return result if sides == 2 else result[0]
+    return result
 
 
 def take_kernel(deps, place, *refs):
-    refs[-1][...] = refs[0][...]
+    refs[-2][...] = refs[0][...]
+    mark(refs[-1])
 
 
 def take(w, at, axis, parts, deps=()):
@@ -599,9 +628,9 @@
             num_scalar_prefetch=1,
             grid=(1,),
             in_specs=[pl.BlockSpec(block, where)] + [pl.BlockSpec(memory_space=pl.ANY)] * len(deps),
-            out_specs=pl.BlockSpec(block, lambda i, p: (0, 0)),
-        ),
-        out_shape=jax.ShapeDtypeStruct(block, w.dtype),
+            out_specs=[pl.BlockSpec(block, lambda i, p: (0, 0)), token_spec()],
+        ),
+        out_shape=[jax.ShapeDtypeStruct(block, w.dtype), TOKEN],
         compiler_params=vmem(32),
         cost_estimate=pl.CostEstimate(flops=0, bytes_accessed=4 * block[0] * block[1], transcendentals=0),
         name="take",
@@ -619,27 +648,60 @@
     )(x, dep)
 
 
-def gather_kernel(turn, n, deps, order, *refs):
-    pieces, refs = refs[:n], refs[n + deps :]
-    out = refs[0]
-    rows = pieces[0].shape[0]
-    held = refs[1] if turn else out
-    for k, piece in enumerate(pieces):
-        at = pl.ds(pl.multiple_of(order[k] * rows, rows), rows)
-        held[at, :] = piece[...].astype(held.dtype)
-    if turn:
-        out[...] = held[...].T.astype(f32)
+def gather_kernel(turn, n, order, *refs):
+    out, token = refs[-2:]
+    mark(token)
+    for k in range(n):
+
+        @pl.when(pl.program_id(0) == k)
+        def _():
+            piece = refs[k][...]
+            out[...] = (piece.T if turn else piece).astype(f32)
 
 
 def gathered(pieces, order, turn, deps=(), start=0, cols=None):
     n = len(pieces)
     rows = pieces[0].shape[0]
     cols = cols or pieces[0].shape[1]
-    wide = 128 if turn or cols % 256 or start % 256 else 256
+    base = start // cols
+    total = n * rows
+    return pl.pallas_call(
+        functools.partial(gather_kernel, turn, n),
+        grid_spec=pltpu.PrefetchScalarGridSpec(
+            num_scalar_prefetch=1,
+            grid=(n,),
+            in_specs=[pl.BlockSpec((rows, cols), lambda i, o: (0, base), pipeline_mode=pl.Buffered(1))] * n
+            + [ANY] * len(deps),
+            out_specs=[
+                pl.BlockSpec((cols, rows), lambda i, o: (0, o[i])) if turn else pl.BlockSpec((rows, cols), lambda i, o: (o[i], 0)),
+                token_spec(),
+            ],
+        ),
+        out_shape=[jax.ShapeDtypeStruct((cols, total) if turn else (total, cols), f32), TOKEN],
+        compiler_params=vmem(60),
+        cost_estimate=pl.CostEstimate(flops=0, bytes_accessed=6 * total * cols, transcendentals=0),
+        name="gathered",
+    )(order, *pieces, *deps)
+
+
+def gather_tiles_kernel(turn, n, order, *refs):
+    out = refs[-1] if not turn else refs[-2]
+    held = refs[-1]
+    rows = refs[0].shape[0]
+    for k in range(n):
+        at = pl.ds(pl.multiple_of(order[k] * rows, rows), rows)
+        held[at, :] = refs[k][...].astype(held.dtype)
+    if turn:
+        out[...] = held[...].T.astype(f32)
+
+
+def gathered_tiles(pieces, order, turn, deps, start, cols, wide=256):
+    n = len(pieces)
+    rows = pieces[0].shape[0]
     base = start // wide
     total = n * rows
     return pl.pallas_call(
-        functools.partial(gather_kernel, turn, n, len(deps)),
+        functools.partial(gather_tiles_kernel, turn, n),
         grid_spec=pltpu.PrefetchScalarGridSpec(
             num_scalar_prefetch=1,
             grid=(cols // wide,),
@@ -668,9 +730,10 @@
     gains[...] = held[...].T[half : half + 8, :]
 
 
-def gathered_small(pieces, order, kn, half, deps=()):
+def gathered_small(pieces, order, kn, half, deps=(), start=0):
     n = len(pieces)
-    rows, cols = pieces[0].shape
+    rows, cols = pieces[0].shape[0], kn + 128
+    base = start // cols
     total = n * rows
     full = lambda a: pl.BlockSpec(a, lambda i, o: (0, 0))
     shapes = [(total, kn), (total, half), (8, total)]
@@ -679,7 +742,7 @@
         grid_spec=pltpu.PrefetchScalarGridSpec(
             num_scalar_prefetch=1,
             grid=(1,),
-            in_specs=[full((rows, cols))] * n + [ANY] * len(deps),
+            in_specs=[pl.BlockSpec((rows, cols), lambda i, o: (0, base))] * n + [ANY] * len(deps),
             out_specs=[full(a) for a in shapes],
             scratch_shapes=[pltpu.VMEM((total, 128), f32)],
         ),
@@ -692,7 +755,8 @@
 
 def wgrad_kernel(n, deps, place, l_ref, *refs):
     right, refs = refs[:n], refs[n + deps :]
-    keep, send, lT = refs
+    keep, send, token, lT = refs
+    mark(token)
     lT[...] = l_ref[...].T
     core = place[0]
     hw = keep.shape[0]
@@ -721,10 +785,10 @@
             num_scalar_prefetch=1,
             grid=(1,),
             in_specs=[full(left.shape)] + [spec(r, k) for r, k in right] + [ANY] * len(deps),
-            out_specs=[full(part.shape)] * 2,
+            out_specs=[full(part.shape)] * 2 + [token_spec()],
             scratch_shapes=[pltpu.VMEM((width, rows), bf16)],
         ),
-        out_shape=[part] * 2,
+        out_shape=[part] * 2 + [TOKEN],
         compiler_params=vmem(48),
         cost_estimate=pl.CostEstimate(flops=4 * rows * width * cols, bytes_accessed=4 * rows * width, transcendentals=0),
         name="weight_grads",
@@ -732,75 +796,83 @@
 
 
 def back_kernel(n, *refs):
-    tgs, sgs, out = refs[:n], refs[n : 2 * n], refs[2 * n]
-    hd = tgs[0].shape[1]
-    for k, tg in enumerate(tgs):
-        out[k * hd : (k + 1) * hd, :] = tg[0].astype(bf16)
+    tgs, sgs = refs[:n], refs[n : 2 * n]
+    out, token = refs[-2:]
+    mark(token)
+    per, hd, _ = tgs[0].shape
+    for g in range(n * per):
+        out[g * hd : (g + 1) * hd, :] = tgs[g // per][g % per].astype(bf16)
     total = sgs[0][...]
     for s in sgs[1:]:
         total = total + s[...]
-    out[n * hd :, :] = total.astype(bf16)
-
-
-def back_call(tgs, sgs):
+    out[n * per * hd :, :] = total.astype(bf16)
+
+
+def back_call(tgs, sgs, deps=()):
     n = len(tgs)
-    _, hd, two = tgs[0].shape
+    per, hd, two = tgs[0].shape
     rows = two // 2
+    total = n * per * hd + hd // 2
     return pl.pallas_call(
         functools.partial(back_kernel, n),
         grid=(1,),
-        in_specs=[pl.BlockSpec((1, hd, rows), lambda i: (0, 0, 0))] * n
-        + [pl.BlockSpec((hd // 2, rows), lambda i: (0, 0))] * n,
-        out_specs=pl.BlockSpec((n * hd + hd // 2, rows), lambda i: (0, 0)),
-        out_shape=jax.ShapeDtypeStruct((n * hd + hd // 2, rows), bf16),
+        in_specs=[pl.BlockSpec((per, hd, rows), lambda i: (0, 0, 0))] * n
+        + [pl.BlockSpec((hd // 2, rows), lambda i: (0, 0))] * n
+        + [ANY] * len(deps),
+        out_specs=[pl.BlockSpec((total, rows), lambda i: (0, 0)), token_spec()],
+        out_shape=[jax.ShapeDtypeStruct((total, rows), bf16), TOKEN],
         compiler_params=vmem(32),
-        cost_estimate=pl.CostEstimate(flops=0, bytes_accessed=6 * n * hd * rows, transcendentals=0),
+        cost_estimate=pl.CostEstimate(flops=0, bytes_accessed=6 * total * rows, transcendentals=0),
         name="partner_key_grads",
-    )(*tgs, *sgs)
-
-
-def own_kernel(n, deps, *refs):
-    tgs, sgs, back, cos_ref, sin_ref = refs[:n], refs[n : 2 * n], refs[2 * n], refs[2 * n + 1], refs[2 * n + 2]
-    out = refs[2 * n + 3 + deps]
-    hd = tgs[0].shape[1]
-    for k, tg in enumerate(tgs):
-        other = (k + n // 2) % n
-        mine = back[other * hd : (other + 1) * hd, :].astype(f32)
-        out[k * hd : (k + 1) * hd, :] = (tg[0] + mine).astype(bf16)
-    total = back[n * hd :, :].astype(f32)
+    )(*tgs, *sgs, *deps)
+
+
+def own_kernel(n, *refs):
+    tgs, sgs = refs[: 2 * n], refs[2 * n : 4 * n]
+    back_a, back_b, cos_ref, sin_ref = refs[4 * n : 4 * n + 4]
+    out, token = refs[-2:]
+    mark(token)
+    per, hd, _ = tgs[0].shape
+    kv = n * per * hd
+    for k in range(2 * n * per):
+        back = (back_a, back_b)[k // (n * per)]
+        at = k % (n * per) * hd
+        mine = tgs[k // per][k % per]
+        out[k * hd : (k + 1) * hd, :] = (mine + back[at : at + hd, :].astype(f32)).astype(bf16)
+    total = back_a[kv:, :].astype(f32) + back_b[kv:, :].astype(f32)
     for s in sgs:
         total = total + s[...]
-    out[n * hd :, :] = turned_rows(total, cos_ref[...], -sin_ref[...], hd // 4).astype(bf16)
-
-
-def own_call(tgs, sgs, back, cosT, sinT, deps=()):
+    out[2 * kv :, :] = turned_rows(total, cos_ref[...], -sin_ref[...], hd // 4).astype(bf16)
+
+
+def own_call(tgs, sgs, backs, cosT, sinT, deps=()):
     n = len(tgs)
-    _, hd, two = tgs[0].shape
+    per, hd, two = tgs[0].shape
     rows = two // 2
+    total = n * per * hd + hd // 2
     full = lambda a: pl.BlockSpec(a.shape, lambda i: (0, 0))
     return pl.pallas_call(
-        functools.partial(own_kernel, n, len(deps)),
+        functools.partial(own_kernel, n // 2),
         grid=(1,),
-        in_specs=[pl.BlockSpec((1, hd, rows), lambda i: (0, 0, 1))] * n
+        in_specs=[pl.BlockSpec((per, hd, rows), lambda i: (0, 0, 1))] * n
         + [pl.BlockSpec((hd // 2, rows), lambda i: (0, 1))] * n
-        + [full(back), full(cosT), full(sinT)]
+        + [full(backs[0]), full(backs[1]), full(cosT), full(sinT)]
         + [ANY] * len(deps),
-        out_specs=full(back),
-        out_shape=jax.ShapeDtypeStruct(back.shape, bf16),
+        out_specs=[pl.BlockSpec((total, rows), lambda i: (0, 0)), token_spec()],
+        out_shape=[jax.ShapeDtypeStruct((total, rows), bf16), TOKEN],
         compiler_params=vmem(32),
-        cost_estimate=pl.CostEstimate(flops=0, bytes_accessed=8 * n * hd * rows, transcendentals=0),
+        cost_estimate=pl.CostEstimate(flops=0, bytes_accessed=8 * total * rows, transcendentals=0),
         name="own_key_grads",
-    )(*tgs, *sgs, back, cosT, sinT, *deps)
-
-
-def post_kernel(nq, deps, x_ref, mg_ref, gain_ref, kv_ref, wqa, wqb, wka, wkb, wr, *refs):
-    dqs, refs = refs[:nq], refs[nq + deps :]
-    out, gain_out = refs
+    )(*tgs, *sgs, *backs, cosT, sinT, *deps)
+
+
+def post_kernel(deps, x_ref, mg_ref, gain_ref, kv_ref, wqa, wqb, wka, wkb, wr, *refs):
+    dqs = refs[:2]
+    out, gain_out = refs[2 + deps :]
     kn = wka.shape[1]
     hn = wqa.shape[1]
-    g = [r[0] for r in dqs]
-    qa = jnp.concatenate(g[: nq // 2], axis=0).T
-    qb = jnp.concatenate(g[nq // 2 :], axis=0).T
+    qa = dqs[0][...].reshape(hn, -1).T
+    qb = dqs[1][...].reshape(hn, -1).T
     kv = kv_ref[...]
     first = dot_nt(qa, wqa[...]) + dot_nt(qb, wqb[...])
     first = first + dot_nt(kv[:kn].T, wka[...]) + dot_nt(kv[kn : 2 * kn].T, wkb[...])
@@ -825,11 +897,11 @@
     row = pl.BlockSpec((bt, width), lambda i: (i, 0))
     one = pl.BlockSpec((1, width), lambda i: (0, 0))
     return pl.pallas_call(
-        functools.partial(post_kernel, len(dqs), len(deps)),
+        functools.partial(post_kernel, len(deps)),
         grid=(rows // bt,),
         in_specs=[row, row, one, pl.BlockSpec((kv.shape[0], bt), lambda i: (0, i))]
         + [full(w) for w in weights]
-        + [pl.BlockSpec((1, d.shape[1], bt), lambda i: (0, 0, i)) for d in dqs]
+        + [pl.BlockSpec((*d.shape[:2], bt), lambda i: (0, 0, i)) for d in dqs]
         + [ANY] * len(deps),
         out_specs=[row, one],
         out_shape=[jax.ShapeDtypeStruct((rows, width), bf16), jax.ShapeDtypeStruct((1, width), f32)],
@@ -839,7 +911,8 @@
     )(x, middle_grad, gain[None, :], kv, *weights, *dqs, *deps)
 
 
-def small_kernel(kn, half, place, f_ref, kv_ref, gain_a, gain_b, keep_a, send_a, keep_b, send_b, lT, rows_s, rows_g):
+def small_kernel(kn, half, place, f_ref, kv_ref, gain_a, gain_b, keep_a, send_a, keep_b, send_b, token, lT, rows_s, rows_g):
+    mark(token)
     lT[...] = f_ref[...].T
     rows_s[...] = jnp.zeros_like(rows_s)
     rows_s[:half, :] = kv_ref[2 * kn :, :]
@@ -873,10 +946,10 @@
             num_scalar_prefetch=1,
             grid=(1,),
             in_specs=[full(f.shape), full(kv.shape), full((1, width)), full((1, width))],
-            out_specs=[full(part.shape)] * 4,
+            out_specs=[full(part.shape)] * 4 + [token_spec()],
             scratch_shapes=[pltpu.VMEM((width, rows), bf16), pltpu.VMEM((128, rows), bf16), pltpu.VMEM((128, width), f32)],
         ),
-        out_shape=[part] * 4,
+        out_shape=[part] * 4 + [TOKEN],
         compiler_params=vmem(48),
         cost_estimate=pl.CostEstimate(flops=2 * rows * width * 512, bytes_accessed=3 * rows * width, transcendentals=0),
         name="small_grads",
@@ -912,11 +985,11 @@
         self.last = first
 
     def after(self, out):
-        self.last = out[0] if isinstance(out, (tuple, list)) else out
-        return out
-
-    def fold(self, groups, bit=None):
-        return self.after(fold(groups, bit, (self.last,)))
+        *out, self.last = out
+        return out if len(out) > 1 else out[0]
+
+    def fold(self, groups, bit=None, deps=()):
+        return self.after(fold(groups, bit, (self.last, *deps)))
 
 
 def spread(piece, steps):
@@ -943,7 +1016,10 @@
         self.steps = [2, 1]
 
     def z(self):
-        self.keep, send = self.run.fold([[self.keep, self.got]], self.bits[2])
+        self.start([[self.keep, self.got]])
+
+    def start(self, groups):
+        self.keep, send = self.run.fold(groups, self.bits[2])
         self.got = swap(send, "dp", 4)
         self.steps = [4, 2, 1]
 
@@ -951,12 +1027,12 @@
         self.keep = self.run.fold([[self.keep, self.got]])
         self.got = swap(self.keep, "dp", step)
 
-    def end(self):
+    def end(self, deps=()):
         step = 16
         while step < lax.axis_size("dp"):
             self.line(step)
             step *= 2
-        self.keep = self.run.fold([[self.keep, self.got]])
+        self.keep = self.run.fold([[self.keep, self.got]], None, deps)
         self.pieces = spread(self.keep, self.steps)
         self.order = piece_order(self.bits[: len(self.steps)])
 
@@ -976,15 +1052,15 @@
     per = q_own // kv_own
     ff = w_gate.shape[1]
     own0 = rows
-    bq_f, bk_f, bq_b, bk_b = 256, 512, 512, 256
+    bq_f, bk_f, bq_b, bk_b = 256, 256, 512, 256
     place = jnp.stack([core, core, 1 - core]).astype(jnp.int32)
 
-    kv_piece = take(w_kv, core, 0, 2)
+    kv_piece, taken = take(w_kv, core, 0, 2)
     kv_got = swap(kv_piece, "tensor", 1)
-    q_piece = take(w_query, core, 0, 2, (kv_piece,))
+    q_piece, taken = take(w_query, core, 0, 2, (taken,))
     q_got = swap(q_piece, "tensor", 1)
-    gate_piece = take(w_gate, core, 0, 2, (q_piece,))
-    gate_got = swap(gate_piece, "tensor", 1)
+    out_piece, taken = take(w_out, core, 0, 2, (taken,))
+    out_got = swap(out_piece, "tensor", 1)
 
     slot, position, valid, start, bounds_f = local_layout(lengths[0], t, rows, bq_f, bk_f, own0)
     bounds_b = local_layout(lengths[0], t, rows, bq_b, bk_b, own0)[4]
@@ -996,44 +1072,39 @@
     first_in, tied_a, shared, q_a = pre_call(tokens, attn_gain, w_kv, w_rope, w_query, cosT, sinT, hd, per)
     sent, w_kv_o = kv_call(place, first_in, kv_got, swap(kv_got, "dp", 1), tied_a, shared)
     got = lax.ppermute(sent, "tensor", [(i, i + 1) for i in range(shards - 1)])
-    up_piece = take(w_up, core, 0, 2, (got,))
+    q_b, w_query_o, q_done = query_call(place, first_in, q_got, swap(q_got, "dp", 1), cosT, sinT, hd, groups, per)
+    gate_piece, taken = take(w_gate, core, 0, 2, (got, q_done))
+    gate_got = swap(gate_piece, "tensor", 1)
+    up_piece, taken = take(w_up, core, 0, 2, (taken,))
     up_got = swap(up_piece, "tensor", 1)
-    out_piece = take(w_out, core, 0, 2, (up_piece,))
-    out_got = swap(out_piece, "tensor", 1)
-    down_piece = take(w_down, core, 1, 2, (out_piece,))
+    down_piece, taken = take(w_down, core, 1, 2, (taken,))
     down_got = swap(down_piece, "tensor", 1)
 
     def both(p):
         return p, swap(p, "dp", 1)
 
-    at_a, at_b = (0, groups), (groups, 0)
-    mixed_a, lse_a = attn_fwd(bounds_f, start, q_a, sent, got, hd, at_a, bq_f, bk_f, (down_piece,))
-    q_got = hold(q_got, mixed_a)
-    q_b, w_query_o = query_call(place, first_in, q_got, swap(q_got, "dp", 1), cosT, sinT, hd, groups, per)
-    mixed_b, lse_b = attn_fwd(bounds_f, start, q_b, sent, got, hd, at_b, bq_f, bk_f)
-    out_got = hold(out_got, mixed_b)
     w_out_o = joined(out_got, swap(out_got, "dp", 1), core)
+    mixed_a, mixed_b, lse_a, lse_b = attn_fwd(
+        bounds_f, start, q_a, q_b, sent, got, hd, bq_f, bk_f, (taken, w_out_o)
+    )
     mix_a, mix_b = mixed_a.reshape(-1, rows), mixed_b.reshape(-1, rows)
     inputs = tokens.astype(f32)
     middle = inputs + mm(mix_a, w_out, 0, 0) + mm(mix_b, w_out_o, 0, 0)
     normed_two, factor_two = rms_parts(middle)
     second_in = (normed_two * mlp_gain).astype(bf16)
 
-    hid_a, gg_a, ug_a, keep_a, send_a, in_T, back_T = mlp_call(
+    hid_a, gg_a, ug_a, keep_a, *send_a, in_T, back_T, done_a = mlp_call(
         place, second_in, out_grad, None, (w_gate, w_up, w_down), 0, ff
     )
-    core_a = swap(send_a, "dp", 1)
-    gates, ups, downs = both(hold(gate_got, mixed_b)), both(hold(up_got, mixed_b)), both(hold(down_got, hid_a))
-    second_a = mm(hold(gg_a, downs[0]), w_gate, 1, 1) + mm(hold(ug_a, downs[0]), w_up, 1, 1)
-    hid_b, gg_b, ug_b, keep_b, send_b, w_gate_o, w_up_o, w_down_o = mlp_call(
+    core_a = [swap(s, "dp", 1) for s in send_a]
+    gates, ups, downs = both(hold(gate_got, done_a)), both(hold(up_got, done_a)), both(hold(down_got, done_a))
+    second_a = mm(gg_a, w_gate, 1, 1) + mm(ug_a, w_up, 1, 1)
+    hid_b, gg_b, ug_b, keep_b, *send_b, w_gate_o, w_up_o, w_down_o, done_b = mlp_call(
         place, second_in, out_grad, (in_T, back_T), (*gates, *ups, *downs), 0, ff, deps=(second_a,)
     )
-    core_b = swap(send_b, "dp", 1)
-    hid_a = hold(hid_a, hid_b)
-    layer_out = (middle + mm(hid_a, w_down, 1, 0) + mm(hid_b, w_down_o, 1, 0)).astype(bf16)
-    run = Order(layer_out)
-    ysend = [run.fold([[(keep_b, k), (core_b, k)]]) for k in range(3)]
-    ygot = [swap(y, "tensor", 1) for y in ysend]
+    core_b = [swap(s, "dp", 1) for s in send_b]
+    run = Order(done_b)
+    gate_y = swap(run.fold([[(keep_b, 0), core_b[0]]]), "tensor", 1)
     gg_b, ug_b = hold(gg_b, run.last), hold(ug_b, run.last)
     second_grad = second_a + mm(gg_b, w_gate_o, 1, 1) + mm(ug_b, w_up_o, 1, 1)
     mlp_gain_part = jnp.sum(second_grad * normed_two, axis=0, keepdims=True)
@@ -1046,10 +1117,11 @@
     def parts(x):
         return [(x, k) for k in range(groups)]
 
-    def back(q, mixed, lse, grad, at, k):
+    def back(q, mixed, lse, grad, side, deps=()):
         return run.after(
             attn_bwd(
-                bounds_b, start, q, sent, got, mixed, lse, grad, cosT, sinT, hd, at, k, 1, bq_b, bk_b, (run.last,)
+                bounds_b, start, q, sent, got, mixed, lse, grad, cosT, sinT, hd, side, 0, groups, bq_b, bk_b,
+                (run.last, *deps),
             )
         )
 
@@ -1057,35 +1129,34 @@
     wo_core_b = swap(wo_send_b, "dp", 1)
     wo_keep_a, wo_send_a = run.after(wgrad(place, attn_back, parts(mixed_a), (run.last,)))
     wo_core_a = swap(wo_send_a, "dp", 1)
-
-    gate_s, up_s, down_s, rest_s, small_s = (Sum(run, bits) for _ in range(5))
-    gate_s.x([[(keep_a, 0), (core_a, 0), ygot[0]]])
-    dq_b0, tg_b0, sg_b0 = back(q_b, mixed_b, lse_b, mixed_grad_b, at_b, 0)
-    wo_got = swap(run.fold([[wo_keep_b, wo_core_b]]), "tensor", 1)
+    up_y = swap(run.fold([[(keep_b, 1), core_b[1]]]), "tensor", 1)
+    down_kb, down_sb = run.fold([[(keep_b, 2), core_b[2]]], bits[1])
+    down_xb = swap(down_sb, "dp", 2)
+    down_ka, down_sa = run.fold([[(keep_a, 2), core_a[2]]], bits[1])
+    down_xa = swap(down_sa, "dp", 2)
+    gate_s, up_s, down_s, rest_s = (Sum(run, bits) for _ in range(4))
+    dq_b, tg_b, sg_b = back(q_b, mixed_b, lse_b, mixed_grad_b, 1, (mixed_grad_a,))
+    wq_keep_b, wq_send_b = run.after(wgrad(place, first_in, parts(dq_b), (run.last,)))
+    wq_core_b = swap(wq_send_b, "dp", 1)
+    key_b = run.after(back_call((tg_b,), (sg_b,), (run.last,)))
+    to_lower = [(i + 1, i) for i in range(shards - 1)]
+    key_got_a = lax.ppermute(key_b, "tensor", to_lower)
+    gate_s.x([[(keep_a, 0), core_a[0], gate_y]])
+    up_s.x([[(keep_a, 1), core_a[1], up_y]])
+    down_y = swap(run.fold([[down_kb, down_xb]]), "tensor", 1)
+    wo_y = swap(run.fold([[wo_keep_b, wo_core_b]]), "tensor", 1)
+    wq_y = swap(run.fold([[wq_keep_b, wq_core_b]]), "tensor", 1)
+    dq_a, tg_a, sg_a = back(q_a, mixed_a, lse_a, mixed_grad_a, 0)
+    key_a = run.after(back_call((tg_a,), (sg_a,), (run.last,)))
+    key_got_b = lax.ppermute(key_a, "tensor", to_lower)
     gate_s.z()
-    dq_b1, tg_b1, sg_b1 = back(q_b, mixed_b, lse_b, mixed_grad_b, at_b, 1)
-    wq_keep_b, wq_send_b = run.after(wgrad(place, first_in, [(dq_b0, 0), (dq_b1, 0)], (run.last,)))
-    wq_core_b = swap(wq_send_b, "dp", 1)
-    up_s.x([[(keep_a, 1), (core_a, 1), ygot[1]]])
-    gate_s.line()
-    dq_a0, tg_a0, sg_a0 = back(q_a, mixed_a, lse_a, mixed_grad_a, at_a, 0)
-    wq_got = swap(run.fold([[wq_keep_b, wq_core_b]]), "tensor", 1)
     up_s.z()
-    down_s.x([[(keep_a, 2), (core_a, 2), ygot[2]]])
-    gate_s.end()
-    dq_a1, tg_a1, sg_a1 = back(q_a, mixed_a, lse_a, mixed_grad_a, at_a, 1)
-    tgs, sgs = (tg_a0, tg_a1, tg_b0, tg_b1), (sg_a0, sg_a1, sg_b0, sg_b1)
-    key_back = run.after(back_call(tgs, sgs))
-    key_got = lax.ppermute(key_back, "tensor", [(i + 1, i) for i in range(shards - 1)])
-    wq_keep_a, wq_send_a = run.after(wgrad(place, first_in, [(dq_a0, 0), (dq_a1, 0)], (run.last,)))
+    down_s.start([[down_ka, down_xa, down_y]])
+    wq_keep_a, wq_send_a = run.after(wgrad(place, first_in, parts(dq_a), (run.last,)))
     wq_core_a = swap(wq_send_a, "dp", 1)
-    down_s.z()
-    up_s.line()
-    rest_s.x([[wo_keep_a, wo_core_a, wo_got], [wq_keep_a, wq_core_a, wq_got]])
-    kv_grad = run.after(own_call(tgs, sgs, key_got, cosT, sinT, (run.last,)))
+    kv_grad = run.after(own_call((tg_a, tg_b), (sg_a, sg_b), (key_got_a, key_got_b), cosT, sinT, (run.last,)))
     tokens_grad, attn_gain_part = post_call(
-        tokens, middle_grad, attn_gain, kv_grad, (w_query, w_query_o, w_kv, w_kv_o, w_rope),
-        (dq_a0, dq_a1, dq_b0, dq_b1), (run.last,),
+        tokens, middle_grad, attn_gain, kv_grad, (w_query, w_query_o, w_kv, w_kv_o, w_rope), (dq_a, dq_b), (run.last,)
     )
     run.last = attn_gain_part
     sm_keep_a, sm_send_a, sm_keep_b, sm_send_b = run.after(
@@ -1093,23 +1164,26 @@
     )
     sm_core_b = swap(sm_send_b, "dp", 1)
     sm_core_a = swap(sm_send_a, "dp", 1)
-    down_s.line()
+    gate_s.line()
+    sm_y = swap(run.fold([[sm_keep_b, sm_core_b]]), "tensor", 1)
+    up_s.line()
+    rest_s.x([[wo_keep_a, wo_core_a, wo_y], [wq_keep_a, wq_core_a, wq_y], [sm_keep_a, sm_core_a, sm_y]])
+    hid_a, hid_b = hold(hid_a, run.last), hold(hid_b, run.last)
+    layer_out = (middle + mm(hid_a, w_down, 1, 0) + mm(hid_b, w_down_o, 1, 0)).astype(bf16)
+
+    gate_s.end((layer_out,))
     rest_s.z()
     up_s.end()
-    sm_got = swap(run.fold([[sm_keep_b, sm_core_b]]), "tensor", 1)
+    down_s.line()
+    rest_s.line()
     gate_sum = run.after(gathered(gate_s.pieces, gate_s.order, False, (run.last,)))
-    small_s.x([[sm_keep_a, sm_core_a, sm_got]])
-    rest_s.line()
     down_s.end()
-    small_s.line(4)
-    small_s.line()
     rest_s.end()
     up_sum = run.after(gathered(up_s.pieces, up_s.order, False, (run.last,)))
-    small_s.end()
     down_sum = run.after(gathered(down_s.pieces, down_s.order, True, (run.last,)))
-    out_sum = run.after(gathered(rest_s.pieces, rest_s.order, True, (run.last,), 0, q_own))
-    query_sum = run.after(gathered(rest_s.pieces, rest_s.order, False, (run.last,), q_own, q_own))
-    kv_sum, rope_sum, gains = gathered_small(small_s.pieces, small_s.order, kv_own, half, (run.last,))
+    kv_sum, rope_sum, gains = gathered_small(rest_s.pieces, rest_s.order, kv_own, half, (run.last,), 2 * q_own)
+    out_sum = gathered_tiles(rest_s.pieces, rest_s.order, True, (run.last,), 0, q_own)
+    query_sum = gathered_tiles(rest_s.pieces, rest_s.order, False, (run.last,), q_own, q_own)
     return (
         layer_out,
         tokens_grad,

time: 556 us -> 536 us (0.964)
  local copies, waits for them, and re-layouts: 70.9 us -> 46.2 us
  waiting for transfers between devices: 93.3 us -> 115 us
  starting transfers between devices: 102 us -> 82 us
    ppermute x72 -> x71, waiting for transfers between devices: 83.2 us -> 112 us  [swap(): return lax.ppermute(x, axis, [(i, i ^ bit) for i in range(n)])]
    unnamed x282 -> x268, local copies, waits for them, and re-layouts: 67.8 us -> 43.9 us
    ppermute x72 -> x71, starting transfers between devices: 95.7 us -> 76.2 us  [swap(): return lax.ppermute(x, axis, [(i, i ^ bit) for i in range(n)])]
    ppermute x1, waiting for transfers between devices: 10.1 us -> 0.01 us  [body(): got = lax.ppermute(sent, 'tensor', [(i, i + 1) for i in range(shards - 1)])]
    pallas_call x26 -> x23, Pallas kernels: 30.4 us -> 27.1 us  [fold(): pl.pallas_call(functools.partial(fold_kernel, [len(g) for g in groups], s...]
    pallas_call x13 -> x10, Pallas kernels: 108 us -> 105 us  [the longest x2 46.4 us: attn_bwd(): pl.pallas_call(functools.partial(bwd_kernel, n, first, partner, heads, bk...]
  transfers between devices with their start and end apart: 74 -> 74, of which waited for: 15 -> 19; matrix products, arithmetic and copies ran while one was open for 11% -> 12% of each run, Pallas kernels for 35% -> 35%
where the time goes in v3:
time: 536 us; the launch traced here: 528 us
  Pallas kernels  222 us (41%)
  waiting for transfers between devices  115 us (21%)
  starting transfers between devices  82 us (15%)
  local copies, waits for them, and re-layouts  46.2 us (9%)
  matrix products  43 us (8%)
  other arithmetic  16 us (3%)
    ppermute x71, waiting for transfers between devices, swap(): return lax.ppermute(x, axis, [(i, i ^ bit) for i in range(n)])  112 us
    ppermute x71, starting transfers between devices, swap(): return lax.ppermute(x, axis, [(i, i ^ bit) for i in range(n)])  76.2 us
    pallas_call x2, Pallas kernels, mlp_call(): pl.pallas_call(functools.partial(mlp_kernel, first, pieces, edge, len(dep...  58.3 us
    pallas_call x2, Pallas kernels, attn_bwd(): pl.pallas_call(functools.partial(bwd_kernel, n, first, partner, heads, bk...  46.4 us
    unnamed x268, local copies, waits for them, and re-layouts  43.9 us
    dot_general x10, matrix products, mm(): lax.dot_general(a, b, (((ca,), (cb,)), ((), ())), preferred_element_type=...  43 us
    pallas_call x23, Pallas kernels, fold(): pl.pallas_call(functools.partial(fold_kernel, [len(g) for g in groups], s...  27.1 us
    pallas_call x1, Pallas kernels, attn_fwd(): pl.pallas_call(functools.partial(fwd_kernel, n, heads, bk, len(deps)), gr...  26 us
  transfers between devices with their start and end apart: 74, of which 19 were waited for; matrix products, arithmetic and copies ran while one was open for 12% of the time, Pallas kernels for 35%

profile of v3, /device:TPU:0, one launch (start us, length us, event | category | flops | bytes accessed | tf_op | source)
XLA Modules:
  0.0 527.9 jit_solution(11707660303689558574)
XLA Ops:
  1.6 3.0 collective-permute-start.2
  8.8 2.0 collective-permute-start
  19.2 4.4 first_projections.1
  26.2 2.2 other_keys.1
  29.1 3.3 collective-permute-start.4
  39.2 4.3 other_queries.1
  54.8 26.0 %attn_fwd.1 = (bf16[2,256,1024]{2,1,0:T(8,128)(2,1)}, bf16[2,256,1024]{2,1,0:T(8,128)(2,1)}, f32[2,4,1024]{2,1,0:T(4,128)}, f32[2,4,1024]{2,1,0:T(4,128)}) custom-call(s32[4,4]{1,0:T(4,128)} %add_select_fusion.4.bounds, s32[1,1024]{1,0:T(1,128)} %compare_select_fusion.start_ref, bf16[2,256,1024]{2,1,0:T(8,128)(2,1)} %copy-done.93, ...), custom_call_target="tpu_custom_call" | custom-call | flops 51539607552 | bytes 4194304 | tf_op jit(solution)/shard_map/attn_fwd/pallas_call | solution.py:130
  80.8 2.7 fusion.21
  85.3 2.0 copy-done.95
  89.0 29.1 %mlp_grads.2 = (bf16[1024,1408]{1,0:T(8,128)(2,1)}, bf16[1024,1408]{1,0:T(8,128)(2,1)}, bf16[1024,1408]{1,0:T(8,128)(2,1)}, bf16[3,512,1408]{2,1,0:T(8,128)(2,1)...) custom-call(s32[3]{0:T(128)} %copy-done.66, ...), custom_call_target="tpu_custom_call" | custom-call | flops 32480690176 | bytes 34340864 | tf_op jit(solution)/shard_map/mlp_grads/pallas_call | solution.py:545
  118.1 27.7 %collective-permute-done.7.a = bf16[512,1408]{1,0:T(8,128)(2,1)S(1)} collective-permute-done((bf16[512,1408]{1,0:T(8,128)(2,1)}, bf16[512,1408]{1,0:T(8,128)(2,1)S(1)}, u32[]{:S(2)}, u32[]{:S(2)}) %collective-permute-start.7) | collective-permute-done | bytes 1441824 | tf_op jit(solution)/shard_map/ppermute | solution.py:975
  148.8 5.4 %fusion.22 = f32[1024,1024]{1,0:T(8,128)S(1)} fusion(bf16[1024,1408]{1,0:T(8,128)(2,1)} %get-tuple-element.171, bf16[1024,1408]{1,0:T(8,128)(2,1)S(1)} %copy-done.10), kind=kOutput, calls=%fused_computation.102 | convolution fusion | flops 2952790016 | bytes 9961472 | tf_op jit(solution)/shard_map/dot_general | solution.py:970
  154.2 5.1 convolution_add_fusion.refs_10_
  160.4 29.2 %mlp_grads.3 = (bf16[1024,1408]{1,0:T(8,128)(2,1)}, bf16[1024,1408]{1,0:T(8,128)(2,1)}, bf16[1024,1408]{1,0:T(8,128)(2,1)}, bf16[3,512,1408]{2,1,0:T(8,128)(2,1)...) custom-call(s32[3]{0:T(128)} %copy-done.66, ...), custom_call_target="tpu_custom_call" | custom-call | flops 32480690176 | bytes 34340864 | tf_op jit(solution)/shard_map/mlp_grads/pallas_call | solution.py:545
  194.1 2.2 copy-done
  197.0 3.6 fold.23
  201.3 8.2 %fusion.23 = f32[1024,1024]{1,0:T(8,128)} fusion(bf16[1024,1408]{1,0:T(8,128)(2,1)} %hold.10, bf16[1024,1408]{1,0:T(8,128)(2,1)} %get-tuple-element.184), kind=kOutput, calls=%fused_computation.103 | convolution fusion | flops 2952790016 | bytes 9961472 | tf_op jit(solution)/shard_map/dot_general | solution.py:970
  209.5 6.5 %multiply_reduce_fusion = (f32[1024]{0:T(1024)S(1)}, f32[1024]{0:T(1024)S(1)}, f32[1024,1024]{1,0:T(8,128)S(1)}) fusion(f32[1024,1024]{1,0:T(8,128)S(1)} %copy-done.96, f32[1024]{0:T(1024)S(1)} %add_rsqrt_fusion, f32[1024]{0:T(1024)S(1)} %copy-done.120, f32[1024,1024]{1,0:T(8,128)S(1)} %copy-done.123, f32[1024,1024]{1,0:T(8,128)} %fusion.23, ...), kind=kOutput, calls=%fused_computation.1 | convolution fusion | flops 2961176576 | bytes 22560768 | tf_op jit(solution)/shard_map/dot_general | solution.py:970
  216.1 3.0 fusion.19
  219.1 2.7 weight_grads.4
  221.8 2.4 weight_grads.5
  224.6 3.7 fold.24
  230.1 2.3 fusion
  232.4 2.3 fusion.1
  236.4 2.2 fold.26
  240.0 23.2 %attn_bwd.2 = (bf16[2,256,1024]{2,1,0:T(8,128)(2,1)}, f32[2,64,2048]{2,1,0:T(8,128)}, f32[32,2048]{1,0:T(8,128)}, f32[8,128]{1,0:T(8,128)}) custom-call(s32[2,4]{1,0:T(2,128)} %add_select_fusion.5.bounds, s32[1,1024]{1,0:T(1,128)} %compare_select_fusion.start_ref, bf16[2,256,1024]{2,1,0:T(8,128)(2,1)} %copy-done.92, ...), custom_call_target="tpu_custom_call" | custom-call | flops 48318382080 | bytes 4194304 | tf_op jit(solution)/shard_map/attn_bwd/pallas_call | solution.py:247
  267.0 2.4 weight_grads.6
  271.7 2.3 fold.27
  275.5 13.5 %collective-permute-done.20 = bf16[512,1408]{1,0:T(8,128)(2,1)} collective-permute-done((bf16[512,1408]{1,0:T(8,128)(2,1)}, bf16[512,1408]{1,0:T(8,128)(2,1)}, u32[]{:S(2)}, u32[]{:S(2)}) %collective-permute-start.20) | collective-permute-done | bytes 1441824 | tf_op jit(solution)/shard_map/ppermute | solution.py:975
  290.3 2.8 fold.28
  295.6 2.7 collective-permute-start.27
  301.5 23.2 %attn_bwd.3 = (bf16[2,256,1024]{2,1,0:T(8,128)(2,1)}, f32[2,64,2048]{2,1,0:T(8,128)}, f32[32,2048]{1,0:T(8,128)}, f32[8,128]{1,0:T(8,128)}) custom-call(s32[2,4]{1,0:T(2,128)} %add_select_fusion.5.bounds, s32[1,1024]{1,0:T(1,128)} %compare_select_fusion.start_ref, bf16[2,256,1024]{2,1,0:T(8,128)(2,1)} %copy-done.93, ...), custom_call_target="tpu_custom_call" | custom-call | flops 48318382080 | bytes 4194304 | tf_op jit(solution)/shard_map/attn_bwd/pallas_call | solution.py:247
  329.7 2.0 fold.32
  337.2 2.4 weight_grads.7
  339.7 2.9 collective-permute-done.33.refs_5_
  346.3 7.6 %token_grads.1 = (bf16[1024,1024]{1,0:T(8,128)(2,1)}, f32[1,1024]{1,0:T(1,128)S(1)}) custom-call(bf16[1024,1024]{1,0:T(8,128)(2,1)S(1)} %copy-done.28, f32[1024,1024]{1,0:T(8,128)S(1)} %copy-done.5, f32[1,1024]{1,0:T(1,128)S(1)} %bitcast.163, bf16[288,1024]{1,0:T(8,128)(2,1)S(1)} %get-tuple-element.243.kv_ref, bf16[1024,512]{1,0:T(8,128)(2,1)S(1)} %copy-done.34, ...), custom_call_target="tpu_custom_call" | custom-call | flops 5368709120 | bytes 16777216 | tf_op jit(solution)/shard_map/token_grads/pallas_call | solution.py:899
  353.9 2.4 small_grads.1
  357.0 6.8 %collective-permute-start.31 = (bf16[512,512]{1,0:T(8,128)(2,1)S(1)}, bf16[512,512]{1,0:T(8,128)(2,1)S(1)}, u32[]{:S(2)}, u32[]{:S(2)}) collective-permute-start(bf16[512,512]{1,0:T(8,128)(2,1)S(1)} %copy-done.75), channel_id=1, source_target_pairs={{0,1},{1,0},{2,3},{3,2},{4,5},{5,4},{6,7},{7,6},{8,9},{9,8},{10,11... | collective-permute-start | bytes 1572872 | tf_op jit(solution)/shard_map/ppermute | solution.py:975
  365.4 2.0 collective-permute-done.38
  367.4 5.1 collective-permute-start.37
  373.3 3.3 collective-permute-done.31
  376.6 9.3 %collective-permute-start.43 = (bf16[128,1408]{1,0:T(8,128)(2,1)}, bf16[128,1408]{1,0:T(8,128)(2,1)}, u32[]{:S(2)}, u32[]{:S(2)}) collective-permute-start(bf16[128,1408]{1,0:T(8,128)(2,1)} %get-tuple-element.273), channel_id=1, source_target_pairs={{0,16},{2,18},{4,20},{6,22},{8,24},{10,26},{12,28},{14,30},{16,0},... | collective-permute-start | bytes 1081352 | tf_op jit(solution)/shard_map/ppermute | solution.py:975
  387.8 9.3 %collective-permute-start.40 = (bf16[128,1408]{1,0:T(8,128)(2,1)}, bf16[128,1408]{1,0:T(8,128)(2,1)}, u32[]{:S(2)}, u32[]{:S(2)}) collective-permute-start(bf16[128,1408]{1,0:T(8,128)(2,1)} %get-tuple-element.267), channel_id=1, source_target_pairs={{0,16},{2,18},{4,20},{6,22},{8,24},{10,26},{12,28},{14,30},{16,0},... | collective-permute-start | bytes 1081352 | tf_op jit(solution)/shard_map/ppermute | solution.py:975
  399.1 4.1 collective-permute-start.39
  403.2 5.2 fusion.24
  408.5 3.6 add_convert_fusion.refs_3_
  412.2 4.8 collective-permute-done.40
  419.6 2.0 collective-permute-start.42
  421.6 6.4 %collective-permute-done.47.refs_2_ = bf16[128,1408]{1,0:T(8,128)(2,1)S(1)} collective-permute-done((bf16[128,1408]{1,0:T(8,128)(2,1)S(1)}, bf16[128,1408]{1,0:T(8,128)(2,1)S(1)}, u32[]{:S(2)}, u32[]{:S(2)}) %collective-permute-start.47) | collective-permute-done | bytes 360480 | tf_op jit(solution)/shard_map/ppermute | solution.py:975
  428.1 2.8 collective-permute-done.46.refs_1_
  433.1 4.2 collective-permute-done.42
  438.7 3.4 collective-permute-start.45
  442.5 11.8 %collective-permute-done.41 = bf16[128,1280]{1,0:T(8,128)(2,1)S(1)} collective-permute-done((bf16[128,1280]{1,0:T(8,128)(2,1)S(1)}, bf16[128,1280]{1,0:T(8,128)(2,1)S(1)}, u32[]{:S(2)}, u32[]{:S(2)}) %collective-permute-start.41) | collective-permute-done | bytes 327712 | tf_op jit(solution)/shard_map/ppermute | solution.py:975
  456.9 7.6 %collective-permute-done.67.refs_1_ = bf16[128,1408]{1,0:T(8,128)(2,1)S(1)} collective-permute-done((bf16[128,1408]{1,0:T(8,128)(2,1)S(1)}, bf16[128,1408]{1,0:T(8,128)(2,1)S(1)}, u32[]{:S(2)}, u32[]{:S(2)}) %collective-permute-start.67) | collective-permute-done | bytes 360480 | tf_op jit(solution)/shard_map/ppermute | solution.py:975
  466.0 6.4 %gathered.5 = (f32[1024,1408]{1,0:T(8,128)}, f32[8,128]{1,0:T(8,128)}) custom-call(s32[8]{0:T(128)} %stack.41.order, bf16[128,1408]{1,0:T(8,128)(2,1)} %copy-done.41, bf16[128,1408]{1,0:T(8,128)(2,1)} %copy-done.108, bf16[128,1408]{1,0:T(8,128)(2,1)} %copy-done.107, bf16[128,1408]{1,0:T(8,128)(2,1)} %copy-done.112, bf16[128,1408]{1,0:T(8,128)(2,1)} %copy-done.109, ...), custom_call_target="tpu_custom_call" | custom-call | bytes 8650752 | tf_op jit(solution)/shard_map/gathered/pallas_call | solution.py:668
  478.1 6.3 %collective-permute-done.60.refs_1_ = bf16[128,1408]{1,0:T(8,128)(2,1)S(1)} collective-permute-done((bf16[128,1408]{1,0:T(8,128)(2,1)S(1)}, bf16[128,1408]{1,0:T(8,128)(2,1)S(1)}, u32[]{:S(2)}, u32[]{:S(2)}) %collective-permute-start.60) | collective-permute-done | bytes 360480 | tf_op jit(solution)/shard_map/ppermute | solution.py:975
  484.4 2.1 collective-permute-start.62
  487.0 5.0 collective-permute-done.54.refs_2_
  493.7 6.1 %collective-permute-done.62.refs_3_ = bf16[128,1408]{1,0:T(8,128)(2,1)} collective-permute-done((bf16[128,1408]{1,0:T(8,128)(2,1)S(1)}, bf16[128,1408]{1,0:T(8,128)(2,1)}, u32[]{:S(2)}, u32[]{:S(2)}) %collective-permute-start.62) | collective-permute-done | bytes 360480 | tf_op jit(solution)/shard_map/ppermute | solution.py:975
  501.0 5.2 collective-permute-done.55.refs_3_
  506.3 6.7 %gathered.6 = (f32[1024,1408]{1,0:T(8,128)}, f32[8,128]{1,0:T(8,128)}) custom-call(s32[8]{0:T(128)} %stack.41.order, bf16[128,1408]{1,0:T(8,128)(2,1)} %copy-done.40, bf16[128,1408]{1,0:T(8,128)(2,1)} %copy-done.105, bf16[128,1408]{1,0:T(8,128)(2,1)} %copy-done.104, bf16[128,1408]{1,0:T(8,128)(2,1)} %collective-permute-done.69.refs_3_, ...), custom_call_target="tpu_custom_call" | custom-call | bytes 8650752 | tf_op jit(solution)/shard_map/gathered/pallas_call | solution.py:668
  512.9 6.8 %gathered.7 = (f32[1408,1024]{1,0:T(8,128)}, f32[8,128]{1,0:T(8,128)}) custom-call(s32[8]{0:T(128)} %stack.41.order, bf16[128,1408]{1,0:T(8,128)(2,1)} %copy-done.42, bf16[128,1408]{1,0:T(8,128)(2,1)} %copy-done.113, bf16[128,1408]{1,0:T(8,128)(2,1)} %copy-done.115, bf16[128,1408]{1,0:T(8,128)(2,1)} %collective-permute-done.62.refs_3_, ...), custom_call_target="tpu_custom_call" | custom-call | bytes 8650752 | tf_op jit(solution)/shard_map/gathered/pallas_call | solution.py:668
  523.3 2.2 gathered.9
  525.6 2.1 gathered.8
  (461 shorter events, 111.6 us)
Async XLA Ops:
  1.6 23.1 %collective-permute-start.2 = (bf16[512,128]{1,0:T(8,128)(2,1)S(1)}, bf16[512,128]{1,0:T(8,128)(2,1)S(1)}, u32[]{:S(2)}, u32[]{:S(2)}) collective-permute-start(bf16[512,128]{1,0:T(8,128)(2,1)S(1)} %get-tuple-element.158), channel_id=1, source_target_pairs={{0,1},{1,0},{2,3},{3,2},{4,5},{5,4},{6,7},{7,6},{8,9},{9,8},{10,11... | collective-permute-start | bytes 393224 | tf_op jit(solution)/shard_map/ppermute | solution.py:975
  8.8 25.6 %collective-permute-start.5 = (bf16[256,1024]{1,0:T(8,128)(2,1)}, bf16[256,1024]{1,0:T(8,128)(2,1)}, u32[]{:S(2)}, u32[]{:S(2)}) collective-permute-start(bf16[256,1024]{1,0:T(8,128)(2,1)} %get-tuple-element.167), channel_id=1, source_target_pairs={{0,1},{1,0},{2,3},{3,2},{4,5},{5,4},{6,7},{7,6},{8,9},{9,8},{10,11... | collective-permute-start | bytes 1572872 | tf_op jit(solution)/shard_map/ppermute | solution.py:975
  8.8 24.9 %collective-permute-start = (bf16[512,512]{1,0:T(8,128)(2,1)}, bf16[512,512]{1,0:T(8,128)(2,1)}, u32[]{:S(2)}, u32[]{:S(2)}) collective-permute-start(bf16[512,512]{1,0:T(8,128)(2,1)} %get-tuple-element.156), channel_id=1, source_target_pairs={{0,1},{1,0},{2,3},{3,2},{4,5},{5,4},{6,7},{7,6},{8,9},{9,8},{10,11... | collective-permute-start | bytes 1572872 | tf_op jit(solution)/shard_map/ppermute | solution.py:975
  29.1 16.4 %collective-permute-start.4 = (bf16[288,1024]{1,0:T(8,128)(2,1)}, bf16[288,1024]{1,0:T(8,128)(2,1)}, u32[]{:S(2)}, u32[]{:S(2)}) collective-permute-start(bf16[288,1024]{1,0:T(8,128)(2,1)} %get-tuple-element.161.sent_ref), channel_id=1, source_target_pairs={{0,1},{2,3},{4,5},{6,7},{8,9},{10,11},{12,13},{14,15},{16,17},{18,... | collective-permute-start | bytes 1769480 | tf_op jit(solution)/shard_map/ppermute | solution.py:1074
  34.4 18.1 %collective-permute-start.6 = (bf16[256,1024]{1,0:T(8,128)(2,1)}, bf16[256,1024]{1,0:T(8,128)(2,1)S(1)}, u32[]{:S(2)}, u32[]{:S(2)}) collective-permute-start(bf16[256,1024]{1,0:T(8,128)(2,1)} %collective-permute-done.5), channel_id=1, source_target_pairs={{0,2},{2,0},{4,6},{6,4},{8,10},{10,8},{12,14},{14,12},{16,18},{18,... | collective-permute-start | bytes 1572872 | tf_op jit(solution)/shard_map/ppermute | solution.py:975
  50.3 97.2 %collective-permute-start.11 = (bf16[1408,512]{1,0:T(8,128)(2,1)}, bf16[1408,512]{1,0:T(8,128)(2,1)}, u32[]{:S(2)}, u32[]{:S(2)}) collective-permute-start(bf16[1408,512]{1,0:T(8,128)(2,1)} %get-tuple-element.178), channel_id=1, source_target_pairs={{0,1},{1,0},{2,3},{3,2},{4,5},{5,4},{6,7},{7,6},{8,9},{9,8},{10,11... | collective-permute-start | bytes 4325384 | tf_op jit(solution)/shard_map/ppermute | solution.py:975
  50.5 96.5 %collective-permute-start.9 = (bf16[512,1408]{1,0:T(8,128)(2,1)}, bf16[512,1408]{1,0:T(8,128)(2,1)}, u32[]{:S(2)}, u32[]{:S(2)}) collective-permute-start(bf16[512,1408]{1,0:T(8,128)(2,1)} %get-tuple-element.177), channel_id=1, source_target_pairs={{0,1},{1,0},{2,3},{3,2},{4,5},{5,4},{6,7},{7,6},{8,9},{9,8},{10,11... | collective-permute-start | bytes 4325384 | tf_op jit(solution)/shard_map/ppermute | solution.py:975
  52.3 93.5 %collective-permute-start.7 = (bf16[512,1408]{1,0:T(8,128)(2,1)}, bf16[512,1408]{1,0:T(8,128)(2,1)S(1)}, u32[]{:S(2)}, u32[]{:S(2)}) collective-permute-start(bf16[512,1408]{1,0:T(8,128)(2,1)} %get-tuple-element.175), channel_id=1, source_target_pairs={{0,1},{1,0},{2,3},{3,2},{4,5},{5,4},{6,7},{7,6},{8,9},{9,8},{10,11... | collective-permute-start | bytes 4325384 | tf_op jit(solution)/shard_map/ppermute | solution.py:975
  146.9 12.3 %collective-permute-start.8 = (bf16[512,1408]{1,0:T(8,128)(2,1)}, bf16[512,1408]{1,0:T(8,128)(2,1)}, u32[]{:S(2)}, u32[]{:S(2)}) collective-permute-start(bf16[512,1408]{1,0:T(8,128)(2,1)} %hold.7.refs_4_), channel_id=1, source_target_pairs={{0,2},{2,0},{4,6},{6,4},{8,10},{10,8},{12,14},{14,12},{16,18},{18,... | collective-permute-start | bytes 4325384 | tf_op jit(solution)/shard_map/ppermute | solution.py:975
  147.0 12.3 %collective-permute-start.10 = (bf16[512,1408]{1,0:T(8,128)(2,1)}, bf16[512,1408]{1,0:T(8,128)(2,1)}, u32[]{:S(2)}, u32[]{:S(2)}) collective-permute-start(bf16[512,1408]{1,0:T(8,128)(2,1)} %hold.8.refs_6_), channel_id=1, source_target_pairs={{0,2},{2,0},{4,6},{6,4},{8,10},{10,8},{12,14},{14,12},{16,18},{18,... | collective-permute-start | bytes 4325384 | tf_op jit(solution)/shard_map/ppermute | solution.py:975
  147.5 11.8 %collective-permute-start.12 = (bf16[1408,512]{1,0:T(8,128)(2,1)}, bf16[1408,512]{1,0:T(8,128)(2,1)S(1)}, u32[]{:S(2)}, u32[]{:S(2)}) collective-permute-start(bf16[1408,512]{1,0:T(8,128)(2,1)} %hold.9.refs_8_), channel_id=1, source_target_pairs={{0,2},{2,0},{4,6},{6,4},{8,10},{10,8},{12,14},{14,12},{16,18},{18,... | collective-permute-start | bytes 4325384 | tf_op jit(solution)/shard_map/ppermute | solution.py:975
  192.6 82.3 %collective-permute-start.19 = (bf16[512,1408]{1,0:T(8,128)(2,1)}, bf16[512,1408]{1,0:T(8,128)(2,1)S(1)}, u32[]{:S(2)}, u32[]{:S(2)}) collective-permute-start(bf16[512,1408]{1,0:T(8,128)(2,1)} %get-tuple-element.199), channel_id=1, source_target_pairs={{0,2},{2,0},{4,6},{6,4},{8,10},{10,8},{12,14},{14,12},{16,18},{18,... | collective-permute-start | bytes 4325384 | tf_op jit(solution)/shard_map/ppermute | solution.py:975
  193.1 70.0 %collective-permute-start.21 = (bf16[512,1408]{1,0:T(8,128)(2,1)}, bf16[512,1408]{1,0:T(8,128)(2,1)S(1)}, u32[]{:S(2)}, u32[]{:S(2)}) collective-permute-start(bf16[512,1408]{1,0:T(8,128)(2,1)} %get-tuple-element.201), channel_id=1, source_target_pairs={{0,2},{2,0},{4,6},{6,4},{8,10},{10,8},{12,14},{14,12},{16,18},{18,... | collective-permute-start | bytes 4325384 | tf_op jit(solution)/shard_map/ppermute | solution.py:975
  193.1 41.5 %collective-permute-start.23 = (bf16[512,1408]{1,0:T(8,128)(2,1)}, bf16[512,1408]{1,0:T(8,128)(2,1)}, u32[]{:S(2)}, u32[]{:S(2)}) collective-permute-start(bf16[512,1408]{1,0:T(8,128)(2,1)} %get-tuple-element.204), channel_id=1, source_target_pairs={{0,2},{2,0},{4,6},{6,4},{8,10},{10,8},{12,14},{14,12},{16,18},{18,... | collective-permute-start | bytes 4325384 | tf_op jit(solution)/shard_map/ppermute | solution.py:975
  193.6 34.7 %collective-permute-start.16 = (bf16[512,1408]{1,0:T(8,128)(2,1)}, bf16[512,1408]{1,0:T(8,128)(2,1)}, u32[]{:S(2)}, u32[]{:S(2)}) collective-permute-start(bf16[512,1408]{1,0:T(8,128)(2,1)} %get-tuple-element.192), channel_id=1, source_target_pairs={{0,2},{2,0},{4,6},{6,4},{8,10},{10,8},{12,14},{14,12},{16,18},{18,... | collective-permute-start | bytes 4325384 | tf_op jit(solution)/shard_map/ppermute | solution.py:975
  193.6 30.6 %collective-permute-start.17 = (bf16[512,1408]{1,0:T(8,128)(2,1)}, bf16[512,1408]{1,0:T(8,128)(2,1)}, u32[]{:S(2)}, u32[]{:S(2)}) collective-permute-start(bf16[512,1408]{1,0:T(8,128)(2,1)} %get-tuple-element.193), channel_id=1, source_target_pairs={{0,2},{2,0},{4,6},{6,4},{8,10},{10,8},{12,14},{14,12},{16,18},{18,... | collective-permute-start | bytes 4325384 | tf_op jit(solution)/shard_map/ppermute | solution.py:975
  224.2 45.2 %collective-permute-start.22 = (bf16[512,1408]{1,0:T(8,128)(2,1)}, bf16[512,1408]{1,0:T(8,128)(2,1)}, u32[]{:S(2)}, u32[]{:S(2)}) collective-permute-start(bf16[512,1408]{1,0:T(8,128)(2,1)} %get-tuple-element.202), channel_id=1, source_target_pairs={{0,1},{1,0},{2,3},{3,2},{4,5},{5,4},{6,7},{7,6},{8,9},{9,8},{10,11... | collective-permute-start | bytes 4325384 | tf_op jit(solution)/shard_map/ppermute | solution.py:975
  228.3 67.3 %collective-permute-start.15 = (bf16[512,512]{1,0:T(8,128)(2,1)}, bf16[512,512]{1,0:T(8,128)(2,1)}, u32[]{:S(2)}, u32[]{:S(2)}) collective-permute-start(bf16[512,512]{1,0:T(8,128)(2,1)} %get-tuple-element.191), channel_id=1, source_target_pairs={{0,2},{2,0},{4,6},{6,4},{8,10},{10,8},{12,14},{14,12},{16,18},{18,... | collective-permute-start | bytes 1572872 | tf_op jit(solution)/shard_map/ppermute | solution.py:975
  234.6 54.4 %collective-permute-start.20 = (bf16[512,1408]{1,0:T(8,128)(2,1)}, bf16[512,1408]{1,0:T(8,128)(2,1)}, u32[]{:S(2)}, u32[]{:S(2)}) collective-permute-start(bf16[512,1408]{1,0:T(8,128)(2,1)} %get-tuple-element.200), channel_id=1, source_target_pairs={{0,1},{1,0},{2,3},{3,2},{4,5},{5,4},{6,7},{7,6},{8,9},{9,8},{10,11... | collective-permute-start | bytes 4325384 | tf_op jit(solution)/shard_map/ppermute | solution.py:975
  263.1 30.0 %collective-permute-start.18 = (bf16[256,1408]{1,0:T(8,128)(2,1)}, bf16[256,1408]{1,0:T(8,128)(2,1)S(1)}, u32[]{:S(2)}, u32[]{:S(2)}) collective-permute-start(bf16[256,1408]{1,0:T(8,128)(2,1)} %copy-done.68), channel_id=1, source_target_pairs={{0,4},{2,6},{4,0},{6,2},{8,12},{10,14},{12,8},{14,10},{16,20},{18,... | collective-permute-start | bytes 2162696 | tf_op jit(solution)/shard_map/ppermute | solution.py:975
  269.4 29.9 %collective-permute-start.25 = (bf16[512,512]{1,0:T(8,128)(2,1)S(1)}, bf16[512,512]{1,0:T(8,128)(2,1)S(1)}, u32[]{:S(2)}, u32[]{:S(2)}) collective-permute-start(bf16[512,512]{1,0:T(8,128)(2,1)S(1)} %get-tuple-element.219), channel_id=1, source_target_pairs={{0,2},{2,0},{4,6},{6,4},{8,10},{10,8},{12,14},{14,12},{16,18},{18,... | collective-permute-start | bytes 1572872 | tf_op jit(solution)/shard_map/ppermute | solution.py:975
  274.9 60.2 %collective-permute-start.26 = (bf16[256,1408]{1,0:T(8,128)(2,1)}, bf16[256,1408]{1,0:T(8,128)(2,1)S(1)}, u32[]{:S(2)}, u32[]{:S(2)}) collective-permute-start(bf16[256,1408]{1,0:T(8,128)(2,1)} %get-tuple-element.224), channel_id=1, source_target_pairs={{0,4},{2,6},{4,0},{6,2},{8,12},{10,14},{12,8},{14,10},{16,20},{18,... | collective-permute-start | bytes 2162696 | tf_op jit(solution)/shard_map/ppermute | solution.py:975
  289.0 50.6 %collective-permute-start.32 = (bf16[160,1024]{1,0:T(8,128)(2,1)}, bf16[160,1024]{1,0:T(8,128)(2,1)S(1)}, u32[]{:S(2)}, u32[]{:S(2)}) collective-permute-start(bf16[160,1024]{1,0:T(8,128)(2,1)} %get-tuple-element.240), channel_id=1, source_target_pairs={{1,0},{3,2},{5,4},{7,6},{9,8},{11,10},{13,12},{15,14},{17,16},{19,... | collective-permute-start | bytes 983048 | tf_op jit(solution)/shard_map/ppermute | solution.py:1143
  293.1 35.2 %collective-permute-start.29 = (bf16[256,1408]{1,0:T(8,128)(2,1)}, bf16[256,1408]{1,0:T(8,128)(2,1)}, u32[]{:S(2)}, u32[]{:S(2)}) collective-permute-start(bf16[256,1408]{1,0:T(8,128)(2,1)} %get-tuple-element.229), channel_id=1, source_target_pairs={{0,4},{2,6},{4,0},{6,2},{8,12},{10,14},{12,8},{14,10},{16,20},{18,... | collective-permute-start | bytes 2162696 | tf_op jit(solution)/shard_map/ppermute | solution.py:975
  295.6 39.6 %collective-permute-start.27 = (bf16[256,1408]{1,0:T(8,128)(2,1)}, bf16[256,1408]{1,0:T(8,128)(2,1)S(1)}, u32[]{:S(2)}, u32[]{:S(2)}) collective-permute-start(bf16[256,1408]{1,0:T(8,128)(2,1)} %get-tuple-element.225), channel_id=1, source_target_pairs={{0,1},{1,0},{2,3},{3,2},{4,5},{5,4},{6,7},{7,6},{8,9},{9,8},{10,11... | collective-permute-start | bytes 2162696 | tf_op jit(solution)/shard_map/ppermute | solution.py:975
  299.4 32.3 %collective-permute-start.28 = (bf16[256,1408]{1,0:T(8,128)(2,1)}, bf16[256,1408]{1,0:T(8,128)(2,1)}, u32[]{:S(2)}, u32[]{:S(2)}) collective-permute-start(bf16[256,1408]{1,0:T(8,128)(2,1)} %get-tuple-element.227), channel_id=1, source_target_pairs={{0,4},{2,6},{4,0},{6,2},{8,12},{10,14},{12,8},{14,10},{16,20},{18,... | collective-permute-start | bytes 2162696 | tf_op jit(solution)/shard_map/ppermute | solution.py:975
  328.3 14.2 %collective-permute-start.33 = (bf16[160,1024]{1,0:T(8,128)(2,1)}, bf16[160,1024]{1,0:T(8,128)(2,1)}, u32[]{:S(2)}, u32[]{:S(2)}) collective-permute-start(bf16[160,1024]{1,0:T(8,128)(2,1)} %get-tuple-element.241), channel_id=1, source_target_pairs={{1,0},{3,2},{5,4},{7,6},{9,8},{11,10},{13,12},{15,14},{17,16},{19,... | collective-permute-start | bytes 983048 | tf_op jit(solution)/shard_map/ppermute | solution.py:1151
  331.7 32.2 %collective-permute-start.36 = (bf16[128,1408]{1,0:T(8,128)(2,1)}, bf16[128,1408]{1,0:T(8,128)(2,1)S(1)}, u32[]{:S(2)}, u32[]{:S(2)}) collective-permute-start(bf16[128,1408]{1,0:T(8,128)(2,1)} %get-tuple-element.253), channel_id=1, source_target_pairs={{0,8},{2,10},{4,12},{6,14},{8,0},{10,2},{12,4},{14,6},{16,24},{18,... | collective-permute-start | bytes 1081352 | tf_op jit(solution)/shard_map/ppermute | solution.py:975
  357.0 19.6 %collective-permute-start.31 = (bf16[512,512]{1,0:T(8,128)(2,1)S(1)}, bf16[512,512]{1,0:T(8,128)(2,1)S(1)}, u32[]{:S(2)}, u32[]{:S(2)}) collective-permute-start(bf16[512,512]{1,0:T(8,128)(2,1)S(1)} %copy-done.75), channel_id=1, source_target_pairs={{0,1},{1,0},{2,3},{3,2},{4,5},{5,4},{6,7},{7,6},{8,9},{9,8},{10,11... | collective-permute-start | bytes 1572872 | tf_op jit(solution)/shard_map/ppermute | solution.py:975
  363.8 24.0 %collective-permute-start.24 = (bf16[512,512]{1,0:T(8,128)(2,1)S(1)}, bf16[512,512]{1,0:T(8,128)(2,1)S(1)}, u32[]{:S(2)}, u32[]{:S(2)}) collective-permute-start(bf16[512,512]{1,0:T(8,128)(2,1)S(1)} %copy-done.73), channel_id=1, source_target_pairs={{0,1},{1,0},{2,3},{3,2},{4,5},{5,4},{6,7},{7,6},{8,9},{9,8},{10,11... | collective-permute-start | bytes 1572872 | tf_op jit(solution)/shard_map/ppermute | solution.py:975
  363.9 33.2 %collective-permute-start.30 = (bf16[512,512]{1,0:T(8,128)(2,1)S(1)}, bf16[512,512]{1,0:T(8,128)(2,1)S(1)}, u32[]{:S(2)}, u32[]{:S(2)}) collective-permute-start(bf16[512,512]{1,0:T(8,128)(2,1)S(1)} %get-tuple-element.238), channel_id=1, source_target_pairs={{0,2},{2,0},{4,6},{6,4},{8,10},{10,8},{12,14},{14,12},{16,18},{18,... | collective-permute-start | bytes 1572872 | tf_op jit(solution)/shard_map/ppermute | solution.py:975
  364.8 32.3 %collective-permute-start.34 = (bf16[512,256]{1,0:T(8,128)(2,1)S(1)}, bf16[512,256]{1,0:T(8,128)(2,1)S(1)}, u32[]{:S(2)}, u32[]{:S(2)}) collective-permute-start(bf16[512,256]{1,0:T(8,128)(2,1)S(1)} %get-tuple-element.249), channel_id=1, source_target_pairs={{0,2},{2,0},{4,6},{6,4},{8,10},{10,8},{12,14},{14,12},{16,18},{18,... | collective-permute-start | bytes 786440 | tf_op jit(solution)/shard_map/ppermute | solution.py:975
  367.4 29.8 %collective-permute-start.37 = (bf16[512,256]{1,0:T(8,128)(2,1)S(1)}, bf16[512,256]{1,0:T(8,128)(2,1)S(1)}, u32[]{:S(2)}, u32[]{:S(2)}) collective-permute-start(bf16[512,256]{1,0:T(8,128)(2,1)S(1)} %get-tuple-element.256), channel_id=1, source_target_pairs={{0,1},{1,0},{2,3},{3,2},{4,5},{5,4},{6,7},{7,6},{8,9},{9,8},{10,11... | collective-permute-start | bytes 786440 | tf_op jit(solution)/shard_map/ppermute | solution.py:975
  376.6 45.1 %collective-permute-start.43 = (bf16[128,1408]{1,0:T(8,128)(2,1)}, bf16[128,1408]{1,0:T(8,128)(2,1)}, u32[]{:S(2)}, u32[]{:S(2)}) collective-permute-start(bf16[128,1408]{1,0:T(8,128)(2,1)} %get-tuple-element.273), channel_id=1, source_target_pairs={{0,16},{2,18},{4,20},{6,22},{8,24},{10,26},{12,28},{14,30},{16,0},... | collective-permute-start | bytes 1081352 | tf_op jit(solution)/shard_map/ppermute | solution.py:975
  387.8 29.2 %collective-permute-start.40 = (bf16[128,1408]{1,0:T(8,128)(2,1)}, bf16[128,1408]{1,0:T(8,128)(2,1)}, u32[]{:S(2)}, u32[]{:S(2)}) collective-permute-start(bf16[128,1408]{1,0:T(8,128)(2,1)} %get-tuple-element.267), channel_id=1, source_target_pairs={{0,16},{2,18},{4,20},{6,22},{8,24},{10,26},{12,28},{14,30},{16,0},... | collective-permute-start | bytes 1081352 | tf_op jit(solution)/shard_map/ppermute | solution.py:975
  399.1 31.8 %collective-permute-start.39 = (bf16[256,1280]{1,0:T(8,128)(2,1)}, bf16[256,1280]{1,0:T(8,128)(2,1)S(1)}, u32[]{:S(2)}, u32[]{:S(2)}) collective-permute-start(bf16[256,1280]{1,0:T(8,128)(2,1)} %copy-done.69), channel_id=1, source_target_pairs={{0,4},{2,6},{4,0},{6,2},{8,12},{10,14},{12,8},{14,10},{16,20},{18,... | collective-permute-start | bytes 1966088 | tf_op jit(solution)/shard_map/ppermute | solution.py:975
  419.6 11.3 %collective-permute-start.46 = (bf16[128,1408]{1,0:T(8,128)(2,1)S(1)}, bf16[128,1408]{1,0:T(8,128)(2,1)S(1)}, u32[]{:S(2)}, u32[]{:S(2)}) collective-permute-start(bf16[128,1408]{1,0:T(8,128)(2,1)S(1)} %get-tuple-element.279.refs_0_), channel_id=1, source_target_pairs={{0,8},{2,10},{4,12},{6,14},{8,0},{10,2},{12,4},{14,6},{16,24},{18,... | collective-permute-start | bytes 1081352 | tf_op jit(solution)/shard_map/ppermute | solution.py:975
  419.6 17.7 %collective-permute-start.42 = (bf16[128,1408]{1,0:T(8,128)(2,1)S(1)}, bf16[128,1408]{1,0:T(8,128)(2,1)S(1)}, u32[]{:S(2)}, u32[]{:S(2)}) collective-permute-start(bf16[128,1408]{1,0:T(8,128)(2,1)S(1)} %copy-done.77), channel_id=1, source_target_pairs={{0,8},{2,10},{4,12},{6,14},{8,0},{10,2},{12,4},{14,6},{16,24},{18,... | collective-permute-start | bytes 1081352 | tf_op jit(solution)/shard_map/ppermute | solution.py:975
  421.6 15.9 %collective-permute-start.49 = (bf16[128,1408]{1,0:T(8,128)(2,1)S(1)}, bf16[128,1408]{1,0:T(8,128)(2,1)S(1)}, u32[]{:S(2)}, u32[]{:S(2)}) collective-permute-start(bf16[128,1408]{1,0:T(8,128)(2,1)S(1)} %get-tuple-element.279.refs_0_), channel_id=1, source_target_pairs={{0,2},{2,0},{4,6},{6,4},{8,10},{10,8},{12,14},{14,12},{16,18},{18,... | collective-permute-start | bytes 1081352 | tf_op jit(solution)/shard_map/ppermute | solution.py:975
  430.9 11.2 %collective-permute-start.50 = (bf16[128,1408]{1,0:T(8,128)(2,1)S(1)}, bf16[128,1408]{1,0:T(8,128)(2,1)S(1)}, u32[]{:S(2)}, u32[]{:S(2)}) collective-permute-start(bf16[128,1408]{1,0:T(8,128)(2,1)S(1)} %collective-permute-done.46.refs_1_), channel_id=1, source_target_pairs={{0,2},{2,0},{4,6},{6,4},{8,10},{10,8},{12,14},{14,12},{16,18},{18,... | collective-permute-start | bytes 1081352 | tf_op jit(solution)/shard_map/ppermute | solution.py:975
  430.9 11.6 %collective-permute-start.48 = (bf16[128,1408]{1,0:T(8,128)(2,1)S(1)}, bf16[128,1408]{1,0:T(8,128)(2,1)S(1)}, u32[]{:S(2)}, u32[]{:S(2)}) collective-permute-start(bf16[128,1408]{1,0:T(8,128)(2,1)S(1)} %collective-permute-done.46.refs_1_), channel_id=1, source_target_pairs={{0,4},{2,6},{4,0},{6,2},{8,12},{10,14},{12,8},{14,10},{16,20},{18,... | collective-permute-start | bytes 1081352 | tf_op jit(solution)/shard_map/ppermute | solution.py:975
  437.3 17.1 %collective-permute-start.41 = (bf16[128,1280]{1,0:T(8,128)(2,1)S(1)}, bf16[128,1280]{1,0:T(8,128)(2,1)S(1)}, u32[]{:S(2)}, u32[]{:S(2)}) collective-permute-start(bf16[128,1280]{1,0:T(8,128)(2,1)S(1)} %get-tuple-element.270), channel_id=1, source_target_pairs={{0,8},{2,10},{4,12},{6,14},{8,0},{10,2},{12,4},{14,6},{16,24},{18,... | collective-permute-start | bytes 983048 | tf_op jit(solution)/shard_map/ppermute | solution.py:975
  437.5 16.8 %collective-permute-start.68 = (bf16[128,1408]{1,0:T(8,128)(2,1)S(1)}, bf16[128,1408]{1,0:T(8,128)(2,1)S(1)}, u32[]{:S(2)}, u32[]{:S(2)}) collective-permute-start(bf16[128,1408]{1,0:T(8,128)(2,1)S(1)} %get-tuple-element.285.refs_0_), channel_id=1, source_target_pairs={{0,4},{2,6},{4,0},{6,2},{8,12},{10,14},{12,8},{14,10},{16,20},{18,... | collective-permute-start | bytes 1081352 | tf_op jit(solution)/shard_map/ppermute | solution.py:975
  438.7 18.1 %collective-permute-start.45 = (bf16[128,1408]{1,0:T(8,128)(2,1)S(1)}, bf16[128,1408]{1,0:T(8,128)(2,1)S(1)}, u32[]{:S(2)}, u32[]{:S(2)}) collective-permute-start(bf16[128,1408]{1,0:T(8,128)(2,1)S(1)} %get-tuple-element.278), channel_id=1, source_target_pairs={{0,16},{2,18},{4,20},{6,22},{8,24},{10,26},{12,28},{14,30},{16,0},... | collective-permute-start | bytes 1081352 | tf_op jit(solution)/shard_map/ppermute | solution.py:975
  442.2 22.3 %collective-permute-start.67 = (bf16[128,1408]{1,0:T(8,128)(2,1)S(1)}, bf16[128,1408]{1,0:T(8,128)(2,1)S(1)}, u32[]{:S(2)}, u32[]{:S(2)}) collective-permute-start(bf16[128,1408]{1,0:T(8,128)(2,1)S(1)} %get-tuple-element.285.refs_0_), channel_id=1, source_target_pairs={{0,8},{2,10},{4,12},{6,14},{8,0},{10,2},{12,4},{14,6},{16,24},{18,... | collective-permute-start | bytes 1081352 | tf_op jit(solution)/shard_map/ppermute | solution.py:975
  442.5 21.9 %collective-permute-start.52 = (bf16[128,1408]{1,0:T(8,128)(2,1)S(1)}, bf16[128,1408]{1,0:T(8,128)(2,1)S(1)}, u32[]{:S(2)}, u32[]{:S(2)}) collective-permute-start(bf16[128,1408]{1,0:T(8,128)(2,1)S(1)} %collective-permute-done.48.refs_3_), channel_id=1, source_target_pairs={{0,2},{2,0},{4,6},{6,4},{8,10},{10,8},{12,14},{14,12},{16,18},{18,... | collective-permute-start | bytes 1081352 | tf_op jit(solution)/shard_map/ppermute | solution.py:975
  454.4 18.8 %collective-permute-start.70 = (bf16[128,1408]{1,0:T(8,128)(2,1)S(1)}, bf16[128,1408]{1,0:T(8,128)(2,1)S(1)}, u32[]{:S(2)}, u32[]{:S(2)}) collective-permute-start(bf16[128,1408]{1,0:T(8,128)(2,1)S(1)} %get-tuple-element.285.refs_0_), channel_id=1, source_target_pairs={{0,2},{2,0},{4,6},{6,4},{8,10},{10,8},{12,14},{14,12},{16,18},{18,... | collective-permute-start | bytes 1081352 | tf_op jit(solution)/shard_map/ppermute | solution.py:975
  454.4 19.4 %collective-permute-start.72 = (bf16[128,1408]{1,0:T(8,128)(2,1)S(1)}, bf16[128,1408]{1,0:T(8,128)(2,1)}, u32[]{:S(2)}, u32[]{:S(2)}) collective-permute-start(bf16[128,1408]{1,0:T(8,128)(2,1)S(1)} %collective-permute-done.68.refs_2_), channel_id=1, source_target_pairs={{0,2},{2,0},{4,6},{6,4},{8,10},{10,8},{12,14},{14,12},{16,18},{18,... | collective-permute-start | bytes 1081352 | tf_op jit(solution)/shard_map/ppermute | solution.py:975
  456.8 16.8 %collective-permute-start.44 = (bf16[128,1280]{1,0:T(8,128)(2,1)S(1)}, bf16[128,1280]{1,0:T(8,128)(2,1)S(1)}, u32[]{:S(2)}, u32[]{:S(2)}) collective-permute-start(bf16[128,1280]{1,0:T(8,128)(2,1)S(1)} %get-tuple-element.277), channel_id=1, source_target_pairs={{0,16},{2,18},{4,20},{6,22},{8,24},{10,26},{12,28},{14,30},{16,0},... | collective-permute-start | bytes 983048 | tf_op jit(solution)/shard_map/ppermute | solution.py:975
  464.4 11.7 %collective-permute-start.71 = (bf16[128,1408]{1,0:T(8,128)(2,1)S(1)}, bf16[128,1408]{1,0:T(8,128)(2,1)}, u32[]{:S(2)}, u32[]{:S(2)}) collective-permute-start(bf16[128,1408]{1,0:T(8,128)(2,1)S(1)} %collective-permute-done.67.refs_1_), channel_id=1, source_target_pairs={{0,2},{2,0},{4,6},{6,4},{8,10},{10,8},{12,14},{14,12},{16,18},{18,... | collective-permute-start | bytes 1081352 | tf_op jit(solution)/shard_map/ppermute | solution.py:975
  473.2 11.3 %collective-permute-start.60 = (bf16[128,1408]{1,0:T(8,128)(2,1)S(1)}, bf16[128,1408]{1,0:T(8,128)(2,1)S(1)}, u32[]{:S(2)}, u32[]{:S(2)}) collective-permute-start(bf16[128,1408]{1,0:T(8,128)(2,1)S(1)} %get-tuple-element.284.refs_0_), channel_id=1, source_target_pairs={{0,8},{2,10},{4,12},{6,14},{8,0},{10,2},{12,4},{14,6},{16,24},{18,... | collective-permute-start | bytes 1081352 | tf_op jit(solution)/shard_map/ppermute | solution.py:975
  473.5 13.0 %collective-permute-start.63 = (bf16[128,1408]{1,0:T(8,128)(2,1)S(1)}, bf16[128,1408]{1,0:T(8,128)(2,1)S(1)}, u32[]{:S(2)}, u32[]{:S(2)}) collective-permute-start(bf16[128,1408]{1,0:T(8,128)(2,1)S(1)} %get-tuple-element.284.refs_0_), channel_id=1, source_target_pairs={{0,2},{2,0},{4,6},{6,4},{8,10},{10,8},{12,14},{14,12},{16,18},{18,... | collective-permute-start | bytes 1081352 | tf_op jit(solution)/shard_map/ppermute | solution.py:975
  473.7 12.8 %collective-permute-start.61 = (bf16[128,1408]{1,0:T(8,128)(2,1)S(1)}, bf16[128,1408]{1,0:T(8,128)(2,1)S(1)}, u32[]{:S(2)}, u32[]{:S(2)}) collective-permute-start(bf16[128,1408]{1,0:T(8,128)(2,1)S(1)} %get-tuple-element.284.refs_0_), channel_id=1, source_target_pairs={{0,4},{2,6},{4,0},{6,2},{8,12},{10,14},{12,8},{14,10},{16,20},{18,... | collective-permute-start | bytes 1081352 | tf_op jit(solution)/shard_map/ppermute | solution.py:975
  476.2 15.8 %collective-permute-start.54 = (bf16[128,1280]{1,0:T(8,128)(2,1)S(1)}, bf16[128,1280]{1,0:T(8,128)(2,1)S(1)}, u32[]{:S(2)}, u32[]{:S(2)}) collective-permute-start(bf16[128,1280]{1,0:T(8,128)(2,1)S(1)} %get-tuple-element.283.refs_0_), channel_id=1, source_target_pairs={{0,4},{2,6},{4,0},{6,2},{8,12},{10,14},{12,8},{14,10},{16,20},{18,... | collective-permute-start | bytes 983048 | tf_op jit(solution)/shard_map/ppermute | solution.py:975
  476.4 15.5 %collective-permute-start.53 = (bf16[128,1280]{1,0:T(8,128)(2,1)S(1)}, bf16[128,1280]{1,0:T(8,128)(2,1)S(1)}, u32[]{:S(2)}, u32[]{:S(2)}) collective-permute-start(bf16[128,1280]{1,0:T(8,128)(2,1)S(1)} %get-tuple-element.283.refs_0_), channel_id=1, source_target_pairs={{0,8},{2,10},{4,12},{6,14},{8,0},{10,2},{12,4},{14,6},{16,24},{18,... | collective-permute-start | bytes 983048 | tf_op jit(solution)/shard_map/ppermute | solution.py:975
  484.4 15.4 %collective-permute-start.62 = (bf16[128,1408]{1,0:T(8,128)(2,1)S(1)}, bf16[128,1408]{1,0:T(8,128)(2,1)}, u32[]{:S(2)}, u32[]{:S(2)}) collective-permute-start(bf16[128,1408]{1,0:T(8,128)(2,1)S(1)} %collective-permute-done.60.refs_1_), channel_id=1, source_target_pairs={{0,4},{2,6},{4,0},{6,2},{8,12},{10,14},{12,8},{14,10},{16,20},{18,... | collective-permute-start | bytes 1081352 | tf_op jit(solution)/shard_map/ppermute | solution.py:975
  486.5 13.3 %collective-permute-start.73 = (bf16[128,1408]{1,0:T(8,128)(2,1)}, bf16[128,1408]{1,0:T(8,128)(2,1)}, u32[]{:S(2)}, u32[]{:S(2)}) collective-permute-start(bf16[128,1408]{1,0:T(8,128)(2,1)} %collective-permute-done.69.refs_3_), channel_id=1, source_target_pairs={{0,2},{2,0},{4,6},{6,4},{8,10},{10,8},{12,14},{14,12},{16,18},{18,... | collective-permute-start | bytes 1081352 | tf_op jit(solution)/shard_map/ppermute | solution.py:975
  486.5 13.8 %collective-permute-start.65 = (bf16[128,1408]{1,0:T(8,128)(2,1)S(1)}, bf16[128,1408]{1,0:T(8,128)(2,1)S(1)}, u32[]{:S(2)}, u32[]{:S(2)}) collective-permute-start(bf16[128,1408]{1,0:T(8,128)(2,1)S(1)} %collective-permute-done.61.refs_2_), channel_id=1, source_target_pairs={{0,2},{2,0},{4,6},{6,4},{8,10},{10,8},{12,14},{14,12},{16,18},{18,... | collective-permute-start | bytes 1081352 | tf_op jit(solution)/shard_map/ppermute | solution.py:975
  492.0 14.2 %collective-permute-start.55 = (bf16[128,1280]{1,0:T(8,128)(2,1)S(1)}, bf16[128,1280]{1,0:T(8,128)(2,1)S(1)}, u32[]{:S(2)}, u32[]{:S(2)}) collective-permute-start(bf16[128,1280]{1,0:T(8,128)(2,1)S(1)} %collective-permute-done.53.refs_1_), channel_id=1, source_target_pairs={{0,4},{2,6},{4,0},{6,2},{8,12},{10,14},{12,8},{14,10},{16,20},{18,... | collective-permute-start | bytes 983048 | tf_op jit(solution)/shard_map/ppermute | solution.py:975
  499.8 13.1 %collective-permute-start.66 = (bf16[128,1408]{1,0:T(8,128)(2,1)}, bf16[128,1408]{1,0:T(8,128)(2,1)}, u32[]{:S(2)}, u32[]{:S(2)}) collective-permute-start(bf16[128,1408]{1,0:T(8,128)(2,1)} %collective-permute-done.62.refs_3_), channel_id=1, source_target_pairs={{0,2},{2,0},{4,6},{6,4},{8,10},{10,8},{12,14},{14,12},{16,18},{18,... | collective-permute-start | bytes 1081352 | tf_op jit(solution)/shard_map/ppermute | solution.py:975
  499.8 19.9 %collective-permute-start.56 = (bf16[128,1280]{1,0:T(8,128)(2,1)S(1)}, bf16[128,1280]{1,0:T(8,128)(2,1)S(1)}, u32[]{:S(2)}, u32[]{:S(2)}) collective-permute-start(bf16[128,1280]{1,0:T(8,128)(2,1)S(1)} %get-tuple-element.283.refs_0_), channel_id=1, source_target_pairs={{0,2},{2,0},{4,6},{6,4},{8,10},{10,8},{12,14},{14,12},{16,18},{18,... | collective-permute-start | bytes 983048 | tf_op jit(solution)/shard_map/ppermute | solution.py:975
  500.3 19.4 %collective-permute-start.57 = (bf16[128,1280]{1,0:T(8,128)(2,1)S(1)}, bf16[128,1280]{1,0:T(8,128)(2,1)S(1)}, u32[]{:S(2)}, u32[]{:S(2)}) collective-permute-start(bf16[128,1280]{1,0:T(8,128)(2,1)S(1)} %collective-permute-done.53.refs_1_), channel_id=1, source_target_pairs={{0,2},{2,0},{4,6},{6,4},{8,10},{10,8},{12,14},{14,12},{16,18},{18,... | collective-permute-start | bytes 983048 | tf_op jit(solution)/shard_map/ppermute | solution.py:975
  500.4 19.3 %collective-permute-start.58 = (bf16[128,1280]{1,0:T(8,128)(2,1)S(1)}, bf16[128,1280]{1,0:T(8,128)(2,1)S(1)}, u32[]{:S(2)}, u32[]{:S(2)}) collective-permute-start(bf16[128,1280]{1,0:T(8,128)(2,1)S(1)} %collective-permute-done.54.refs_2_), channel_id=1, source_target_pairs={{0,2},{2,0},{4,6},{6,4},{8,10},{10,8},{12,14},{14,12},{16,18},{18,... | collective-permute-start | bytes 983048 | tf_op jit(solution)/shard_map/ppermute | solution.py:975
  506.2 13.6 %collective-permute-start.59 = (bf16[128,1280]{1,0:T(8,128)(2,1)S(1)}, bf16[128,1280]{1,0:T(8,128)(2,1)S(1)}, u32[]{:S(2)}, u32[]{:S(2)}) collective-permute-start(bf16[128,1280]{1,0:T(8,128)(2,1)S(1)} %collective-permute-done.55.refs_3_), channel_id=1, source_target_pairs={{0,2},{2,0},{4,6},{6,4},{8,10},{10,8},{12,14},{14,12},{16,18},{18,... | collective-permute-start | bytes 983048 | tf_op jit(solution)/shard_map/ppermute | solution.py:975
  (143 other events, 1203.1 us)

commit v4 on v3

--- a/solution.py
+++ b/solution.py
@@ -651,29 +651,35 @@
 def gather_kernel(turn, n, order, *refs):
     out, token = refs[-2:]
     mark(token)
-    for k in range(n):
-
-        @pl.when(pl.program_id(0) == k)
+    rows = refs[0].shape[0]
+    for k in range(0, n, 2):
+
+        @pl.when(pl.program_id(0) == k // 2)
         def _():
-            piece = refs[k][...]
-            out[...] = (piece.T if turn else piece).astype(f32)
-
-
-def gathered(pieces, order, turn, deps=(), start=0, cols=None):
+            for j in (k, k + 1):
+                at = pl.ds(pl.multiple_of(order[j] % 2 * rows, rows), rows)
+                if turn:
+                    out[:, at] = refs[j][...].T.astype(f32)
+                else:
+                    out[at, :] = refs[j][...].astype(f32)
+
+
+def gathered(pieces, order, turn, deps=()):
     n = len(pieces)
-    rows = pieces[0].shape[0]
-    cols = cols or pieces[0].shape[1]
-    base = start // cols
+    rows, cols = pieces[0].shape
     total = n * rows
+    two = 2 * rows
     return pl.pallas_call(
         functools.partial(gather_kernel, turn, n),
         grid_spec=pltpu.PrefetchScalarGridSpec(
             num_scalar_prefetch=1,
-            grid=(n,),
-            in_specs=[pl.BlockSpec((rows, cols), lambda i, o: (0, base), pipeline_mode=pl.Buffered(1))] * n
+            grid=(n // 2,),
+            in_specs=[pl.BlockSpec((rows, cols), lambda i, o: (0, 0), pipeline_mode=pl.Buffered(1))] * n
             + [ANY] * len(deps),
             out_specs=[
-                pl.BlockSpec((cols, rows), lambda i, o: (0, o[i])) if turn else pl.BlockSpec((rows, cols), lambda i, o: (o[i], 0)),
+                pl.BlockSpec((cols, two), lambda i, o: (0, o[2 * i] // 2))
+                if turn
+                else pl.BlockSpec((two, cols), lambda i, o: (o[2 * i] // 2, 0)),
                 token_spec(),
             ],
         ),
@@ -1073,12 +1079,12 @@
     sent, w_kv_o = kv_call(place, first_in, kv_got, swap(kv_got, "dp", 1), tied_a, shared)
     got = lax.ppermute(sent, "tensor", [(i, i + 1) for i in range(shards - 1)])
     q_b, w_query_o, q_done = query_call(place, first_in, q_got, swap(q_got, "dp", 1), cosT, sinT, hd, groups, per)
-    gate_piece, taken = take(w_gate, core, 0, 2, (got, q_done))
-    gate_got = swap(gate_piece, "tensor", 1)
+    gate_piece, taken = take(w_gate, core, 0, 2, (q_done,))
+    gate_got = swap(hold(gate_piece, got), "tensor", 1)
     up_piece, taken = take(w_up, core, 0, 2, (taken,))
-    up_got = swap(up_piece, "tensor", 1)
+    up_got = swap(hold(up_piece, got), "tensor", 1)
     down_piece, taken = take(w_down, core, 1, 2, (taken,))
-    down_got = swap(down_piece, "tensor", 1)
+    down_got = swap(hold(down_piece, got), "tensor", 1)
 
     def both(p):
         return p, swap(p, "dp", 1)
@@ -1127,8 +1133,6 @@
 
     wo_keep_b, wo_send_b = run.after(wgrad(place, attn_back, parts(mixed_b), (run.last,)))
     wo_core_b = swap(wo_send_b, "dp", 1)
-    wo_keep_a, wo_send_a = run.after(wgrad(place, attn_back, parts(mixed_a), (run.last,)))
-    wo_core_a = swap(wo_send_a, "dp", 1)
     up_y = swap(run.fold([[(keep_b, 1), core_b[1]]]), "tensor", 1)
     down_kb, down_sb = run.fold([[(keep_b, 2), core_b[2]]], bits[1])
     down_xb = swap(down_sb, "dp", 2)
@@ -1164,6 +1168,8 @@
     )
     sm_core_b = swap(sm_send_b, "dp", 1)
     sm_core_a = swap(sm_send_a, "dp", 1)
+    wo_keep_a, wo_send_a = run.after(wgrad(place, attn_back, parts(mixed_a), (run.last,)))
+    wo_core_a = swap(wo_send_a, "dp", 1)
     gate_s.line()
     sm_y = swap(run.fold([[sm_keep_b, sm_core_b]]), "tensor", 1)
     up_s.line()

time: 536 us -> 520 us (0.970)
  starting transfers between devices: 82 us -> 69.2 us
    ppermute x71, starting transfers between devices: 76.2 us -> 63.4 us  [swap(): return lax.ppermute(x, axis, [(i, i ^ bit) for i in range(n)])]
    unnamed x268 -> x262, local copies, waits for them, and re-layouts: 43.9 us -> 48.4 us
  transfers between devices with their start and end apart: 74 -> 74, of which waited for: 19 -> 17; matrix products, arithmetic and copies ran while one was open for 12% -> 12% of each run, Pallas kernels for 35% -> 35%
where the time goes in v4:
time: 520 us; the launch traced here: 516 us
  Pallas kernels  217 us (42%)
  waiting for transfers between devices  116 us (22%)
  starting transfers between devices  69.2 us (13%)
  local copies, waits for them, and re-layouts  50.6 us (10%)
  matrix products  43.7 us (8%)
  other arithmetic  15.9 us (3%)
    ppermute x71, waiting for transfers between devices, swap(): return lax.ppermute(x, axis, [(i, i ^ bit) for i in range(n)])  116 us
    ppermute x71, starting transfers between devices, swap(): return lax.ppermute(x, axis, [(i, i ^ bit) for i in range(n)])  63.4 us
    pallas_call x2, Pallas kernels, mlp_call(): pl.pallas_call(functools.partial(mlp_kernel, first, pieces, edge, len(dep...  58.3 us
    unnamed x262, local copies, waits for them, and re-layouts  48.4 us
    pallas_call x2, Pallas kernels, attn_bwd(): pl.pallas_call(functools.partial(bwd_kernel, n, first, partner, heads, bk...  46.3 us
    dot_general x10, matrix products, mm(): lax.dot_general(a, b, (((ca,), (cb,)), ((), ())), preferred_element_type=...  43.7 us
    pallas_call x23, Pallas kernels, fold(): pl.pallas_call(functools.partial(fold_kernel, [len(g) for g in groups], s...  28.5 us
    pallas_call x1, Pallas kernels, attn_fwd(): pl.pallas_call(functools.partial(fwd_kernel, n, heads, bk, len(deps)), gr...  25.6 us
  transfers between devices with their start and end apart: 74, of which 17 were waited for; matrix products, arithmetic and copies ran while one was open for 12% of the time, Pallas kernels for 35%

profile of v4, /device:TPU:0, one launch (start us, length us, event | category | flops | bytes accessed | tf_op | source)
XLA Modules:
  0.0 515.5 jit_solution(16572179819404602192)
XLA Ops:
  1.6 3.0 collective-permute-start.2
  8.8 2.0 collective-permute-start
  19.1 4.4 first_projections.1
  26.0 2.2 other_keys.1
  28.9 3.2 collective-permute-start.4
  39.1 4.3 other_queries.1
  56.3 25.6 %attn_fwd.1 = (bf16[2,256,1024]{2,1,0:T(8,128)(2,1)}, bf16[2,256,1024]{2,1,0:T(8,128)(2,1)}, f32[2,4,1024]{2,1,0:T(4,128)}, f32[2,4,1024]{2,1,0:T(4,128)}) custom-call(s32[4,4]{1,0:T(4,128)} %add_select_fusion.4.bounds, s32[1,1024]{1,0:T(1,128)} %compare_select_fusion.start_ref, bf16[2,256,1024]{2,1,0:T(8,128)(2,1)} %copy-done.90, ...), custom_call_target="tpu_custom_call" | custom-call | flops 51539607552 | bytes 4194304 | tf_op jit(solution)/shard_map/attn_fwd/pallas_call | solution.py:130
  82.0 2.7 fusion.21
  84.7 1.8 multiply_reduce_fusion.2
  86.5 2.0 copy-done.92
  90.2 29.1 %mlp_grads.2 = (bf16[1024,1408]{1,0:T(8,128)(2,1)}, bf16[1024,1408]{1,0:T(8,128)(2,1)}, bf16[1024,1408]{1,0:T(8,128)(2,1)}, bf16[3,512,1408]{2,1,0:T(8,128)(2,1)...) custom-call(s32[3]{0:T(128)} %copy-done.69, ...), custom_call_target="tpu_custom_call" | custom-call | flops 32480690176 | bytes 34340864 | tf_op jit(solution)/shard_map/mlp_grads/pallas_call | solution.py:545
  119.3 25.2 %collective-permute-done.7.a = bf16[512,1408]{1,0:T(8,128)(2,1)S(1)} collective-permute-done((bf16[512,1408]{1,0:T(8,128)(2,1)}, bf16[512,1408]{1,0:T(8,128)(2,1)S(1)}, u32[]{:S(2)}, u32[]{:S(2)}) %collective-permute-start.7) | collective-permute-done | bytes 1441824 | tf_op jit(solution)/shard_map/ppermute | solution.py:981
  147.4 5.4 %fusion.22 = f32[1024,1024]{1,0:T(8,128)S(1)} fusion(bf16[1024,1408]{1,0:T(8,128)(2,1)} %get-tuple-element.171, bf16[1024,1408]{1,0:T(8,128)(2,1)S(1)} %copy-done.10), kind=kOutput, calls=%fused_computation.102 | convolution fusion | flops 2952790016 | bytes 9961472 | tf_op jit(solution)/shard_map/dot_general | solution.py:976
  152.8 5.0 convolution_add_fusion.refs_10_
  159.0 29.2 %mlp_grads.3 = (bf16[1024,1408]{1,0:T(8,128)(2,1)}, bf16[1024,1408]{1,0:T(8,128)(2,1)}, bf16[1024,1408]{1,0:T(8,128)(2,1)}, bf16[3,512,1408]{2,1,0:T(8,128)(2,1)...) custom-call(s32[3]{0:T(128)} %copy-done.69, ...), custom_call_target="tpu_custom_call" | custom-call | flops 32480690176 | bytes 34340864 | tf_op jit(solution)/shard_map/mlp_grads/pallas_call | solution.py:545
  192.6 2.2 copy-done
  195.5 3.6 fold.23
  199.7 8.3 %fusion.23 = f32[1024,1024]{1,0:T(8,128)} fusion(bf16[1024,1408]{1,0:T(8,128)(2,1)} %hold.16, bf16[1024,1408]{1,0:T(8,128)(2,1)} %get-tuple-element.184), kind=kOutput, calls=%fused_computation.103 | convolution fusion | flops 2952790016 | bytes 9961472 | tf_op jit(solution)/shard_map/dot_general | solution.py:976
  208.0 6.4 %multiply_reduce_fusion = (f32[1024]{0:T(1024)S(1)}, f32[1024]{0:T(1024)S(1)}, f32[1024,1024]{1,0:T(8,128)S(1)}) fusion(f32[1024,1024]{1,0:T(8,128)S(1)} %copy-done.93, f32[1024]{0:T(1024)S(1)} %add_rsqrt_fusion, f32[1024]{0:T(1024)S(1)} %copy-done.117, f32[1024,1024]{1,0:T(8,128)S(1)} %copy-done.120, f32[1024,1024]{1,0:T(8,128)} %fusion.23, ...), kind=kOutput, calls=%fused_computation.1 | convolution fusion | flops 2961176576 | bytes 22560768 | tf_op jit(solution)/shard_map/dot_general | solution.py:976
  214.6 2.9 fusion.19
  217.5 2.7 weight_grads.4
  220.6 3.7 fold.24
  226.0 2.3 fusion.1
  228.2 2.3 fusion
  232.1 2.2 fold.26
  235.8 23.1 %attn_bwd.2 = (bf16[2,256,1024]{2,1,0:T(8,128)(2,1)}, f32[2,64,2048]{2,1,0:T(8,128)}, f32[32,2048]{1,0:T(8,128)}, f32[8,128]{1,0:T(8,128)}) custom-call(s32[2,4]{1,0:T(2,128)} %add_select_fusion.5.bounds, s32[1,1024]{1,0:T(1,128)} %compare_select_fusion.start_ref, bf16[2,256,1024]{2,1,0:T(8,128)(2,1)} %copy-done.89, ...), custom_call_target="tpu_custom_call" | custom-call | flops 48318382080 | bytes 4194304 | tf_op jit(solution)/shard_map/attn_bwd/pallas_call | solution.py:247
  264.3 2.4 weight_grads.5
  267.6 2.3 fold.27
  271.3 13.6 %collective-permute-done.21 = bf16[512,1408]{1,0:T(8,128)(2,1)} collective-permute-done((bf16[512,1408]{1,0:T(8,128)(2,1)}, bf16[512,1408]{1,0:T(8,128)(2,1)}, u32[]{:S(2)}, u32[]{:S(2)}) %collective-permute-start.21) | collective-permute-done | bytes 1441824 | tf_op jit(solution)/shard_map/ppermute | solution.py:981
  286.2 2.8 fold.28
  291.5 2.7 collective-permute-start.27
  294.1 1.8 fold.30
  297.9 23.2 %attn_bwd.3 = (bf16[2,256,1024]{2,1,0:T(8,128)(2,1)}, f32[2,64,2048]{2,1,0:T(8,128)}, f32[32,2048]{1,0:T(8,128)}, f32[8,128]{1,0:T(8,128)}) custom-call(s32[2,4]{1,0:T(2,128)} %add_select_fusion.5.bounds, s32[1,1024]{1,0:T(1,128)} %compare_select_fusion.start_ref, bf16[2,256,1024]{2,1,0:T(8,128)(2,1)} %copy-done.90, ...), custom_call_target="tpu_custom_call" | custom-call | flops 48318382080 | bytes 4194304 | tf_op jit(solution)/shard_map/attn_bwd/pallas_call | solution.py:247
  326.0 2.0 fold.32
  328.0 7.4 %collective-permute-start.33 = (bf16[512,512]{1,0:T(8,128)(2,1)}, bf16[512,512]{1,0:T(8,128)(2,1)S(1)}, u32[]{:S(2)}, u32[]{:S(2)}) collective-permute-start(bf16[512,512]{1,0:T(8,128)(2,1)} %get-tuple-element.247), channel_id=1, source_target_pairs={{0,1},{1,0},{2,3},{3,2},{4,5},{5,4},{6,7},{7,6},{8,9},{9,8},{10,11... | collective-permute-start | bytes 1572872 | tf_op jit(solution)/shard_map/ppermute | solution.py:981
  336.8 4.1 collective-permute-start.36
  342.8 2.4 weight_grads.6
  349.9 7.6 %token_grads.1 = (bf16[1024,1024]{1,0:T(8,128)(2,1)}, f32[1,1024]{1,0:T(1,128)S(1)}) custom-call(bf16[1024,1024]{1,0:T(8,128)(2,1)S(1)} %copy-done.28, f32[1024,1024]{1,0:T(8,128)S(1)} %copy-done.5, f32[1,1024]{1,0:T(1,128)S(1)} %bitcast.163, bf16[288,1024]{1,0:T(8,128)(2,1)S(1)} %get-tuple-element.236.kv_ref, bf16[1024,512]{1,0:T(8,128)(2,1)S(1)} %copy-done.37, ...), custom_call_target="tpu_custom_call" | custom-call | flops 5368709120 | bytes 16777216 | tf_op jit(solution)/shard_map/token_grads/pallas_call | solution.py:905
  357.5 2.4 small_grads.1
  360.0 3.6 collective-permute-start.35
  363.6 2.4 weight_grads.7
  370.2 5.5 %collective-permute-start.43 = (bf16[128,1408]{1,0:T(8,128)(2,1)}, bf16[128,1408]{1,0:T(8,128)(2,1)}, u32[]{:S(2)}, u32[]{:S(2)}) collective-permute-start(bf16[128,1408]{1,0:T(8,128)(2,1)} %get-tuple-element.273), channel_id=1, source_target_pairs={{0,16},{2,18},{4,20},{6,22},{8,24},{10,26},{12,28},{14,30},{16,0},... | collective-permute-start | bytes 1081352 | tf_op jit(solution)/shard_map/ppermute | solution.py:981
  380.1 6.0 %fusion.24 = f32[1024,1024]{1,0:T(8,128)S(1)} fusion(bf16[1024,1408]{1,0:T(8,128)(2,1)} %hold.18, bf16[1408,1024]{1,0:T(8,128)(2,1)S(1)} %copy-done.14), kind=kOutput, calls=%fused_computation.104 | convolution fusion | flops 2952790016 | bytes 9961472 | tf_op jit(solution)/shard_map/dot_general | solution.py:976
  386.1 3.6 add_convert_fusion.refs_3_
  389.8 17.8 %collective-permute-done.40 = bf16[128,1408]{1,0:T(8,128)(2,1)} collective-permute-done((bf16[128,1408]{1,0:T(8,128)(2,1)}, bf16[128,1408]{1,0:T(8,128)(2,1)}, u32[]{:S(2)}, u32[]{:S(2)}) %collective-permute-start.40) | collective-permute-done | bytes 360480 | tf_op jit(solution)/shard_map/ppermute | solution.py:981
  411.0 7.6 %collective-permute-done.47.refs_2_ = bf16[128,1408]{1,0:T(8,128)(2,1)S(1)} collective-permute-done((bf16[128,1408]{1,0:T(8,128)(2,1)S(1)}, bf16[128,1408]{1,0:T(8,128)(2,1)S(1)}, u32[]{:S(2)}, u32[]{:S(2)}) %collective-permute-start.47) | collective-permute-done | bytes 360480 | tf_op jit(solution)/shard_map/ppermute | solution.py:981
  420.4 2.0 collective-permute-start.48
  423.7 2.7 collective-permute-done.42
  429.0 3.4 collective-permute-start.45
  432.8 10.2 %collective-permute-done.41 = bf16[128,1280]{1,0:T(8,128)(2,1)S(1)} collective-permute-done((bf16[128,1280]{1,0:T(8,128)(2,1)S(1)}, bf16[128,1280]{1,0:T(8,128)(2,1)S(1)}, u32[]{:S(2)}, u32[]{:S(2)}) %collective-permute-start.41) | collective-permute-done | bytes 327712 | tf_op jit(solution)/shard_map/ppermute | solution.py:981
  444.1 2.6 collective-permute-done.45
  446.8 8.1 %collective-permute-done.67.refs_1_ = bf16[128,1408]{1,0:T(8,128)(2,1)S(1)} collective-permute-done((bf16[128,1408]{1,0:T(8,128)(2,1)S(1)}, bf16[128,1408]{1,0:T(8,128)(2,1)S(1)}, u32[]{:S(2)}, u32[]{:S(2)}) %collective-permute-start.67) | collective-permute-done | bytes 360480 | tf_op jit(solution)/shard_map/ppermute | solution.py:981
  456.3 5.6 %gathered.5 = (f32[1024,1408]{1,0:T(8,128)}, f32[8,128]{1,0:T(8,128)}) custom-call(s32[8]{0:T(128)} %stack.41.order, bf16[128,1408]{1,0:T(8,128)(2,1)} %copy-done.44, bf16[128,1408]{1,0:T(8,128)(2,1)} %copy-done.105, bf16[128,1408]{1,0:T(8,128)(2,1)} %copy-done.104, bf16[128,1408]{1,0:T(8,128)(2,1)} %copy-done.109, bf16[128,1408]{1,0:T(8,128)(2,1)} %copy-done.106, ...), custom_call_target="tpu_custom_call" | custom-call | bytes 8650752 | tf_op jit(solution)/shard_map/gathered/pallas_call | solution.py:672
  463.3 2.0 collective-permute-start.61
  467.7 6.3 %collective-permute-done.60.refs_1_ = bf16[128,1408]{1,0:T(8,128)(2,1)S(1)} collective-permute-done((bf16[128,1408]{1,0:T(8,128)(2,1)S(1)}, bf16[128,1408]{1,0:T(8,128)(2,1)S(1)}, u32[]{:S(2)}, u32[]{:S(2)}) %collective-permute-start.60) | collective-permute-done | bytes 360480 | tf_op jit(solution)/shard_map/ppermute | solution.py:981
  474.0 2.1 collective-permute-start.62
  476.6 5.0 collective-permute-done.54.refs_2_
  481.6 1.9 collective-permute-start.55
  483.5 5.9 %collective-permute-done.62.refs_3_ = bf16[128,1408]{1,0:T(8,128)(2,1)} collective-permute-done((bf16[128,1408]{1,0:T(8,128)(2,1)S(1)}, bf16[128,1408]{1,0:T(8,128)(2,1)}, u32[]{:S(2)}, u32[]{:S(2)}) %collective-permute-start.62) | collective-permute-done | bytes 360480 | tf_op jit(solution)/shard_map/ppermute | solution.py:981
  490.6 5.6 %collective-permute-done.55.refs_3_ = bf16[128,1280]{1,0:T(8,128)(2,1)S(1)} collective-permute-done((bf16[128,1280]{1,0:T(8,128)(2,1)S(1)}, bf16[128,1280]{1,0:T(8,128)(2,1)S(1)}, u32[]{:S(2)}, u32[]{:S(2)}) %collective-permute-start.55) | collective-permute-done | bytes 327712 | tf_op jit(solution)/shard_map/ppermute | solution.py:981
  496.2 5.4 %gathered.6 = (f32[1024,1408]{1,0:T(8,128)}, f32[8,128]{1,0:T(8,128)}) custom-call(s32[8]{0:T(128)} %stack.41.order, bf16[128,1408]{1,0:T(8,128)(2,1)} %copy-done.43, bf16[128,1408]{1,0:T(8,128)(2,1)} %copy-done.102, bf16[128,1408]{1,0:T(8,128)(2,1)} %copy-done.101, bf16[128,1408]{1,0:T(8,128)(2,1)} %collective-permute-done.69.refs_3_, ...), custom_call_target="tpu_custom_call" | custom-call | bytes 8650752 | tf_op jit(solution)/shard_map/gathered/pallas_call | solution.py:672
  501.7 5.6 %gathered.7 = (f32[1408,1024]{1,0:T(8,128)}, f32[8,128]{1,0:T(8,128)}) custom-call(s32[8]{0:T(128)} %stack.41.order, bf16[128,1408]{1,0:T(8,128)(2,1)} %copy-done.45, bf16[128,1408]{1,0:T(8,128)(2,1)} %copy-done.110, bf16[128,1408]{1,0:T(8,128)(2,1)} %copy-done.112, bf16[128,1408]{1,0:T(8,128)(2,1)} %collective-permute-done.62.refs_3_, ...), custom_call_target="tpu_custom_call" | custom-call | bytes 8650752 | tf_op jit(solution)/shard_map/gathered/pallas_call | solution.py:672
  510.9 2.2 gathered.9
  513.2 2.1 gathered.8
  (458 shorter events, 107.7 us)
Async XLA Ops:
  1.6 23.0 %collective-permute-start.2 = (bf16[512,128]{1,0:T(8,128)(2,1)S(1)}, bf16[512,128]{1,0:T(8,128)(2,1)S(1)}, u32[]{:S(2)}, u32[]{:S(2)}) collective-permute-start(bf16[512,128]{1,0:T(8,128)(2,1)S(1)} %get-tuple-element.158), channel_id=1, source_target_pairs={{0,1},{1,0},{2,3},{3,2},{4,5},{5,4},{6,7},{7,6},{8,9},{9,8},{10,11... | collective-permute-start | bytes 393224 | tf_op jit(solution)/shard_map/ppermute | solution.py:981
  8.8 25.6 %collective-permute-start.5 = (bf16[256,1024]{1,0:T(8,128)(2,1)}, bf16[256,1024]{1,0:T(8,128)(2,1)}, u32[]{:S(2)}, u32[]{:S(2)}) collective-permute-start(bf16[256,1024]{1,0:T(8,128)(2,1)} %get-tuple-element.167), channel_id=1, source_target_pairs={{0,1},{1,0},{2,3},{3,2},{4,5},{5,4},{6,7},{7,6},{8,9},{9,8},{10,11... | collective-permute-start | bytes 1572872 | tf_op jit(solution)/shard_map/ppermute | solution.py:981
  8.8 24.9 %collective-permute-start = (bf16[512,512]{1,0:T(8,128)(2,1)}, bf16[512,512]{1,0:T(8,128)(2,1)}, u32[]{:S(2)}, u32[]{:S(2)}) collective-permute-start(bf16[512,512]{1,0:T(8,128)(2,1)} %get-tuple-element.156), channel_id=1, source_target_pairs={{0,1},{1,0},{2,3},{3,2},{4,5},{5,4},{6,7},{7,6},{8,9},{9,8},{10,11... | collective-permute-start | bytes 1572872 | tf_op jit(solution)/shard_map/ppermute | solution.py:981
  28.9 20.0 %collective-permute-start.4 = (bf16[288,1024]{1,0:T(8,128)(2,1)}, bf16[288,1024]{1,0:T(8,128)(2,1)}, u32[]{:S(2)}, u32[]{:S(2)}) collective-permute-start(bf16[288,1024]{1,0:T(8,128)(2,1)} %get-tuple-element.161.sent_ref), channel_id=1, source_target_pairs={{0,1},{2,3},{4,5},{6,7},{8,9},{10,11},{12,13},{14,15},{16,17},{18,... | collective-permute-start | bytes 1769480 | tf_op jit(solution)/shard_map/ppermute | solution.py:1080
  34.4 19.5 %collective-permute-start.6 = (bf16[256,1024]{1,0:T(8,128)(2,1)}, bf16[256,1024]{1,0:T(8,128)(2,1)}, u32[]{:S(2)}, u32[]{:S(2)}) collective-permute-start(bf16[256,1024]{1,0:T(8,128)(2,1)} %collective-permute-done.5), channel_id=1, source_target_pairs={{0,2},{2,0},{4,6},{6,4},{8,10},{10,8},{12,14},{14,12},{16,18},{18,... | collective-permute-start | bytes 1572872 | tf_op jit(solution)/shard_map/ppermute | solution.py:981
  49.0 96.6 %collective-permute-start.9 = (bf16[512,1408]{1,0:T(8,128)(2,1)}, bf16[512,1408]{1,0:T(8,128)(2,1)}, u32[]{:S(2)}, u32[]{:S(2)}) collective-permute-start(bf16[512,1408]{1,0:T(8,128)(2,1)} %hold.12), channel_id=1, source_target_pairs={{0,1},{1,0},{2,3},{3,2},{4,5},{5,4},{6,7},{7,6},{8,9},{9,8},{10,11... | collective-permute-start | bytes 4325384 | tf_op jit(solution)/shard_map/ppermute | solution.py:981
  51.9 94.2 %collective-permute-start.11 = (bf16[1408,512]{1,0:T(8,128)(2,1)}, bf16[1408,512]{1,0:T(8,128)(2,1)}, u32[]{:S(2)}, u32[]{:S(2)}) collective-permute-start(bf16[1408,512]{1,0:T(8,128)(2,1)} %hold.14), channel_id=1, source_target_pairs={{0,1},{1,0},{2,3},{3,2},{4,5},{5,4},{6,7},{7,6},{8,9},{9,8},{10,11... | collective-permute-start | bytes 4325384 | tf_op jit(solution)/shard_map/ppermute | solution.py:981
  52.8 91.7 %collective-permute-start.7 = (bf16[512,1408]{1,0:T(8,128)(2,1)}, bf16[512,1408]{1,0:T(8,128)(2,1)S(1)}, u32[]{:S(2)}, u32[]{:S(2)}) collective-permute-start(bf16[512,1408]{1,0:T(8,128)(2,1)} %hold.10), channel_id=1, source_target_pairs={{0,1},{1,0},{2,3},{3,2},{4,5},{5,4},{6,7},{7,6},{8,9},{9,8},{10,11... | collective-permute-start | bytes 4325384 | tf_op jit(solution)/shard_map/ppermute | solution.py:981
  145.6 12.3 %collective-permute-start.8 = (bf16[512,1408]{1,0:T(8,128)(2,1)}, bf16[512,1408]{1,0:T(8,128)(2,1)}, u32[]{:S(2)}, u32[]{:S(2)}) collective-permute-start(bf16[512,1408]{1,0:T(8,128)(2,1)} %hold.11.refs_4_), channel_id=1, source_target_pairs={{0,2},{2,0},{4,6},{6,4},{8,10},{10,8},{12,14},{14,12},{16,18},{18,... | collective-permute-start | bytes 4325384 | tf_op jit(solution)/shard_map/ppermute | solution.py:981
  145.6 12.3 %collective-permute-start.10 = (bf16[512,1408]{1,0:T(8,128)(2,1)}, bf16[512,1408]{1,0:T(8,128)(2,1)}, u32[]{:S(2)}, u32[]{:S(2)}) collective-permute-start(bf16[512,1408]{1,0:T(8,128)(2,1)} %hold.13.refs_6_), channel_id=1, source_target_pairs={{0,2},{2,0},{4,6},{6,4},{8,10},{10,8},{12,14},{14,12},{16,18},{18,... | collective-permute-start | bytes 4325384 | tf_op jit(solution)/shard_map/ppermute | solution.py:981
  146.1 11.8 %collective-permute-start.12 = (bf16[1408,512]{1,0:T(8,128)(2,1)}, bf16[1408,512]{1,0:T(8,128)(2,1)S(1)}, u32[]{:S(2)}, u32[]{:S(2)}) collective-permute-start(bf16[1408,512]{1,0:T(8,128)(2,1)} %hold.15.refs_8_), channel_id=1, source_target_pairs={{0,2},{2,0},{4,6},{6,4},{8,10},{10,8},{12,14},{14,12},{16,18},{18,... | collective-permute-start | bytes 4325384 | tf_op jit(solution)/shard_map/ppermute | solution.py:981
  191.1 39.4 %collective-permute-start.14 = (bf16[512,1408]{1,0:T(8,128)(2,1)}, bf16[512,1408]{1,0:T(8,128)(2,1)}, u32[]{:S(2)}, u32[]{:S(2)}) collective-permute-start(bf16[512,1408]{1,0:T(8,128)(2,1)} %get-tuple-element.190), channel_id=1, source_target_pairs={{0,2},{2,0},{4,6},{6,4},{8,10},{10,8},{12,14},{14,12},{16,18},{18,... | collective-permute-start | bytes 4325384 | tf_op jit(solution)/shard_map/ppermute | solution.py:981
  191.6 79.2 %collective-permute-start.20 = (bf16[512,1408]{1,0:T(8,128)(2,1)}, bf16[512,1408]{1,0:T(8,128)(2,1)S(1)}, u32[]{:S(2)}, u32[]{:S(2)}) collective-permute-start(bf16[512,1408]{1,0:T(8,128)(2,1)} %get-tuple-element.205), channel_id=1, source_target_pairs={{0,2},{2,0},{4,6},{6,4},{8,10},{10,8},{12,14},{14,12},{16,18},{18,... | collective-permute-start | bytes 4325384 | tf_op jit(solution)/shard_map/ppermute | solution.py:981
  191.6 67.3 %collective-permute-start.22 = (bf16[512,1408]{1,0:T(8,128)(2,1)}, bf16[512,1408]{1,0:T(8,128)(2,1)S(1)}, u32[]{:S(2)}, u32[]{:S(2)}) collective-permute-start(bf16[512,1408]{1,0:T(8,128)(2,1)} %get-tuple-element.207), channel_id=1, source_target_pairs={{0,2},{2,0},{4,6},{6,4},{8,10},{10,8},{12,14},{14,12},{16,18},{18,... | collective-permute-start | bytes 4325384 | tf_op jit(solution)/shard_map/ppermute | solution.py:981
  192.1 32.2 %collective-permute-start.15 = (bf16[512,1408]{1,0:T(8,128)(2,1)}, bf16[512,1408]{1,0:T(8,128)(2,1)}, u32[]{:S(2)}, u32[]{:S(2)}) collective-permute-start(bf16[512,1408]{1,0:T(8,128)(2,1)} %get-tuple-element.191), channel_id=1, source_target_pairs={{0,2},{2,0},{4,6},{6,4},{8,10},{10,8},{12,14},{14,12},{16,18},{18,... | collective-permute-start | bytes 4325384 | tf_op jit(solution)/shard_map/ppermute | solution.py:981
  192.1 28.1 %collective-permute-start.16 = (bf16[512,1408]{1,0:T(8,128)(2,1)}, bf16[512,1408]{1,0:T(8,128)(2,1)}, u32[]{:S(2)}, u32[]{:S(2)}) collective-permute-start(bf16[512,1408]{1,0:T(8,128)(2,1)} %get-tuple-element.192), channel_id=1, source_target_pairs={{0,2},{2,0},{4,6},{6,4},{8,10},{10,8},{12,14},{14,12},{16,18},{18,... | collective-permute-start | bytes 4325384 | tf_op jit(solution)/shard_map/ppermute | solution.py:981
  220.2 46.5 %collective-permute-start.23 = (bf16[512,1408]{1,0:T(8,128)(2,1)}, bf16[512,1408]{1,0:T(8,128)(2,1)}, u32[]{:S(2)}, u32[]{:S(2)}) collective-permute-start(bf16[512,1408]{1,0:T(8,128)(2,1)} %get-tuple-element.208), channel_id=1, source_target_pairs={{0,1},{1,0},{2,3},{3,2},{4,5},{5,4},{6,7},{7,6},{8,9},{9,8},{10,11... | collective-permute-start | bytes 4325384 | tf_op jit(solution)/shard_map/ppermute | solution.py:981
  224.3 67.2 %collective-permute-start.18 = (bf16[512,512]{1,0:T(8,128)(2,1)}, bf16[512,512]{1,0:T(8,128)(2,1)}, u32[]{:S(2)}, u32[]{:S(2)}) collective-permute-start(bf16[512,512]{1,0:T(8,128)(2,1)} %get-tuple-element.202), channel_id=1, source_target_pairs={{0,2},{2,0},{4,6},{6,4},{8,10},{10,8},{12,14},{14,12},{16,18},{18,... | collective-permute-start | bytes 1572872 | tf_op jit(solution)/shard_map/ppermute | solution.py:981
  230.5 54.4 %collective-permute-start.21 = (bf16[512,1408]{1,0:T(8,128)(2,1)}, bf16[512,1408]{1,0:T(8,128)(2,1)}, u32[]{:S(2)}, u32[]{:S(2)}) collective-permute-start(bf16[512,1408]{1,0:T(8,128)(2,1)} %get-tuple-element.206), channel_id=1, source_target_pairs={{0,1},{1,0},{2,3},{3,2},{4,5},{5,4},{6,7},{7,6},{8,9},{9,8},{10,11... | collective-permute-start | bytes 4325384 | tf_op jit(solution)/shard_map/ppermute | solution.py:981
  258.9 30.1 %collective-permute-start.19 = (bf16[256,1408]{1,0:T(8,128)(2,1)}, bf16[256,1408]{1,0:T(8,128)(2,1)S(1)}, u32[]{:S(2)}, u32[]{:S(2)}) collective-permute-start(bf16[256,1408]{1,0:T(8,128)(2,1)} %copy-done.71), channel_id=1, source_target_pairs={{0,4},{2,6},{4,0},{6,2},{8,12},{10,14},{12,8},{14,10},{16,20},{18,... | collective-permute-start | bytes 2162696 | tf_op jit(solution)/shard_map/ppermute | solution.py:981
  266.7 29.2 %collective-permute-start.17 = (bf16[512,512]{1,0:T(8,128)(2,1)S(1)}, bf16[512,512]{1,0:T(8,128)(2,1)S(1)}, u32[]{:S(2)}, u32[]{:S(2)}) collective-permute-start(bf16[512,512]{1,0:T(8,128)(2,1)S(1)} %get-tuple-element.200), channel_id=1, source_target_pairs={{0,2},{2,0},{4,6},{6,4},{8,10},{10,8},{12,14},{14,12},{16,18},{18,... | collective-permute-start | bytes 1572872 | tf_op jit(solution)/shard_map/ppermute | solution.py:981
  270.8 65.9 %collective-permute-start.26 = (bf16[256,1408]{1,0:T(8,128)(2,1)}, bf16[256,1408]{1,0:T(8,128)(2,1)S(1)}, u32[]{:S(2)}, u32[]{:S(2)}) collective-permute-start(bf16[256,1408]{1,0:T(8,128)(2,1)} %get-tuple-element.225), channel_id=1, source_target_pairs={{0,4},{2,6},{4,0},{6,2},{8,12},{10,14},{12,8},{14,10},{16,20},{18,... | collective-permute-start | bytes 2162696 | tf_op jit(solution)/shard_map/ppermute | solution.py:981
  284.9 60.3 %collective-permute-start.24 = (bf16[160,1024]{1,0:T(8,128)(2,1)}, bf16[160,1024]{1,0:T(8,128)(2,1)S(1)}, u32[]{:S(2)}, u32[]{:S(2)}) collective-permute-start(bf16[160,1024]{1,0:T(8,128)(2,1)} %get-tuple-element.220), channel_id=1, source_target_pairs={{1,0},{3,2},{5,4},{7,6},{9,8},{11,10},{13,12},{15,14},{17,16},{19,... | collective-permute-start | bytes 983048 | tf_op jit(solution)/shard_map/ppermute | solution.py:1147
  289.0 35.7 %collective-permute-start.29 = (bf16[256,1408]{1,0:T(8,128)(2,1)}, bf16[256,1408]{1,0:T(8,128)(2,1)}, u32[]{:S(2)}, u32[]{:S(2)}) collective-permute-start(bf16[256,1408]{1,0:T(8,128)(2,1)} %get-tuple-element.230), channel_id=1, source_target_pairs={{0,4},{2,6},{4,0},{6,2},{8,12},{10,14},{12,8},{14,10},{16,20},{18,... | collective-permute-start | bytes 2162696 | tf_op jit(solution)/shard_map/ppermute | solution.py:981
  291.5 45.3 %collective-permute-start.27 = (bf16[256,1408]{1,0:T(8,128)(2,1)}, bf16[256,1408]{1,0:T(8,128)(2,1)S(1)}, u32[]{:S(2)}, u32[]{:S(2)}) collective-permute-start(bf16[256,1408]{1,0:T(8,128)(2,1)} %get-tuple-element.226), channel_id=1, source_target_pairs={{0,1},{1,0},{2,3},{3,2},{4,5},{5,4},{6,7},{7,6},{8,9},{9,8},{10,11... | collective-permute-start | bytes 2162696 | tf_op jit(solution)/shard_map/ppermute | solution.py:981
  295.9 32.1 %collective-permute-start.28 = (bf16[256,1408]{1,0:T(8,128)(2,1)}, bf16[256,1408]{1,0:T(8,128)(2,1)}, u32[]{:S(2)}, u32[]{:S(2)}) collective-permute-start(bf16[256,1408]{1,0:T(8,128)(2,1)} %get-tuple-element.228), channel_id=1, source_target_pairs={{0,4},{2,6},{4,0},{6,2},{8,12},{10,14},{12,8},{14,10},{16,20},{18,... | collective-permute-start | bytes 2162696 | tf_op jit(solution)/shard_map/ppermute | solution.py:981
  324.7 20.6 %collective-permute-start.25 = (bf16[160,1024]{1,0:T(8,128)(2,1)}, bf16[160,1024]{1,0:T(8,128)(2,1)}, u32[]{:S(2)}, u32[]{:S(2)}) collective-permute-start(bf16[160,1024]{1,0:T(8,128)(2,1)} %get-tuple-element.222), channel_id=1, source_target_pairs={{1,0},{3,2},{5,4},{7,6},{9,8},{11,10},{13,12},{15,14},{17,16},{19,... | collective-permute-start | bytes 983048 | tf_op jit(solution)/shard_map/ppermute | solution.py:1155
  328.0 38.1 %collective-permute-start.33 = (bf16[512,512]{1,0:T(8,128)(2,1)}, bf16[512,512]{1,0:T(8,128)(2,1)S(1)}, u32[]{:S(2)}, u32[]{:S(2)}) collective-permute-start(bf16[512,512]{1,0:T(8,128)(2,1)} %get-tuple-element.247), channel_id=1, source_target_pairs={{0,1},{1,0},{2,3},{3,2},{4,5},{5,4},{6,7},{7,6},{8,9},{9,8},{10,11... | collective-permute-start | bytes 1572872 | tf_op jit(solution)/shard_map/ppermute | solution.py:981
  336.7 33.5 %collective-permute-start.31 = (bf16[512,512]{1,0:T(8,128)(2,1)}, bf16[512,512]{1,0:T(8,128)(2,1)S(1)}, u32[]{:S(2)}, u32[]{:S(2)}) collective-permute-start(bf16[512,512]{1,0:T(8,128)(2,1)} %get-tuple-element.244), channel_id=1, source_target_pairs={{0,1},{1,0},{2,3},{3,2},{4,5},{5,4},{6,7},{7,6},{8,9},{9,8},{10,11... | collective-permute-start | bytes 1572872 | tf_op jit(solution)/shard_map/ppermute | solution.py:981
  336.8 29.4 %collective-permute-start.36 = (bf16[128,1408]{1,0:T(8,128)(2,1)}, bf16[128,1408]{1,0:T(8,128)(2,1)S(1)}, u32[]{:S(2)}, u32[]{:S(2)}) collective-permute-start(bf16[128,1408]{1,0:T(8,128)(2,1)} %get-tuple-element.253), channel_id=1, source_target_pairs={{0,8},{2,10},{4,12},{6,14},{8,0},{10,2},{12,4},{14,6},{16,24},{18,... | collective-permute-start | bytes 1081352 | tf_op jit(solution)/shard_map/ppermute | solution.py:981
  345.2 22.4 %collective-permute-start.38 = (bf16[128,1408]{1,0:T(8,128)(2,1)S(1)}, bf16[128,1408]{1,0:T(8,128)(2,1)S(1)}, u32[]{:S(2)}, u32[]{:S(2)}) collective-permute-start(bf16[128,1408]{1,0:T(8,128)(2,1)S(1)} %get-tuple-element.258), channel_id=1, source_target_pairs={{0,8},{2,10},{4,12},{6,14},{8,0},{10,2},{12,4},{14,6},{16,24},{18,... | collective-permute-start | bytes 1081352 | tf_op jit(solution)/shard_map/ppermute | solution.py:981
  370.2 40.8 %collective-permute-start.43 = (bf16[128,1408]{1,0:T(8,128)(2,1)}, bf16[128,1408]{1,0:T(8,128)(2,1)}, u32[]{:S(2)}, u32[]{:S(2)}) collective-permute-start(bf16[128,1408]{1,0:T(8,128)(2,1)} %get-tuple-element.273), channel_id=1, source_target_pairs={{0,16},{2,18},{4,20},{6,22},{8,24},{10,26},{12,28},{14,30},{16,0},... | collective-permute-start | bytes 1081352 | tf_op jit(solution)/shard_map/ppermute | solution.py:981
  375.7 31.9 %collective-permute-start.40 = (bf16[128,1408]{1,0:T(8,128)(2,1)}, bf16[128,1408]{1,0:T(8,128)(2,1)}, u32[]{:S(2)}, u32[]{:S(2)}) collective-permute-start(bf16[128,1408]{1,0:T(8,128)(2,1)} %get-tuple-element.267), channel_id=1, source_target_pairs={{0,16},{2,18},{4,20},{6,22},{8,24},{10,26},{12,28},{14,30},{16,0},... | collective-permute-start | bytes 1081352 | tf_op jit(solution)/shard_map/ppermute | solution.py:981
  378.3 42.0 %collective-permute-start.39 = (bf16[256,1280]{1,0:T(8,128)(2,1)}, bf16[256,1280]{1,0:T(8,128)(2,1)S(1)}, u32[]{:S(2)}, u32[]{:S(2)}) collective-permute-start(bf16[256,1280]{1,0:T(8,128)(2,1)} %copy-done.72), channel_id=1, source_target_pairs={{0,4},{2,6},{4,0},{6,2},{8,12},{10,14},{12,8},{14,10},{16,20},{18,... | collective-permute-start | bytes 1966088 | tf_op jit(solution)/shard_map/ppermute | solution.py:981
  408.9 11.4 %collective-permute-start.46 = (bf16[128,1408]{1,0:T(8,128)(2,1)S(1)}, bf16[128,1408]{1,0:T(8,128)(2,1)S(1)}, u32[]{:S(2)}, u32[]{:S(2)}) collective-permute-start(bf16[128,1408]{1,0:T(8,128)(2,1)S(1)} %get-tuple-element.279.refs_0_), channel_id=1, source_target_pairs={{0,8},{2,10},{4,12},{6,14},{8,0},{10,2},{12,4},{14,6},{16,24},{18,... | collective-permute-start | bytes 1081352 | tf_op jit(solution)/shard_map/ppermute | solution.py:981
  409.4 17.0 %collective-permute-start.42 = (bf16[128,1408]{1,0:T(8,128)(2,1)S(1)}, bf16[128,1408]{1,0:T(8,128)(2,1)S(1)}, u32[]{:S(2)}, u32[]{:S(2)}) collective-permute-start(bf16[128,1408]{1,0:T(8,128)(2,1)S(1)} %copy-done.76), channel_id=1, source_target_pairs={{0,8},{2,10},{4,12},{6,14},{8,0},{10,2},{12,4},{14,6},{16,24},{18,... | collective-permute-start | bytes 1081352 | tf_op jit(solution)/shard_map/ppermute | solution.py:981
  411.0 16.2 %collective-permute-start.49 = (bf16[128,1408]{1,0:T(8,128)(2,1)S(1)}, bf16[128,1408]{1,0:T(8,128)(2,1)S(1)}, u32[]{:S(2)}, u32[]{:S(2)}) collective-permute-start(bf16[128,1408]{1,0:T(8,128)(2,1)S(1)} %get-tuple-element.279.refs_0_), channel_id=1, source_target_pairs={{0,2},{2,0},{4,6},{6,4},{8,10},{10,8},{12,14},{14,12},{16,18},{18,... | collective-permute-start | bytes 1081352 | tf_op jit(solution)/shard_map/ppermute | solution.py:981
  418.6 10.3 %collective-permute-start.51 = (bf16[128,1408]{1,0:T(8,128)(2,1)S(1)}, bf16[128,1408]{1,0:T(8,128)(2,1)S(1)}, u32[]{:S(2)}, u32[]{:S(2)}) collective-permute-start(bf16[128,1408]{1,0:T(8,128)(2,1)S(1)} %collective-permute-done.47.refs_2_), channel_id=1, source_target_pairs={{0,2},{2,0},{4,6},{6,4},{8,10},{10,8},{12,14},{14,12},{16,18},{18,... | collective-permute-start | bytes 1081352 | tf_op jit(solution)/shard_map/ppermute | solution.py:981
  420.3 12.1 %collective-permute-start.50 = (bf16[128,1408]{1,0:T(8,128)(2,1)S(1)}, bf16[128,1408]{1,0:T(8,128)(2,1)S(1)}, u32[]{:S(2)}, u32[]{:S(2)}) collective-permute-start(bf16[128,1408]{1,0:T(8,128)(2,1)S(1)} %collective-permute-done.46.refs_1_), channel_id=1, source_target_pairs={{0,2},{2,0},{4,6},{6,4},{8,10},{10,8},{12,14},{14,12},{16,18},{18,... | collective-permute-start | bytes 1081352 | tf_op jit(solution)/shard_map/ppermute | solution.py:981
  420.4 12.4 %collective-permute-start.48 = (bf16[128,1408]{1,0:T(8,128)(2,1)S(1)}, bf16[128,1408]{1,0:T(8,128)(2,1)S(1)}, u32[]{:S(2)}, u32[]{:S(2)}) collective-permute-start(bf16[128,1408]{1,0:T(8,128)(2,1)S(1)} %collective-permute-done.46.refs_1_), channel_id=1, source_target_pairs={{0,4},{2,6},{4,0},{6,2},{8,12},{10,14},{12,8},{14,10},{16,20},{18,... | collective-permute-start | bytes 1081352 | tf_op jit(solution)/shard_map/ppermute | solution.py:981
  426.4 16.5 %collective-permute-start.41 = (bf16[128,1280]{1,0:T(8,128)(2,1)S(1)}, bf16[128,1280]{1,0:T(8,128)(2,1)S(1)}, u32[]{:S(2)}, u32[]{:S(2)}) collective-permute-start(bf16[128,1280]{1,0:T(8,128)(2,1)S(1)} %get-tuple-element.270), channel_id=1, source_target_pairs={{0,8},{2,10},{4,12},{6,14},{8,0},{10,2},{12,4},{14,6},{16,24},{18,... | collective-permute-start | bytes 983048 | tf_op jit(solution)/shard_map/ppermute | solution.py:981
  427.2 15.8 %collective-permute-start.68 = (bf16[128,1408]{1,0:T(8,128)(2,1)S(1)}, bf16[128,1408]{1,0:T(8,128)(2,1)S(1)}, u32[]{:S(2)}, u32[]{:S(2)}) collective-permute-start(bf16[128,1408]{1,0:T(8,128)(2,1)S(1)} %get-tuple-element.285.refs_0_), channel_id=1, source_target_pairs={{0,4},{2,6},{4,0},{6,2},{8,12},{10,14},{12,8},{14,10},{16,20},{18,... | collective-permute-start | bytes 1081352 | tf_op jit(solution)/shard_map/ppermute | solution.py:981
  429.0 17.8 %collective-permute-start.45 = (bf16[128,1408]{1,0:T(8,128)(2,1)S(1)}, bf16[128,1408]{1,0:T(8,128)(2,1)S(1)}, u32[]{:S(2)}, u32[]{:S(2)}) collective-permute-start(bf16[128,1408]{1,0:T(8,128)(2,1)S(1)} %get-tuple-element.278), channel_id=1, source_target_pairs={{0,16},{2,18},{4,20},{6,22},{8,24},{10,26},{12,28},{14,30},{16,0},... | collective-permute-start | bytes 1081352 | tf_op jit(solution)/shard_map/ppermute | solution.py:981
  432.4 22.4 %collective-permute-start.67 = (bf16[128,1408]{1,0:T(8,128)(2,1)S(1)}, bf16[128,1408]{1,0:T(8,128)(2,1)S(1)}, u32[]{:S(2)}, u32[]{:S(2)}) collective-permute-start(bf16[128,1408]{1,0:T(8,128)(2,1)S(1)} %get-tuple-element.285.refs_0_), channel_id=1, source_target_pairs={{0,8},{2,10},{4,12},{6,14},{8,0},{10,2},{12,4},{14,6},{16,24},{18,... | collective-permute-start | bytes 1081352 | tf_op jit(solution)/shard_map/ppermute | solution.py:981
  432.8 22.1 %collective-permute-start.52 = (bf16[128,1408]{1,0:T(8,128)(2,1)S(1)}, bf16[128,1408]{1,0:T(8,128)(2,1)S(1)}, u32[]{:S(2)}, u32[]{:S(2)}) collective-permute-start(bf16[128,1408]{1,0:T(8,128)(2,1)S(1)} %collective-permute-done.48.refs_3_), channel_id=1, source_target_pairs={{0,2},{2,0},{4,6},{6,4},{8,10},{10,8},{12,14},{14,12},{16,18},{18,... | collective-permute-start | bytes 1081352 | tf_op jit(solution)/shard_map/ppermute | solution.py:981
  442.9 19.7 %collective-permute-start.70 = (bf16[128,1408]{1,0:T(8,128)(2,1)S(1)}, bf16[128,1408]{1,0:T(8,128)(2,1)S(1)}, u32[]{:S(2)}, u32[]{:S(2)}) collective-permute-start(bf16[128,1408]{1,0:T(8,128)(2,1)S(1)} %get-tuple-element.285.refs_0_), channel_id=1, source_target_pairs={{0,2},{2,0},{4,6},{6,4},{8,10},{10,8},{12,14},{14,12},{16,18},{18,... | collective-permute-start | bytes 1081352 | tf_op jit(solution)/shard_map/ppermute | solution.py:981
  443.0 20.3 %collective-permute-start.72 = (bf16[128,1408]{1,0:T(8,128)(2,1)S(1)}, bf16[128,1408]{1,0:T(8,128)(2,1)}, u32[]{:S(2)}, u32[]{:S(2)}) collective-permute-start(bf16[128,1408]{1,0:T(8,128)(2,1)S(1)} %collective-permute-done.68.refs_2_), channel_id=1, source_target_pairs={{0,2},{2,0},{4,6},{6,4},{8,10},{10,8},{12,14},{14,12},{16,18},{18,... | collective-permute-start | bytes 1081352 | tf_op jit(solution)/shard_map/ppermute | solution.py:981
  446.8 16.0 %collective-permute-start.44 = (bf16[128,1280]{1,0:T(8,128)(2,1)S(1)}, bf16[128,1280]{1,0:T(8,128)(2,1)S(1)}, u32[]{:S(2)}, u32[]{:S(2)}) collective-permute-start(bf16[128,1280]{1,0:T(8,128)(2,1)S(1)} %get-tuple-element.277), channel_id=1, source_target_pairs={{0,16},{2,18},{4,20},{6,22},{8,24},{10,26},{12,28},{14,30},{16,0},... | collective-permute-start | bytes 983048 | tf_op jit(solution)/shard_map/ppermute | solution.py:981
  454.8 11.1 %collective-permute-start.71 = (bf16[128,1408]{1,0:T(8,128)(2,1)S(1)}, bf16[128,1408]{1,0:T(8,128)(2,1)}, u32[]{:S(2)}, u32[]{:S(2)}) collective-permute-start(bf16[128,1408]{1,0:T(8,128)(2,1)S(1)} %collective-permute-done.67.refs_1_), channel_id=1, source_target_pairs={{0,2},{2,0},{4,6},{6,4},{8,10},{10,8},{12,14},{14,12},{16,18},{18,... | collective-permute-start | bytes 1081352 | tf_op jit(solution)/shard_map/ppermute | solution.py:981
  455.7 10.9 %collective-permute-start.69 = (bf16[128,1408]{1,0:T(8,128)(2,1)S(1)}, bf16[128,1408]{1,0:T(8,128)(2,1)}, u32[]{:S(2)}, u32[]{:S(2)}) collective-permute-start(bf16[128,1408]{1,0:T(8,128)(2,1)S(1)} %collective-permute-done.67.refs_1_), channel_id=1, source_target_pairs={{0,4},{2,6},{4,0},{6,2},{8,12},{10,14},{12,8},{14,10},{16,20},{18,... | collective-permute-start | bytes 1081352 | tf_op jit(solution)/shard_map/ppermute | solution.py:981
  462.7 11.3 %collective-permute-start.60 = (bf16[128,1408]{1,0:T(8,128)(2,1)S(1)}, bf16[128,1408]{1,0:T(8,128)(2,1)S(1)}, u32[]{:S(2)}, u32[]{:S(2)}) collective-permute-start(bf16[128,1408]{1,0:T(8,128)(2,1)S(1)} %get-tuple-element.284.refs_0_), channel_id=1, source_target_pairs={{0,8},{2,10},{4,12},{6,14},{8,0},{10,2},{12,4},{14,6},{16,24},{18,... | collective-permute-start | bytes 1081352 | tf_op jit(solution)/shard_map/ppermute | solution.py:981
  462.8 13.3 %collective-permute-start.63 = (bf16[128,1408]{1,0:T(8,128)(2,1)S(1)}, bf16[128,1408]{1,0:T(8,128)(2,1)S(1)}, u32[]{:S(2)}, u32[]{:S(2)}) collective-permute-start(bf16[128,1408]{1,0:T(8,128)(2,1)S(1)} %get-tuple-element.284.refs_0_), channel_id=1, source_target_pairs={{0,2},{2,0},{4,6},{6,4},{8,10},{10,8},{12,14},{14,12},{16,18},{18,... | collective-permute-start | bytes 1081352 | tf_op jit(solution)/shard_map/ppermute | solution.py:981
  463.3 12.8 %collective-permute-start.61 = (bf16[128,1408]{1,0:T(8,128)(2,1)S(1)}, bf16[128,1408]{1,0:T(8,128)(2,1)S(1)}, u32[]{:S(2)}, u32[]{:S(2)}) collective-permute-start(bf16[128,1408]{1,0:T(8,128)(2,1)S(1)} %get-tuple-element.284.refs_0_), channel_id=1, source_target_pairs={{0,4},{2,6},{4,0},{6,2},{8,12},{10,14},{12,8},{14,10},{16,20},{18,... | collective-permute-start | bytes 1081352 | tf_op jit(solution)/shard_map/ppermute | solution.py:981
  466.0 15.6 %collective-permute-start.54 = (bf16[128,1280]{1,0:T(8,128)(2,1)S(1)}, bf16[128,1280]{1,0:T(8,128)(2,1)S(1)}, u32[]{:S(2)}, u32[]{:S(2)}) collective-permute-start(bf16[128,1280]{1,0:T(8,128)(2,1)S(1)} %get-tuple-element.283.refs_0_), channel_id=1, source_target_pairs={{0,4},{2,6},{4,0},{6,2},{8,12},{10,14},{12,8},{14,10},{16,20},{18,... | collective-permute-start | bytes 983048 | tf_op jit(solution)/shard_map/ppermute | solution.py:981
  466.5 15.1 %collective-permute-start.53 = (bf16[128,1280]{1,0:T(8,128)(2,1)S(1)}, bf16[128,1280]{1,0:T(8,128)(2,1)S(1)}, u32[]{:S(2)}, u32[]{:S(2)}) collective-permute-start(bf16[128,1280]{1,0:T(8,128)(2,1)S(1)} %get-tuple-element.283.refs_0_), channel_id=1, source_target_pairs={{0,8},{2,10},{4,12},{6,14},{8,0},{10,2},{12,4},{14,6},{16,24},{18,... | collective-permute-start | bytes 983048 | tf_op jit(solution)/shard_map/ppermute | solution.py:981
  474.0 15.4 %collective-permute-start.62 = (bf16[128,1408]{1,0:T(8,128)(2,1)S(1)}, bf16[128,1408]{1,0:T(8,128)(2,1)}, u32[]{:S(2)}, u32[]{:S(2)}) collective-permute-start(bf16[128,1408]{1,0:T(8,128)(2,1)S(1)} %collective-permute-done.60.refs_1_), channel_id=1, source_target_pairs={{0,4},{2,6},{4,0},{6,2},{8,12},{10,14},{12,8},{14,10},{16,20},{18,... | collective-permute-start | bytes 1081352 | tf_op jit(solution)/shard_map/ppermute | solution.py:981
  476.1 13.4 %collective-permute-start.73 = (bf16[128,1408]{1,0:T(8,128)(2,1)}, bf16[128,1408]{1,0:T(8,128)(2,1)}, u32[]{:S(2)}, u32[]{:S(2)}) collective-permute-start(bf16[128,1408]{1,0:T(8,128)(2,1)} %collective-permute-done.69.refs_3_), channel_id=1, source_target_pairs={{0,2},{2,0},{4,6},{6,4},{8,10},{10,8},{12,14},{14,12},{16,18},{18,... | collective-permute-start | bytes 1081352 | tf_op jit(solution)/shard_map/ppermute | solution.py:981
  476.1 13.9 %collective-permute-start.65 = (bf16[128,1408]{1,0:T(8,128)(2,1)S(1)}, bf16[128,1408]{1,0:T(8,128)(2,1)S(1)}, u32[]{:S(2)}, u32[]{:S(2)}) collective-permute-start(bf16[128,1408]{1,0:T(8,128)(2,1)S(1)} %collective-permute-done.61.refs_2_), channel_id=1, source_target_pairs={{0,2},{2,0},{4,6},{6,4},{8,10},{10,8},{12,14},{14,12},{16,18},{18,... | collective-permute-start | bytes 1081352 | tf_op jit(solution)/shard_map/ppermute | solution.py:981
  481.6 14.5 %collective-permute-start.55 = (bf16[128,1280]{1,0:T(8,128)(2,1)S(1)}, bf16[128,1280]{1,0:T(8,128)(2,1)S(1)}, u32[]{:S(2)}, u32[]{:S(2)}) collective-permute-start(bf16[128,1280]{1,0:T(8,128)(2,1)S(1)} %collective-permute-done.53.refs_1_), channel_id=1, source_target_pairs={{0,4},{2,6},{4,0},{6,2},{8,12},{10,14},{12,8},{14,10},{16,20},{18,... | collective-permute-start | bytes 983048 | tf_op jit(solution)/shard_map/ppermute | solution.py:981
  489.4 12.2 %collective-permute-start.66 = (bf16[128,1408]{1,0:T(8,128)(2,1)}, bf16[128,1408]{1,0:T(8,128)(2,1)}, u32[]{:S(2)}, u32[]{:S(2)}) collective-permute-start(bf16[128,1408]{1,0:T(8,128)(2,1)} %collective-permute-done.62.refs_3_), channel_id=1, source_target_pairs={{0,2},{2,0},{4,6},{6,4},{8,10},{10,8},{12,14},{14,12},{16,18},{18,... | collective-permute-start | bytes 1081352 | tf_op jit(solution)/shard_map/ppermute | solution.py:981
  489.4 17.9 %collective-permute-start.56 = (bf16[128,1280]{1,0:T(8,128)(2,1)S(1)}, bf16[128,1280]{1,0:T(8,128)(2,1)S(1)}, u32[]{:S(2)}, u32[]{:S(2)}) collective-permute-start(bf16[128,1280]{1,0:T(8,128)(2,1)S(1)} %get-tuple-element.283.refs_0_), channel_id=1, source_target_pairs={{0,2},{2,0},{4,6},{6,4},{8,10},{10,8},{12,14},{14,12},{16,18},{18,... | collective-permute-start | bytes 983048 | tf_op jit(solution)/shard_map/ppermute | solution.py:981
  490.0 17.4 %collective-permute-start.57 = (bf16[128,1280]{1,0:T(8,128)(2,1)S(1)}, bf16[128,1280]{1,0:T(8,128)(2,1)S(1)}, u32[]{:S(2)}, u32[]{:S(2)}) collective-permute-start(bf16[128,1280]{1,0:T(8,128)(2,1)S(1)} %collective-permute-done.53.refs_1_), channel_id=1, source_target_pairs={{0,2},{2,0},{4,6},{6,4},{8,10},{10,8},{12,14},{14,12},{16,18},{18,... | collective-permute-start | bytes 983048 | tf_op jit(solution)/shard_map/ppermute | solution.py:981
  490.1 17.3 %collective-permute-start.58 = (bf16[128,1280]{1,0:T(8,128)(2,1)S(1)}, bf16[128,1280]{1,0:T(8,128)(2,1)S(1)}, u32[]{:S(2)}, u32[]{:S(2)}) collective-permute-start(bf16[128,1280]{1,0:T(8,128)(2,1)S(1)} %collective-permute-done.54.refs_2_), channel_id=1, source_target_pairs={{0,2},{2,0},{4,6},{6,4},{8,10},{10,8},{12,14},{14,12},{16,18},{18,... | collective-permute-start | bytes 983048 | tf_op jit(solution)/shard_map/ppermute | solution.py:981
  496.2 11.2 %collective-permute-start.59 = (bf16[128,1280]{1,0:T(8,128)(2,1)S(1)}, bf16[128,1280]{1,0:T(8,128)(2,1)S(1)}, u32[]{:S(2)}, u32[]{:S(2)}) collective-permute-start(bf16[128,1280]{1,0:T(8,128)(2,1)S(1)} %collective-permute-done.55.refs_3_), channel_id=1, source_target_pairs={{0,2},{2,0},{4,6},{6,4},{8,10},{10,8},{12,14},{14,12},{16,18},{18,... | collective-permute-start | bytes 983048 | tf_op jit(solution)/shard_map/ppermute | solution.py:981
  (140 other events, 1157.8 us)
